TPU v7x, 32 devices: a whole 2x2x4 slice. The times are simulated.
32 devices in a mesh: groups: 2 (over x), ex: 16 (over z, y, core).
Axes of the slice: x: 2, y: 2, z: 4, core: 2. Of those that a mesh axis runs over, the one named last changes fastest.
Arguments:
- inputs: bfloat16 [8192, 4096], P('ex', 'groups'), parts along dimension 1, may hold values from -6 to 6
- out_grads: bfloat16 [28672, 4096], P('ex', 'groups'), parts along dimension 1, may hold values from -6 to 6
- proj_in: bfloat16 [8192, 64], P('ex'), may hold values from -0.0625 to 0.0625
- proj_out: bfloat16 [28672, 64], P('ex'), may hold values from -0.03125 to 0.03125
- queries: bfloat16 [128, 4096], P('ex'), may hold values from -0.01171875 to 0.01171875
Outputs:
- scores: float32 [64, 128], P(('groups', 'ex')), parts along dimension 0
There are 2 independent parts, one for each index of `groups`. A program takes and returns all parts, laid end to end along the dimension named above; an argument that names none is the same for every part. Nothing has to cross between parts.
All inputs are finite; a program needn't handle non-finite values.
Results may differ from a plain program's by a relative error of at most 0.0029.
Values may be sent and summed in bfloat16 or wider, within the bound.
No kernel may reach another device: no remote copies, remote signals or barrier semaphores. Data moves between devices by JAX's collectives and lax.ppermute only.
A program may use at most 64 MiB of HBM per device.

v0:
```python
import jax
import jax.numpy as jnp
from jax import lax
from jax.sharding import PartitionSpec as P

SEQ = 64


def project_rows(features, matrix):
    return lax.dot_general(
        features, matrix, (((0,), (0,)), ((), ())), preferred_element_type=jnp.float32
    )


def shards(inputs, out_grads, proj_in, proj_out, queries):
    devices = lax.axis_size("ex")
    rank = proj_in.shape[1]
    own_rows = inputs.shape[1] // devices
    combined = lax.psum_scatter(
        jnp.concatenate([project_rows(inputs, proj_in), project_rows(out_grads, proj_out)], 1),
        "ex",
        scatter_dimension=0,
        tiled=True,
    )
    low_in = combined[:, :rank]
    low_out = combined[:, rank:]
    examples_here = own_rows // SEQ
    per_in = low_in.reshape(examples_here, SEQ, rank)
    per_out = low_out.reshape(examples_here, SEQ, rank)
    grads = jnp.einsum("nsi,nsj->nij", per_out, per_in, precision=lax.Precision.HIGHEST)
    grads = grads.reshape(examples_here, rank * rank).astype(jnp.bfloat16)
    every_grad = lax.all_gather(grads, "ex", axis=0, tiled=True)
    local_scores = jnp.dot(every_grad, queries.T, preferred_element_type=jnp.float32)
    scores = lax.all_to_all(local_scores, "ex", split_axis=0, concat_axis=1, tiled=True)
    return scores


def solution(mesh):
    return jax.shard_map(
        shards,
        mesh=mesh,
        in_specs=(
            P("ex", "groups"),
            P("ex", "groups"),
            P("ex", None),
            P("ex", None),
            P("ex", None),
        ),
        out_specs=P(("groups", "ex"), None),
        check_vma=False,
    )
```

profile of v0, /device:TPU:0, one launch (start us, length us, event | category | flops | bytes accessed | tf_op | source)
XLA Modules:
  0.0 113.6 jit_solution(7739743904777422714)
XLA Ops:
  6.5 0.0 copy-start
  6.5 0.0 copy-start.1
  6.5 0.0 reduce-scatter.2.cloned.1.call-start
  6.5 1.6 %copy-done = bf16[512,2048]{1,0:T(8,128)(2,1)S(1)} copy-done((bf16[512,2048]{1,0:T(8,128)(2,1)S(1)}, bf16[512,2048]{1,0:T(8,128)(2,1)}, u32[]{:S(2)}) %copy-start) | copy-done | bytes 2097176
  8.1 1.3 %fusion.3 = f32[2048,64]{0,1:T(8,128)S(1)} fusion(bf16[512,64]{0,1:T(8,128)(2,1)} %param.7, bf16[512,2048]{1,0:T(8,128)(2,1)S(1)} %copy-done), kind=kOutput, calls=%fused_computation.5 | convolution fusion | flops 134217728 | bytes 2686976 | tf_op jit(solution)/shard_map/dot_general | solution.py:10
  9.4 4.6 %fusion.4 = f32[2048,64]{0,1:T(8,128)S(1)} fusion(bf16[1792,64]{0,1:T(8,128)(2,1)} %param.8, bf16[1792,2048]{1,0:T(8,128)(2,1)} %param.6), kind=kOutput, calls=%fused_computation.6 | convolution fusion | flops 469762048 | bytes 8093696 | tf_op jit(solution)/shard_map/dot_general | solution.py:10
  14.1 1.0 pad_maximum_fusion
  15.1 0.0 reduce-scatter.2.cloned.1.call-update
  15.1 60.3 %reduce-scatter.2.cloned.1.call-done = f32[128,128]{0,1:T(8,128)} async-done(((f32[2048,128]{0,1:T(8,128)}), f32[128,128]{0,1:T(8,128)}) %reduce-scatter.2.cloned.1.call-update) | async-done | bytes 65552 | tf_op jit(solution)/shard_map/reduce_scatter | solution.py:19
  75.4 0.8 fusion.1
  76.2 0.1 reshape.11
  76.3 0.1 copy.18
  76.4 0.2 convolution_convert_fusion
  76.6 0.1 reshape.13
  76.7 20.1 %all-gather = bf16[16,2,4096]{2,1,0:T(2,128)(2,1)S(1)} all-gather(bf16[1,2,4096]{2,1,0:T(2,128)(2,1)S(1)} %reshape.13), channel_id=1, replica_groups=mesh['groups'=2,'ex'=16] {'ex'}, dimensions={0}, use_global_device_ids=true | all-gather | bytes 278528 | tf_op jit(solution)/shard_map/all_gather | solution.py:32
  96.7 0.1 reshape.14
  96.9 0.0 copy-done.1
  96.9 0.2 fusion.2
  97.1 9.1 %all_to_all.19 = f32[16,2,8]{2,1,0:T(2,128)S(1)} all-to-all(f32[16,2,8]{2,1,0:T(2,128)S(1)} %bitcast.14), channel_id=1, replica_groups=mesh['groups'=2,'ex'=16] {'ex'}, dimensions={0} | all-to-all | bytes 2048 | tf_op jit(solution)/shard_map/all_to_all | solution.py:34
  106.1 0.7 all_to_all.17
  (1 shorter events, 0.0 us)
Async XLA Ops:
  6.5 1.6 %copy-start = (bf16[512,2048]{1,0:T(8,128)(2,1)S(1)}, bf16[512,2048]{1,0:T(8,128)(2,1)}, u32[]{:S(2)}) copy-start(bf16[512,2048]{1,0:T(8,128)(2,1)} %param.5) | copy-start | bytes 6291460
  6.5 90.3 %copy-start.1 = (bf16[8,4096]{1,0:T(8,128)(2,1)S(1)}, bf16[8,4096]{1,0:T(8,128)(2,1)}, u32[]{:S(2)}) copy-start(bf16[8,4096]{1,0:T(8,128)(2,1)} %param.9) | copy-start | bytes 196612
  6.5 68.9 %reduce-scatter.2.cloned.1.call-start = ((), (), s32[]{:S(2)}) async-start(), calls=%async_computation.2 | async-start | bytes 1114112 | tf_op jit(solution)/shard_map/reduce_scatter | solution.py:19
Sparse Core Ops, SparseCore 0:
  15.2 60.1 reduce-scatter.1
where the time goes:
time: 114 us
  waiting for transfers between devices  60.3 us (53%)
  blocking collectives  29.1 us (26%)
  between operations  13.4 us (12%)
  matrix products  6.31 us (6%)
  local copies, waits for them, and re-layouts  3.41 us (3%)
    reduce_scatter x1, waiting for transfers between devices, shards(): lax.psum_scatter(jnp.concatenate([project_rows(inputs, proj_in), project_...  60.3 us
    all_gather x1, blocking collectives, shards(): every_grad = lax.all_gather(grads, 'ex', axis=0, tiled=True)  20.1 us
    all_to_all x1, blocking collectives, shards(): lax.all_to_all(local_scores, 'ex', split_axis=0, concat_axis=1, tiled=True)  9.08 us
    dot_general x2, matrix products, project_rows(): lax.dot_general(features, matrix, (((0,), (0,)), ((), ())), preferred_ele...  5.92 us
  transfers between devices with their start and end apart: 1, of which 1 were waited for; matrix products, arithmetic and copies ran while one was open for 0% of the time, Pallas kernels for 0%

commit v1 on v0

v1 whole, which is shorter than its diff:
```python
import functools

import jax
import jax.numpy as jnp
from jax import lax
from jax.experimental import pallas as pl
from jax.experimental.pallas import tpu as pltpu
from jax.sharding import PartitionSpec as P

SEQ = 64
VMEM_BYTES = 48 * 1024 * 1024
ROWS_BY_ROWS = (((0,), (0,)), ((), ()))
LANES_BY_LANES = (((1,), (1,)), ((), ()))


def project_kernel(
    other_core, width, x_hbm, w_hbm, p_in_hbm, p_out_hbm, out_ref, x_buf, w_buf, p_in, p_out, p_sems, x_sems, w_sems
):
    here = lax.axis_index("ex")
    blocks = out_ref.shape[0]
    rank = p_in.shape[1]
    copies = [
        pltpu.make_async_copy(p_in_hbm, p_in, p_sems.at[0]),
        pltpu.make_async_copy(p_out_hbm, p_out, p_sems.at[1]),
    ]
    for block in range(blocks):
        owner = lax.bitwise_xor(here, 2 * block + other_core)
        columns = pl.ds(pl.multiple_of(owner * width, width), width)
        place = pl.ds((block % 2) * width, width)
        copies.append(pltpu.make_async_copy(x_hbm.at[:, columns], x_buf.at[block // 2, :, place], x_sems.at[block]))
        copies.append(pltpu.make_async_copy(w_hbm.at[:, columns], w_buf.at[block // 2, :, place], w_sems.at[block]))
    for copy in copies:
        copy.start()
    copies[0].wait()
    copies[1].wait()
    p_in_t = p_in[...].T
    p_out_t = p_out[...].T
    for pair in range(blocks // 2):
        for copy in copies[2 + 4 * pair : 6 + 4 * pair]:
            copy.wait()
        low_in = jnp.dot(p_in_t, x_buf[pair], preferred_element_type=jnp.float32)
        low_out = jnp.dot(p_out_t, w_buf[pair], preferred_element_type=jnp.float32)
        for side in range(2):
            out_ref[2 * pair + side, :rank, :] = low_in[:, side * width : (side + 1) * width]
            out_ref[2 * pair + side, rank:, :] = low_out[:, side * width : (side + 1) * width]


def project(other_core, inputs, out_grads, proj_in, proj_out, devices):
    width = inputs.shape[1] // devices
    blocks = devices // 2
    rank = proj_in.shape[1]
    features, units = inputs.shape[0], out_grads.shape[0]
    hbm = pl.BlockSpec(memory_space=pltpu.HBM)
    return pl.pallas_call(
        functools.partial(project_kernel, other_core, width),
        out_shape=jax.ShapeDtypeStruct((blocks, 2 * rank, width), jnp.float32),
        in_specs=[hbm] * 4,
        out_specs=pl.BlockSpec(memory_space=pltpu.VMEM),
        scratch_shapes=[
            pltpu.VMEM((blocks // 2, features, 2 * width), jnp.bfloat16),
            pltpu.VMEM((blocks // 2, units, 2 * width), jnp.bfloat16),
            pltpu.VMEM(proj_in.shape, jnp.bfloat16),
            pltpu.VMEM(proj_out.shape, jnp.bfloat16),
            pltpu.SemaphoreType.DMA((2,)),
            pltpu.SemaphoreType.DMA((blocks,)),
            pltpu.SemaphoreType.DMA((blocks,)),
        ],
        compiler_params=pltpu.CompilerParams(vmem_limit_bytes=VMEM_BYTES),
        cost_estimate=pl.CostEstimate(
            flops=2 * (features + units) * rank * blocks * width,
            bytes_accessed=2 * (features + units) * blocks * width,
            transcendentals=0,
        ),
    )(inputs, out_grads, proj_in, proj_out)


def add_kernel(kept_ref, came_ref, *out_refs):
    for block, out_ref in enumerate(out_refs):
        out_ref[...] = (kept_ref[block] + came_ref[block]).astype(out_ref.dtype)


def add_halves(kept, came, types):
    return pl.pallas_call(
        add_kernel,
        out_shape=[jax.ShapeDtypeStruct(kept.shape[1:], dtype) for dtype in types],
        compiler_params=pltpu.CompilerParams(vmem_limit_bytes=VMEM_BYTES),
    )(kept, came)


def score_kernel(rank, *refs):
    *parts, queries_ref, out_ref, total_ref, grads_ref = refs
    total = parts[0][...]
    for part in parts[1:]:
        total = total + part[...].astype(jnp.float32)
    total_ref[...] = total
    tokens = total.shape[1]
    examples = tokens // SEQ
    low_in = total_ref[:rank, :]
    even = total_ref[pl.ds(rank, rank // 2, stride=2), :]
    odd = total_ref[pl.ds(rank + 1, rank // 2, stride=2), :]
    token = lax.broadcasted_iota(jnp.int32, (rank, tokens), 1)
    for n in range(examples):
        mine = jnp.where((token >= n * SEQ) & (token < (n + 1) * SEQ), low_in, 0.0)
        for side, rows in enumerate((even, odd)):
            grads_ref[n, :, side * rank : (side + 1) * rank] = lax.dot_general(
                rows, mine, LANES_BY_LANES, precision=lax.Precision.HIGHEST, preferred_element_type=jnp.float32
            )
    ones = jnp.ones((8, 2 * rank), jnp.float32)
    step = min(128, queries_ref.shape[0])
    for first in range(0, queries_ref.shape[0], step):
        sums = [jnp.zeros((step, 2 * rank), jnp.float32) for _ in range(examples)]
        for k in range(rank // 2):
            query = queries_ref[first : first + step, k * 2 * rank : (k + 1) * 2 * rank].astype(jnp.float32)
            for n in range(examples):
                sums[n] = sums[n] + query * grads_ref[n, k : k + 1, :]
        for n in range(examples):
            row = lax.dot_general(
                ones, sums[n], LANES_BY_LANES, precision=lax.Precision.HIGHEST, preferred_element_type=jnp.float32
            )
            out_ref[n : n + 1, first : first + step] = row[0:1, :]


def score(parts, queries, rank):
    tokens = parts[0].shape[1]
    examples = tokens // SEQ
    return pl.pallas_call(
        functools.partial(score_kernel, rank),
        out_shape=jax.ShapeDtypeStruct((examples, queries.shape[0]), jnp.float32),
        scratch_shapes=[
            pltpu.VMEM((2 * rank, tokens), jnp.float32),
            pltpu.VMEM((examples, rank // 2, 2 * rank), jnp.float32),
        ],
        compiler_params=pltpu.CompilerParams(vmem_limit_bytes=VMEM_BYTES),
    )(*parts, queries)


def shards(inputs, out_grads, proj_in, proj_out, queries):
    devices = lax.axis_size("ex")
    chips = devices // 2
    rank = proj_in.shape[1]
    every_query = lax.all_gather(queries, "ex", axis=0, tiled=True)

    def swap(array, distance):
        return lax.ppermute(array, "ex", [(i, i ^ distance) for i in range(devices)])

    given = project(1, inputs, out_grads, proj_in, proj_out, devices)
    came = swap(given, 1)
    kept = project(0, inputs, out_grads, proj_in, proj_out, devices)
    types = [jnp.float32 if block < chips // 2 else jnp.bfloat16 for block in range(chips)]
    sums = add_halves(kept, came, types)
    parts = [sums[0]] + [swap(sums[block], 2 * block) for block in range(1, chips)]
    return score(parts, every_query, rank)


def solution(mesh):
    return jax.shard_map(
        shards,
        mesh=mesh,
        in_specs=(
            P("ex", "groups"),
            P("ex", "groups"),
            P("ex", None),
            P("ex", None),
            P("ex", None),
        ),
        out_specs=P(("groups", "ex"), None),
        check_vma=False,
    )
```

time: 114 us -> 61.2 us (0.54)
  waiting for transfers between devices: 60.3 us -> 20.1 us
  blocking collectives: 29.1 us -> 0 us
  starting transfers between devices: 0.01 us -> 13.5 us
  Pallas kernels: 0 us -> 8.95 us
  matrix products: 6.31 us -> 0 us
  local copies, waits for them, and re-layouts: 3.41 us -> 4.98 us
    reduce_scatter x1 -> x0, waiting for transfers between devices: 60.3 us -> none  [shards(): lax.psum_scatter(jnp.concatenate([project_rows(inputs, proj_in), project_...]
    all_gather x1 -> x0, blocking collectives: 20.1 us -> none  [shards(): every_grad = lax.all_gather(grads, 'ex', axis=0, tiled=True)]
    all_gather x0 -> x1, waiting for transfers between devices: none -> 13.7 us  [shards(): every_query = lax.all_gather(queries, 'ex', axis=0, tiled=True)]
    ppermute x0 -> x8, starting transfers between devices: none -> 13.5 us  [swap(): lax.ppermute(array, 'ex', [(i, i ^ distance) for i in range(devices)])]
    all_to_all x1 -> x0, blocking collectives: 9.08 us -> none  [shards(): lax.all_to_all(local_scores, 'ex', split_axis=0, concat_axis=1, tiled=True)]
    pallas_call x0 -> x4, Pallas kernels: none -> 8.95 us  [the longest x2 7.26 us: project(): pl.pallas_call(functools.partial(project_kernel, other_core, width), out_...]
    dot_general x4 -> x0, matrix products: 6.31 us -> none  [the longest x2 5.92 us: project_rows(): lax.dot_general(features, matrix, (((0,), (0,)), ((), ())), preferred_ele...]
    ppermute x0 -> x8, waiting for transfers between devices: none -> 5.72 us  [swap(): lax.ppermute(array, 'ex', [(i, i ^ distance) for i in range(devices)])]
  transfers between devices with their start and end apart: 1 -> 9, of which waited for: 1 -> 3; matrix products, arithmetic and copies ran while one was open for 0% -> 4% of each run, Pallas kernels for 0% -> 12%
where the time goes in v1:
time: 61.2 us; the launch traced here: 61 us
  waiting for transfers between devices  20.1 us (33%)
  starting transfers between devices  13.5 us (22%)
  between operations  13.5 us (22%)
  Pallas kernels  8.95 us (15%)
  local copies, waits for them, and re-layouts  4.98 us (8%)
    all_gather x1, waiting for transfers between devices, shards(): every_query = lax.all_gather(queries, 'ex', axis=0, tiled=True)  13.7 us
    ppermute x8, starting transfers between devices, swap(): lax.ppermute(array, 'ex', [(i, i ^ distance) for i in range(devices)])  13.5 us
    pallas_call x2, Pallas kernels, project(): pl.pallas_call(functools.partial(project_kernel, other_core, width), out_...  7.26 us
    ppermute x8, waiting for transfers between devices, swap(): lax.ppermute(array, 'ex', [(i, i ^ distance) for i in range(devices)])  5.72 us
    unnamed x6, local copies, waits for them, and re-layouts  4.98 us
    pallas_call x1, Pallas kernels, score(): pl.pallas_call(functools.partial(score_kernel, rank), out_shape=jax.Shape...  1.63 us
  transfers between devices with their start and end apart: 9, of which 3 were waited for; matrix products, arithmetic and copies ran while one was open for 4% of the time, Pallas kernels for 12%

profile of v1, /device:TPU:0, one launch (start us, length us, event | category | flops | bytes accessed | tf_op | source)
XLA Modules:
  0.0 61.0 jit_solution(13466916123536493013)
XLA Ops:
  6.5 0.0 all-gather.2.cloned.1.call-start
  6.5 0.7 %all-gather.2.cloned.1.call-update = ((bf16[8,4096]{1,0:T(8,128)(2,1)}), bf16[128,4096]{1,0:T(8,128)(2,1)}) async-update(((), (), s32[]{:S(2)}) %all-gather.2.cloned.1.call-start, bf16[8,4096]{1,0:T(8,128)(2,1)} %param.9) | async-update | bytes 1179672
  7.3 1.0 %copy.6.p_in_hbm = bf16[512,64]{1,0:T(8,128)(2,1)S(1)} copy(bf16[512,64]{0,1:T(8,128)(2,1)} %param.7) | data formatting | bytes 131072 | tf_op args[2]
  8.2 1.2 %copy.7.p_out_hbm = bf16[1792,64]{1,0:T(8,128)(2,1)S(1)} copy(bf16[1792,64]{0,1:T(8,128)(2,1)} %param.8) | data formatting | bytes 458752 | tf_op args[3]
  9.4 0.0 copy-start
  9.4 1.6 %copy-done = bf16[512,2048]{1,0:T(8,128)(2,1)S(1)} copy-done((bf16[512,2048]{1,0:T(8,128)(2,1)S(1)}, bf16[512,2048]{1,0:T(8,128)(2,1)}, u32[]{:S(2)}) %copy-start) | copy-done | bytes 2097176
  11.0 3.6 %shard_map.56 = f32[8,128,128]{2,1,0:T(8,128)S(1)} custom-call(bf16[512,2048]{1,0:T(8,128)(2,1)S(1)} %copy-done, bf16[1792,2048]{1,0:T(8,128)(2,1)} %w_hbm.3, bf16[512,64]{1,0:T(8,128)(2,1)S(1)} %copy.6.p_in_hbm, bf16[1792,64]{1,0:T(8,128)(2,1)S(1)} %copy.7.p_out_hbm), custom_call_target="tpu_custom_call" | custom-call | flops 301989888 | bytes 4718592 | tf_op jit(solution)/shard_map/pallas_call | solution.py:54
  14.7 0.5 collective-permute-start
  15.2 3.6 %shard_map.55.kept_ref = f32[8,128,128]{2,1,0:T(8,128)S(1)} custom-call(bf16[512,2048]{1,0:T(8,128)(2,1)S(1)} %copy-done, bf16[1792,2048]{1,0:T(8,128)(2,1)} %w_hbm.3, bf16[512,64]{1,0:T(8,128)(2,1)S(1)} %copy.6.p_in_hbm, bf16[1792,64]{1,0:T(8,128)(2,1)S(1)} %copy.7.p_out_hbm), custom_call_target="tpu_custom_call" | custom-call | flops 301989888 | bytes 4718592 | tf_op jit(solution)/shard_map/pallas_call | solution.py:54
  18.8 0.0 collective-permute-done.came_ref
  18.8 0.1 shard_map.57
  18.9 3.7 %collective-permute-start.4 = (bf16[128,128]{1,0:T(8,128)(2,1)S(1)}, bf16[128,128]{1,0:T(8,128)(2,1)S(1)}, u32[]{:S(2)}, u32[]{:S(2)}) collective-permute-start(bf16[128,128]{1,0:T(8,128)(2,1)S(1)} %get-tuple-element.17), channel_id=1, source_target_pairs={{0,8},{1,9},{2,10},{3,11},{4,12},{5,13},{6,14},{7,15},{8,0},{9,1},... | collective-permute-start | bytes 98312 | tf_op jit(solution)/shard_map/ppermute | solution.py:144
  22.6 1.3 %collective-permute-start.5 = (bf16[128,128]{1,0:T(8,128)(2,1)S(1)}, bf16[128,128]{1,0:T(8,128)(2,1)S(1)}, u32[]{:S(2)}, u32[]{:S(2)}) collective-permute-start(bf16[128,128]{1,0:T(8,128)(2,1)S(1)} %get-tuple-element.18), channel_id=1, source_target_pairs={{0,10},{1,11},{2,8},{3,9},{4,14},{5,15},{6,12},{7,13},{8,2},{9,3},... | collective-permute-start | bytes 98312 | tf_op jit(solution)/shard_map/ppermute | solution.py:144
  23.9 0.2 collective-permute-start.1
  24.2 1.8 %collective-permute-start.2 = (f32[128,128]{1,0:T(8,128)S(1)}, f32[128,128]{1,0:T(8,128)S(1)}, u32[]{:S(2)}, u32[]{:S(2)}) collective-permute-start(f32[128,128]{1,0:T(8,128)S(1)} %get-tuple-element.15), channel_id=1, source_target_pairs={{0,4},{1,5},{2,6},{3,7},{4,0},{5,1},{6,2},{7,3},{8,12},{9,13},{10,... | collective-permute-start | bytes 196616 | tf_op jit(solution)/shard_map/ppermute | solution.py:144
  26.0 1.4 %collective-permute-start.3 = (f32[128,128]{1,0:T(8,128)S(1)}, f32[128,128]{1,0:T(8,128)S(1)}, u32[]{:S(2)}, u32[]{:S(2)}) collective-permute-start(f32[128,128]{1,0:T(8,128)S(1)} %get-tuple-element.16), channel_id=1, source_target_pairs={{0,6},{1,7},{2,4},{3,5},{4,2},{5,3},{6,0},{7,1},{8,14},{9,15},{10,... | collective-permute-start | bytes 196616 | tf_op jit(solution)/shard_map/ppermute | solution.py:144
  27.4 0.0 collective-permute-done.4.refs_4_
  27.4 3.6 %collective-permute-start.6 = (bf16[128,128]{1,0:T(8,128)(2,1)S(1)}, bf16[128,128]{1,0:T(8,128)(2,1)S(1)}, u32[]{:S(2)}, u32[]{:S(2)}) collective-permute-start(bf16[128,128]{1,0:T(8,128)(2,1)S(1)} %get-tuple-element.19), channel_id=1, source_target_pairs={{0,12},{1,13},{2,14},{3,15},{4,8},{5,9},{6,10},{7,11},{8,4},{9,5},... | collective-permute-start | bytes 98312 | tf_op jit(solution)/shard_map/ppermute | solution.py:144
  31.0 0.0 collective-permute-done.5.refs_5_
  31.0 0.9 %collective-permute-start.7 = (bf16[128,128]{1,0:T(8,128)(2,1)S(1)}, bf16[128,128]{1,0:T(8,128)(2,1)S(1)}, u32[]{:S(2)}, u32[]{:S(2)}) collective-permute-start(bf16[128,128]{1,0:T(8,128)(2,1)S(1)} %get-tuple-element.20), channel_id=1, source_target_pairs={{0,14},{1,15},{2,12},{3,13},{4,10},{5,11},{6,8},{7,9},{8,6},{9,7},... | collective-permute-start | bytes 98312 | tf_op jit(solution)/shard_map/ppermute | solution.py:144
  31.9 1.8 %collective-permute-done.6.refs_6_ = bf16[128,128]{1,0:T(8,128)(2,1)S(1)} collective-permute-done((bf16[128,128]{1,0:T(8,128)(2,1)S(1)}, bf16[128,128]{1,0:T(8,128)(2,1)S(1)}, u32[]{:S(2)}, u32[]{:S(2)}) %collective-permute-start.6) | collective-permute-done | bytes 32800 | tf_op jit(solution)/shard_map/ppermute | solution.py:144
  33.7 3.9 %collective-permute-done.7.refs_7_ = bf16[128,128]{1,0:T(8,128)(2,1)S(1)} collective-permute-done((bf16[128,128]{1,0:T(8,128)(2,1)S(1)}, bf16[128,128]{1,0:T(8,128)(2,1)S(1)}, u32[]{:S(2)}, u32[]{:S(2)}) %collective-permute-start.7) | collective-permute-done | bytes 32800 | tf_op jit(solution)/shard_map/ppermute | solution.py:144
  37.6 0.0 collective-permute-done.1.refs_1_
  37.6 0.0 collective-permute-done.2.refs_2_
  37.6 0.0 collective-permute-done.3.refs_3_
  37.6 13.7 %all-gather.2.cloned.1.call-done.refs_8_ = bf16[128,4096]{1,0:T(8,128)(2,1)} async-done(((bf16[8,4096]{1,0:T(8,128)(2,1)}), bf16[128,4096]{1,0:T(8,128)(2,1)}) %all-gather.2.cloned.1.call-update) | async-done | bytes 1048592 | tf_op jit(solution)/shard_map/all_gather | solution.py:141
  51.3 0.0 copy-start.1
  51.3 1.2 %copy-done.1 = bf16[128,4096]{1,0:T(8,128)(2,1)S(1)} copy-done((bf16[128,4096]{1,0:T(8,128)(2,1)S(1)}, bf16[128,4096]{1,0:T(8,128)(2,1)}, u32[]{:S(2)}) %copy-start.1) | copy-done | bytes 1048600
  52.5 1.6 %shard_map.58 = f32[2,128]{1,0:T(2,128)} custom-call(f32[128,128]{1,0:T(8,128)S(1)} %get-tuple-element.13.refs_0_, f32[128,128]{1,0:T(8,128)S(1)} %collective-permute-done.1.refs_1_, f32[128,128]{1,0:T(8,128)S(1)} %collective-permute-done.2.refs_2_, f32[128,128]{1,0:T(8,128)S(1)} %collective-permute-done.3.refs_3_, ...), custom_call_target="tpu_custom_call" | custom-call | tf_op jit(solution)/shard_map/pallas_call | solution.py:126
Async XLA Ops:
  6.5 44.7 %all-gather.2.cloned.1.call-start = ((), (), s32[]{:S(2)}) async-start(), calls=%async_computation | async-start | bytes 1114112 | tf_op jit(solution)/shard_map/all_gather | solution.py:141
  9.4 1.6 %copy-start = (bf16[512,2048]{1,0:T(8,128)(2,1)S(1)}, bf16[512,2048]{1,0:T(8,128)(2,1)}, u32[]{:S(2)}) copy-start(bf16[512,2048]{1,0:T(8,128)(2,1)} %x_hbm.3) | copy-start | bytes 6291460
  14.7 4.2 %collective-permute-start = (f32[8,128,128]{2,1,0:T(8,128)S(1)}, f32[8,128,128]{2,1,0:T(8,128)S(1)}, u32[]{:S(2)}, u32[]{:S(2)}) collective-permute-start(f32[8,128,128]{2,1,0:T(8,128)S(1)} %shard_map.56), channel_id=1, source_target_pairs={{0,1},{1,0},{2,3},{3,2},{4,5},{5,4},{6,7},{7,6},{8,9},{9,8},{10,11... | collective-permute-start | bytes 1572872 | tf_op jit(solution)/shard_map/ppermute | solution.py:144
  18.9 8.5 %collective-permute-start.4 = (bf16[128,128]{1,0:T(8,128)(2,1)S(1)}, bf16[128,128]{1,0:T(8,128)(2,1)S(1)}, u32[]{:S(2)}, u32[]{:S(2)}) collective-permute-start(bf16[128,128]{1,0:T(8,128)(2,1)S(1)} %get-tuple-element.17), channel_id=1, source_target_pairs={{0,8},{1,9},{2,10},{3,11},{4,12},{5,13},{6,14},{7,15},{8,0},{9,1},... | collective-permute-start | bytes 98312 | tf_op jit(solution)/shard_map/ppermute | solution.py:144
  22.6 8.4 %collective-permute-start.5 = (bf16[128,128]{1,0:T(8,128)(2,1)S(1)}, bf16[128,128]{1,0:T(8,128)(2,1)S(1)}, u32[]{:S(2)}, u32[]{:S(2)}) collective-permute-start(bf16[128,128]{1,0:T(8,128)(2,1)S(1)} %get-tuple-element.18), channel_id=1, source_target_pairs={{0,10},{1,11},{2,8},{3,9},{4,14},{5,15},{6,12},{7,13},{8,2},{9,3},... | collective-permute-start | bytes 98312 | tf_op jit(solution)/shard_map/ppermute | solution.py:144
  23.9 13.7 %collective-permute-start.1 = (f32[128,128]{1,0:T(8,128)S(1)}, f32[128,128]{1,0:T(8,128)S(1)}, u32[]{:S(2)}, u32[]{:S(2)}) collective-permute-start(f32[128,128]{1,0:T(8,128)S(1)} %get-tuple-element.14), channel_id=1, source_target_pairs={{0,2},{1,3},{2,0},{3,1},{4,6},{5,7},{6,4},{7,5},{8,10},{9,11},{10,... | collective-permute-start | bytes 196616 | tf_op jit(solution)/shard_map/ppermute | solution.py:144
  24.2 13.5 %collective-permute-start.2 = (f32[128,128]{1,0:T(8,128)S(1)}, f32[128,128]{1,0:T(8,128)S(1)}, u32[]{:S(2)}, u32[]{:S(2)}) collective-permute-start(f32[128,128]{1,0:T(8,128)S(1)} %get-tuple-element.15), channel_id=1, source_target_pairs={{0,4},{1,5},{2,6},{3,7},{4,0},{5,1},{6,2},{7,3},{8,12},{9,13},{10,... | collective-permute-start | bytes 196616 | tf_op jit(solution)/shard_map/ppermute | solution.py:144
  26.0 11.6 %collective-permute-start.3 = (f32[128,128]{1,0:T(8,128)S(1)}, f32[128,128]{1,0:T(8,128)S(1)}, u32[]{:S(2)}, u32[]{:S(2)}) collective-permute-start(f32[128,128]{1,0:T(8,128)S(1)} %get-tuple-element.16), channel_id=1, source_target_pairs={{0,6},{1,7},{2,4},{3,5},{4,2},{5,3},{6,0},{7,1},{8,14},{9,15},{10,... | collective-permute-start | bytes 196616 | tf_op jit(solution)/shard_map/ppermute | solution.py:144
  27.4 6.3 %collective-permute-start.6 = (bf16[128,128]{1,0:T(8,128)(2,1)S(1)}, bf16[128,128]{1,0:T(8,128)(2,1)S(1)}, u32[]{:S(2)}, u32[]{:S(2)}) collective-permute-start(bf16[128,128]{1,0:T(8,128)(2,1)S(1)} %get-tuple-element.19), channel_id=1, source_target_pairs={{0,12},{1,13},{2,14},{3,15},{4,8},{5,9},{6,10},{7,11},{8,4},{9,5},... | collective-permute-start | bytes 98312 | tf_op jit(solution)/shard_map/ppermute | solution.py:144
  31.0 6.6 %collective-permute-start.7 = (bf16[128,128]{1,0:T(8,128)(2,1)S(1)}, bf16[128,128]{1,0:T(8,128)(2,1)S(1)}, u32[]{:S(2)}, u32[]{:S(2)}) collective-permute-start(bf16[128,128]{1,0:T(8,128)(2,1)S(1)} %get-tuple-element.20), channel_id=1, source_target_pairs={{0,14},{1,15},{2,12},{3,13},{4,10},{5,11},{6,8},{7,9},{8,6},{9,7},... | collective-permute-start | bytes 98312 | tf_op jit(solution)/shard_map/ppermute | solution.py:144
  51.3 1.2 %copy-start.1 = (bf16[128,4096]{1,0:T(8,128)(2,1)S(1)}, bf16[128,4096]{1,0:T(8,128)(2,1)}, u32[]{:S(2)}) copy-start(bf16[128,4096]{1,0:T(8,128)(2,1)} %all-gather.2.cloned.1.call-done.refs_8_) | copy-start | bytes 3145732
Sparse Core Ops, SparseCore 0:
  9.5 41.7 all-gather.1

commit v2 on v1

v2 whole, which is shorter than its diff:
```python
import functools

import jax
import jax.numpy as jnp
from jax import lax
from jax.experimental import pallas as pl
from jax.experimental.pallas import tpu as pltpu
from jax.sharding import PartitionSpec as P

SEQ = 64
VMEM_BYTES = 48 * 1024 * 1024
LANES_BY_LANES = (((1,), (1,)), ((), ()))


def project_kernel(
    other_core, width, x_hbm, w_hbm, p_in_hbm, p_out_hbm, out_ref, x_buf, w_buf, p_in, p_out, p_sems, x_sems, w_sems
):
    core = lax.rem(lax.axis_index("ex") + other_core, 2)
    blocks = out_ref.shape[0]
    rank = p_in.shape[0]
    copies = [
        pltpu.make_async_copy(p_in_hbm, p_in, p_sems.at[0]),
        pltpu.make_async_copy(p_out_hbm, p_out, p_sems.at[1]),
    ]
    for block in range(blocks):
        columns = pl.ds(pl.multiple_of((2 * block + core) * width, width), width)
        place = pl.ds((block % 2) * width, width)
        copies.append(pltpu.make_async_copy(x_hbm.at[:, columns], x_buf.at[block // 2, :, place], x_sems.at[block]))
        copies.append(pltpu.make_async_copy(w_hbm.at[:, columns], w_buf.at[block // 2, :, place], w_sems.at[block]))
    for copy in copies:
        copy.start()
    copies[0].wait()
    copies[1].wait()
    for pair in range(blocks // 2):
        for copy in copies[2 + 4 * pair : 6 + 4 * pair]:
            copy.wait()
        low_in = jnp.dot(p_in[...], x_buf[pair], preferred_element_type=jnp.float32)
        low_out = jnp.dot(p_out[...], w_buf[pair], preferred_element_type=jnp.float32)
        for side in range(2):
            out_ref[2 * pair + side, :rank, :] = low_in[:, side * width : (side + 1) * width]
            out_ref[2 * pair + side, rank:, :] = low_out[:, side * width : (side + 1) * width]


def project(other_core, inputs, out_grads, proj_in_t, proj_out_t, devices):
    width = inputs.shape[1] // devices
    blocks = devices // 2
    rank = proj_in_t.shape[0]
    features, units = inputs.shape[0], out_grads.shape[0]
    hbm = pl.BlockSpec(memory_space=pltpu.HBM)
    return pl.pallas_call(
        functools.partial(project_kernel, other_core, width),
        out_shape=jax.ShapeDtypeStruct((blocks, 2 * rank, width), jnp.float32),
        in_specs=[hbm] * 4,
        out_specs=pl.BlockSpec(memory_space=pltpu.VMEM),
        scratch_shapes=[
            pltpu.VMEM((blocks // 2, features, 2 * width), jnp.bfloat16),
            pltpu.VMEM((blocks // 2, units, 2 * width), jnp.bfloat16),
            pltpu.VMEM(proj_in_t.shape, jnp.bfloat16),
            pltpu.VMEM(proj_out_t.shape, jnp.bfloat16),
            pltpu.SemaphoreType.DMA((2,)),
            pltpu.SemaphoreType.DMA((blocks,)),
            pltpu.SemaphoreType.DMA((blocks,)),
        ],
        compiler_params=pltpu.CompilerParams(vmem_limit_bytes=VMEM_BYTES),
        cost_estimate=pl.CostEstimate(
            flops=2 * (features + units) * rank * blocks * width,
            bytes_accessed=2 * (features + units) * blocks * width,
            transcendentals=0,
        ),
    )(inputs, out_grads, proj_in_t, proj_out_t)


def add_kernel(rank, kept_ref, came_ref, out_ref):
    total = kept_ref[...] + came_ref[...]
    low_in = total[:, :rank, :]
    high = low_in.astype(jnp.bfloat16)
    out_ref[:, :rank, :] = high
    out_ref[:, rank : 2 * rank, :] = total[:, rank:, :].astype(jnp.bfloat16)
    out_ref[:, 2 * rank :, :] = (low_in - high.astype(jnp.float32)).astype(jnp.bfloat16)


def add_halves(kept, came, rank):
    blocks, _, width = kept.shape
    return pl.pallas_call(
        functools.partial(add_kernel, rank),
        out_shape=jax.ShapeDtypeStruct((blocks, 3 * rank, width), jnp.bfloat16),
        compiler_params=pltpu.CompilerParams(vmem_limit_bytes=VMEM_BYTES),
    )(kept, came)


def score_kernel(parts_ref, own_ref, other_ref, out_ref, out_t_ref, grads_ref, sums_ref):
    rank = parts_ref.shape[1] // 3
    tokens = parts_ref.shape[2]
    examples = tokens // SEQ
    core = lax.rem(lax.axis_index("ex"), 2)
    total = jnp.sum(parts_ref[...].astype(jnp.float32), axis=0)
    low_in = total[:rank, :] + total[2 * rank :, :]
    out_t_ref[...] = total[rank : 2 * rank, :]
    even = out_t_ref[pl.ds(0, rank // 2, stride=2), :]
    odd = out_t_ref[pl.ds(1, rank // 2, stride=2), :]
    token = lax.broadcasted_iota(jnp.int32, (rank, tokens), 1)
    for n in range(examples):
        mine = jnp.where((token >= n * SEQ) & (token < (n + 1) * SEQ), low_in, 0.0)
        for side, rows in enumerate((even, odd)):
            grads_ref[n, :, side * rank : (side + 1) * rank] = lax.dot_general(
                rows, mine, LANES_BY_LANES, precision=lax.Precision.HIGHEST, preferred_element_type=jnp.float32
            )
    chips, held = sums_ref.shape[1], sums_ref.shape[3]
    for offset, queries_ref in enumerate((own_ref, other_ref)):
        place = lax.rem(core + offset, 2)
        step = min(8, chips)
        for first in range(0, chips, step):
            sums = [jnp.zeros((step * held, 2 * rank), jnp.float32) for _ in range(examples)]
            for k in range(rank // 2):
                query = queries_ref[first * held : (first + step) * held, k * 2 * rank : (k + 1) * 2 * rank]
                query = query.astype(jnp.float32)
                for n in range(examples):
                    sums[n] = sums[n] + query * grads_ref[n, k : k + 1, :]
            for n in range(examples):
                sums_ref[n, first : first + step, place] = sums[n].reshape(step, held, 2 * rank)
    ones = jnp.ones((8, 2 * rank), jnp.float32)
    for n in range(examples):
        row = lax.dot_general(
            ones,
            sums_ref[n].reshape(chips * 2 * held, 2 * rank),
            LANES_BY_LANES,
            precision=lax.Precision.HIGHEST,
            preferred_element_type=jnp.float32,
        )
        out_ref[n : n + 1, :] = row[0:1, :]


def score(parts, own_queries, other_queries):
    chips, rows, tokens = parts.shape
    rank = rows // 3
    examples = tokens // SEQ
    held = own_queries.shape[0] // chips
    return pl.pallas_call(
        score_kernel,
        out_shape=jax.ShapeDtypeStruct((examples, 2 * own_queries.shape[0]), jnp.float32),
        scratch_shapes=[
            pltpu.VMEM((rank, tokens), jnp.float32),
            pltpu.VMEM((examples, rank // 2, 2 * rank), jnp.float32),
            pltpu.VMEM((examples, chips, 2, held, 2 * rank), jnp.float32),
        ],
        compiler_params=pltpu.CompilerParams(vmem_limit_bytes=VMEM_BYTES),
    )(parts, own_queries, other_queries)


def shards(inputs, out_grads, proj_in, proj_out, queries):
    devices = lax.axis_size("ex")
    rank = proj_in.shape[1]
    same_core = [list(range(core, devices, 2)) for core in range(2)]
    other_core = [(i, i ^ 1) for i in range(devices)]
    own_queries = lax.all_gather(queries, "ex", axis=0, tiled=True, axis_index_groups=same_core)
    inputs = pltpu.with_memory_space_constraint(inputs, pltpu.HBM)
    out_grads = pltpu.with_memory_space_constraint(out_grads, pltpu.HBM)
    given = project(1, inputs, out_grads, proj_in.T, proj_out.T, devices)
    came = lax.ppermute(given, "ex", other_core)
    kept = project(0, inputs, out_grads, proj_in.T, proj_out.T, devices)
    sums = add_halves(kept, came, rank)
    parts = lax.all_to_all(sums, "ex", split_axis=0, concat_axis=0, tiled=True, axis_index_groups=same_core)
    own_queries, parts = lax.optimization_barrier((own_queries, parts))
    other_queries = lax.ppermute(own_queries, "ex", other_core)
    return score(parts, own_queries, other_queries)


def solution(mesh):
    return jax.shard_map(
        shards,
        mesh=mesh,
        in_specs=(
            P("ex", "groups"),
            P("ex", "groups"),
            P("ex", None),
            P("ex", None),
            P("ex", None),
        ),
        out_specs=P(("groups", "ex"), None),
        check_vma=False,
    )
```

time: 61.2 us -> 58 us (0.948)
  blocking collectives: 0 us -> 36.8 us
  waiting for transfers between devices: 20.1 us -> 1.91 us
  between operations: 13.5 us -> 0.04 us
  starting transfers between devices: 13.5 us -> 7.41 us
  local copies, waits for them, and re-layouts: 4.98 us -> 1.78 us
  Pallas kernels: 8.95 us -> 9.79 us
    all_gather x0 -> x1, blocking collectives: none -> 36.8 us  [shards(): lax.all_gather(queries, 'ex', axis=0, tiled=True, axis_index_groups=same_...]
    all_gather x1 -> x0, waiting for transfers between devices: 13.7 us -> none  [shards(): every_query = lax.all_gather(queries, 'ex', axis=0, tiled=True)]
    ppermute x8 -> x2, starting transfers between devices: 13.5 us -> 0.52 us  [the longest x1 0.52 us: shards(): came = lax.ppermute(given, 'ex', other_core)]
    all_to_all x0 -> x1, starting transfers between devices: none -> 6.89 us  [shards(): lax.all_to_all(sums, 'ex', split_axis=0, concat_axis=0, tiled=True, axis_...]
    ppermute x8 -> x2, waiting for transfers between devices: 5.72 us -> 1.91 us  [the longest x1 1.91 us: shards(): other_queries = lax.ppermute(own_queries, 'ex', other_core)]
    unnamed x6, local copies, waits for them, and re-layouts: 4.98 us -> 1.78 us
    pallas_call x2, Pallas kernels: 1.69 us -> 2.5 us  [the longest x1 1.68 us: score(): pl.pallas_call(score_kernel, out_shape=jax.ShapeDtypeStruct((examples, 2...]
    unnamed x1 -> x0, waiting for transfers between devices: 0.71 us -> none
  transfers between devices with their start and end apart: 9 -> 3, of which waited for: 3 -> 1; matrix products, arithmetic and copies ran while one was open for 4% -> 0% of each run, Pallas kernels for 12% -> 6%
where the time goes in v2:
time: 58 us; the launch traced here: 57.7 us
  blocking collectives  36.8 us (63%)
  Pallas kernels  9.79 us (17%)
  starting transfers between devices  7.41 us (13%)
  waiting for transfers between devices  1.91 us (3%)
  local copies, waits for them, and re-layouts  1.78 us (3%)
    all_gather x1, blocking collectives, shards(): lax.all_gather(queries, 'ex', axis=0, tiled=True, axis_index_groups=same_...  36.8 us
    pallas_call x2, Pallas kernels, project(): pl.pallas_call(functools.partial(project_kernel, other_core, width), out_...  7.29 us
    all_to_all x1, starting transfers between devices, shards(): lax.all_to_all(sums, 'ex', split_axis=0, concat_axis=0, tiled=True, axis_...  6.89 us
    ppermute x1, waiting for transfers between devices, shards(): other_queries = lax.ppermute(own_queries, 'ex', other_core)  1.91 us
    unnamed x6, local copies, waits for them, and re-layouts  1.78 us
    pallas_call x1, Pallas kernels, score(): pl.pallas_call(score_kernel, out_shape=jax.ShapeDtypeStruct((examples, 2...  1.68 us
  transfers between devices with their start and end apart: 3, of which 1 were waited for; matrix products, arithmetic and copies ran while one was open for 0% of the time, Pallas kernels for 6%

profile of v2, /device:TPU:0, one launch (start us, length us, event | category | flops | bytes accessed | tf_op | source)
XLA Modules:
  0.0 57.7 jit_solution(9084335576534048599)
XLA Ops:
  0.0 0.0 copy-start
  0.0 0.9 %copy-done = bf16[1792,64]{0,1:T(8,128)(2,1)S(1)} copy-done((bf16[1792,64]{0,1:T(8,128)(2,1)S(1)}, bf16[1792,64]{0,1:T(8,128)(2,1)}, u32[]{:S(2)}) %copy-start) | copy-done | bytes 229400
  0.9 0.0 copy-start.1
  0.9 0.8 %copy-done.1 = bf16[512,64]{0,1:T(8,128)(2,1)S(1)} copy-done((bf16[512,64]{0,1:T(8,128)(2,1)S(1)}, bf16[512,64]{0,1:T(8,128)(2,1)}, u32[]{:S(2)}) %copy-start.1) | copy-done | bytes 65560
  1.8 3.6 %shard_map.56 = f32[8,128,128]{2,1,0:T(8,128)S(1)} custom-call(bf16[512,2048]{1,0:T(8,128)(2,1)} %x_hbm.3, bf16[1792,2048]{1,0:T(8,128)(2,1)} %w_hbm.3, bf16[64,512]{1,0:T(8,128)(2,1)S(1)} %bitcast.4, bf16[64,1792]{1,0:T(8,128)(2,1)S(1)} %bitcast.2), custom_call_target="tpu_custom_call" | custom-call | flops 301989888 | bytes 4718592 | tf_op jit(solution)/shard_map/pallas_call | solution.py:50
  5.4 0.0 copy-start.2
  5.4 0.5 collective-permute-start
  6.0 3.6 %shard_map.55.kept_ref = f32[8,128,128]{2,1,0:T(8,128)S(1)} custom-call(bf16[512,2048]{1,0:T(8,128)(2,1)} %x_hbm.3, bf16[1792,2048]{1,0:T(8,128)(2,1)} %w_hbm.3, bf16[64,512]{1,0:T(8,128)(2,1)S(1)} %bitcast.5, bf16[64,1792]{1,0:T(8,128)(2,1)S(1)} %bitcast.3), custom_call_target="tpu_custom_call" | custom-call | flops 301989888 | bytes 4718592 | tf_op jit(solution)/shard_map/pallas_call | solution.py:50
  9.6 0.0 collective-permute-done.came_ref
  9.6 0.8 %shard_map.57 = bf16[8,192,128]{2,1,0:T(8,128)(2,1)} custom-call(f32[8,128,128]{2,1,0:T(8,128)S(1)} %shard_map.55.kept_ref, f32[8,128,128]{2,1,0:T(8,128)S(1)} %collective-permute-done.came_ref), custom_call_target="tpu_custom_call" | custom-call | tf_op jit(solution)/shard_map/pallas_call | solution.py:84
  10.4 6.9 %all-to-all-start = ((bf16[8,192,128]{2,1,0:T(8,128)(2,1)}), bf16[8,192,128]{2,1,0:T(8,128)(2,1)S(1)}, u32[]{:S(2)}, u32[]{:S(2)}) async-start(bf16[8,192,128]{2,1,0:T(8,128)(2,1)} %shard_map.57), calls=%async_computation | async-start | bytes 786432 | tf_op jit(solution)/shard_map/all_to_all | solution.py:162
  17.3 0.0 copy-done.2
  17.3 36.8 %all_gather.3.own_ref = bf16[64,4096]{1,0:T(8,128)(2,1)S(1)} all-gather(bf16[8,4096]{1,0:T(8,128)(2,1)S(1)} %copy-done.2), channel_id=1, replica_groups={{0,2,4,6,8,10,12,14},{1,3,5,7,9,11,13,15},{16,18,20,22,24,26,28,30},{17..., dimensions={0}, use_global_device_ids=true | all-gather | bytes 589824 | tf_op jit(solution)/shard_map/all_gather | solution.py:155
  54.1 0.0 all-to-all-done.parts_ref
  54.1 0.0 collective-permute-start.1
  54.1 1.9 %collective-permute-done.1.other_ref = bf16[64,4096]{1,0:T(8,128)(2,1)S(1)} collective-permute-done((bf16[64,4096]{1,0:T(8,128)(2,1)S(1)}, bf16[64,4096]{1,0:T(8,128)(2,1)S(1)}, u32[]{:S(2)}, u32[]{:S(2)}) %collective-permute-start.1) | collective-permute-done | bytes 524320 | tf_op jit(solution)/shard_map/ppermute | solution.py:164
  56.0 1.7 %shard_map.58 = f32[2,128]{1,0:T(2,128)} custom-call(bf16[8,192,128]{2,1,0:T(8,128)(2,1)S(1)} %all-to-all-done.parts_ref, bf16[64,4096]{1,0:T(8,128)(2,1)S(1)} %all_gather.3.own_ref, bf16[64,4096]{1,0:T(8,128)(2,1)S(1)} %collective-permute-done.1.other_ref), custom_call_target="tpu_custom_call" | custom-call | tf_op jit(solution)/shard_map/pallas_call | solution.py:138
Async XLA Ops:
  0.0 0.9 %copy-start = (bf16[1792,64]{0,1:T(8,128)(2,1)S(1)}, bf16[1792,64]{0,1:T(8,128)(2,1)}, u32[]{:S(2)}) copy-start(bf16[1792,64]{0,1:T(8,128)(2,1)} %param.8) | copy-start | bytes 688132
  0.9 0.8 %copy-start.1 = (bf16[512,64]{0,1:T(8,128)(2,1)S(1)}, bf16[512,64]{0,1:T(8,128)(2,1)}, u32[]{:S(2)}) copy-start(bf16[512,64]{0,1:T(8,128)(2,1)} %param.7) | copy-start | bytes 196612
  5.4 11.9 %copy-start.2 = (bf16[8,4096]{1,0:T(8,128)(2,1)S(1)}, bf16[8,4096]{1,0:T(8,128)(2,1)}, u32[]{:S(2)}) copy-start(bf16[8,4096]{1,0:T(8,128)(2,1)} %param.9) | copy-start | bytes 196612
  5.4 4.2 %collective-permute-start = (f32[8,128,128]{2,1,0:T(8,128)S(1)}, f32[8,128,128]{2,1,0:T(8,128)S(1)}, u32[]{:S(2)}, u32[]{:S(2)}) collective-permute-start(f32[8,128,128]{2,1,0:T(8,128)S(1)} %shard_map.56), channel_id=1, source_target_pairs={{0,1},{1,0},{2,3},{3,2},{4,5},{5,4},{6,7},{7,6},{8,9},{9,8},{10,11... | collective-permute-start | bytes 1572872 | tf_op jit(solution)/shard_map/ppermute | solution.py:159
  10.4 43.7 %all-to-all-start = ((bf16[8,192,128]{2,1,0:T(8,128)(2,1)}), bf16[8,192,128]{2,1,0:T(8,128)(2,1)S(1)}, u32[]{:S(2)}, u32[]{:S(2)}) async-start(bf16[8,192,128]{2,1,0:T(8,128)(2,1)} %shard_map.57), calls=%async_computation | async-start | bytes 786432 | tf_op jit(solution)/shard_map/all_to_all | solution.py:162
  54.1 1.9 %collective-permute-start.1 = (bf16[64,4096]{1,0:T(8,128)(2,1)S(1)}, bf16[64,4096]{1,0:T(8,128)(2,1)S(1)}, u32[]{:S(2)}, u32[]{:S(2)}) collective-permute-start(bf16[64,4096]{1,0:T(8,128)(2,1)S(1)} %all_gather.3.own_ref), channel_id=1, source_target_pairs={{0,1},{1,0},{2,3},{3,2},{4,5},{5,4},{6,7},{7,6},{8,9},{9,8},{10,11... | collective-permute-start | bytes 1572872 | tf_op jit(solution)/shard_map/ppermute | solution.py:164

commit v3 on v0

v3 whole, which is shorter than its diff:
```python
import functools

import jax
import jax.numpy as jnp
from jax import lax
from jax.experimental import pallas as pl
from jax.experimental.pallas import tpu as pltpu
from jax.sharding import PartitionSpec as P

SEQ = 64
VMEM_BYTES = 32 * 1024 * 1024
LANES_BY_LANES = (((1,), (1,)), ((), ()))
HBM_SPEC = pl.BlockSpec(memory_space=pltpu.HBM)
VMEM_SPEC = pl.BlockSpec(memory_space=pltpu.VMEM)
PARAMS = pltpu.CompilerParams(vmem_limit_bytes=VMEM_BYTES)


def slab_copies(flip, width, x_hbm, w_hbm, x_buf, w_buf, sems):
    here = lax.axis_index("ex")
    copies = []
    for block in range(2 * x_buf.shape[0]):
        owner = lax.bitwise_xor(here, 4 * block + flip)
        columns = pl.ds(pl.multiple_of(owner * width, width), width)
        place = pl.ds((block % 2) * width, width)
        copies.append(pltpu.make_async_copy(x_hbm.at[:, columns], x_buf.at[block // 2, :, place], sems.at[0, block]))
        copies.append(pltpu.make_async_copy(w_hbm.at[:, columns], w_buf.at[block // 2, :, place], sems.at[1, block]))
    return copies


def project_slab(slab, width, p_in, p_out, x_buf, w_buf, low_ref):
    rank = p_in.shape[0]
    low_in = jnp.dot(p_in[...], x_buf[slab], preferred_element_type=jnp.float32)
    low_out = jnp.dot(p_out[...], w_buf[slab], preferred_element_type=jnp.float32)
    for side in range(2):
        low_ref[2 * slab + side, :rank, :] = low_in[:, side * width : (side + 1) * width]
        low_ref[2 * slab + side, rank:, :] = low_out[:, side * width : (side + 1) * width]


def first_kernel(
    flip, next_flip, x_hbm, w_hbm, p_in_hbm, p_out_hbm, low_ref, p_in, p_out, x_next, w_next, x_buf, w_buf, p_sems, sems, next_sems
):
    width = low_ref.shape[2]
    p_copies = [
        pltpu.make_async_copy(p_in_hbm, p_in, p_sems.at[0]),
        pltpu.make_async_copy(p_out_hbm, p_out, p_sems.at[1]),
    ]
    copies = slab_copies(flip, width, x_hbm, w_hbm, x_buf, w_buf, sems)
    next_copies = slab_copies(next_flip, width, x_hbm, w_hbm, x_next, w_next, next_sems)
    for copy in p_copies + copies + next_copies:
        copy.start()
    for copy in p_copies:
        copy.wait()
    for slab in range(x_buf.shape[0]):
        for copy in copies[4 * slab : 4 * slab + 4]:
            copy.wait()
        project_slab(slab, width, p_in, p_out, x_buf, w_buf, low_ref)
    for copy in next_copies:
        copy.wait()


def middle_kernel(next_flip, x_hbm, w_hbm, p_in, p_out, x_buf, w_buf, low_ref, x_next, w_next, next_sems):
    width = low_ref.shape[2]
    next_copies = slab_copies(next_flip, width, x_hbm, w_hbm, x_next, w_next, next_sems)
    for copy in next_copies:
        copy.start()
    for slab in range(x_buf.shape[0]):
        project_slab(slab, width, p_in, p_out, x_buf, w_buf, low_ref)
    for copy in next_copies:
        copy.wait()


def last_kernel(p_in, p_out, x_buf, w_buf, low_ref):
    for slab in range(x_buf.shape[0]):
        project_slab(slab, low_ref.shape[2], p_in, p_out, x_buf, w_buf, low_ref)


class Projection:
    def __init__(self, inputs, out_grads, proj_in_t, proj_out_t, devices):
        self.hbm = [pltpu.with_memory_space_constraint(a, pltpu.HBM) for a in (inputs, out_grads)]
        self.proj = [pltpu.with_memory_space_constraint(a, pltpu.HBM) for a in (proj_in_t, proj_out_t)]
        self.blocks = devices // 4
        width = inputs.shape[1] // devices
        rank = proj_in_t.shape[0]
        self.low = jax.ShapeDtypeStruct((self.blocks, 2 * rank, width), jnp.float32)
        sizes = (inputs.shape[0], out_grads.shape[0])
        self.slabs = [(self.blocks // 2, size, 2 * width) for size in sizes]
        self.slab_types = [jax.ShapeDtypeStruct(slab, jnp.bfloat16) for slab in self.slabs]
        self.cost = pl.CostEstimate(
            flops=2 * sum(sizes) * rank * self.blocks * width,
            bytes_accessed=2 * sum(sizes) * self.blocks * width,
            transcendentals=0,
        )
        self.sems = pltpu.SemaphoreType.DMA((2, self.blocks))

    def first(self, flip, next_flip):
        proj_types = [jax.ShapeDtypeStruct(a.shape, a.dtype) for a in self.proj]
        low, p_in, p_out, x_next, w_next = pl.pallas_call(
            functools.partial(first_kernel, flip, next_flip),
            out_shape=[self.low] + proj_types + self.slab_types,
            in_specs=[HBM_SPEC] * 4,
            out_specs=[VMEM_SPEC] * 5,
            scratch_shapes=[pltpu.VMEM(slab, jnp.bfloat16) for slab in self.slabs]
            + [pltpu.SemaphoreType.DMA((2,)), self.sems, self.sems],
            compiler_params=PARAMS,
            cost_estimate=self.cost,
        )(*self.hbm, *self.proj)
        return low, (p_in, p_out), (x_next, w_next)

    def middle(self, next_flip, proj, slabs):
        low, x_next, w_next = pl.pallas_call(
            functools.partial(middle_kernel, next_flip),
            out_shape=[self.low] + self.slab_types,
            in_specs=[HBM_SPEC] * 2 + [VMEM_SPEC] * 4,
            out_specs=[VMEM_SPEC] * 3,
            scratch_shapes=[self.sems],
            compiler_params=PARAMS,
            cost_estimate=self.cost,
        )(*self.hbm, *proj, *slabs)
        return low, (x_next, w_next)

    def last(self, proj, slabs):
        return pl.pallas_call(
            last_kernel,
            out_shape=self.low,
            in_specs=[VMEM_SPEC] * 4,
            out_specs=VMEM_SPEC,
            compiler_params=PARAMS,
            cost_estimate=self.cost,
        )(*proj, *slabs)


def put_split(out_ref, low):
    rank = low.shape[0] // 2
    low_in = low[:rank, :]
    high = low_in.astype(jnp.bfloat16)
    out_ref[:rank, :] = high
    out_ref[rank : 2 * rank, :] = low[rank:, :].astype(jnp.bfloat16)
    out_ref[2 * rank :, :] = (low_in - high.astype(jnp.float32)).astype(jnp.bfloat16)


def get_split(ref):
    rank = ref.shape[0] // 3
    low_in = ref[:rank, :].astype(jnp.float32) + ref[2 * rank :, :].astype(jnp.float32)
    return jnp.concatenate([low_in, ref[rank : 2 * rank, :].astype(jnp.float32)], axis=0)


def add_given_kernel(kept_ref, came_ref, out_ref):
    for block in range(out_ref.shape[0]):
        put_split(out_ref.at[block], kept_ref[block] + came_ref[block])


def add_given(kept, came):
    blocks, rows, width = kept.shape
    return pl.pallas_call(
        add_given_kernel,
        out_shape=jax.ShapeDtypeStruct((blocks, rows // 2 * 3, width), jnp.bfloat16),
        compiler_params=PARAMS,
    )(kept, came)


def add_kept_kernel(kept_ref, came_ref, across_ref, *out_refs):
    for block, out_ref in enumerate(out_refs):
        total = kept_ref[block] + came_ref[block] + get_split(across_ref.at[block])
        if out_ref.dtype == jnp.float32:
            out_ref[...] = total
        else:
            put_split(out_ref, total)


def add_kept(kept, came, across):
    blocks, rows, width = kept.shape
    wide = jax.ShapeDtypeStruct((rows, width), jnp.float32)
    split = jax.ShapeDtypeStruct((rows // 2 * 3, width), jnp.bfloat16)
    return pl.pallas_call(
        add_kept_kernel,
        out_shape=[wide if 2 * block < blocks else split for block in range(blocks)],
        compiler_params=PARAMS,
    )(kept, came, across)


def stack_kernel(left_ref, right_ref, out_ref):
    out_ref[: left_ref.shape[0]] = left_ref[...]
    out_ref[left_ref.shape[0] :] = right_ref[...]


def stack(left, right):
    return pl.pallas_call(
        stack_kernel,
        out_shape=jax.ShapeDtypeStruct((2 * left.shape[0],) + left.shape[1:], left.dtype),
        compiler_params=PARAMS,
    )(left, right)


def score_kernel(parts_count, distances, *refs):
    part_refs, query_refs = refs[:parts_count], refs[parts_count : parts_count + 4]
    out_ref, out_t_ref, grads_ref, sums_ref = refs[parts_count + 4 :]
    rank, tokens = out_t_ref.shape
    examples = tokens // SEQ
    here = lax.axis_index("ex")
    core, chip = lax.rem(here, 2), lax.div(here, 2)
    total = part_refs[0][...]
    for part_ref in part_refs[1:]:
        total = total + (part_ref[...] if part_ref.dtype == jnp.float32 else get_split(part_ref))
    out_t_ref[...] = total[rank:, :]
    even = out_t_ref[pl.ds(0, rank // 2, stride=2), :]
    odd = out_t_ref[pl.ds(1, rank // 2, stride=2), :]
    token = lax.broadcasted_iota(jnp.int32, (rank, tokens), 1)
    for n in range(examples):
        mine = jnp.where((token >= n * SEQ) & (token < (n + 1) * SEQ), total[:rank, :], 0.0)
        for side, rows in enumerate((even, odd)):
            grads_ref[n, :, side * rank : (side + 1) * rank] = lax.dot_general(
                rows, mine, LANES_BY_LANES, precision=lax.Precision.HIGHEST, preferred_element_type=jnp.float32
            )
    chips, held = sums_ref.shape[1], sums_ref.shape[3]
    for index, queries_ref in enumerate(query_refs):
        place = lax.rem(core + index // 2, 2)
        count = queries_ref.shape[0]
        step = min(4, count)
        for first in range(0, count, step):
            sums = [jnp.zeros((step * held, 2 * rank), jnp.float32) for _ in range(examples)]
            for k in range(rank // 2):
                query = queries_ref[first : first + step, :, k * 2 * rank : (k + 1) * 2 * rank].astype(jnp.float32)
                query = query.reshape(step * held, 2 * rank)
                for n in range(examples):
                    sums[n] = sums[n] + query * grads_ref[n, k : k + 1, :]
            for part in range(step):
                source = lax.bitwise_xor(chip, distances[index % 2][first + part])
                for n in range(examples):
                    sums_ref[n, source, place] = sums[n][part * held : (part + 1) * held, :]
    ones = jnp.ones((8, 2 * rank), jnp.float32)
    for n in range(examples):
        row = lax.dot_general(
            ones,
            sums_ref[n].reshape(chips * 2 * held, 2 * rank),
            LANES_BY_LANES,
            precision=lax.Precision.HIGHEST,
            preferred_element_type=jnp.float32,
        )
        out_ref[n : n + 1, :] = row[0:1, :]


def score(parts, queries, distances, rank):
    tokens = parts[0].shape[1]
    examples = tokens // SEQ
    chips = len(distances[0]) + len(distances[1])
    held = queries[0].shape[1]
    return pl.pallas_call(
        functools.partial(score_kernel, len(parts), distances),
        out_shape=jax.ShapeDtypeStruct((examples, 2 * chips * held), jnp.float32),
        scratch_shapes=[
            pltpu.VMEM((rank, tokens), jnp.float32),
            pltpu.VMEM((examples, rank // 2, 2 * rank), jnp.float32),
            pltpu.VMEM((examples, chips, 2, held, 2 * rank), jnp.float32),
        ],
        compiler_params=PARAMS,
    )(*parts, *queries)


def shards(inputs, out_grads, proj_in, proj_out, queries):
    devices = lax.axis_size("ex")
    chips = devices // 2
    rank = proj_in.shape[1]

    def swap(array, distance):
        return lax.ppermute(array, "ex", [(i, i ^ distance) for i in range(devices)])

    together = lax.optimization_barrier

    steps = [1 << bit for bit in reversed(range(chips.bit_length() - 1))]
    held, distances = queries[None], [0]
    came_held = swap(held, 2 * steps[0])

    projection = Projection(inputs, out_grads, proj_in.T, proj_out.T, devices)
    low_11, proj, slabs = projection.first(3, 2)
    came_11 = swap(low_11, 1)
    low_10, slabs = projection.middle(1, proj, slabs)
    came_held, low_10 = together((came_held, low_10))
    across = add_given(low_10, came_11)
    for last, step in zip(steps, steps[1:-1]):
        held, distances = stack(held, came_held), distances + [distance ^ last for distance in distances]
        came_held = swap(held, 2 * step)
    held, across, slabs = together((held, across, slabs))
    across = swap(across, 2)
    low_01, slabs = projection.middle(0, proj, slabs)
    came_01 = swap(low_01, 1)
    came_held, low_01, across = together((came_held, low_01, across))
    held, distances = stack(held, came_held), distances + [distance ^ steps[-2] for distance in distances]
    held, slabs = together((held, slabs))
    came_held = swap(held, 2 * steps[-1])
    low_00 = projection.last(proj, slabs)
    sums = add_kept(low_00, came_01, across)
    order = list(range(chips // 4, chips // 2)) + list(range(1, chips // 4))
    came = {distance: swap(sums[distance], 4 * distance) for distance in order}
    held, came_held, came[order[0]] = together((held, came_held, came[order[0]]))
    parts = [sums[0]] + [came[distance] for distance in sorted(came)]
    every = [held, came_held]
    every = every + [swap(array, 1) for array in every]
    return score(parts, every, (distances, [distance ^ steps[-1] for distance in distances]), rank)


def solution(mesh):
    return jax.shard_map(
        shards,
        mesh=mesh,
        in_specs=(
            P("ex", "groups"),
            P("ex", "groups"),
            P("ex", None),
            P("ex", None),
            P("ex", None),
        ),
        out_specs=P(("groups", "ex"), None),
        check_vma=False,
    )
```

time: 114 us -> 35.4 us (0.31)
  waiting for transfers between devices: 60.3 us -> 10.7 us
  blocking collectives: 29.1 us -> 0 us
  starting transfers between devices: 0.01 us -> 14.8 us
  between operations: 13.4 us -> 0.09 us
  Pallas kernels: 0 us -> 9.65 us
  matrix products: 6.31 us -> 0 us
  local copies, waits for them, and re-layouts: 3.41 us -> 0.01 us
    reduce_scatter x1 -> x0, waiting for transfers between devices: 60.3 us -> none  [shards(): lax.psum_scatter(jnp.concatenate([project_rows(inputs, proj_in), project_...]
    all_gather x1 -> x0, blocking collectives: 20.1 us -> none  [shards(): every_grad = lax.all_gather(grads, 'ex', axis=0, tiled=True)]
    ppermute x0 -> x11, starting transfers between devices: none -> 14.8 us  [swap(): lax.ppermute(array, 'ex', [(i, i ^ distance) for i in range(devices)])]
    ppermute x0 -> x11, waiting for transfers between devices: none -> 10.7 us  [swap(): lax.ppermute(array, 'ex', [(i, i ^ distance) for i in range(devices)])]
    pallas_call x0 -> x9, Pallas kernels: none -> 9.65 us  [the longest x2 4.04 us: middle(): pl.pallas_call(functools.partial(middle_kernel, next_flip), out_shape=[se...]
    all_to_all x1 -> x0, blocking collectives: 9.08 us -> none  [shards(): lax.all_to_all(local_scores, 'ex', split_axis=0, concat_axis=1, tiled=True)]
    dot_general x4 -> x0, matrix products: 6.31 us -> none  [the longest x2 5.92 us: project_rows(): lax.dot_general(features, matrix, (((0,), (0,)), ((), ())), preferred_ele...]
    unnamed x6 -> x2, local copies, waits for them, and re-layouts: 1.79 us -> 0.01 us
  transfers between devices with their start and end apart: 1 -> 11, of which waited for: 1 -> 4; matrix products, arithmetic and copies ran while one was open for 0% -> 0% of each run, Pallas kernels for 0% -> 13%
where the time goes in v3:
time: 35.4 us; the launch traced here: 35.2 us
  starting transfers between devices  14.8 us (42%)
  waiting for transfers between devices  10.7 us (30%)
  Pallas kernels  9.65 us (27%)
    ppermute x11, starting transfers between devices, swap(): lax.ppermute(array, 'ex', [(i, i ^ distance) for i in range(devices)])  14.8 us
    ppermute x11, waiting for transfers between devices, swap(): lax.ppermute(array, 'ex', [(i, i ^ distance) for i in range(devices)])  10.7 us
    pallas_call x2, Pallas kernels, middle(): pl.pallas_call(functools.partial(middle_kernel, next_flip), out_shape=[se...  4.04 us
    pallas_call x1, Pallas kernels, first(): pl.pallas_call(functools.partial(first_kernel, flip, next_flip), out_shap...  3.4 us
    pallas_call x1, Pallas kernels, score(): pl.pallas_call(functools.partial(score_kernel, len(parts), distances), ou...  1.59 us
  transfers between devices with their start and end apart: 11, of which 4 were waited for; matrix products, arithmetic and copies ran while one was open for 0% of the time, Pallas kernels for 13%

profile of v3, /device:TPU:0, one launch (start us, length us, event | category | flops | bytes accessed | tf_op | source)
XLA Modules:
  0.0 35.2 jit_solution(13542827443735831830)
XLA Ops:
  0.0 0.0 copy-start
  0.0 3.4 %shard_map.55 = (f32[4,128,128]{2,1,0:T(8,128)S(1)}, bf16[64,512]{1,0:T(8,128)(2,1)S(1)}, bf16[64,1792]{1,0:T(8,128)(2,1)S(1)}, bf16[2,512,256]{2,1,0:T(8,128)(2,1)S(1)}, bf16[2,1792,256]{2,1,0:T(8,128)(2,1)S(1)}) custom-call(bf16[512,2048]{1,0:T(8,128)(2,1)} %x_hbm.5, bf16[1792,2048]{1,0:T(8,128)(2,1)} %w_hbm.5, bf16[64,512]{1,0:T(8,128)(2,1)} %bitcast.6, ...), custom_call_target="tpu_custom_call" | custom-call | flops 150994944 | bytes 2359296 | tf_op jit(solution)/shard_map/pallas_call | solution.py:97
  3.4 0.5 %collective-permute-start.1 = (f32[4,128,128]{2,1,0:T(8,128)S(1)}, f32[4,128,128]{2,1,0:T(8,128)S(1)}, u32[]{:S(2)}, u32[]{:S(2)}) collective-permute-start(f32[4,128,128]{2,1,0:T(8,128)S(1)} %get-tuple-element.41), channel_id=1, source_target_pairs={{0,1},{1,0},{2,3},{3,2},{4,5},{5,4},{6,7},{7,6},{8,9},{9,8},{10,11... | collective-permute-start | bytes 786440 | tf_op jit(solution)/shard_map/ppermute | solution.py:265
  3.9 0.0 copy-done
  3.9 3.7 %collective-permute-start = (bf16[1,8,4096]{2,1,0:T(8,128)(2,1)S(1)}, bf16[1,8,4096]{2,1,0:T(8,128)(2,1)S(1)}, u32[]{:S(2)}, u32[]{:S(2)}) collective-permute-start(bf16[1,8,4096]{2,1,0:T(8,128)(2,1)S(1)} %bitcast.3), channel_id=1, source_target_pairs={{0,8},{1,9},{2,10},{3,11},{4,12},{5,13},{6,14},{7,15},{8,0},{9,1},... | collective-permute-start | bytes 196616 | tf_op jit(solution)/shard_map/ppermute | solution.py:265
  7.6 2.1 %shard_map.56 = (f32[4,128,128]{2,1,0:T(8,128)S(1)}, bf16[2,512,256]{2,1,0:T(8,128)(2,1)S(1)}, bf16[2,1792,256]{2,1,0:T(8,128)(2,1)S(1)}) custom-call(bf16[512,2048]{1,0:T(8,128)(2,1)} %x_hbm.5, bf16[1792,2048]{1,0:T(8,128)(2,1)} %w_hbm.5, bf16[64,512]{1,0:T(8,128)(2,1)S(1)} %get-tuple-element.34.p_in, bf16[64,1792]{1,0:T(8,128)(2,1)S(1)} %get-tuple-element.35.p_out, ...), custom_call_target="tpu_custom_call" | custom-call | flops 150994944 | bytes 2359296 | tf_op jit(solution)/shard_map/pallas_call | solution.py:110
  9.7 2.0 %collective-permute-done.right_ref = bf16[1,8,4096]{2,1,0:T(8,128)(2,1)S(1)} collective-permute-done((bf16[1,8,4096]{2,1,0:T(8,128)(2,1)S(1)}, bf16[1,8,4096]{2,1,0:T(8,128)(2,1)S(1)}, u32[]{:S(2)}, u32[]{:S(2)}) %collective-permute-start) | collective-permute-done | bytes 65568 | tf_op jit(solution)/shard_map/ppermute | solution.py:265
  11.7 0.0 collective-permute-done.1.came_ref
  11.7 1.7 %collective-permute-start.3 = (bf16[4,192,128]{2,1,0:T(8,128)(2,1)S(1)}, bf16[4,192,128]{2,1,0:T(8,128)(2,1)S(1)}, u32[]{:S(2)}, u32[]{:S(2)}) collective-permute-start(bf16[4,192,128]{2,1,0:T(8,128)(2,1)S(1)} %shard_map.58), channel_id=1, source_target_pairs={{0,2},{1,3},{2,0},{3,1},{4,6},{5,7},{6,4},{7,5},{8,10},{9,11},{10,... | collective-permute-start | bytes 589832 | tf_op jit(solution)/shard_map/ppermute | solution.py:265
  13.4 0.7 %collective-permute-start.2 = (bf16[2,8,4096]{2,1,0:T(8,128)(2,1)S(1)}, bf16[2,8,4096]{2,1,0:T(8,128)(2,1)S(1)}, u32[]{:S(2)}, u32[]{:S(2)}) collective-permute-start(bf16[2,8,4096]{2,1,0:T(8,128)(2,1)S(1)} %shard_map.57.left_ref), channel_id=1, source_target_pairs={{0,4},{1,5},{2,6},{3,7},{4,0},{5,1},{6,2},{7,3},{8,12},{9,13},{10,... | collective-permute-start | bytes 393224 | tf_op jit(solution)/shard_map/ppermute | solution.py:265
  14.1 1.9 %shard_map.59 = (f32[4,128,128]{2,1,0:T(8,128)S(1)}, bf16[2,512,256]{2,1,0:T(8,128)(2,1)S(1)}, bf16[2,1792,256]{2,1,0:T(8,128)(2,1)S(1)}) custom-call(bf16[512,2048]{1,0:T(8,128)(2,1)} %x_hbm.5, bf16[1792,2048]{1,0:T(8,128)(2,1)} %w_hbm.5, bf16[64,512]{1,0:T(8,128)(2,1)S(1)} %get-tuple-element.34.p_in, bf16[64,1792]{1,0:T(8,128)(2,1)S(1)} %get-tuple-element.35.p_out, ...), custom_call_target="tpu_custom_call" | custom-call | flops 150994944 | bytes 2359296 | tf_op jit(solution)/shard_map/pallas_call | solution.py:110
  16.0 0.1 collective-permute-start.4
  16.1 2.3 %collective-permute-done.2.right_ref = bf16[2,8,4096]{2,1,0:T(8,128)(2,1)S(1)} collective-permute-done((bf16[2,8,4096]{2,1,0:T(8,128)(2,1)S(1)}, bf16[2,8,4096]{2,1,0:T(8,128)(2,1)S(1)}, u32[]{:S(2)}, u32[]{:S(2)}) %collective-permute-start.2) | collective-permute-done | bytes 131104 | tf_op jit(solution)/shard_map/ppermute | solution.py:265
  18.4 0.0 collective-permute-done.3.across_ref
  18.4 0.8 %collective-permute-start.6 = (bf16[4,8,4096]{2,1,0:T(8,128)(2,1)S(1)}, bf16[4,8,4096]{2,1,0:T(8,128)(2,1)S(1)}, u32[]{:S(2)}, u32[]{:S(2)}) collective-permute-start(bf16[4,8,4096]{2,1,0:T(8,128)(2,1)S(1)} %shard_map.60.refs_4_), channel_id=1, source_target_pairs={{0,2},{1,3},{2,0},{3,1},{4,6},{5,7},{6,4},{7,5},{8,10},{9,11},{10,... | collective-permute-start | bytes 786440 | tf_op jit(solution)/shard_map/ppermute | solution.py:265
  19.2 0.5 %shard_map.61.kept_ref = f32[4,128,128]{2,1,0:T(8,128)S(1)} custom-call(bf16[64,512]{1,0:T(8,128)(2,1)S(1)} %get-tuple-element.34.p_in, bf16[64,1792]{1,0:T(8,128)(2,1)S(1)} %get-tuple-element.35.p_out, bf16[2,512,256]{2,1,0:T(8,128)(2,1)S(1)} %get-tuple-element.52.x_buf, bf16[2,1792,256]{2,1,0:T(8,128)(2,1)S(1)} %get-tuple-element.53.w_buf), custom_call_target="tpu_custom_call" | custom-call | flops 150994944 | bytes 2359296 | tf_op jit(solution)/shard_map/pallas_call | solution.py:122
  19.7 0.0 collective-permute-done.4.came_ref
  19.8 2.4 %collective-permute-start.7 = (bf16[192,128]{1,0:T(8,128)(2,1)S(1)}, bf16[192,128]{1,0:T(8,128)(2,1)S(1)}, u32[]{:S(2)}, u32[]{:S(2)}) collective-permute-start(bf16[192,128]{1,0:T(8,128)(2,1)S(1)} %get-tuple-element.58), channel_id=1, source_target_pairs={{0,8},{1,9},{2,10},{3,11},{4,12},{5,13},{6,14},{7,15},{8,0},{9,1},... | collective-permute-start | bytes 147464 | tf_op jit(solution)/shard_map/ppermute | solution.py:265
  22.2 3.2 %collective-permute-done.7.refs_2_ = bf16[192,128]{1,0:T(8,128)(2,1)S(1)} collective-permute-done((bf16[192,128]{1,0:T(8,128)(2,1)S(1)}, bf16[192,128]{1,0:T(8,128)(2,1)S(1)}, u32[]{:S(2)}, u32[]{:S(2)}) %collective-permute-start.7) | collective-permute-done | bytes 49184 | tf_op jit(solution)/shard_map/ppermute | solution.py:265
  25.3 0.0 collective-permute-done.6.refs_5_
  25.3 0.0 collective-permute-start.10
  25.3 0.5 %collective-permute-start.9 = (bf16[4,8,4096]{2,1,0:T(8,128)(2,1)S(1)}, bf16[4,8,4096]{2,1,0:T(8,128)(2,1)S(1)}, u32[]{:S(2)}, u32[]{:S(2)}) collective-permute-start(bf16[4,8,4096]{2,1,0:T(8,128)(2,1)S(1)} %shard_map.60.refs_4_), channel_id=1, source_target_pairs={{0,1},{1,0},{2,3},{3,2},{4,5},{5,4},{6,7},{7,6},{8,9},{9,8},{10,11... | collective-permute-start | bytes 786440 | tf_op jit(solution)/shard_map/ppermute | solution.py:265
  25.8 1.8 %collective-permute-start.5 = (f32[128,128]{1,0:T(8,128)S(1)}, f32[128,128]{1,0:T(8,128)S(1)}, u32[]{:S(2)}, u32[]{:S(2)}) collective-permute-start(f32[128,128]{1,0:T(8,128)S(1)} %get-tuple-element.56), channel_id=1, source_target_pairs={{0,4},{1,5},{2,6},{3,7},{4,0},{5,1},{6,2},{7,3},{8,12},{9,13},{10,... | collective-permute-start | bytes 196616 | tf_op jit(solution)/shard_map/ppermute | solution.py:265
  27.7 2.7 %collective-permute-start.8 = (bf16[192,128]{1,0:T(8,128)(2,1)S(1)}, bf16[192,128]{1,0:T(8,128)(2,1)S(1)}, u32[]{:S(2)}, u32[]{:S(2)}) collective-permute-start(bf16[192,128]{1,0:T(8,128)(2,1)S(1)} %get-tuple-element.60), channel_id=1, source_target_pairs={{0,12},{1,13},{2,14},{3,15},{4,8},{5,9},{6,10},{7,11},{8,4},{9,5},... | collective-permute-start | bytes 147464 | tf_op jit(solution)/shard_map/ppermute | solution.py:265
  30.4 3.2 %collective-permute-done.8.refs_3_ = bf16[192,128]{1,0:T(8,128)(2,1)S(1)} collective-permute-done((bf16[192,128]{1,0:T(8,128)(2,1)S(1)}, bf16[192,128]{1,0:T(8,128)(2,1)S(1)}, u32[]{:S(2)}, u32[]{:S(2)}) %collective-permute-start.8) | collective-permute-done | bytes 49184 | tf_op jit(solution)/shard_map/ppermute | solution.py:265
  33.6 0.0 collective-permute-done.5.refs_1_
  33.6 0.0 collective-permute-done.10.refs_7_
  33.7 0.0 collective-permute-done.9.refs_6_
  33.7 1.6 %shard_map.63 = f32[2,128]{1,0:T(2,128)} custom-call(f32[128,128]{1,0:T(8,128)S(1)} %get-tuple-element.55.refs_0_, f32[128,128]{1,0:T(8,128)S(1)} %collective-permute-done.5.refs_1_, bf16[192,128]{1,0:T(8,128)(2,1)S(1)} %collective-permute-done.7.refs_2_, bf16[192,128]{1,0:T(8,128)(2,1)S(1)} %collective-permute-done.8.refs_3_, ...), custom_call_target="tpu_custom_call" | custom-call | tf_op jit(solution)/shard_map/pallas_call | solution.py:247
  (4 shorter events, 0.1 us)
Async XLA Ops:
  0.0 3.9 %copy-start = (bf16[8,4096]{1,0:T(8,128)(2,1)S(1)}, bf16[8,4096]{1,0:T(8,128)(2,1)}, u32[]{:S(2)}) copy-start(bf16[8,4096]{1,0:T(8,128)(2,1)} %param.9) | copy-start | bytes 196612
  3.4 8.3 %collective-permute-start.1 = (f32[4,128,128]{2,1,0:T(8,128)S(1)}, f32[4,128,128]{2,1,0:T(8,128)S(1)}, u32[]{:S(2)}, u32[]{:S(2)}) collective-permute-start(f32[4,128,128]{2,1,0:T(8,128)S(1)} %get-tuple-element.41), channel_id=1, source_target_pairs={{0,1},{1,0},{2,3},{3,2},{4,5},{5,4},{6,7},{7,6},{8,9},{9,8},{10,11... | collective-permute-start | bytes 786440 | tf_op jit(solution)/shard_map/ppermute | solution.py:265
  3.9 7.8 %collective-permute-start = (bf16[1,8,4096]{2,1,0:T(8,128)(2,1)S(1)}, bf16[1,8,4096]{2,1,0:T(8,128)(2,1)S(1)}, u32[]{:S(2)}, u32[]{:S(2)}) collective-permute-start(bf16[1,8,4096]{2,1,0:T(8,128)(2,1)S(1)} %bitcast.3), channel_id=1, source_target_pairs={{0,8},{1,9},{2,10},{3,11},{4,12},{5,13},{6,14},{7,15},{8,0},{9,1},... | collective-permute-start | bytes 196616 | tf_op jit(solution)/shard_map/ppermute | solution.py:265
  11.7 6.6 %collective-permute-start.3 = (bf16[4,192,128]{2,1,0:T(8,128)(2,1)S(1)}, bf16[4,192,128]{2,1,0:T(8,128)(2,1)S(1)}, u32[]{:S(2)}, u32[]{:S(2)}) collective-permute-start(bf16[4,192,128]{2,1,0:T(8,128)(2,1)S(1)} %shard_map.58), channel_id=1, source_target_pairs={{0,2},{1,3},{2,0},{3,1},{4,6},{5,7},{6,4},{7,5},{8,10},{9,11},{10,... | collective-permute-start | bytes 589832 | tf_op jit(solution)/shard_map/ppermute | solution.py:265
  13.4 5.0 %collective-permute-start.2 = (bf16[2,8,4096]{2,1,0:T(8,128)(2,1)S(1)}, bf16[2,8,4096]{2,1,0:T(8,128)(2,1)S(1)}, u32[]{:S(2)}, u32[]{:S(2)}) collective-permute-start(bf16[2,8,4096]{2,1,0:T(8,128)(2,1)S(1)} %shard_map.57.left_ref), channel_id=1, source_target_pairs={{0,4},{1,5},{2,6},{3,7},{4,0},{5,1},{6,2},{7,3},{8,12},{9,13},{10,... | collective-permute-start | bytes 393224 | tf_op jit(solution)/shard_map/ppermute | solution.py:265
  16.0 3.7 %collective-permute-start.4 = (f32[4,128,128]{2,1,0:T(8,128)S(1)}, f32[4,128,128]{2,1,0:T(8,128)S(1)}, u32[]{:S(2)}, u32[]{:S(2)}) collective-permute-start(f32[4,128,128]{2,1,0:T(8,128)S(1)} %get-tuple-element.47), channel_id=1, source_target_pairs={{0,1},{1,0},{2,3},{3,2},{4,5},{5,4},{6,7},{7,6},{8,9},{9,8},{10,11... | collective-permute-start | bytes 786440 | tf_op jit(solution)/shard_map/ppermute | solution.py:265
  18.4 6.9 %collective-permute-start.6 = (bf16[4,8,4096]{2,1,0:T(8,128)(2,1)S(1)}, bf16[4,8,4096]{2,1,0:T(8,128)(2,1)S(1)}, u32[]{:S(2)}, u32[]{:S(2)}) collective-permute-start(bf16[4,8,4096]{2,1,0:T(8,128)(2,1)S(1)} %shard_map.60.refs_4_), channel_id=1, source_target_pairs={{0,2},{1,3},{2,0},{3,1},{4,6},{5,7},{6,4},{7,5},{8,10},{9,11},{10,... | collective-permute-start | bytes 786440 | tf_op jit(solution)/shard_map/ppermute | solution.py:265
  19.8 5.6 %collective-permute-start.7 = (bf16[192,128]{1,0:T(8,128)(2,1)S(1)}, bf16[192,128]{1,0:T(8,128)(2,1)S(1)}, u32[]{:S(2)}, u32[]{:S(2)}) collective-permute-start(bf16[192,128]{1,0:T(8,128)(2,1)S(1)} %get-tuple-element.58), channel_id=1, source_target_pairs={{0,8},{1,9},{2,10},{3,11},{4,12},{5,13},{6,14},{7,15},{8,0},{9,1},... | collective-permute-start | bytes 147464 | tf_op jit(solution)/shard_map/ppermute | solution.py:265
  25.3 8.3 %collective-permute-start.10 = (bf16[4,8,4096]{2,1,0:T(8,128)(2,1)S(1)}, bf16[4,8,4096]{2,1,0:T(8,128)(2,1)S(1)}, u32[]{:S(2)}, u32[]{:S(2)}) collective-permute-start(bf16[4,8,4096]{2,1,0:T(8,128)(2,1)S(1)} %collective-permute-done.6.refs_5_), channel_id=1, source_target_pairs={{0,1},{1,0},{2,3},{3,2},{4,5},{5,4},{6,7},{7,6},{8,9},{9,8},{10,11... | collective-permute-start | bytes 786440 | tf_op jit(solution)/shard_map/ppermute | solution.py:265
  25.3 8.3 %collective-permute-start.9 = (bf16[4,8,4096]{2,1,0:T(8,128)(2,1)S(1)}, bf16[4,8,4096]{2,1,0:T(8,128)(2,1)S(1)}, u32[]{:S(2)}, u32[]{:S(2)}) collective-permute-start(bf16[4,8,4096]{2,1,0:T(8,128)(2,1)S(1)} %shard_map.60.refs_4_), channel_id=1, source_target_pairs={{0,1},{1,0},{2,3},{3,2},{4,5},{5,4},{6,7},{7,6},{8,9},{9,8},{10,11... | collective-permute-start | bytes 786440 | tf_op jit(solution)/shard_map/ppermute | solution.py:265
  25.8 7.8 %collective-permute-start.5 = (f32[128,128]{1,0:T(8,128)S(1)}, f32[128,128]{1,0:T(8,128)S(1)}, u32[]{:S(2)}, u32[]{:S(2)}) collective-permute-start(f32[128,128]{1,0:T(8,128)S(1)} %get-tuple-element.56), channel_id=1, source_target_pairs={{0,4},{1,5},{2,6},{3,7},{4,0},{5,1},{6,2},{7,3},{8,12},{9,13},{10,... | collective-permute-start | bytes 196616 | tf_op jit(solution)/shard_map/ppermute | solution.py:265
  27.7 6.0 %collective-permute-start.8 = (bf16[192,128]{1,0:T(8,128)(2,1)S(1)}, bf16[192,128]{1,0:T(8,128)(2,1)S(1)}, u32[]{:S(2)}, u32[]{:S(2)}) collective-permute-start(bf16[192,128]{1,0:T(8,128)(2,1)S(1)} %get-tuple-element.60), channel_id=1, source_target_pairs={{0,12},{1,13},{2,14},{3,15},{4,8},{5,9},{6,10},{7,11},{8,4},{9,5},... | collective-permute-start | bytes 147464 | tf_op jit(solution)/shard_map/ppermute | solution.py:265

commit v4 on v0

v4 whole, which is shorter than its diff:
```python
import functools

import jax
import jax.numpy as jnp
from jax import lax
from jax.experimental import pallas as pl
from jax.experimental.pallas import tpu as pltpu
from jax.sharding import PartitionSpec as P

SEQ = 64
VMEM_BYTES = 32 * 1024 * 1024
LANES_BY_LANES = (((1,), (1,)), ((), ()))
HBM_SPEC = pl.BlockSpec(memory_space=pltpu.HBM)
VMEM_SPEC = pl.BlockSpec(memory_space=pltpu.VMEM)
PARAMS = pltpu.CompilerParams(vmem_limit_bytes=VMEM_BYTES)


def project_kernel(
    x_hbm, w_hbm, p_in_hbm, p_out_hbm, given_ref, kept_ref, x_buf, w_buf, p_in, p_out, low, p_sems, x_sems, w_sems
):
    here = lax.axis_index("ex")
    chips = given_ref.shape[0]
    rank, width = given_ref.shape[1] // 2, given_ref.shape[2]
    copies = [
        pltpu.make_async_copy(p_in_hbm, p_in, p_sems.at[0]),
        pltpu.make_async_copy(p_out_hbm, p_out, p_sems.at[1]),
    ]
    sides = []
    for top, hbm, buf, sems, matrix in ((0, x_hbm, x_buf, x_sems, p_in), (rank, w_hbm, w_buf, w_sems, p_out)):
        rows = buf.shape[0] // sems.shape[0]
        for chunk in range(sems.shape[0]):
            part = pl.ds(chunk * rows, rows)
            copy = pltpu.make_async_copy(hbm.at[part, :], buf.at[part, :], sems.at[chunk])
            sides.append((slice(top, top + rank), part, buf, matrix, copy, chunk == 0))
            copies.append(copy)
    for copy in copies:
        copy.start()
    for copy in copies[:2]:
        copy.wait()
    step = min(1024, low.shape[1])
    for lines, part, buf, matrix, copy, first in sides:
        copy.wait()
        for column in range(0, low.shape[1], step):
            columns = slice(column, column + step)
            product = jnp.dot(matrix[:, part], buf[part, columns], preferred_element_type=jnp.float32)
            low[lines, columns] = product if first else low[lines, columns] + product
    core = lax.rem(here, 2)
    chip = lax.div(here, 2)
    for distance in range(chips):
        place = lax.bitwise_xor(chip, distance)
        both = low[:, pl.ds(pl.multiple_of(place * 2 * width, 2 * width), 2 * width)]
        left, right = both[:, :width], both[:, width:]
        given_ref[distance] = jnp.where(core == 0, right, left)
        kept_ref[distance] = jnp.where(core == 0, left, right)


def project(inputs, out_grads, proj_in_t, proj_out_t, devices):
    arrays = [pltpu.with_memory_space_constraint(a, pltpu.HBM) for a in (inputs, out_grads, proj_in_t, proj_out_t)]
    width = inputs.shape[1] // devices
    rank = proj_in_t.shape[0]
    half = jax.ShapeDtypeStruct((devices // 2, 2 * rank, width), jnp.float32)
    chunks = [a.shape[0] // 256 if a.shape[0] % 256 == 0 else 1 for a in (inputs, out_grads)]
    return pl.pallas_call(
        project_kernel,
        out_shape=[half] * 2,
        in_specs=[HBM_SPEC] * 4,
        out_specs=[VMEM_SPEC] * 2,
        scratch_shapes=[pltpu.VMEM(a.shape, jnp.bfloat16) for a in arrays]
        + [pltpu.VMEM((2 * rank, inputs.shape[1]), jnp.float32), pltpu.SemaphoreType.DMA((2,))]
        + [pltpu.SemaphoreType.DMA((count,)) for count in chunks],
        compiler_params=PARAMS,
        cost_estimate=pl.CostEstimate(
            flops=2 * rank * (inputs.size + out_grads.size),
            bytes_accessed=2 * (inputs.size + out_grads.size),
            transcendentals=0,
        ),
    )(*arrays)


def add_kernel(kept_ref, came_ref, *out_refs):
    for block, out_ref in enumerate(out_refs):
        out_ref[...] = (kept_ref[block] + came_ref[block]).astype(out_ref.dtype)


def add_halves(kept, came, types):
    return pl.pallas_call(
        add_kernel,
        out_shape=[jax.ShapeDtypeStruct(kept.shape[1:], dtype) for dtype in types],
        compiler_params=PARAMS,
    )(kept, came)


def stack_kernel(*refs):
    *in_refs, out_ref = refs
    first = 0
    for in_ref in in_refs:
        out_ref[first : first + in_ref.shape[0]] = in_ref[...]
        first += in_ref.shape[0]


def stack(arrays):
    count = sum(array.shape[0] for array in arrays)
    return pl.pallas_call(
        stack_kernel,
        out_shape=jax.ShapeDtypeStruct((count,) + arrays[0].shape[1:], arrays[0].dtype),
        compiler_params=PARAMS,
    )(*arrays)


def score_kernel(parts_count, distances, *refs):
    part_refs, query_refs = refs[:parts_count], refs[parts_count : parts_count + len(distances)]
    out_ref, out_t_ref, grads_ref, sums_ref = refs[parts_count + len(distances) :]
    rank, tokens = out_t_ref.shape
    examples = tokens // SEQ
    here = lax.axis_index("ex")
    core, chip = lax.rem(here, 2), lax.div(here, 2)
    total = part_refs[0][...]
    for part_ref in part_refs[1:]:
        total = total + part_ref[...].astype(jnp.float32)
    out_t_ref[...] = total[rank:, :]
    even = out_t_ref[pl.ds(0, rank // 2, stride=2), :]
    odd = out_t_ref[pl.ds(1, rank // 2, stride=2), :]
    token = lax.broadcasted_iota(jnp.int32, (rank, tokens), 1)
    for n in range(examples):
        mine = jnp.where((token >= n * SEQ) & (token < (n + 1) * SEQ), total[:rank, :], 0.0)
        for side, rows in enumerate((even, odd)):
            grads_ref[n, :, side * rank : (side + 1) * rank] = lax.dot_general(
                rows, mine, LANES_BY_LANES, precision=lax.Precision.HIGHEST, preferred_element_type=jnp.float32
            )
    chips, held = sums_ref.shape[1], sums_ref.shape[3]
    for index, queries_ref in enumerate(query_refs):
        place = lax.rem(core + distances[index][0], 2)
        count = queries_ref.shape[0]
        step = 4 if count % 4 == 0 else 2
        for first in range(0, count, step):
            sums = [jnp.zeros((step * held, 2 * rank), jnp.float32) for _ in range(examples)]
            for k in range(rank // 2):
                query = queries_ref[first : first + step, :, k * 2 * rank : (k + 1) * 2 * rank].astype(jnp.float32)
                query = query.reshape(step * held, 2 * rank)
                for n in range(examples):
                    sums[n] = sums[n] + query * grads_ref[n, k : k + 1, :]
            for part in range(step):
                source = lax.bitwise_xor(chip, distances[index][1][first + part])
                for n in range(examples):
                    sums_ref[n, source, place] = sums[n][part * held : (part + 1) * held, :]
    ones = jnp.ones((8, 2 * rank), jnp.float32)
    for n in range(examples):
        row = lax.dot_general(
            ones,
            sums_ref[n].reshape(chips * 2 * held, 2 * rank),
            LANES_BY_LANES,
            precision=lax.Precision.HIGHEST,
            preferred_element_type=jnp.float32,
        )
        out_ref[n : n + 1, :] = row[0:1, :]


def score(parts, queries, distances, rank):
    tokens = parts[0].shape[1]
    examples = tokens // SEQ
    chips = sum(len(chip_distances) for _, chip_distances in distances) // 2
    held = queries[0].shape[1]
    return pl.pallas_call(
        functools.partial(score_kernel, len(parts), distances),
        out_shape=jax.ShapeDtypeStruct((examples, 2 * chips * held), jnp.float32),
        scratch_shapes=[
            pltpu.VMEM((rank, tokens), jnp.float32),
            pltpu.VMEM((examples, rank // 2, 2 * rank), jnp.float32),
            pltpu.VMEM((examples, chips, 2, held, 2 * rank), jnp.float32),
        ],
        compiler_params=PARAMS,
    )(*parts, *queries)


def shards(inputs, out_grads, proj_in, proj_out, queries):
    devices = lax.axis_size("ex")
    chips = devices // 2
    middle = chips // 2
    rank = proj_in.shape[1]
    together = lax.optimization_barrier

    def swap(array, chip=0, core=0):
        distance = 2 * chip + core
        return lax.ppermute(array, "ex", [(i, i ^ distance) for i in range(devices)])

    query = queries[None]
    y_queries = [query, swap(query, chip=1)]
    z_queries = [swap(query, chip=chip) for chip in [middle] + list(range(2, middle, 2))]
    given, kept = project(inputs, out_grads, proj_in.T, proj_out.T, devices)
    y_queries, z_queries, given, kept = together((y_queries, z_queries, given, kept))
    came = swap(given, core=1)
    here_queries = stack(z_queries)
    there_queries = swap(here_queries, chip=1)
    early = stack(y_queries + [here_queries])
    early_other = swap(early, core=1)
    came, early_other = together((came, early_other))

    types = [jnp.float32 if chip < middle else jnp.bfloat16 for chip in range(chips)]
    parts = list(add_halves(kept, came, types))
    parts[middle:] = [swap(parts[chip], chip=chip) for chip in range(middle, chips)]
    first = slice(1, middle + middle // 2)
    there_queries, parts[first] = together((there_queries, parts[first]))
    corner = stack([here_queries[:1], there_queries[:1]])
    late = [there_queries] + [swap(corner, chip=chip) for chip in range(2, middle, 2)]
    parts[1:middle] = [swap(parts[chip], chip=chip) for chip in range(1, middle)]
    late, parts[1 : middle - 1], parts[middle + middle // 2 :] = together((late, parts[1 : middle - 1], parts[middle + middle // 2 :]))
    late = stack(late)
    late_other = swap(late, core=1)
    z_chips = [middle] + list(range(2, middle, 2))
    early_chips = [0, 1] + z_chips
    late_chips = [chip + 1 for chip in z_chips] + [middle + chip + y for chip in z_chips[1:] for y in range(2)]
    held = [early, early_other, late, late_other]
    return score(parts, held, [(0, early_chips), (1, early_chips), (0, late_chips), (1, late_chips)], rank)


def solution(mesh):
    return jax.shard_map(
        shards,
        mesh=mesh,
        in_specs=(
            P("ex", "groups"),
            P("ex", "groups"),
            P("ex", None),
            P("ex", None),
            P("ex", None),
        ),
        out_specs=P(("groups", "ex"), None),
        check_vma=False,
    )
```

time: 114 us -> 40.4 us (0.35)
  waiting for transfers between devices: 60.3 us -> 14.2 us
  blocking collectives: 29.1 us -> 0 us
  starting transfers between devices: 0.01 us -> 18.7 us
  between operations: 13.4 us -> 0.11 us
  Pallas kernels: 0 us -> 7.14 us
  matrix products: 6.31 us -> 0 us
  local copies, waits for them, and re-layouts: 3.41 us -> 0.01 us
    reduce_scatter x1 -> x0, waiting for transfers between devices: 60.3 us -> none  [shards(): lax.psum_scatter(jnp.concatenate([project_rows(inputs, proj_in), project_...]
    all_gather x1 -> x0, blocking collectives: 20.1 us -> none  [shards(): every_grad = lax.all_gather(grads, 'ex', axis=0, tiled=True)]
    ppermute x0 -> x15, starting transfers between devices: none -> 18.7 us  [swap(): lax.ppermute(array, 'ex', [(i, i ^ distance) for i in range(devices)])]
    ppermute x0 -> x15, waiting for transfers between devices: none -> 14.2 us  [swap(): lax.ppermute(array, 'ex', [(i, i ^ distance) for i in range(devices)])]
    all_to_all x1 -> x0, blocking collectives: 9.08 us -> none  [shards(): lax.all_to_all(local_scores, 'ex', split_axis=0, concat_axis=1, tiled=True)]
    pallas_call x0 -> x7, Pallas kernels: none -> 7.14 us  [the longest x1 5.43 us: project(): pl.pallas_call(project_kernel, out_shape=[half] * 2, in_specs=[HBM_SPEC]...]
    dot_general x4 -> x0, matrix products: 6.31 us -> none  [the longest x2 5.92 us: project_rows(): lax.dot_general(features, matrix, (((0,), (0,)), ((), ())), preferred_ele...]
    unnamed x6 -> x2, local copies, waits for them, and re-layouts: 1.79 us -> 0.01 us
  transfers between devices with their start and end apart: 1 -> 15, of which waited for: 1 -> 7; matrix products, arithmetic and copies ran while one was open for 0% -> 0% of each run, Pallas kernels for 0% -> 14%
where the time goes in v4:
time: 40.4 us; the launch traced here: 40.2 us
  starting transfers between devices  18.7 us (46%)
  waiting for transfers between devices  14.2 us (35%)
  Pallas kernels  7.14 us (18%)
    ppermute x15, starting transfers between devices, swap(): lax.ppermute(array, 'ex', [(i, i ^ distance) for i in range(devices)])  18.7 us
    ppermute x15, waiting for transfers between devices, swap(): lax.ppermute(array, 'ex', [(i, i ^ distance) for i in range(devices)])  14.2 us
    pallas_call x1, Pallas kernels, project(): pl.pallas_call(project_kernel, out_shape=[half] * 2, in_specs=[HBM_SPEC]...  5.43 us
    pallas_call x1, Pallas kernels, score(): pl.pallas_call(functools.partial(score_kernel, len(parts), distances), ou...  1.59 us
  transfers between devices with their start and end apart: 15, of which 7 were waited for; matrix products, arithmetic and copies ran while one was open for 0% of the time, Pallas kernels for 14%

profile of v4, /device:TPU:0, one launch (start us, length us, event | category | flops | bytes accessed | tf_op | source)
XLA Modules:
  0.0 40.2 jit_solution(6717339090363513559)
XLA Ops:
  0.0 0.0 copy-start
  0.0 3.0 %collective-permute-start = (bf16[1,8,4096]{2,1,0:T(8,128)(2,1)}, bf16[1,8,4096]{2,1,0:T(8,128)(2,1)S(1)}, u32[]{:S(2)}, u32[]{:S(2)}) collective-permute-start(bf16[1,8,4096]{2,1,0:T(8,128)(2,1)} %bitcast.3), channel_id=1, source_target_pairs={{0,2},{1,3},{2,0},{3,1},{4,6},{5,7},{6,4},{7,5},{8,10},{9,11},{10,... | collective-permute-start | bytes 196616 | tf_op jit(solution)/shard_map/ppermute | solution.py:184
  3.0 2.6 %collective-permute-start.1 = (bf16[1,8,4096]{2,1,0:T(8,128)(2,1)}, bf16[1,8,4096]{2,1,0:T(8,128)(2,1)S(1)}, u32[]{:S(2)}, u32[]{:S(2)}) collective-permute-start(bf16[1,8,4096]{2,1,0:T(8,128)(2,1)} %bitcast.4), channel_id=1, source_target_pairs={{0,8},{1,9},{2,10},{3,11},{4,12},{5,13},{6,14},{7,15},{8,0},{9,1},... | collective-permute-start | bytes 196616 | tf_op jit(solution)/shard_map/ppermute | solution.py:184
  5.6 1.6 %collective-permute-start.2 = (bf16[1,8,4096]{2,1,0:T(8,128)(2,1)}, bf16[1,8,4096]{2,1,0:T(8,128)(2,1)S(1)}, u32[]{:S(2)}, u32[]{:S(2)}) collective-permute-start(bf16[1,8,4096]{2,1,0:T(8,128)(2,1)} %bitcast.5), channel_id=1, source_target_pairs={{0,4},{1,5},{2,6},{3,7},{4,0},{5,1},{6,2},{7,3},{8,12},{9,13},{10,... | collective-permute-start | bytes 196616 | tf_op jit(solution)/shard_map/ppermute | solution.py:184
  7.1 5.4 %shard_map.55 = (f32[8,128,128]{2,1,0:T(8,128)S(1)}, f32[8,128,128]{2,1,0:T(8,128)S(1)}) custom-call(bf16[512,2048]{1,0:T(8,128)(2,1)} %x_hbm.1, bf16[1792,2048]{1,0:T(8,128)(2,1)} %w_hbm.1, bf16[64,512]{1,0:T(8,128)(2,1)} %bitcast.8, bf16[64,1792]{1,0:T(8,128)(2,1)} %bitcast.7), custom_call_target="tpu_custom_call" | custom-call | flops 603979776 | bytes 9437184 | tf_op jit(solution)/shard_map/pallas_call | solution.py:63
  12.6 0.0 collective-permute-done.refs_1_
  12.6 0.0 collective-permute-done.1.refs_0_
  12.6 0.0 collective-permute-done.2.refs_1_
  12.6 0.1 collective-permute-start.3
  12.7 0.0 copy-done
  12.7 0.6 %collective-permute-start.4 = (bf16[4,8,4096]{2,1,0:T(8,128)(2,1)S(1)}, bf16[4,8,4096]{2,1,0:T(8,128)(2,1)S(1)}, u32[]{:S(2)}, u32[]{:S(2)}) collective-permute-start(bf16[4,8,4096]{2,1,0:T(8,128)(2,1)S(1)} %shard_map.57.refs_8_), channel_id=1, source_target_pairs={{0,1},{1,0},{2,3},{3,2},{4,5},{5,4},{6,7},{7,6},{8,9},{9,8},{10,11... | collective-permute-start | bytes 786440 | tf_op jit(solution)/shard_map/ppermute | solution.py:184
  13.3 0.5 %collective-permute-start.5 = (bf16[2,8,4096]{2,1,0:T(8,128)(2,1)S(1)}, bf16[2,8,4096]{2,1,0:T(8,128)(2,1)S(1)}, u32[]{:S(2)}, u32[]{:S(2)}) collective-permute-start(bf16[2,8,4096]{2,1,0:T(8,128)(2,1)S(1)} %shard_map.56.refs_2_), channel_id=1, source_target_pairs={{0,2},{1,3},{2,0},{3,1},{4,6},{5,7},{6,4},{7,5},{8,10},{9,11},{10,... | collective-permute-start | bytes 393224 | tf_op jit(solution)/shard_map/ppermute | solution.py:184
  13.8 1.2 %collective-permute-done.4.refs_9_ = bf16[4,8,4096]{2,1,0:T(8,128)(2,1)S(1)} collective-permute-done((bf16[4,8,4096]{2,1,0:T(8,128)(2,1)S(1)}, bf16[4,8,4096]{2,1,0:T(8,128)(2,1)S(1)}, u32[]{:S(2)}, u32[]{:S(2)}) %collective-permute-start.4) | collective-permute-done | bytes 262176 | tf_op jit(solution)/shard_map/ppermute | solution.py:184
  15.0 0.0 collective-permute-done.3.came_ref
  15.0 0.1 shard_map.58
  15.0 0.4 %collective-permute-start.6 = (bf16[128,128]{1,0:T(8,128)(2,1)S(1)}, bf16[128,128]{1,0:T(8,128)(2,1)S(1)}, u32[]{:S(2)}, u32[]{:S(2)}) collective-permute-start(bf16[128,128]{1,0:T(8,128)(2,1)S(1)} %get-tuple-element.48), channel_id=1, source_target_pairs={{0,8},{1,9},{2,10},{3,11},{4,12},{5,13},{6,14},{7,15},{8,0},{9,1},... | collective-permute-start | bytes 98312 | tf_op jit(solution)/shard_map/ppermute | solution.py:184
  15.4 2.5 %collective-permute-start.7 = (bf16[128,128]{1,0:T(8,128)(2,1)S(1)}, bf16[128,128]{1,0:T(8,128)(2,1)S(1)}, u32[]{:S(2)}, u32[]{:S(2)}) collective-permute-start(bf16[128,128]{1,0:T(8,128)(2,1)S(1)} %get-tuple-element.49), channel_id=1, source_target_pairs={{0,10},{1,11},{2,8},{3,9},{4,14},{5,15},{6,12},{7,13},{8,2},{9,3},... | collective-permute-start | bytes 98312 | tf_op jit(solution)/shard_map/ppermute | solution.py:184
  18.0 0.8 %collective-permute-done.5.refs_0_ = bf16[2,8,4096]{2,1,0:T(8,128)(2,1)S(1)} collective-permute-done((bf16[2,8,4096]{2,1,0:T(8,128)(2,1)S(1)}, bf16[2,8,4096]{2,1,0:T(8,128)(2,1)S(1)}, u32[]{:S(2)}, u32[]{:S(2)}) %collective-permute-start.5) | collective-permute-done | bytes 131104 | tf_op jit(solution)/shard_map/ppermute | solution.py:184
  18.8 2.1 %collective-permute-done.6.refs_4_ = bf16[128,128]{1,0:T(8,128)(2,1)S(1)} collective-permute-done((bf16[128,128]{1,0:T(8,128)(2,1)S(1)}, bf16[128,128]{1,0:T(8,128)(2,1)S(1)}, u32[]{:S(2)}, u32[]{:S(2)}) %collective-permute-start.6) | collective-permute-done | bytes 32800 | tf_op jit(solution)/shard_map/ppermute | solution.py:184
  20.8 0.6 %collective-permute-done.7.refs_5_ = bf16[128,128]{1,0:T(8,128)(2,1)S(1)} collective-permute-done((bf16[128,128]{1,0:T(8,128)(2,1)S(1)}, bf16[128,128]{1,0:T(8,128)(2,1)S(1)}, u32[]{:S(2)}, u32[]{:S(2)}) %collective-permute-start.7) | collective-permute-done | bytes 32800 | tf_op jit(solution)/shard_map/ppermute | solution.py:184
  21.5 0.3 collective-permute-start.8
  21.8 1.3 %collective-permute-start.9 = (f32[128,128]{1,0:T(8,128)S(1)}, f32[128,128]{1,0:T(8,128)S(1)}, u32[]{:S(2)}, u32[]{:S(2)}) collective-permute-start(f32[128,128]{1,0:T(8,128)S(1)} %get-tuple-element.51), channel_id=1, source_target_pairs={{0,2},{1,3},{2,0},{3,1},{4,6},{5,7},{6,4},{7,5},{8,10},{9,11},{10,... | collective-permute-start | bytes 196616 | tf_op jit(solution)/shard_map/ppermute | solution.py:184
  23.0 1.9 %collective-permute-start.10 = (f32[128,128]{1,0:T(8,128)S(1)}, f32[128,128]{1,0:T(8,128)S(1)}, u32[]{:S(2)}, u32[]{:S(2)}) collective-permute-start(f32[128,128]{1,0:T(8,128)S(1)} %get-tuple-element.52), channel_id=1, source_target_pairs={{0,4},{1,5},{2,6},{3,7},{4,0},{5,1},{6,2},{7,3},{8,12},{9,13},{10,... | collective-permute-start | bytes 196616 | tf_op jit(solution)/shard_map/ppermute | solution.py:184
  25.0 1.5 %collective-permute-start.11 = (bf16[128,128]{1,0:T(8,128)(2,1)S(1)}, bf16[128,128]{1,0:T(8,128)(2,1)S(1)}, u32[]{:S(2)}, u32[]{:S(2)}) collective-permute-start(bf16[128,128]{1,0:T(8,128)(2,1)S(1)} %get-tuple-element.53), channel_id=1, source_target_pairs={{0,12},{1,13},{2,14},{3,15},{4,8},{5,9},{6,10},{7,11},{8,4},{9,5},... | collective-permute-start | bytes 98312 | tf_op jit(solution)/shard_map/ppermute | solution.py:184
  26.5 2.4 %collective-permute-start.12 = (bf16[128,128]{1,0:T(8,128)(2,1)S(1)}, bf16[128,128]{1,0:T(8,128)(2,1)S(1)}, u32[]{:S(2)}, u32[]{:S(2)}) collective-permute-start(bf16[128,128]{1,0:T(8,128)(2,1)S(1)} %get-tuple-element.54), channel_id=1, source_target_pairs={{0,14},{1,15},{2,12},{3,13},{4,10},{5,11},{6,8},{7,9},{8,6},{9,7},... | collective-permute-start | bytes 98312 | tf_op jit(solution)/shard_map/ppermute | solution.py:184
  28.9 1.8 %collective-permute-done.11.refs_6_ = bf16[128,128]{1,0:T(8,128)(2,1)S(1)} collective-permute-done((bf16[128,128]{1,0:T(8,128)(2,1)S(1)}, bf16[128,128]{1,0:T(8,128)(2,1)S(1)}, u32[]{:S(2)}, u32[]{:S(2)}) %collective-permute-start.11) | collective-permute-done | bytes 32800 | tf_op jit(solution)/shard_map/ppermute | solution.py:184
  30.7 2.4 %collective-permute-done.12.refs_7_ = bf16[128,128]{1,0:T(8,128)(2,1)S(1)} collective-permute-done((bf16[128,128]{1,0:T(8,128)(2,1)S(1)}, bf16[128,128]{1,0:T(8,128)(2,1)S(1)}, u32[]{:S(2)}, u32[]{:S(2)}) %collective-permute-start.12) | collective-permute-done | bytes 32800 | tf_op jit(solution)/shard_map/ppermute | solution.py:184
  33.1 0.0 collective-permute-done.9.refs_1_
  33.1 0.0 collective-permute-done.10.refs_2_
  33.1 0.0 collective-permute-done.8.refs_1_
  33.1 0.1 collective-permute-start.14
  33.2 0.1 collective-permute-start.13
  33.3 5.3 %collective-permute-done.13.refs_3_ = f32[128,128]{1,0:T(8,128)S(1)} collective-permute-done((f32[128,128]{1,0:T(8,128)S(1)}, f32[128,128]{1,0:T(8,128)S(1)}, u32[]{:S(2)}, u32[]{:S(2)}) %collective-permute-start.13) | collective-permute-done | bytes 65568 | tf_op jit(solution)/shard_map/ppermute | solution.py:184
  38.6 0.0 collective-permute-done.14.refs_11_
  38.6 1.6 %shard_map.61 = f32[2,128]{1,0:T(2,128)} custom-call(f32[128,128]{1,0:T(8,128)S(1)} %get-tuple-element.44.refs_0_, f32[128,128]{1,0:T(8,128)S(1)} %collective-permute-done.9.refs_1_, f32[128,128]{1,0:T(8,128)S(1)} %collective-permute-done.10.refs_2_, f32[128,128]{1,0:T(8,128)S(1)} %collective-permute-done.13.refs_3_, ...), custom_call_target="tpu_custom_call" | custom-call | tf_op jit(solution)/shard_map/pallas_call | solution.py:163
  (6 shorter events, 0.1 us)
Async XLA Ops:
  0.0 12.7 %copy-start = (bf16[8,4096]{1,0:T(8,128)(2,1)S(1)}, bf16[8,4096]{1,0:T(8,128)(2,1)}, u32[]{:S(2)}) copy-start(bf16[8,4096]{1,0:T(8,128)(2,1)} %param.9) | copy-start | bytes 196612
  0.0 12.6 %collective-permute-start = (bf16[1,8,4096]{2,1,0:T(8,128)(2,1)}, bf16[1,8,4096]{2,1,0:T(8,128)(2,1)S(1)}, u32[]{:S(2)}, u32[]{:S(2)}) collective-permute-start(bf16[1,8,4096]{2,1,0:T(8,128)(2,1)} %bitcast.3), channel_id=1, source_target_pairs={{0,2},{1,3},{2,0},{3,1},{4,6},{5,7},{6,4},{7,5},{8,10},{9,11},{10,... | collective-permute-start | bytes 196616 | tf_op jit(solution)/shard_map/ppermute | solution.py:184
  3.0 9.6 %collective-permute-start.1 = (bf16[1,8,4096]{2,1,0:T(8,128)(2,1)}, bf16[1,8,4096]{2,1,0:T(8,128)(2,1)S(1)}, u32[]{:S(2)}, u32[]{:S(2)}) collective-permute-start(bf16[1,8,4096]{2,1,0:T(8,128)(2,1)} %bitcast.4), channel_id=1, source_target_pairs={{0,8},{1,9},{2,10},{3,11},{4,12},{5,13},{6,14},{7,15},{8,0},{9,1},... | collective-permute-start | bytes 196616 | tf_op jit(solution)/shard_map/ppermute | solution.py:184
  5.6 7.0 %collective-permute-start.2 = (bf16[1,8,4096]{2,1,0:T(8,128)(2,1)}, bf16[1,8,4096]{2,1,0:T(8,128)(2,1)S(1)}, u32[]{:S(2)}, u32[]{:S(2)}) collective-permute-start(bf16[1,8,4096]{2,1,0:T(8,128)(2,1)} %bitcast.5), channel_id=1, source_target_pairs={{0,4},{1,5},{2,6},{3,7},{4,0},{5,1},{6,2},{7,3},{8,12},{9,13},{10,... | collective-permute-start | bytes 196616 | tf_op jit(solution)/shard_map/ppermute | solution.py:184
  12.6 2.4 %collective-permute-start.3 = (f32[8,128,128]{2,1,0:T(8,128)S(1)}, f32[8,128,128]{2,1,0:T(8,128)S(1)}, u32[]{:S(2)}, u32[]{:S(2)}) collective-permute-start(f32[8,128,128]{2,1,0:T(8,128)S(1)} %get-tuple-element.38), channel_id=1, source_target_pairs={{0,1},{1,0},{2,3},{3,2},{4,5},{5,4},{6,7},{7,6},{8,9},{9,8},{10,11... | collective-permute-start | bytes 1572872 | tf_op jit(solution)/shard_map/ppermute | solution.py:184
  12.7 2.2 %collective-permute-start.4 = (bf16[4,8,4096]{2,1,0:T(8,128)(2,1)S(1)}, bf16[4,8,4096]{2,1,0:T(8,128)(2,1)S(1)}, u32[]{:S(2)}, u32[]{:S(2)}) collective-permute-start(bf16[4,8,4096]{2,1,0:T(8,128)(2,1)S(1)} %shard_map.57.refs_8_), channel_id=1, source_target_pairs={{0,1},{1,0},{2,3},{3,2},{4,5},{5,4},{6,7},{7,6},{8,9},{9,8},{10,11... | collective-permute-start | bytes 786440 | tf_op jit(solution)/shard_map/ppermute | solution.py:184
  13.3 5.5 %collective-permute-start.5 = (bf16[2,8,4096]{2,1,0:T(8,128)(2,1)S(1)}, bf16[2,8,4096]{2,1,0:T(8,128)(2,1)S(1)}, u32[]{:S(2)}, u32[]{:S(2)}) collective-permute-start(bf16[2,8,4096]{2,1,0:T(8,128)(2,1)S(1)} %shard_map.56.refs_2_), channel_id=1, source_target_pairs={{0,2},{1,3},{2,0},{3,1},{4,6},{5,7},{6,4},{7,5},{8,10},{9,11},{10,... | collective-permute-start | bytes 393224 | tf_op jit(solution)/shard_map/ppermute | solution.py:184
  15.0 5.8 %collective-permute-start.6 = (bf16[128,128]{1,0:T(8,128)(2,1)S(1)}, bf16[128,128]{1,0:T(8,128)(2,1)S(1)}, u32[]{:S(2)}, u32[]{:S(2)}) collective-permute-start(bf16[128,128]{1,0:T(8,128)(2,1)S(1)} %get-tuple-element.48), channel_id=1, source_target_pairs={{0,8},{1,9},{2,10},{3,11},{4,12},{5,13},{6,14},{7,15},{8,0},{9,1},... | collective-permute-start | bytes 98312 | tf_op jit(solution)/shard_map/ppermute | solution.py:184
  15.4 6.1 %collective-permute-start.7 = (bf16[128,128]{1,0:T(8,128)(2,1)S(1)}, bf16[128,128]{1,0:T(8,128)(2,1)S(1)}, u32[]{:S(2)}, u32[]{:S(2)}) collective-permute-start(bf16[128,128]{1,0:T(8,128)(2,1)S(1)} %get-tuple-element.49), channel_id=1, source_target_pairs={{0,10},{1,11},{2,8},{3,9},{4,14},{5,15},{6,12},{7,13},{8,2},{9,3},... | collective-permute-start | bytes 98312 | tf_op jit(solution)/shard_map/ppermute | solution.py:184
  21.5 11.6 %collective-permute-start.8 = (bf16[2,8,4096]{2,1,0:T(8,128)(2,1)S(1)}, bf16[2,8,4096]{2,1,0:T(8,128)(2,1)S(1)}, u32[]{:S(2)}, u32[]{:S(2)}) collective-permute-start(bf16[2,8,4096]{2,1,0:T(8,128)(2,1)S(1)} %shard_map.59), channel_id=1, source_target_pairs={{0,4},{1,5},{2,6},{3,7},{4,0},{5,1},{6,2},{7,3},{8,12},{9,13},{10,... | collective-permute-start | bytes 393224 | tf_op jit(solution)/shard_map/ppermute | solution.py:184
  21.8 11.3 %collective-permute-start.9 = (f32[128,128]{1,0:T(8,128)S(1)}, f32[128,128]{1,0:T(8,128)S(1)}, u32[]{:S(2)}, u32[]{:S(2)}) collective-permute-start(f32[128,128]{1,0:T(8,128)S(1)} %get-tuple-element.51), channel_id=1, source_target_pairs={{0,2},{1,3},{2,0},{3,1},{4,6},{5,7},{6,4},{7,5},{8,10},{9,11},{10,... | collective-permute-start | bytes 196616 | tf_op jit(solution)/shard_map/ppermute | solution.py:184
  23.0 10.1 %collective-permute-start.10 = (f32[128,128]{1,0:T(8,128)S(1)}, f32[128,128]{1,0:T(8,128)S(1)}, u32[]{:S(2)}, u32[]{:S(2)}) collective-permute-start(f32[128,128]{1,0:T(8,128)S(1)} %get-tuple-element.52), channel_id=1, source_target_pairs={{0,4},{1,5},{2,6},{3,7},{4,0},{5,1},{6,2},{7,3},{8,12},{9,13},{10,... | collective-permute-start | bytes 196616 | tf_op jit(solution)/shard_map/ppermute | solution.py:184
  25.0 5.7 %collective-permute-start.11 = (bf16[128,128]{1,0:T(8,128)(2,1)S(1)}, bf16[128,128]{1,0:T(8,128)(2,1)S(1)}, u32[]{:S(2)}, u32[]{:S(2)}) collective-permute-start(bf16[128,128]{1,0:T(8,128)(2,1)S(1)} %get-tuple-element.53), channel_id=1, source_target_pairs={{0,12},{1,13},{2,14},{3,15},{4,8},{5,9},{6,10},{7,11},{8,4},{9,5},... | collective-permute-start | bytes 98312 | tf_op jit(solution)/shard_map/ppermute | solution.py:184
  26.5 6.6 %collective-permute-start.12 = (bf16[128,128]{1,0:T(8,128)(2,1)S(1)}, bf16[128,128]{1,0:T(8,128)(2,1)S(1)}, u32[]{:S(2)}, u32[]{:S(2)}) collective-permute-start(bf16[128,128]{1,0:T(8,128)(2,1)S(1)} %get-tuple-element.54), channel_id=1, source_target_pairs={{0,14},{1,15},{2,12},{3,13},{4,10},{5,11},{6,8},{7,9},{8,6},{9,7},... | collective-permute-start | bytes 98312 | tf_op jit(solution)/shard_map/ppermute | solution.py:184
  33.1 5.5 %collective-permute-start.14 = (bf16[4,8,4096]{2,1,0:T(8,128)(2,1)S(1)}, bf16[4,8,4096]{2,1,0:T(8,128)(2,1)S(1)}, u32[]{:S(2)}, u32[]{:S(2)}) collective-permute-start(bf16[4,8,4096]{2,1,0:T(8,128)(2,1)S(1)} %shard_map.60.refs_10_), channel_id=1, source_target_pairs={{0,1},{1,0},{2,3},{3,2},{4,5},{5,4},{6,7},{7,6},{8,9},{9,8},{10,11... | collective-permute-start | bytes 786440 | tf_op jit(solution)/shard_map/ppermute | solution.py:184
  33.2 5.4 %collective-permute-start.13 = (f32[128,128]{1,0:T(8,128)S(1)}, f32[128,128]{1,0:T(8,128)S(1)}, u32[]{:S(2)}, u32[]{:S(2)}) collective-permute-start(f32[128,128]{1,0:T(8,128)S(1)} %get-tuple-element.57), channel_id=1, source_target_pairs={{0,6},{1,7},{2,4},{3,5},{4,2},{5,3},{6,0},{7,1},{8,14},{9,15},{10,... | collective-permute-start | bytes 196616 | tf_op jit(solution)/shard_map/ppermute | solution.py:184

commit v5 on v0

v5 whole, which is shorter than its diff:
```python
import functools

import jax
import jax.numpy as jnp
from jax import lax
from jax.experimental import pallas as pl
from jax.experimental.pallas import tpu as pltpu
from jax.sharding import PartitionSpec as P

SEQ = 64
VMEM_BYTES = 32 * 1024 * 1024
LANES_BY_LANES = (((1,), (1,)), ((), ()))
HBM_SPEC = pl.BlockSpec(memory_space=pltpu.HBM)
VMEM_SPEC = pl.BlockSpec(memory_space=pltpu.VMEM)
PARAMS = pltpu.CompilerParams(vmem_limit_bytes=VMEM_BYTES)


def project_kernel(flip, x_hbm, w_hbm, p_in_hbm, p_out_hbm, *refs):
    here = lax.axis_index("ex")
    core, chip = lax.rem(here, 2), lax.div(here, 2)
    *given_refs, kept_ref, x_buf, w_buf, p_in, p_out, p_sems, sems = refs
    depth = kept_ref.shape[0]
    rank, width = kept_ref.shape[1] // 2, kept_ref.shape[2]
    copies = [
        pltpu.make_async_copy(p_in_hbm, p_in, p_sems.at[0]),
        pltpu.make_async_copy(p_out_hbm, p_out, p_sems.at[1]),
    ]
    for z in range(depth):
        place = lax.bitwise_xor(chip, 2 * z + flip)
        columns = pl.ds(pl.multiple_of(place * 2 * width, 2 * width), 2 * width)
        copies.append(pltpu.make_async_copy(x_hbm.at[:, columns], x_buf.at[z], sems.at[0, z]))
        copies.append(pltpu.make_async_copy(w_hbm.at[:, columns], w_buf.at[z], sems.at[1, z]))
    for copy in copies:
        copy.start()
    for copy in copies[:2]:
        copy.wait()
    for z in range(depth):
        for copy in copies[2 + 2 * z : 4 + 2 * z]:
            copy.wait()
        low_in = jnp.dot(p_in[...], x_buf[z], preferred_element_type=jnp.float32)
        low_out = jnp.dot(p_out[...], w_buf[z], preferred_element_type=jnp.float32)
        for rows, low in ((slice(0, rank), low_in), (slice(rank, 2 * rank), low_out)):
            left, right = low[:, :width], low[:, width:]
            given_ref = given_refs[z * len(given_refs) // depth]
            given_ref[z % given_ref.shape[0], rows, :] = jnp.where(core == 0, right, left)
            kept_ref[z, rows, :] = jnp.where(core == 0, left, right)


def project(flip, arrays, devices, splits):
    inputs, out_grads, proj_in_t, proj_out_t = arrays
    depth = devices // 4
    width = inputs.shape[1] // devices
    rank = proj_in_t.shape[0]
    kept = jax.ShapeDtypeStruct((depth, 2 * rank, width), jnp.float32)
    given = jax.ShapeDtypeStruct((depth // splits, 2 * rank, width), jnp.float32)
    *given, kept = pl.pallas_call(
        functools.partial(project_kernel, flip),
        out_shape=[given] * splits + [kept],
        in_specs=[HBM_SPEC] * 4,
        out_specs=[VMEM_SPEC] * (splits + 1),
        scratch_shapes=[
            pltpu.VMEM((depth, inputs.shape[0], 2 * width), jnp.bfloat16),
            pltpu.VMEM((depth, out_grads.shape[0], 2 * width), jnp.bfloat16),
            pltpu.VMEM(proj_in_t.shape, jnp.bfloat16),
            pltpu.VMEM(proj_out_t.shape, jnp.bfloat16),
            pltpu.SemaphoreType.DMA((2,)),
            pltpu.SemaphoreType.DMA((2, depth)),
        ],
        compiler_params=PARAMS,
        cost_estimate=pl.CostEstimate(
            flops=rank * (inputs.size + out_grads.size),
            bytes_accessed=inputs.size + out_grads.size,
            transcendentals=0,
        ),
    )(*arrays)
    return given, kept


def put_split(out_ref, low):
    rank = low.shape[0] // 2
    low_in = low[:rank, :]
    high = low_in.astype(jnp.bfloat16)
    out_ref[:rank, :] = high
    out_ref[rank : 2 * rank, :] = low[rank:, :].astype(jnp.bfloat16)
    out_ref[2 * rank :, :] = (low_in - high.astype(jnp.float32)).astype(jnp.bfloat16)


def get_split(ref):
    rank = ref.shape[0] // 3
    low_in = ref[:rank, :].astype(jnp.float32) + ref[2 * rank :, :].astype(jnp.float32)
    return jnp.concatenate([low_in, ref[rank : 2 * rank, :].astype(jnp.float32)], axis=0)


def add_given_kernel(kept_ref, came_ref, out_ref):
    for block in range(out_ref.shape[0]):
        put_split(out_ref.at[block], kept_ref[block] + came_ref[block])


def add_given(kept, came):
    blocks, rows, width = kept.shape
    return pl.pallas_call(
        add_given_kernel,
        out_shape=jax.ShapeDtypeStruct((blocks, rows // 2 * 3, width), jnp.bfloat16),
        compiler_params=PARAMS,
    )(kept, came)


def add_kept_kernel(kept_ref, across_ref, *refs):
    came_refs, out_refs = refs[:2], refs[2:]
    half = came_refs[0].shape[0]
    for block, out_ref in enumerate(out_refs):
        total = kept_ref[block] + came_refs[block // half][block % half] + get_split(across_ref.at[block])
        out_ref[...] = total.astype(out_ref.dtype)


def add_kept(kept, came, across):
    blocks, rows, width = kept.shape
    wide = jax.ShapeDtypeStruct((rows, width), jnp.float32)
    rounded = jax.ShapeDtypeStruct((rows, width), jnp.bfloat16)
    return pl.pallas_call(
        add_kept_kernel,
        out_shape=[wide if 2 * block < blocks else rounded for block in range(blocks)],
        compiler_params=PARAMS,
    )(kept, across, *came)


def stack_kernel(left_ref, right_ref, out_ref):
    out_ref[: left_ref.shape[0]] = left_ref[...]
    out_ref[left_ref.shape[0] :] = right_ref[...]


def stack(left, right):
    return pl.pallas_call(
        stack_kernel,
        out_shape=jax.ShapeDtypeStruct((2 * left.shape[0],) + left.shape[1:], left.dtype),
        compiler_params=PARAMS,
    )(left, right)


def add_scores(queries_ref, chips, place, grads, sums_ref):
    examples, half_rank, lanes = grads.shape
    held = queries_ref.shape[1]
    step = 4 if len(chips) % 4 == 0 else 2
    here = lax.div(lax.axis_index("ex"), 2)
    for first in range(0, len(chips), step):
        sums = [jnp.zeros((step * held, lanes), jnp.float32) for _ in range(examples)]
        for k in range(half_rank):
            query = queries_ref[first : first + step, :, k * lanes : (k + 1) * lanes].astype(jnp.float32)
            query = query.reshape(step * held, lanes)
            for n in range(examples):
                sums[n] = sums[n] + query * grads[n, k : k + 1, :]
        for part in range(step):
            source = lax.bitwise_xor(here, chips[first + part])
            for n in range(examples):
                sums_ref[n, source, place] = sums[n][part * held : (part + 1) * held, :]


def first_score_kernel(parts_count, held, *refs):
    part_refs, query_refs = refs[:parts_count], refs[parts_count : parts_count + len(held)]
    grads_ref, sums_ref, out_t_ref = refs[parts_count + len(held) :]
    rank, tokens = out_t_ref.shape
    core = lax.rem(lax.axis_index("ex"), 2)
    total = part_refs[0][...]
    for part_ref in part_refs[1:]:
        total = total + part_ref[...].astype(jnp.float32)
    out_t_ref[...] = total[rank:, :]
    even = out_t_ref[pl.ds(0, rank // 2, stride=2), :]
    odd = out_t_ref[pl.ds(1, rank // 2, stride=2), :]
    token = lax.broadcasted_iota(jnp.int32, (rank, tokens), 1)
    for n in range(tokens // SEQ):
        mine = jnp.where((token >= n * SEQ) & (token < (n + 1) * SEQ), total[:rank, :], 0.0)
        for side, rows in enumerate((even, odd)):
            grads_ref[n, :, side * rank : (side + 1) * rank] = lax.dot_general(
                rows, mine, LANES_BY_LANES, precision=lax.Precision.HIGHEST, preferred_element_type=jnp.float32
            )
    sums_ref[...] = jnp.zeros_like(sums_ref)
    for queries_ref, (other, chips) in zip(query_refs, held):
        add_scores(queries_ref, chips, lax.rem(core + other, 2), grads_ref, sums_ref)


def last_score_kernel(chips, grads_ref, before_ref, queries_ref, out_ref, sums_ref):
    core = lax.rem(lax.axis_index("ex"), 2)
    sums_ref[...] = before_ref[...]
    add_scores(queries_ref, chips, lax.rem(core + 1, 2), grads_ref, sums_ref)
    examples, *rows, lanes = sums_ref.shape
    ones = jnp.ones((8, lanes), jnp.float32)
    for n in range(examples):
        row = lax.dot_general(
            ones,
            sums_ref[n].reshape(out_ref.shape[1], lanes),
            LANES_BY_LANES,
            precision=lax.Precision.HIGHEST,
            preferred_element_type=jnp.float32,
        )
        out_ref[n : n + 1, :] = row[0:1, :]


def first_scores(parts, queries, held, rank):
    tokens = parts[0].shape[1]
    examples = tokens // SEQ
    chips = 2 * queries[0].shape[0]
    return pl.pallas_call(
        functools.partial(first_score_kernel, len(parts), held),
        out_shape=[
            jax.ShapeDtypeStruct((examples, rank // 2, 2 * rank), jnp.float32),
            jax.ShapeDtypeStruct((examples, chips, 2, queries[0].shape[1], 2 * rank), jnp.float32),
        ],
        scratch_shapes=[pltpu.VMEM((rank, tokens), jnp.float32)],
        compiler_params=PARAMS,
    )(*parts, *queries)


def last_scores(grads, sums, queries, chips):
    examples, all_chips, cores, held, _ = sums.shape
    return pl.pallas_call(
        functools.partial(last_score_kernel, chips),
        out_shape=jax.ShapeDtypeStruct((examples, all_chips * cores * held), jnp.float32),
        scratch_shapes=[pltpu.VMEM(sums.shape, jnp.float32)],
        compiler_params=PARAMS,
    )(grads, sums, queries)


def shards(inputs, out_grads, proj_in, proj_out, queries):
    devices = lax.axis_size("ex")
    chips = devices // 2
    depth = chips // 2
    rank = proj_in.shape[1]
    together = lax.optimization_barrier

    def swap(array, chip=0, core=0):
        distance = 2 * chip + core
        return lax.ppermute(array, "ex", [(i, i ^ distance) for i in range(devices)])

    steps = [1 << bit for bit in reversed(range(chips.bit_length() - 1))]
    held, reach = queries[None], [0]
    came_held = swap(held, chip=steps[0])
    arrays = [pltpu.with_memory_space_constraint(a, pltpu.HBM) for a in (inputs, out_grads, proj_in.T, proj_out.T)]
    given, kept = project(1, arrays, devices, 1)
    came_held, given, kept = together((came_held, given, kept))
    came = swap(given[0], core=1)
    for last, step in zip(steps, steps[1:-1]):
        held, reach = stack(held, came_held), reach + [chip ^ last for chip in reach]
        came_held = swap(held, chip=step)
    message = add_given(kept, came)
    message, arrays = together((message, arrays))
    across = swap(message, chip=1)
    given, kept = project(0, arrays, devices, 2)
    came_held, given, kept = together((came_held, given, kept))
    came = [swap(array, core=1) for array in given]
    held, reach = stack(held, came_held), reach + [chip ^ steps[-2] for chip in reach]
    came_held = swap(held, chip=1)
    other_held = swap(held, core=1)
    across, came = together((across, came))

    sums = add_kept(kept, came, across)
    parts = list(sums)
    for z in list(range(depth // 2, depth)) + list(range(1, depth // 2)):
        parts[z] = swap(parts[z], chip=2 * z)
    came_held, other_held, parts = together((came_held, other_held, parts))
    other_came = swap(came_held, core=1)
    reach_y = [chip ^ 1 for chip in reach]
    grads, scores = first_scores(parts, [held, other_held, came_held], [(0, reach), (1, reach), (0, reach_y)], rank)
    return last_scores(grads, scores, other_came, reach_y)


def solution(mesh):
    return jax.shard_map(
        shards,
        mesh=mesh,
        in_specs=(
            P("ex", "groups"),
            P("ex", "groups"),
            P("ex", None),
            P("ex", None),
            P("ex", None),
        ),
        out_specs=P(("groups", "ex"), None),
        check_vma=False,
    )
```

time: 114 us -> 29.9 us (0.26)
  waiting for transfers between devices: 60.3 us -> 6.72 us
  blocking collectives: 29.1 us -> 0 us
  between operations: 13.4 us -> 0.11 us
  starting transfers between devices: 0.01 us -> 13 us
  Pallas kernels: 0 us -> 9.92 us
  matrix products: 6.31 us -> 0 us
  local copies, waits for them, and re-layouts: 3.41 us -> 0.01 us
    reduce_scatter x1 -> x0, waiting for transfers between devices: 60.3 us -> none  [shards(): lax.psum_scatter(jnp.concatenate([project_rows(inputs, proj_in), project_...]
    all_gather x1 -> x0, blocking collectives: 20.1 us -> none  [shards(): every_grad = lax.all_gather(grads, 'ex', axis=0, tiled=True)]
    ppermute x0 -> x12, starting transfers between devices: none -> 13 us  [swap(): lax.ppermute(array, 'ex', [(i, i ^ distance) for i in range(devices)])]
    pallas_call x0 -> x8, Pallas kernels: none -> 9.92 us  [the longest x2 8.2 us: project(): pl.pallas_call(functools.partial(project_kernel, flip), out_shape=[given]...]
    all_to_all x1 -> x0, blocking collectives: 9.08 us -> none  [shards(): lax.all_to_all(local_scores, 'ex', split_axis=0, concat_axis=1, tiled=True)]
    ppermute x0 -> x12, waiting for transfers between devices: none -> 6.72 us  [swap(): lax.ppermute(array, 'ex', [(i, i ^ distance) for i in range(devices)])]
    dot_general x4 -> x0, matrix products: 6.31 us -> none  [the longest x2 5.92 us: project_rows(): lax.dot_general(features, matrix, (((0,), (0,)), ((), ())), preferred_ele...]
    unnamed x6 -> x2, local copies, waits for them, and re-layouts: 1.79 us -> 0.01 us
  transfers between devices with their start and end apart: 1 -> 12, of which waited for: 1 -> 5; matrix products, arithmetic and copies ran while one was open for 0% -> 0% of each run, Pallas kernels for 0% -> 30%
where the time goes in v5:
time: 29.9 us; the launch traced here: 29.8 us
  starting transfers between devices  13 us (43%)
  Pallas kernels  9.92 us (33%)
  waiting for transfers between devices  6.72 us (22%)
    ppermute x12, starting transfers between devices, swap(): lax.ppermute(array, 'ex', [(i, i ^ distance) for i in range(devices)])  13 us
    pallas_call x2, Pallas kernels, project(): pl.pallas_call(functools.partial(project_kernel, flip), out_shape=[given]...  8.2 us
    ppermute x12, waiting for transfers between devices, swap(): lax.ppermute(array, 'ex', [(i, i ^ distance) for i in range(devices)])  6.72 us
    pallas_call x1, Pallas kernels, last_scores(): pl.pallas_call(functools.partial(last_score_kernel, chips), out_shape=jax...  0.98 us
    pallas_call x1, Pallas kernels, first_scores(): pl.pallas_call(functools.partial(first_score_kernel, len(parts), held), o...  0.64 us
  transfers between devices with their start and end apart: 12, of which 5 were waited for; matrix products, arithmetic and copies ran while one was open for 0% of the time, Pallas kernels for 30%

profile of v5, /device:TPU:0, one launch (start us, length us, event | category | flops | bytes accessed | tf_op | source)
XLA Modules:
  0.0 29.8 jit_solution(7508607499875172033)
XLA Ops:
  0.0 0.0 copy-start
  0.0 4.0 %collective-permute-start = (bf16[1,8,4096]{2,1,0:T(8,128)(2,1)}, bf16[1,8,4096]{2,1,0:T(8,128)(2,1)S(1)}, u32[]{:S(2)}, u32[]{:S(2)}) collective-permute-start(bf16[1,8,4096]{2,1,0:T(8,128)(2,1)} %bitcast.3), channel_id=1, source_target_pairs={{0,8},{1,9},{2,10},{3,11},{4,12},{5,13},{6,14},{7,15},{8,0},{9,1},... | collective-permute-start | bytes 196616 | tf_op jit(solution)/shard_map/ppermute | solution.py:232
  4.0 4.1 %shard_map.55 = (f32[4,128,128]{2,1,0:T(8,128)S(1)}, f32[4,128,128]{2,1,0:T(8,128)S(1)}) custom-call(bf16[512,2048]{1,0:T(8,128)(2,1)} %x_hbm.2, bf16[1792,2048]{1,0:T(8,128)(2,1)} %w_hbm.2, bf16[64,512]{1,0:T(8,128)(2,1)} %bitcast.7, bf16[64,1792]{1,0:T(8,128)(2,1)} %bitcast.5), custom_call_target="tpu_custom_call" | custom-call | flops 301989888 | bytes 4718592 | tf_op jit(solution)/shard_map/pallas_call | solution.py:56
  8.1 0.0 collective-permute-done.right_ref
  8.2 0.1 collective-permute-start.2
  8.2 0.0 copy-done
  8.3 1.6 %collective-permute-start.1 = (bf16[2,8,4096]{2,1,0:T(8,128)(2,1)S(1)}, bf16[2,8,4096]{2,1,0:T(8,128)(2,1)S(1)}, u32[]{:S(2)}, u32[]{:S(2)}) collective-permute-start(bf16[2,8,4096]{2,1,0:T(8,128)(2,1)S(1)} %shard_map.56.left_ref), channel_id=1, source_target_pairs={{0,4},{1,5},{2,6},{3,7},{4,0},{5,1},{6,2},{7,3},{8,12},{9,13},{10,... | collective-permute-start | bytes 393224 | tf_op jit(solution)/shard_map/ppermute | solution.py:232
  9.9 0.0 collective-permute-done.2.came_ref
  9.9 1.6 %collective-permute-start.5 = (bf16[4,192,128]{2,1,0:T(8,128)(2,1)S(1)}, bf16[4,192,128]{2,1,0:T(8,128)(2,1)S(1)}, u32[]{:S(2)}, u32[]{:S(2)}) collective-permute-start(bf16[4,192,128]{2,1,0:T(8,128)(2,1)S(1)} %shard_map.57), channel_id=1, source_target_pairs={{0,2},{1,3},{2,0},{3,1},{4,6},{5,7},{6,4},{7,5},{8,10},{9,11},{10,... | collective-permute-start | bytes 589832 | tf_op jit(solution)/shard_map/ppermute | solution.py:232
  11.5 4.1 %shard_map.58 = (f32[2,128,128]{2,1,0:T(8,128)S(1)}, f32[2,128,128]{2,1,0:T(8,128)S(1)}, f32[4,128,128]{2,1,0:T(8,128)S(1)}) custom-call(bf16[512,2048]{1,0:T(8,128)(2,1)} %x_hbm.2, bf16[1792,2048]{1,0:T(8,128)(2,1)} %w_hbm.2, bf16[64,512]{1,0:T(8,128)(2,1)} %bitcast.8, bf16[64,1792]{1,0:T(8,128)(2,1)} %bitcast.6), custom_call_target="tpu_custom_call" | custom-call | flops 301989888 | bytes 4718592 | tf_op jit(solution)/shard_map/pallas_call | solution.py:56
  15.6 0.0 collective-permute-done.1.right_ref
  15.7 0.1 collective-permute-start.4
  15.8 0.6 %collective-permute-start.3 = (bf16[4,8,4096]{2,1,0:T(8,128)(2,1)S(1)}, bf16[4,8,4096]{2,1,0:T(8,128)(2,1)S(1)}, u32[]{:S(2)}, u32[]{:S(2)}) collective-permute-start(bf16[4,8,4096]{2,1,0:T(8,128)(2,1)S(1)} %shard_map.59.refs_4_), channel_id=1, source_target_pairs={{0,2},{1,3},{2,0},{3,1},{4,6},{5,7},{6,4},{7,5},{8,10},{9,11},{10,... | collective-permute-start | bytes 786440 | tf_op jit(solution)/shard_map/ppermute | solution.py:232
  16.3 0.2 collective-permute-start.6
  16.5 0.3 %collective-permute-start.7 = (f32[2,128,128]{2,1,0:T(8,128)S(1)}, f32[2,128,128]{2,1,0:T(8,128)S(1)}, u32[]{:S(2)}, u32[]{:S(2)}) collective-permute-start(f32[2,128,128]{2,1,0:T(8,128)S(1)} %get-tuple-element.53), channel_id=1, source_target_pairs={{0,1},{1,0},{2,3},{3,2},{4,5},{5,4},{6,7},{7,6},{8,9},{9,8},{10,11... | collective-permute-start | bytes 393224 | tf_op jit(solution)/shard_map/ppermute | solution.py:232
  16.8 0.8 %collective-permute-done.6.refs_0_ = f32[2,128,128]{2,1,0:T(8,128)S(1)} collective-permute-done((f32[2,128,128]{2,1,0:T(8,128)S(1)}, f32[2,128,128]{2,1,0:T(8,128)S(1)}, u32[]{:S(2)}, u32[]{:S(2)}) %collective-permute-start.6) | collective-permute-done | bytes 131104 | tf_op jit(solution)/shard_map/ppermute | solution.py:232
  17.7 0.2 collective-permute-done.7.refs_1_
  17.9 0.0 collective-permute-done.5.across_ref
  17.9 1.5 %collective-permute-start.8 = (f32[128,128]{1,0:T(8,128)S(1)}, f32[128,128]{1,0:T(8,128)S(1)}, u32[]{:S(2)}, u32[]{:S(2)}) collective-permute-start(f32[128,128]{1,0:T(8,128)S(1)} %get-tuple-element.58), channel_id=1, source_target_pairs={{0,4},{1,5},{2,6},{3,7},{4,0},{5,1},{6,2},{7,3},{8,12},{9,13},{10,... | collective-permute-start | bytes 196616 | tf_op jit(solution)/shard_map/ppermute | solution.py:232
  19.4 2.1 %collective-permute-start.9 = (bf16[128,128]{1,0:T(8,128)(2,1)S(1)}, bf16[128,128]{1,0:T(8,128)(2,1)S(1)}, u32[]{:S(2)}, u32[]{:S(2)}) collective-permute-start(bf16[128,128]{1,0:T(8,128)(2,1)S(1)} %get-tuple-element.59), channel_id=1, source_target_pairs={{0,8},{1,9},{2,10},{3,11},{4,12},{5,13},{6,14},{7,15},{8,0},{9,1},... | collective-permute-start | bytes 98312 | tf_op jit(solution)/shard_map/ppermute | solution.py:232
  21.5 0.9 %collective-permute-start.10 = (bf16[128,128]{1,0:T(8,128)(2,1)S(1)}, bf16[128,128]{1,0:T(8,128)(2,1)S(1)}, u32[]{:S(2)}, u32[]{:S(2)}) collective-permute-start(bf16[128,128]{1,0:T(8,128)(2,1)S(1)} %get-tuple-element.60), channel_id=1, source_target_pairs={{0,12},{1,13},{2,14},{3,15},{4,8},{5,9},{6,10},{7,11},{8,4},{9,5},... | collective-permute-start | bytes 98312 | tf_op jit(solution)/shard_map/ppermute | solution.py:232
  22.4 2.5 %collective-permute-done.9.refs_2_ = bf16[128,128]{1,0:T(8,128)(2,1)S(1)} collective-permute-done((bf16[128,128]{1,0:T(8,128)(2,1)S(1)}, bf16[128,128]{1,0:T(8,128)(2,1)S(1)}, u32[]{:S(2)}, u32[]{:S(2)}) %collective-permute-start.9) | collective-permute-done | bytes 32800 | tf_op jit(solution)/shard_map/ppermute | solution.py:232
  24.9 2.3 %collective-permute-done.10.refs_3_ = bf16[128,128]{1,0:T(8,128)(2,1)S(1)} collective-permute-done((bf16[128,128]{1,0:T(8,128)(2,1)S(1)}, bf16[128,128]{1,0:T(8,128)(2,1)S(1)}, u32[]{:S(2)}, u32[]{:S(2)}) %collective-permute-start.10) | collective-permute-done | bytes 32800 | tf_op jit(solution)/shard_map/ppermute | solution.py:232
  27.2 0.0 collective-permute-done.8.refs_1_
  27.2 0.0 collective-permute-done.4.refs_5_
  27.2 0.0 collective-permute-done.3.refs_6_
  27.2 0.1 collective-permute-start.11
  27.3 0.6 %shard_map.61 = (f32[2,32,128]{2,1,0:T(8,128)S(1)}, f32[2,8,2,8,128]{4,3,2,1,0:T(8,128)S(1)}) custom-call(f32[128,128]{1,0:T(8,128)S(1)} %get-tuple-element.61.refs_0_, f32[128,128]{1,0:T(8,128)S(1)} %collective-permute-done.8.refs_1_, bf16[128,128]{1,0:T(8,128)(2,1)S(1)} %collective-permute-done.9.refs_2_, ...), custom_call_target="tpu_custom_call" | custom-call | tf_op jit(solution)/shard_map/pallas_call | solution.py:202
  27.9 0.9 %collective-permute-done.11.queries_ref = bf16[4,8,4096]{2,1,0:T(8,128)(2,1)S(1)} collective-permute-done((bf16[4,8,4096]{2,1,0:T(8,128)(2,1)S(1)}, bf16[4,8,4096]{2,1,0:T(8,128)(2,1)S(1)}, u32[]{:S(2)}, u32[]{:S(2)}) %collective-permute-start.11) | collective-permute-done | bytes 262176 | tf_op jit(solution)/shard_map/ppermute | solution.py:232
  28.8 1.0 %shard_map.62 = f32[2,128]{1,0:T(2,128)} custom-call(f32[2,32,128]{2,1,0:T(8,128)S(1)} %get-tuple-element.67.grads_ref, f32[2,8,2,8,128]{4,3,2,1,0:T(8,128)S(1)} %get-tuple-element.68.before_ref, bf16[4,8,4096]{2,1,0:T(8,128)(2,1)S(1)} %collective-permute-done.11.queries_ref), custom_call_target="tpu_custom_call" | custom-call | tf_op jit(solution)/shard_map/pallas_call | solution.py:215
  (4 shorter events, 0.1 us)
Async XLA Ops:
  0.0 8.2 %copy-start = (bf16[8,4096]{1,0:T(8,128)(2,1)S(1)}, bf16[8,4096]{1,0:T(8,128)(2,1)}, u32[]{:S(2)}) copy-start(bf16[8,4096]{1,0:T(8,128)(2,1)} %param.9) | copy-start | bytes 196612
  0.0 8.1 %collective-permute-start = (bf16[1,8,4096]{2,1,0:T(8,128)(2,1)}, bf16[1,8,4096]{2,1,0:T(8,128)(2,1)S(1)}, u32[]{:S(2)}, u32[]{:S(2)}) collective-permute-start(bf16[1,8,4096]{2,1,0:T(8,128)(2,1)} %bitcast.3), channel_id=1, source_target_pairs={{0,8},{1,9},{2,10},{3,11},{4,12},{5,13},{6,14},{7,15},{8,0},{9,1},... | collective-permute-start | bytes 196616 | tf_op jit(solution)/shard_map/ppermute | solution.py:232
  8.2 1.8 %collective-permute-start.2 = (f32[4,128,128]{2,1,0:T(8,128)S(1)}, f32[4,128,128]{2,1,0:T(8,128)S(1)}, u32[]{:S(2)}, u32[]{:S(2)}) collective-permute-start(f32[4,128,128]{2,1,0:T(8,128)S(1)} %get-tuple-element.41), channel_id=1, source_target_pairs={{0,1},{1,0},{2,3},{3,2},{4,5},{5,4},{6,7},{7,6},{8,9},{9,8},{10,11... | collective-permute-start | bytes 786440 | tf_op jit(solution)/shard_map/ppermute | solution.py:232
  8.3 7.4 %collective-permute-start.1 = (bf16[2,8,4096]{2,1,0:T(8,128)(2,1)S(1)}, bf16[2,8,4096]{2,1,0:T(8,128)(2,1)S(1)}, u32[]{:S(2)}, u32[]{:S(2)}) collective-permute-start(bf16[2,8,4096]{2,1,0:T(8,128)(2,1)S(1)} %shard_map.56.left_ref), channel_id=1, source_target_pairs={{0,4},{1,5},{2,6},{3,7},{4,0},{5,1},{6,2},{7,3},{8,12},{9,13},{10,... | collective-permute-start | bytes 393224 | tf_op jit(solution)/shard_map/ppermute | solution.py:232
  9.9 7.9 %collective-permute-start.5 = (bf16[4,192,128]{2,1,0:T(8,128)(2,1)S(1)}, bf16[4,192,128]{2,1,0:T(8,128)(2,1)S(1)}, u32[]{:S(2)}, u32[]{:S(2)}) collective-permute-start(bf16[4,192,128]{2,1,0:T(8,128)(2,1)S(1)} %shard_map.57), channel_id=1, source_target_pairs={{0,2},{1,3},{2,0},{3,1},{4,6},{5,7},{6,4},{7,5},{8,10},{9,11},{10,... | collective-permute-start | bytes 589832 | tf_op jit(solution)/shard_map/ppermute | solution.py:232
  15.7 11.5 %collective-permute-start.4 = (bf16[4,8,4096]{2,1,0:T(8,128)(2,1)S(1)}, bf16[4,8,4096]{2,1,0:T(8,128)(2,1)S(1)}, u32[]{:S(2)}, u32[]{:S(2)}) collective-permute-start(bf16[4,8,4096]{2,1,0:T(8,128)(2,1)S(1)} %shard_map.59.refs_4_), channel_id=1, source_target_pairs={{0,1},{1,0},{2,3},{3,2},{4,5},{5,4},{6,7},{7,6},{8,9},{9,8},{10,11... | collective-permute-start | bytes 786440 | tf_op jit(solution)/shard_map/ppermute | solution.py:232
  15.8 11.4 %collective-permute-start.3 = (bf16[4,8,4096]{2,1,0:T(8,128)(2,1)S(1)}, bf16[4,8,4096]{2,1,0:T(8,128)(2,1)S(1)}, u32[]{:S(2)}, u32[]{:S(2)}) collective-permute-start(bf16[4,8,4096]{2,1,0:T(8,128)(2,1)S(1)} %shard_map.59.refs_4_), channel_id=1, source_target_pairs={{0,2},{1,3},{2,0},{3,1},{4,6},{5,7},{6,4},{7,5},{8,10},{9,11},{10,... | collective-permute-start | bytes 786440 | tf_op jit(solution)/shard_map/ppermute | solution.py:232
  16.3 1.3 %collective-permute-start.6 = (f32[2,128,128]{2,1,0:T(8,128)S(1)}, f32[2,128,128]{2,1,0:T(8,128)S(1)}, u32[]{:S(2)}, u32[]{:S(2)}) collective-permute-start(f32[2,128,128]{2,1,0:T(8,128)S(1)} %get-tuple-element.52), channel_id=1, source_target_pairs={{0,1},{1,0},{2,3},{3,2},{4,5},{5,4},{6,7},{7,6},{8,9},{9,8},{10,11... | collective-permute-start | bytes 393224 | tf_op jit(solution)/shard_map/ppermute | solution.py:232
  16.5 1.4 %collective-permute-start.7 = (f32[2,128,128]{2,1,0:T(8,128)S(1)}, f32[2,128,128]{2,1,0:T(8,128)S(1)}, u32[]{:S(2)}, u32[]{:S(2)}) collective-permute-start(f32[2,128,128]{2,1,0:T(8,128)S(1)} %get-tuple-element.53), channel_id=1, source_target_pairs={{0,1},{1,0},{2,3},{3,2},{4,5},{5,4},{6,7},{7,6},{8,9},{9,8},{10,11... | collective-permute-start | bytes 393224 | tf_op jit(solution)/shard_map/ppermute | solution.py:232
  17.9 9.3 %collective-permute-start.8 = (f32[128,128]{1,0:T(8,128)S(1)}, f32[128,128]{1,0:T(8,128)S(1)}, u32[]{:S(2)}, u32[]{:S(2)}) collective-permute-start(f32[128,128]{1,0:T(8,128)S(1)} %get-tuple-element.58), channel_id=1, source_target_pairs={{0,4},{1,5},{2,6},{3,7},{4,0},{5,1},{6,2},{7,3},{8,12},{9,13},{10,... | collective-permute-start | bytes 196616 | tf_op jit(solution)/shard_map/ppermute | solution.py:232
  19.4 5.5 %collective-permute-start.9 = (bf16[128,128]{1,0:T(8,128)(2,1)S(1)}, bf16[128,128]{1,0:T(8,128)(2,1)S(1)}, u32[]{:S(2)}, u32[]{:S(2)}) collective-permute-start(bf16[128,128]{1,0:T(8,128)(2,1)S(1)} %get-tuple-element.59), channel_id=1, source_target_pairs={{0,8},{1,9},{2,10},{3,11},{4,12},{5,13},{6,14},{7,15},{8,0},{9,1},... | collective-permute-start | bytes 98312 | tf_op jit(solution)/shard_map/ppermute | solution.py:232
  21.5 5.7 %collective-permute-start.10 = (bf16[128,128]{1,0:T(8,128)(2,1)S(1)}, bf16[128,128]{1,0:T(8,128)(2,1)S(1)}, u32[]{:S(2)}, u32[]{:S(2)}) collective-permute-start(bf16[128,128]{1,0:T(8,128)(2,1)S(1)} %get-tuple-element.60), channel_id=1, source_target_pairs={{0,12},{1,13},{2,14},{3,15},{4,8},{5,9},{6,10},{7,11},{8,4},{9,5},... | collective-permute-start | bytes 98312 | tf_op jit(solution)/shard_map/ppermute | solution.py:232
  27.2 1.6 %collective-permute-start.11 = (bf16[4,8,4096]{2,1,0:T(8,128)(2,1)S(1)}, bf16[4,8,4096]{2,1,0:T(8,128)(2,1)S(1)}, u32[]{:S(2)}, u32[]{:S(2)}) collective-permute-start(bf16[4,8,4096]{2,1,0:T(8,128)(2,1)S(1)} %collective-permute-done.3.refs_6_), channel_id=1, source_target_pairs={{0,1},{1,0},{2,3},{3,2},{4,5},{5,4},{6,7},{7,6},{8,9},{9,8},{10,11... | collective-permute-start | bytes 786440 | tf_op jit(solution)/shard_map/ppermute | solution.py:232

commit v6 on v5

--- a/solution.py
+++ b/solution.py
@@ -9,71 +9,73 @@
 
 SEQ = 64
 VMEM_BYTES = 32 * 1024 * 1024
+AHEAD = 3
 LANES_BY_LANES = (((1,), (1,)), ((), ()))
 HBM_SPEC = pl.BlockSpec(memory_space=pltpu.HBM)
 VMEM_SPEC = pl.BlockSpec(memory_space=pltpu.VMEM)
 PARAMS = pltpu.CompilerParams(vmem_limit_bytes=VMEM_BYTES)
 
 
-def project_kernel(flip, x_hbm, w_hbm, p_in_hbm, p_out_hbm, *refs):
+def project_kernel(x_hbm, w_hbm, p_in_hbm, p_out_hbm, *refs):
+    given_y, given_here, kept_y, kept_here, x_buf, w_buf, p_in, p_out, low, p_sems, x_sems, w_sems = refs
     here = lax.axis_index("ex")
     core, chip = lax.rem(here, 2), lax.div(here, 2)
-    *given_refs, kept_ref, x_buf, w_buf, p_in, p_out, p_sems, sems = refs
-    depth = kept_ref.shape[0]
-    rank, width = kept_ref.shape[1] // 2, kept_ref.shape[2]
-    copies = [
+    depth = kept_y.shape[0]
+    rank, width = kept_y.shape[1] // 2, kept_y.shape[2]
+    matrices = [
         pltpu.make_async_copy(p_in_hbm, p_in, p_sems.at[0]),
         pltpu.make_async_copy(p_out_hbm, p_out, p_sems.at[1]),
     ]
-    for z in range(depth):
-        place = lax.bitwise_xor(chip, 2 * z + flip)
-        columns = pl.ds(pl.multiple_of(place * 2 * width, 2 * width), 2 * width)
-        copies.append(pltpu.make_async_copy(x_hbm.at[:, columns], x_buf.at[z], sems.at[0, z]))
-        copies.append(pltpu.make_async_copy(w_hbm.at[:, columns], w_buf.at[z], sems.at[1, z]))
-    for copy in copies:
+    chunks = []
+    for top, hbm, buf, sems, matrix in ((0, x_hbm, x_buf, x_sems, p_in), (rank, w_hbm, w_buf, w_sems, p_out)):
+        rows = buf.shape[0] // sems.shape[0]
+        for chunk in range(sems.shape[0]):
+            part = pl.ds(chunk * rows, rows)
+            copy = pltpu.make_async_copy(hbm.at[part, :], buf.at[part, :], sems.at[chunk])
+            chunks.append((slice(top, top + rank), part, buf, matrix, copy, chunk == 0))
+    for copy in matrices + [chunk[4] for chunk in chunks[:AHEAD]]:
         copy.start()
-    for copy in copies[:2]:
+    for copy in matrices:
         copy.wait()
-    for z in range(depth):
-        for copy in copies[2 + 2 * z : 4 + 2 * z]:
-            copy.wait()
-        low_in = jnp.dot(p_in[...], x_buf[z], preferred_element_type=jnp.float32)
-        low_out = jnp.dot(p_out[...], w_buf[z], preferred_element_type=jnp.float32)
-        for rows, low in ((slice(0, rank), low_in), (slice(rank, 2 * rank), low_out)):
-            left, right = low[:, :width], low[:, width:]
-            given_ref = given_refs[z * len(given_refs) // depth]
-            given_ref[z % given_ref.shape[0], rows, :] = jnp.where(core == 0, right, left)
-            kept_ref[z, rows, :] = jnp.where(core == 0, left, right)
-
-
-def project(flip, arrays, devices, splits):
-    inputs, out_grads, proj_in_t, proj_out_t = arrays
-    depth = devices // 4
+    step = min(1024, low.shape[1])
+    for index, (lines, part, buf, matrix, copy, first) in enumerate(chunks):
+        copy.wait()
+        if index + AHEAD < len(chunks):
+            chunks[index + AHEAD][4].start()
+        for column in range(0, low.shape[1], step):
+            columns = slice(column, column + step)
+            product = jnp.dot(matrix[:, part], buf[part, columns], preferred_element_type=jnp.float32)
+            low[lines, columns] = product if first else low[lines, columns] + product
+    for flip, given_ref, kept_ref in ((1, given_y, kept_y), (0, given_here, kept_here)):
+        for z in range(depth):
+            place = lax.bitwise_xor(chip, 2 * z + flip)
+            both = low[:, pl.ds(pl.multiple_of(place * 2 * width, 2 * width), 2 * width)]
+            left, right = both[:, :width], both[:, width:]
+            given_ref[z] = jnp.where(core == 0, right, left)
+            kept_ref[z] = jnp.where(core == 0, left, right)
+
+
+def project(inputs, out_grads, proj_in_t, proj_out_t, devices):
+    arrays = [pltpu.with_memory_space_constraint(a, pltpu.HBM) for a in (inputs, out_grads, proj_in_t, proj_out_t)]
     width = inputs.shape[1] // devices
     rank = proj_in_t.shape[0]
-    kept = jax.ShapeDtypeStruct((depth, 2 * rank, width), jnp.float32)
-    given = jax.ShapeDtypeStruct((depth // splits, 2 * rank, width), jnp.float32)
-    *given, kept = pl.pallas_call(
-        functools.partial(project_kernel, flip),
-        out_shape=[given] * splits + [kept],
+    low = jax.ShapeDtypeStruct((devices // 4, 2 * rank, width), jnp.float32)
+    chunks = [a.shape[0] // 256 if a.shape[0] % 256 == 0 else 1 for a in (inputs, out_grads)]
+    return pl.pallas_call(
+        project_kernel,
+        out_shape=[low] * 4,
         in_specs=[HBM_SPEC] * 4,
-        out_specs=[VMEM_SPEC] * (splits + 1),
-        scratch_shapes=[
-            pltpu.VMEM((depth, inputs.shape[0], 2 * width), jnp.bfloat16),
-            pltpu.VMEM((depth, out_grads.shape[0], 2 * width), jnp.bfloat16),
-            pltpu.VMEM(proj_in_t.shape, jnp.bfloat16),
-            pltpu.VMEM(proj_out_t.shape, jnp.bfloat16),
-            pltpu.SemaphoreType.DMA((2,)),
-            pltpu.SemaphoreType.DMA((2, depth)),
-        ],
+        out_specs=[VMEM_SPEC] * 4,
+        scratch_shapes=[pltpu.VMEM(a.shape, jnp.bfloat16) for a in arrays]
+        + [pltpu.VMEM((2 * rank, inputs.shape[1]), jnp.float32), pltpu.SemaphoreType.DMA((2,))]
+        + [pltpu.SemaphoreType.DMA((count,)) for count in chunks],
         compiler_params=PARAMS,
         cost_estimate=pl.CostEstimate(
-            flops=rank * (inputs.size + out_grads.size),
-            bytes_accessed=inputs.size + out_grads.size,
+            flops=2 * rank * (inputs.size + out_grads.size),
+            bytes_accessed=2 * (inputs.size + out_grads.size),
             transcendentals=0,
         ),
     )(*arrays)
-    return given, kept
 
 
 def put_split(out_ref, low):
@@ -105,11 +107,9 @@
     )(kept, came)
 
 
-def add_kept_kernel(kept_ref, across_ref, *refs):
-    came_refs, out_refs = refs[:2], refs[2:]
-    half = came_refs[0].shape[0]
+def add_kept_kernel(kept_ref, came_ref, across_ref, *out_refs):
     for block, out_ref in enumerate(out_refs):
-        total = kept_ref[block] + came_refs[block // half][block % half] + get_split(across_ref.at[block])
+        total = kept_ref[block] + came_ref[block] + get_split(across_ref.at[block])
         out_ref[...] = total.astype(out_ref.dtype)
 
 
@@ -121,7 +121,7 @@
         add_kept_kernel,
         out_shape=[wide if 2 * block < blocks else rounded for block in range(blocks)],
         compiler_params=PARAMS,
-    )(kept, across, *came)
+    )(kept, came, across)
 
 
 def stack_kernel(left_ref, right_ref, out_ref):
@@ -234,19 +234,15 @@
     steps = [1 << bit for bit in reversed(range(chips.bit_length() - 1))]
     held, reach = queries[None], [0]
     came_held = swap(held, chip=steps[0])
-    arrays = [pltpu.with_memory_space_constraint(a, pltpu.HBM) for a in (inputs, out_grads, proj_in.T, proj_out.T)]
-    given, kept = project(1, arrays, devices, 1)
-    came_held, given, kept = together((came_held, given, kept))
-    came = swap(given[0], core=1)
+    lows = project(inputs, out_grads, proj_in.T, proj_out.T, devices)
+    came_held, lows = together((came_held, lows))
+    given_y, given, kept_y, kept = lows
+    came_y = swap(given_y, core=1)
+    came = swap(given, core=1)
     for last, step in zip(steps, steps[1:-1]):
         held, reach = stack(held, came_held), reach + [chip ^ last for chip in reach]
         came_held = swap(held, chip=step)
-    message = add_given(kept, came)
-    message, arrays = together((message, arrays))
-    across = swap(message, chip=1)
-    given, kept = project(0, arrays, devices, 2)
-    came_held, given, kept = together((came_held, given, kept))
-    came = [swap(array, core=1) for array in given]
+    across = swap(add_given(kept_y, came_y), chip=1)
     held, reach = stack(held, came_held), reach + [chip ^ steps[-2] for chip in reach]
     came_held = swap(held, chip=1)
     other_held = swap(held, core=1)

time: 29.9 us -> 29 us (0.970)
  Pallas kernels: 9.92 us -> 6.85 us
  waiting for transfers between devices: 6.72 us -> 8.37 us
  starting transfers between devices: 13 us -> 13.6 us
    pallas_call x2 -> x1, Pallas kernels: 8.2 us -> 5.14 us  [project(): pl.pallas_call(project_kernel, out_shape=[low] * 4, in_specs=[HBM_SPEC] *...]
    ppermute x12 -> x11, waiting for transfers between devices: 6.72 us -> 8.37 us  [swap(): lax.ppermute(array, 'ex', [(i, i ^ distance) for i in range(devices)])]
    ppermute x12 -> x11, starting transfers between devices: 13 us -> 13.6 us  [swap(): lax.ppermute(array, 'ex', [(i, i ^ distance) for i in range(devices)])]
  transfers between devices with their start and end apart: 12 -> 11, of which waited for: 5 -> 6; matrix products, arithmetic and copies ran while one was open for 0% -> 0% of each run, Pallas kernels for 30% -> 20%
where the time goes in v6:
time: 29 us; the launch traced here: 28.9 us
  starting transfers between devices  13.6 us (47%)
  waiting for transfers between devices  8.37 us (29%)
  Pallas kernels  6.85 us (24%)
    ppermute x11, starting transfers between devices, swap(): lax.ppermute(array, 'ex', [(i, i ^ distance) for i in range(devices)])  13.6 us
    ppermute x11, waiting for transfers between devices, swap(): lax.ppermute(array, 'ex', [(i, i ^ distance) for i in range(devices)])  8.37 us
    pallas_call x1, Pallas kernels, project(): pl.pallas_call(project_kernel, out_shape=[low] * 4, in_specs=[HBM_SPEC] *...  5.14 us
    pallas_call x1, Pallas kernels, last_scores(): pl.pallas_call(functools.partial(last_score_kernel, chips), out_shape=jax...  0.98 us
    pallas_call x1, Pallas kernels, first_scores(): pl.pallas_call(functools.partial(first_score_kernel, len(parts), held), o...  0.64 us
  transfers between devices with their start and end apart: 11, of which 6 were waited for; matrix products, arithmetic and copies ran while one was open for 0% of the time, Pallas kernels for 20%

profile of v6, /device:TPU:0, one launch (start us, length us, event | category | flops | bytes accessed | tf_op | source)
XLA Modules:
  0.0 28.9 jit_solution(2300607360319860070)
XLA Ops:
  0.0 0.0 copy-start
  0.0 4.0 %collective-permute-start = (bf16[1,8,4096]{2,1,0:T(8,128)(2,1)}, bf16[1,8,4096]{2,1,0:T(8,128)(2,1)S(1)}, u32[]{:S(2)}, u32[]{:S(2)}) collective-permute-start(bf16[1,8,4096]{2,1,0:T(8,128)(2,1)} %bitcast.3), channel_id=1, source_target_pairs={{0,8},{1,9},{2,10},{3,11},{4,12},{5,13},{6,14},{7,15},{8,0},{9,1},... | collective-permute-start | bytes 196616 | tf_op jit(solution)/shard_map/ppermute | solution.py:232
  4.0 5.1 %shard_map.55 = (f32[4,128,128]{2,1,0:T(8,128)S(1)}, f32[4,128,128]{2,1,0:T(8,128)S(1)}, f32[4,128,128]{2,1,0:T(8,128)S(1)}, f32[4,128,128]{2,1,0:T(8,128)S(1)}) custom-call(bf16[512,2048]{1,0:T(8,128)(2,1)} %x_hbm.1, bf16[1792,2048]{1,0:T(8,128)(2,1)} %w_hbm.1, bf16[64,512]{1,0:T(8,128)(2,1)} %bitcast.6, bf16[64,1792]{1,0:T(8,128)(2,1)} %bitcast.5), custom_call_target="tpu_custom_call" | custom-call | flops 603979776 | bytes 9437184 | tf_op jit(solution)/shard_map/pallas_call | solution.py:64
  9.2 0.0 collective-permute-done.right_ref
  9.2 0.1 collective-permute-start.4
  9.3 0.0 copy-done
  9.3 1.6 %collective-permute-start.1 = (bf16[2,8,4096]{2,1,0:T(8,128)(2,1)S(1)}, bf16[2,8,4096]{2,1,0:T(8,128)(2,1)S(1)}, u32[]{:S(2)}, u32[]{:S(2)}) collective-permute-start(bf16[2,8,4096]{2,1,0:T(8,128)(2,1)S(1)} %shard_map.56.left_ref), channel_id=1, source_target_pairs={{0,4},{1,5},{2,6},{3,7},{4,0},{5,1},{6,2},{7,3},{8,12},{9,13},{10,... | collective-permute-start | bytes 393224 | tf_op jit(solution)/shard_map/ppermute | solution.py:232
  10.9 0.2 collective-permute-start.6
  11.2 0.0 collective-permute-done.4.came_ref
  11.2 1.6 %collective-permute-start.5 = (bf16[4,192,128]{2,1,0:T(8,128)(2,1)S(1)}, bf16[4,192,128]{2,1,0:T(8,128)(2,1)S(1)}, u32[]{:S(2)}, u32[]{:S(2)}) collective-permute-start(bf16[4,192,128]{2,1,0:T(8,128)(2,1)S(1)} %shard_map.58), channel_id=1, source_target_pairs={{0,2},{1,3},{2,0},{3,1},{4,6},{5,7},{6,4},{7,5},{8,10},{9,11},{10,... | collective-permute-start | bytes 589832 | tf_op jit(solution)/shard_map/ppermute | solution.py:232
  12.8 2.5 %collective-permute-done.1.right_ref = bf16[2,8,4096]{2,1,0:T(8,128)(2,1)S(1)} collective-permute-done((bf16[2,8,4096]{2,1,0:T(8,128)(2,1)S(1)}, bf16[2,8,4096]{2,1,0:T(8,128)(2,1)S(1)}, u32[]{:S(2)}, u32[]{:S(2)}) %collective-permute-start.1) | collective-permute-done | bytes 131104 | tf_op jit(solution)/shard_map/ppermute | solution.py:232
  15.3 1.6 %collective-permute-start.2 = (bf16[4,8,4096]{2,1,0:T(8,128)(2,1)S(1)}, bf16[4,8,4096]{2,1,0:T(8,128)(2,1)S(1)}, u32[]{:S(2)}, u32[]{:S(2)}) collective-permute-start(bf16[4,8,4096]{2,1,0:T(8,128)(2,1)S(1)} %shard_map.57.refs_4_), channel_id=1, source_target_pairs={{0,2},{1,3},{2,0},{3,1},{4,6},{5,7},{6,4},{7,5},{8,10},{9,11},{10,... | collective-permute-start | bytes 786440 | tf_op jit(solution)/shard_map/ppermute | solution.py:232
  16.9 0.0 collective-permute-start.3
  16.9 0.0 collective-permute-done.6.came_ref
  16.9 2.1 %collective-permute-done.5.across_ref = bf16[4,192,128]{2,1,0:T(8,128)(2,1)S(1)} collective-permute-done((bf16[4,192,128]{2,1,0:T(8,128)(2,1)S(1)}, bf16[4,192,128]{2,1,0:T(8,128)(2,1)S(1)}, u32[]{:S(2)}, u32[]{:S(2)}) %collective-permute-start.5) | collective-permute-done | bytes 196640 | tf_op jit(solution)/shard_map/ppermute | solution.py:232
  19.0 0.6 %collective-permute-start.7 = (f32[128,128]{1,0:T(8,128)S(1)}, f32[128,128]{1,0:T(8,128)S(1)}, u32[]{:S(2)}, u32[]{:S(2)}) collective-permute-start(f32[128,128]{1,0:T(8,128)S(1)} %get-tuple-element.40), channel_id=1, source_target_pairs={{0,4},{1,5},{2,6},{3,7},{4,0},{5,1},{6,2},{7,3},{8,12},{9,13},{10,... | collective-permute-start | bytes 196616 | tf_op jit(solution)/shard_map/ppermute | solution.py:232
  19.7 1.0 %collective-permute-start.8 = (bf16[128,128]{1,0:T(8,128)(2,1)S(1)}, bf16[128,128]{1,0:T(8,128)(2,1)S(1)}, u32[]{:S(2)}, u32[]{:S(2)}) collective-permute-start(bf16[128,128]{1,0:T(8,128)(2,1)S(1)} %get-tuple-element.41), channel_id=1, source_target_pairs={{0,8},{1,9},{2,10},{3,11},{4,12},{5,13},{6,14},{7,15},{8,0},{9,1},... | collective-permute-start | bytes 98312 | tf_op jit(solution)/shard_map/ppermute | solution.py:232
  20.6 2.8 %collective-permute-start.9 = (bf16[128,128]{1,0:T(8,128)(2,1)S(1)}, bf16[128,128]{1,0:T(8,128)(2,1)S(1)}, u32[]{:S(2)}, u32[]{:S(2)}) collective-permute-start(bf16[128,128]{1,0:T(8,128)(2,1)S(1)} %get-tuple-element.42), channel_id=1, source_target_pairs={{0,12},{1,13},{2,14},{3,15},{4,8},{5,9},{6,10},{7,11},{8,4},{9,5},... | collective-permute-start | bytes 98312 | tf_op jit(solution)/shard_map/ppermute | solution.py:232
  23.5 0.5 %collective-permute-done.2.refs_6_ = bf16[4,8,4096]{2,1,0:T(8,128)(2,1)S(1)} collective-permute-done((bf16[4,8,4096]{2,1,0:T(8,128)(2,1)S(1)}, bf16[4,8,4096]{2,1,0:T(8,128)(2,1)S(1)}, u32[]{:S(2)}, u32[]{:S(2)}) %collective-permute-start.2) | collective-permute-done | bytes 262176 | tf_op jit(solution)/shard_map/ppermute | solution.py:232
  24.0 0.0 collective-permute-done.3.refs_5_
  24.0 0.6 %collective-permute-done.8.refs_2_ = bf16[128,128]{1,0:T(8,128)(2,1)S(1)} collective-permute-done((bf16[128,128]{1,0:T(8,128)(2,1)S(1)}, bf16[128,128]{1,0:T(8,128)(2,1)S(1)}, u32[]{:S(2)}, u32[]{:S(2)}) %collective-permute-start.8) | collective-permute-done | bytes 32800 | tf_op jit(solution)/shard_map/ppermute | solution.py:232
  24.6 1.7 %collective-permute-done.9.refs_3_ = bf16[128,128]{1,0:T(8,128)(2,1)S(1)} collective-permute-done((bf16[128,128]{1,0:T(8,128)(2,1)S(1)}, bf16[128,128]{1,0:T(8,128)(2,1)S(1)}, u32[]{:S(2)}, u32[]{:S(2)}) %collective-permute-start.9) | collective-permute-done | bytes 32800 | tf_op jit(solution)/shard_map/ppermute | solution.py:232
  26.4 0.0 collective-permute-done.7.refs_1_
  26.4 0.0 collective-permute-start.10
  26.4 0.6 %shard_map.60 = (f32[2,32,128]{2,1,0:T(8,128)S(1)}, f32[2,8,2,8,128]{4,3,2,1,0:T(8,128)S(1)}) custom-call(f32[128,128]{1,0:T(8,128)S(1)} %get-tuple-element.43.refs_0_, f32[128,128]{1,0:T(8,128)S(1)} %collective-permute-done.7.refs_1_, bf16[128,128]{1,0:T(8,128)(2,1)S(1)} %collective-permute-done.8.refs_2_, ...), custom_call_target="tpu_custom_call" | custom-call | tf_op jit(solution)/shard_map/pallas_call | solution.py:202
  27.0 0.9 %collective-permute-done.10.queries_ref = bf16[4,8,4096]{2,1,0:T(8,128)(2,1)S(1)} collective-permute-done((bf16[4,8,4096]{2,1,0:T(8,128)(2,1)S(1)}, bf16[4,8,4096]{2,1,0:T(8,128)(2,1)S(1)}, u32[]{:S(2)}, u32[]{:S(2)}) %collective-permute-start.10) | collective-permute-done | bytes 262176 | tf_op jit(solution)/shard_map/ppermute | solution.py:232
  27.9 1.0 %shard_map.61 = f32[2,128]{1,0:T(2,128)} custom-call(f32[2,32,128]{2,1,0:T(8,128)S(1)} %get-tuple-element.49.grads_ref, f32[2,8,2,8,128]{4,3,2,1,0:T(8,128)S(1)} %get-tuple-element.50.before_ref, bf16[4,8,4096]{2,1,0:T(8,128)(2,1)S(1)} %collective-permute-done.10.queries_ref), custom_call_target="tpu_custom_call" | custom-call | tf_op jit(solution)/shard_map/pallas_call | solution.py:215
  (4 shorter events, 0.1 us)
Async XLA Ops:
  0.0 9.3 %copy-start = (bf16[8,4096]{1,0:T(8,128)(2,1)S(1)}, bf16[8,4096]{1,0:T(8,128)(2,1)}, u32[]{:S(2)}) copy-start(bf16[8,4096]{1,0:T(8,128)(2,1)} %param.9) | copy-start | bytes 196612
  0.0 9.2 %collective-permute-start = (bf16[1,8,4096]{2,1,0:T(8,128)(2,1)}, bf16[1,8,4096]{2,1,0:T(8,128)(2,1)S(1)}, u32[]{:S(2)}, u32[]{:S(2)}) collective-permute-start(bf16[1,8,4096]{2,1,0:T(8,128)(2,1)} %bitcast.3), channel_id=1, source_target_pairs={{0,8},{1,9},{2,10},{3,11},{4,12},{5,13},{6,14},{7,15},{8,0},{9,1},... | collective-permute-start | bytes 196616 | tf_op jit(solution)/shard_map/ppermute | solution.py:232
  9.2 2.0 %collective-permute-start.4 = (f32[4,128,128]{2,1,0:T(8,128)S(1)}, f32[4,128,128]{2,1,0:T(8,128)S(1)}, u32[]{:S(2)}, u32[]{:S(2)}) collective-permute-start(f32[4,128,128]{2,1,0:T(8,128)S(1)} %get-tuple-element.35), channel_id=1, source_target_pairs={{0,1},{1,0},{2,3},{3,2},{4,5},{5,4},{6,7},{7,6},{8,9},{9,8},{10,11... | collective-permute-start | bytes 786440 | tf_op jit(solution)/shard_map/ppermute | solution.py:232
  9.3 6.0 %collective-permute-start.1 = (bf16[2,8,4096]{2,1,0:T(8,128)(2,1)S(1)}, bf16[2,8,4096]{2,1,0:T(8,128)(2,1)S(1)}, u32[]{:S(2)}, u32[]{:S(2)}) collective-permute-start(bf16[2,8,4096]{2,1,0:T(8,128)(2,1)S(1)} %shard_map.56.left_ref), channel_id=1, source_target_pairs={{0,4},{1,5},{2,6},{3,7},{4,0},{5,1},{6,2},{7,3},{8,12},{9,13},{10,... | collective-permute-start | bytes 393224 | tf_op jit(solution)/shard_map/ppermute | solution.py:232
  10.9 5.9 %collective-permute-start.6 = (f32[4,128,128]{2,1,0:T(8,128)S(1)}, f32[4,128,128]{2,1,0:T(8,128)S(1)}, u32[]{:S(2)}, u32[]{:S(2)}) collective-permute-start(f32[4,128,128]{2,1,0:T(8,128)S(1)} %get-tuple-element.36), channel_id=1, source_target_pairs={{0,1},{1,0},{2,3},{3,2},{4,5},{5,4},{6,7},{7,6},{8,9},{9,8},{10,11... | collective-permute-start | bytes 786440 | tf_op jit(solution)/shard_map/ppermute | solution.py:232
  11.2 7.8 %collective-permute-start.5 = (bf16[4,192,128]{2,1,0:T(8,128)(2,1)S(1)}, bf16[4,192,128]{2,1,0:T(8,128)(2,1)S(1)}, u32[]{:S(2)}, u32[]{:S(2)}) collective-permute-start(bf16[4,192,128]{2,1,0:T(8,128)(2,1)S(1)} %shard_map.58), channel_id=1, source_target_pairs={{0,2},{1,3},{2,0},{3,1},{4,6},{5,7},{6,4},{7,5},{8,10},{9,11},{10,... | collective-permute-start | bytes 589832 | tf_op jit(solution)/shard_map/ppermute | solution.py:232
  15.3 8.7 %collective-permute-start.2 = (bf16[4,8,4096]{2,1,0:T(8,128)(2,1)S(1)}, bf16[4,8,4096]{2,1,0:T(8,128)(2,1)S(1)}, u32[]{:S(2)}, u32[]{:S(2)}) collective-permute-start(bf16[4,8,4096]{2,1,0:T(8,128)(2,1)S(1)} %shard_map.57.refs_4_), channel_id=1, source_target_pairs={{0,2},{1,3},{2,0},{3,1},{4,6},{5,7},{6,4},{7,5},{8,10},{9,11},{10,... | collective-permute-start | bytes 786440 | tf_op jit(solution)/shard_map/ppermute | solution.py:232
  16.9 7.1 %collective-permute-start.3 = (bf16[4,8,4096]{2,1,0:T(8,128)(2,1)S(1)}, bf16[4,8,4096]{2,1,0:T(8,128)(2,1)S(1)}, u32[]{:S(2)}, u32[]{:S(2)}) collective-permute-start(bf16[4,8,4096]{2,1,0:T(8,128)(2,1)S(1)} %shard_map.57.refs_4_), channel_id=1, source_target_pairs={{0,1},{1,0},{2,3},{3,2},{4,5},{5,4},{6,7},{7,6},{8,9},{9,8},{10,11... | collective-permute-start | bytes 786440 | tf_op jit(solution)/shard_map/ppermute | solution.py:232
  19.0 7.3 %collective-permute-start.7 = (f32[128,128]{1,0:T(8,128)S(1)}, f32[128,128]{1,0:T(8,128)S(1)}, u32[]{:S(2)}, u32[]{:S(2)}) collective-permute-start(f32[128,128]{1,0:T(8,128)S(1)} %get-tuple-element.40), channel_id=1, source_target_pairs={{0,4},{1,5},{2,6},{3,7},{4,0},{5,1},{6,2},{7,3},{8,12},{9,13},{10,... | collective-permute-start | bytes 196616 | tf_op jit(solution)/shard_map/ppermute | solution.py:232
  19.7 5.0 %collective-permute-start.8 = (bf16[128,128]{1,0:T(8,128)(2,1)S(1)}, bf16[128,128]{1,0:T(8,128)(2,1)S(1)}, u32[]{:S(2)}, u32[]{:S(2)}) collective-permute-start(bf16[128,128]{1,0:T(8,128)(2,1)S(1)} %get-tuple-element.41), channel_id=1, source_target_pairs={{0,8},{1,9},{2,10},{3,11},{4,12},{5,13},{6,14},{7,15},{8,0},{9,1},... | collective-permute-start | bytes 98312 | tf_op jit(solution)/shard_map/ppermute | solution.py:232
  20.6 5.7 %collective-permute-start.9 = (bf16[128,128]{1,0:T(8,128)(2,1)S(1)}, bf16[128,128]{1,0:T(8,128)(2,1)S(1)}, u32[]{:S(2)}, u32[]{:S(2)}) collective-permute-start(bf16[128,128]{1,0:T(8,128)(2,1)S(1)} %get-tuple-element.42), channel_id=1, source_target_pairs={{0,12},{1,13},{2,14},{3,15},{4,8},{5,9},{6,10},{7,11},{8,4},{9,5},... | collective-permute-start | bytes 98312 | tf_op jit(solution)/shard_map/ppermute | solution.py:232
  26.4 1.5 %collective-permute-start.10 = (bf16[4,8,4096]{2,1,0:T(8,128)(2,1)S(1)}, bf16[4,8,4096]{2,1,0:T(8,128)(2,1)S(1)}, u32[]{:S(2)}, u32[]{:S(2)}) collective-permute-start(bf16[4,8,4096]{2,1,0:T(8,128)(2,1)S(1)} %collective-permute-done.2.refs_6_), channel_id=1, source_target_pairs={{0,1},{1,0},{2,3},{3,2},{4,5},{5,4},{6,7},{7,6},{8,9},{9,8},{10,11... | collective-permute-start | bytes 786440 | tf_op jit(solution)/shard_map/ppermute | solution.py:232

commit v7 on v6

--- a/solution.py
+++ b/solution.py
@@ -10,6 +10,7 @@
 SEQ = 64
 VMEM_BYTES = 32 * 1024 * 1024
 AHEAD = 3
+CODE_SCALE = 2.0**-8
 LANES_BY_LANES = (((1,), (1,)), ((), ()))
 HBM_SPEC = pl.BlockSpec(memory_space=pltpu.HBM)
 VMEM_SPEC = pl.BlockSpec(memory_space=pltpu.VMEM)
@@ -29,19 +30,25 @@
     chunks = []
     for top, hbm, buf, sems, matrix in ((0, x_hbm, x_buf, x_sems, p_in), (rank, w_hbm, w_buf, w_sems, p_out)):
         rows = buf.shape[0] // sems.shape[0]
+        pieces = sems.shape[1]
         for chunk in range(sems.shape[0]):
+            copies = []
+            for piece in range(pieces):
+                part = pl.ds(chunk * rows + piece * (rows // pieces), rows // pieces)
+                copies.append(pltpu.make_async_copy(hbm.at[part, :], buf.at[part, :], sems.at[chunk, piece]))
             part = pl.ds(chunk * rows, rows)
-            copy = pltpu.make_async_copy(hbm.at[part, :], buf.at[part, :], sems.at[chunk])
-            chunks.append((slice(top, top + rank), part, buf, matrix, copy, chunk == 0))
-    for copy in matrices + [chunk[4] for chunk in chunks[:AHEAD]]:
+            chunks.append((slice(top, top + rank), part, buf, matrix, copies, chunk == 0))
+    for copy in matrices + [copy for chunk in chunks[:AHEAD] for copy in chunk[4]]:
         copy.start()
     for copy in matrices:
         copy.wait()
     step = min(1024, low.shape[1])
-    for index, (lines, part, buf, matrix, copy, first) in enumerate(chunks):
-        copy.wait()
+    for index, (lines, part, buf, matrix, copies, first) in enumerate(chunks):
+        for copy in copies:
+            copy.wait()
         if index + AHEAD < len(chunks):
-            chunks[index + AHEAD][4].start()
+            for copy in chunks[index + AHEAD][4]:
+                copy.start()
         for column in range(0, low.shape[1], step):
             columns = slice(column, column + step)
             product = jnp.dot(matrix[:, part], buf[part, columns], preferred_element_type=jnp.float32)
@@ -60,7 +67,7 @@
     width = inputs.shape[1] // devices
     rank = proj_in_t.shape[0]
     low = jax.ShapeDtypeStruct((devices // 4, 2 * rank, width), jnp.float32)
-    chunks = [a.shape[0] // 256 if a.shape[0] % 256 == 0 else 1 for a in (inputs, out_grads)]
+    chunks = [(a.shape[0] // 256, 4) if a.shape[0] % 256 == 0 else (1, 1) for a in (inputs, out_grads)]
     return pl.pallas_call(
         project_kernel,
         out_shape=[low] * 4,
@@ -68,7 +75,7 @@
         out_specs=[VMEM_SPEC] * 4,
         scratch_shapes=[pltpu.VMEM(a.shape, jnp.bfloat16) for a in arrays]
         + [pltpu.VMEM((2 * rank, inputs.shape[1]), jnp.float32), pltpu.SemaphoreType.DMA((2,))]
-        + [pltpu.SemaphoreType.DMA((count,)) for count in chunks],
+        + [pltpu.SemaphoreType.DMA(count) for count in chunks],
         compiler_params=PARAMS,
         cost_estimate=pl.CostEstimate(
             flops=2 * rank * (inputs.size + out_grads.size),
@@ -78,48 +85,58 @@
     )(*arrays)
 
 
-def put_split(out_ref, low):
-    rank = low.shape[0] // 2
-    low_in = low[:rank, :]
-    high = low_in.astype(jnp.bfloat16)
-    out_ref[:rank, :] = high
-    out_ref[rank : 2 * rank, :] = low[rank:, :].astype(jnp.bfloat16)
-    out_ref[2 * rank :, :] = (low_in - high.astype(jnp.float32)).astype(jnp.bfloat16)
-
-
-def get_split(ref):
-    rank = ref.shape[0] // 3
-    low_in = ref[:rank, :].astype(jnp.float32) + ref[2 * rank :, :].astype(jnp.float32)
-    return jnp.concatenate([low_in, ref[rank : 2 * rank, :].astype(jnp.float32)], axis=0)
+def put_coded(out_ref, low):
+    rows = low.shape[0]
+    rounded = low.astype(jnp.bfloat16)
+    out_ref[:rows, :] = rounded
+    rounded = rounded.astype(jnp.float32)
+    left = (low - rounded) / jnp.maximum(jnp.abs(rounded) * CODE_SCALE, 1e-30)
+    level = jnp.clip(jnp.floor(2.0 * left) + 2.0, 0.0, 3.0)
+    part = rows // 4
+    word = level[:part, :]
+    for index in range(1, 4):
+        word = word + 4.0**index * level[index * part : (index + 1) * part, :]
+    out_ref[rows:, :] = word.astype(jnp.bfloat16)
+
+
+def get_coded(ref):
+    part = ref.shape[0] // 5
+    word = ref[4 * part :, :].astype(jnp.float32).astype(jnp.int32)
+    level = jnp.concatenate([jnp.bitwise_and(jnp.right_shift(word, 2 * index), 3) for index in range(4)], axis=0)
+    rounded = ref[: 4 * part, :].astype(jnp.float32)
+    return rounded + jnp.abs(rounded) * (CODE_SCALE * 0.5) * (level.astype(jnp.float32) - 1.5)
 
 
 def add_given_kernel(kept_ref, came_ref, out_ref):
     for block in range(out_ref.shape[0]):
-        put_split(out_ref.at[block], kept_ref[block] + came_ref[block])
+        put_coded(out_ref.at[block], kept_ref[block] + came_ref[block])
 
 
 def add_given(kept, came):
     blocks, rows, width = kept.shape
     return pl.pallas_call(
         add_given_kernel,
-        out_shape=jax.ShapeDtypeStruct((blocks, rows // 2 * 3, width), jnp.bfloat16),
+        out_shape=jax.ShapeDtypeStruct((blocks, rows // 4 * 5, width), jnp.bfloat16),
         compiler_params=PARAMS,
     )(kept, came)
 
 
-def add_kept_kernel(kept_ref, came_ref, across_ref, *out_refs):
-    for block, out_ref in enumerate(out_refs):
-        total = kept_ref[block] + came_ref[block] + get_split(across_ref.at[block])
-        out_ref[...] = total.astype(out_ref.dtype)
+def add_kept_kernel(kept_ref, came_ref, across_ref, own_ref, out_ref):
+    here = lax.div(lax.axis_index("ex"), 4)
+    for z in range(out_ref.shape[0]):
+        total = kept_ref[z] + came_ref[z] + get_coded(across_ref.at[z])
+        if z == 0:
+            own_ref[...] = total
+        out_ref[lax.bitwise_xor(here, z)] = total.astype(out_ref.dtype)
 
 
 def add_kept(kept, came, across):
-    blocks, rows, width = kept.shape
-    wide = jax.ShapeDtypeStruct((rows, width), jnp.float32)
-    rounded = jax.ShapeDtypeStruct((rows, width), jnp.bfloat16)
     return pl.pallas_call(
         add_kept_kernel,
-        out_shape=[wide if 2 * block < blocks else rounded for block in range(blocks)],
+        out_shape=[
+            jax.ShapeDtypeStruct(kept.shape[1:], jnp.float32),
+            jax.ShapeDtypeStruct(kept.shape, jnp.bfloat16),
+        ],
         compiler_params=PARAMS,
     )(kept, came, across)
 
@@ -155,14 +172,13 @@
                 sums_ref[n, source, place] = sums[n][part * held : (part + 1) * held, :]
 
 
-def first_score_kernel(parts_count, held, *refs):
-    part_refs, query_refs = refs[:parts_count], refs[parts_count : parts_count + len(held)]
-    grads_ref, sums_ref, out_t_ref = refs[parts_count + len(held) :]
+def first_score_kernel(held, own_ref, parts_ref, *refs):
+    query_refs, (grads_ref, sums_ref, out_t_ref) = refs[: len(held)], refs[len(held) :]
     rank, tokens = out_t_ref.shape
     core = lax.rem(lax.axis_index("ex"), 2)
-    total = part_refs[0][...]
-    for part_ref in part_refs[1:]:
-        total = total + part_ref[...].astype(jnp.float32)
+    total = own_ref[...] - own_ref[...].astype(jnp.bfloat16).astype(jnp.float32)
+    for z in range(parts_ref.shape[0]):
+        total = total + parts_ref[z].astype(jnp.float32)
     out_t_ref[...] = total[rank:, :]
     even = out_t_ref[pl.ds(0, rank // 2, stride=2), :]
     odd = out_t_ref[pl.ds(1, rank // 2, stride=2), :]
@@ -178,10 +194,11 @@
         add_scores(queries_ref, chips, lax.rem(core + other, 2), grads_ref, sums_ref)
 
 
-def last_score_kernel(chips, grads_ref, before_ref, queries_ref, out_ref, sums_ref):
+def last_score_kernel(chips, grads_ref, before_ref, queries_ref, others_ref, out_ref, sums_ref):
     core = lax.rem(lax.axis_index("ex"), 2)
     sums_ref[...] = before_ref[...]
-    add_scores(queries_ref, chips, lax.rem(core + 1, 2), grads_ref, sums_ref)
+    add_scores(queries_ref, chips, core, grads_ref, sums_ref)
+    add_scores(others_ref, chips, lax.rem(core + 1, 2), grads_ref, sums_ref)
     examples, *rows, lanes = sums_ref.shape
     ones = jnp.ones((8, lanes), jnp.float32)
     for n in range(examples):
@@ -195,29 +212,29 @@
         out_ref[n : n + 1, :] = row[0:1, :]
 
 
-def first_scores(parts, queries, held, rank):
-    tokens = parts[0].shape[1]
+def first_scores(own, parts, queries, held, rank):
+    tokens = own.shape[1]
     examples = tokens // SEQ
     chips = 2 * queries[0].shape[0]
     return pl.pallas_call(
-        functools.partial(first_score_kernel, len(parts), held),
+        functools.partial(first_score_kernel, held),
         out_shape=[
             jax.ShapeDtypeStruct((examples, rank // 2, 2 * rank), jnp.float32),
             jax.ShapeDtypeStruct((examples, chips, 2, queries[0].shape[1], 2 * rank), jnp.float32),
         ],
         scratch_shapes=[pltpu.VMEM((rank, tokens), jnp.float32)],
         compiler_params=PARAMS,
-    )(*parts, *queries)
-
-
-def last_scores(grads, sums, queries, chips):
+    )(own, parts, *queries)
+
+
+def last_scores(grads, sums, queries, others, chips):
     examples, all_chips, cores, held, _ = sums.shape
     return pl.pallas_call(
         functools.partial(last_score_kernel, chips),
         out_shape=jax.ShapeDtypeStruct((examples, all_chips * cores * held), jnp.float32),
         scratch_shapes=[pltpu.VMEM(sums.shape, jnp.float32)],
         compiler_params=PARAMS,
-    )(grads, sums, queries)
+    )(grads, sums, queries, others)
 
 
 def shards(inputs, out_grads, proj_in, proj_out, queries):
@@ -248,15 +265,13 @@
     other_held = swap(held, core=1)
     across, came = together((across, came))
 
-    sums = add_kept(kept, came, across)
-    parts = list(sums)
-    for z in list(range(depth // 2, depth)) + list(range(1, depth // 2)):
-        parts[z] = swap(parts[z], chip=2 * z)
+    own, sums = add_kept(kept, came, across)
+    z_lines = [list(range(first, devices, 4)) for first in range(4)]
+    parts = lax.all_to_all(sums, "ex", split_axis=0, concat_axis=0, tiled=True, axis_index_groups=z_lines)
     came_held, other_held, parts = together((came_held, other_held, parts))
     other_came = swap(came_held, core=1)
-    reach_y = [chip ^ 1 for chip in reach]
-    grads, scores = first_scores(parts, [held, other_held, came_held], [(0, reach), (1, reach), (0, reach_y)], rank)
-    return last_scores(grads, scores, other_came, reach_y)
+    grads, scores = first_scores(own, parts, [held, other_held], [(0, reach), (1, reach)], rank)
+    return last_scores(grads, scores, came_held, other_came, [chip ^ 1 for chip in reach])
 
 
 def solution(mesh):

time: 29 us -> 31.3 us (1.079)
  waiting for transfers between devices: 8.37 us -> 9.99 us
  Pallas kernels: 6.85 us -> 8.26 us
  starting transfers between devices: 13.6 us -> 12.7 us
    all_to_all x0 -> x1, waiting for transfers between devices: none -> 4.72 us  [shards(): lax.all_to_all(sums, 'ex', split_axis=0, concat_axis=0, tiled=True, axis_...]
    ppermute x11 -> x8, starting transfers between devices: 13.6 us -> 9.42 us  [swap(): lax.ppermute(array, 'ex', [(i, i ^ distance) for i in range(devices)])]
    all_to_all x0 -> x1, starting transfers between devices: none -> 3.32 us  [shards(): lax.all_to_all(sums, 'ex', split_axis=0, concat_axis=0, tiled=True, axis_...]
    ppermute x11 -> x8, waiting for transfers between devices: 8.37 us -> 5.27 us  [swap(): lax.ppermute(array, 'ex', [(i, i ^ distance) for i in range(devices)])]
    pallas_call x2, Pallas kernels: 0.68 us -> 1.32 us  [the longest x1 0.76 us: add_kept(): pl.pallas_call(add_kept_kernel, out_shape=[jax.ShapeDtypeStruct(kept.shap...]
    pallas_call x1, Pallas kernels: 5.14 us -> 5.72 us  [project(): pl.pallas_call(project_kernel, out_shape=[low] * 4, in_specs=[HBM_SPEC] *...]
  transfers between devices with their start and end apart: 11 -> 9, of which waited for: 6 -> 5; matrix products, arithmetic and copies ran while one was open for 0% -> 0% of each run, Pallas kernels for 20% -> 23%
where the time goes in v7:
time: 31.3 us; the launch traced here: 31.1 us
  starting transfers between devices  12.7 us (41%)
  waiting for transfers between devices  9.99 us (32%)
  Pallas kernels  8.26 us (26%)
    ppermute x8, starting transfers between devices, swap(): lax.ppermute(array, 'ex', [(i, i ^ distance) for i in range(devices)])  9.42 us
    pallas_call x1, Pallas kernels, project(): pl.pallas_call(project_kernel, out_shape=[low] * 4, in_specs=[HBM_SPEC] *...  5.72 us
    ppermute x8, waiting for transfers between devices, swap(): lax.ppermute(array, 'ex', [(i, i ^ distance) for i in range(devices)])  5.27 us
    all_to_all x1, waiting for transfers between devices, shards(): lax.all_to_all(sums, 'ex', split_axis=0, concat_axis=0, tiled=True, axis_...  4.72 us
    all_to_all x1, starting transfers between devices, shards(): lax.all_to_all(sums, 'ex', split_axis=0, concat_axis=0, tiled=True, axis_...  3.32 us
    pallas_call x1, Pallas kernels, last_scores(): pl.pallas_call(functools.partial(last_score_kernel, chips), out_shape=jax...  1.06 us
    pallas_call x1, Pallas kernels, add_kept(): pl.pallas_call(add_kept_kernel, out_shape=[jax.ShapeDtypeStruct(kept.shap...  0.76 us
  transfers between devices with their start and end apart: 9, of which 5 were waited for; matrix products, arithmetic and copies ran while one was open for 0% of the time, Pallas kernels for 23%

profile of v7, /device:TPU:0, one launch (start us, length us, event | category | flops | bytes accessed | tf_op | source)
XLA Modules:
  0.0 31.1 jit_solution(4684447453504377036)
XLA Ops:
  0.0 0.0 copy-start
  0.0 4.0 %collective-permute-start = (bf16[1,8,4096]{2,1,0:T(8,128)(2,1)}, bf16[1,8,4096]{2,1,0:T(8,128)(2,1)S(1)}, u32[]{:S(2)}, u32[]{:S(2)}) collective-permute-start(bf16[1,8,4096]{2,1,0:T(8,128)(2,1)} %bitcast.3), channel_id=1, source_target_pairs={{0,8},{1,9},{2,10},{3,11},{4,12},{5,13},{6,14},{7,15},{8,0},{9,1},... | collective-permute-start | bytes 196616 | tf_op jit(solution)/shard_map/ppermute | solution.py:249
  4.0 5.7 %shard_map.55 = (f32[4,128,128]{2,1,0:T(8,128)S(1)}, f32[4,128,128]{2,1,0:T(8,128)S(1)}, f32[4,128,128]{2,1,0:T(8,128)S(1)}, f32[4,128,128]{2,1,0:T(8,128)S(1)}) custom-call(bf16[512,2048]{1,0:T(8,128)(2,1)} %x_hbm.1, bf16[1792,2048]{1,0:T(8,128)(2,1)} %w_hbm.1, bf16[64,512]{1,0:T(8,128)(2,1)} %bitcast.6, bf16[64,1792]{1,0:T(8,128)(2,1)} %bitcast.5), custom_call_target="tpu_custom_call" | custom-call | flops 603979776 | bytes 9437184 | tf_op jit(solution)/shard_map/pallas_call | solution.py:71
  9.8 0.0 collective-permute-done.right_ref
  9.8 0.1 collective-permute-start.1
  9.9 0.5 %collective-permute-start.3 = (f32[4,128,128]{2,1,0:T(8,128)S(1)}, f32[4,128,128]{2,1,0:T(8,128)S(1)}, u32[]{:S(2)}, u32[]{:S(2)}) collective-permute-start(f32[4,128,128]{2,1,0:T(8,128)S(1)} %get-tuple-element.30), channel_id=1, source_target_pairs={{0,1},{1,0},{2,3},{3,2},{4,5},{5,4},{6,7},{7,6},{8,9},{9,8},{10,11... | collective-permute-start | bytes 786440 | tf_op jit(solution)/shard_map/ppermute | solution.py:249
  10.4 0.0 copy-done
  10.4 1.6 %collective-permute-start.4 = (bf16[2,8,4096]{2,1,0:T(8,128)(2,1)S(1)}, bf16[2,8,4096]{2,1,0:T(8,128)(2,1)S(1)}, u32[]{:S(2)}, u32[]{:S(2)}) collective-permute-start(bf16[2,8,4096]{2,1,0:T(8,128)(2,1)S(1)} %shard_map.58.left_ref), channel_id=1, source_target_pairs={{0,4},{1,5},{2,6},{3,7},{4,0},{5,1},{6,2},{7,3},{8,12},{9,13},{10,... | collective-permute-start | bytes 393224 | tf_op jit(solution)/shard_map/ppermute | solution.py:249
  12.0 0.0 collective-permute-done.1.came_ref
  12.0 0.1 shard_map.56
  12.1 1.6 %collective-permute-start.2 = (bf16[4,160,128]{2,1,0:T(8,128)(2,1)S(1)}, bf16[4,160,128]{2,1,0:T(8,128)(2,1)S(1)}, u32[]{:S(2)}, u32[]{:S(2)}) collective-permute-start(bf16[4,160,128]{2,1,0:T(8,128)(2,1)S(1)} %shard_map.56), channel_id=1, source_target_pairs={{0,2},{1,3},{2,0},{3,1},{4,6},{5,7},{6,4},{7,5},{8,10},{9,11},{10,... | collective-permute-start | bytes 491528 | tf_op jit(solution)/shard_map/ppermute | solution.py:249
  13.7 2.2 %collective-permute-done.4.right_ref = bf16[2,8,4096]{2,1,0:T(8,128)(2,1)S(1)} collective-permute-done((bf16[2,8,4096]{2,1,0:T(8,128)(2,1)S(1)}, bf16[2,8,4096]{2,1,0:T(8,128)(2,1)S(1)}, u32[]{:S(2)}, u32[]{:S(2)}) %collective-permute-start.4) | collective-permute-done | bytes 131104 | tf_op jit(solution)/shard_map/ppermute | solution.py:249
  15.9 1.6 %collective-permute-start.5 = (bf16[4,8,4096]{2,1,0:T(8,128)(2,1)S(1)}, bf16[4,8,4096]{2,1,0:T(8,128)(2,1)S(1)}, u32[]{:S(2)}, u32[]{:S(2)}) collective-permute-start(bf16[4,8,4096]{2,1,0:T(8,128)(2,1)S(1)} %shard_map.59.refs_0_), channel_id=1, source_target_pairs={{0,2},{1,3},{2,0},{3,1},{4,6},{5,7},{6,4},{7,5},{8,10},{9,11},{10,... | collective-permute-start | bytes 786440 | tf_op jit(solution)/shard_map/ppermute | solution.py:249
  17.5 0.0 collective-permute-start.6
  17.5 0.0 collective-permute-done.3.came_ref
  17.5 0.8 %collective-permute-done.2.across_ref = bf16[4,160,128]{2,1,0:T(8,128)(2,1)S(1)} collective-permute-done((bf16[4,160,128]{2,1,0:T(8,128)(2,1)S(1)}, bf16[4,160,128]{2,1,0:T(8,128)(2,1)S(1)}, u32[]{:S(2)}, u32[]{:S(2)}) %collective-permute-start.2) | collective-permute-done | bytes 163872 | tf_op jit(solution)/shard_map/ppermute | solution.py:249
  18.3 0.8 %shard_map.57 = (f32[128,128]{1,0:T(8,128)S(1)}, bf16[4,128,128]{2,1,0:T(8,128)(2,1)}) custom-call(f32[4,128,128]{2,1,0:T(8,128)S(1)} %get-tuple-element.27.kept_ref, f32[4,128,128]{2,1,0:T(8,128)S(1)} %collective-permute-done.3.came_ref, bf16[4,160,128]{2,1,0:T(8,128)(2,1)S(1)} %collective-permute-done.2.across_ref), custom_call_target="tpu_custom_call" | custom-call | tf_op jit(solution)/shard_map/pallas_call | solution.py:134
  19.1 3.3 %all-to-all-start = ((bf16[4,128,128]{2,1,0:T(8,128)(2,1)}), bf16[4,128,128]{2,1,0:T(8,128)(2,1)S(1)}, u32[]{:S(2)}, u32[]{:S(2)}) async-start(bf16[4,128,128]{2,1,0:T(8,128)(2,1)} %get-tuple-element.35), calls=%async_computation | async-start | bytes 262144 | tf_op jit(solution)/shard_map/all_to_all | solution.py:270
  22.4 1.3 %collective-permute-done.5.queries_ref = bf16[4,8,4096]{2,1,0:T(8,128)(2,1)S(1)} collective-permute-done((bf16[4,8,4096]{2,1,0:T(8,128)(2,1)S(1)}, bf16[4,8,4096]{2,1,0:T(8,128)(2,1)S(1)}, u32[]{:S(2)}, u32[]{:S(2)}) %collective-permute-start.5) | collective-permute-done | bytes 262176 | tf_op jit(solution)/shard_map/ppermute | solution.py:249
  23.7 0.0 collective-permute-done.6.refs_1_
  23.7 4.7 %all-to-all-done.parts_ref = bf16[4,128,128]{2,1,0:T(8,128)(2,1)S(1)} async-done(((bf16[4,128,128]{2,1,0:T(8,128)(2,1)}), bf16[4,128,128]{2,1,0:T(8,128)(2,1)S(1)}, u32[]{:S(2)}, u32[]{:S(2)}) %all-to-all-start) | async-done | bytes 131104 | tf_op jit(solution)/shard_map/all_to_all | solution.py:270
  28.5 0.0 collective-permute-start.7
  28.5 0.6 %shard_map.60 = (f32[2,32,128]{2,1,0:T(8,128)S(1)}, f32[2,8,2,8,128]{4,3,2,1,0:T(8,128)S(1)}) custom-call(f32[128,128]{1,0:T(8,128)S(1)} %get-tuple-element.33.own_ref, bf16[4,128,128]{2,1,0:T(8,128)(2,1)S(1)} %all-to-all-done.parts_ref, bf16[4,8,4096]{2,1,0:T(8,128)(2,1)S(1)} %shard_map.59.refs_0_, bf16[4,8,4096]{2,1,0:T(8,128)(2,1)S(1)} %collective-permute-done.6.refs_1_), custom_call_target="tpu_custom_call" | custom-call | tf_op jit(solution)/shard_map/pallas_call | solution.py:219
  29.0 1.0 %collective-permute-done.7.others_ref = bf16[4,8,4096]{2,1,0:T(8,128)(2,1)S(1)} collective-permute-done((bf16[4,8,4096]{2,1,0:T(8,128)(2,1)S(1)}, bf16[4,8,4096]{2,1,0:T(8,128)(2,1)S(1)}, u32[]{:S(2)}, u32[]{:S(2)}) %collective-permute-start.7) | collective-permute-done | bytes 262176 | tf_op jit(solution)/shard_map/ppermute | solution.py:249
  30.0 1.1 %shard_map.61 = f32[2,128]{1,0:T(2,128)} custom-call(f32[2,32,128]{2,1,0:T(8,128)S(1)} %get-tuple-element.38.grads_ref, f32[2,8,2,8,128]{4,3,2,1,0:T(8,128)S(1)} %get-tuple-element.39.before_ref, bf16[4,8,4096]{2,1,0:T(8,128)(2,1)S(1)} %collective-permute-done.5.queries_ref, bf16[4,8,4096]{2,1,0:T(8,128)(2,1)S(1)} %collective-permute-done.7.others_ref), custom_call_target="tpu_custom_call" | custom-call | tf_op jit(solution)/shard_map/pallas_call | solution.py:232
  (2 shorter events, 0.0 us)
Async XLA Ops:
  0.0 10.4 %copy-start = (bf16[8,4096]{1,0:T(8,128)(2,1)S(1)}, bf16[8,4096]{1,0:T(8,128)(2,1)}, u32[]{:S(2)}) copy-start(bf16[8,4096]{1,0:T(8,128)(2,1)} %param.9) | copy-start | bytes 196612
  0.0 9.8 %collective-permute-start = (bf16[1,8,4096]{2,1,0:T(8,128)(2,1)}, bf16[1,8,4096]{2,1,0:T(8,128)(2,1)S(1)}, u32[]{:S(2)}, u32[]{:S(2)}) collective-permute-start(bf16[1,8,4096]{2,1,0:T(8,128)(2,1)} %bitcast.3), channel_id=1, source_target_pairs={{0,8},{1,9},{2,10},{3,11},{4,12},{5,13},{6,14},{7,15},{8,0},{9,1},... | collective-permute-start | bytes 196616 | tf_op jit(solution)/shard_map/ppermute | solution.py:249
  9.8 2.2 %collective-permute-start.1 = (f32[4,128,128]{2,1,0:T(8,128)S(1)}, f32[4,128,128]{2,1,0:T(8,128)S(1)}, u32[]{:S(2)}, u32[]{:S(2)}) collective-permute-start(f32[4,128,128]{2,1,0:T(8,128)S(1)} %get-tuple-element.29), channel_id=1, source_target_pairs={{0,1},{1,0},{2,3},{3,2},{4,5},{5,4},{6,7},{7,6},{8,9},{9,8},{10,11... | collective-permute-start | bytes 786440 | tf_op jit(solution)/shard_map/ppermute | solution.py:249
  9.9 7.7 %collective-permute-start.3 = (f32[4,128,128]{2,1,0:T(8,128)S(1)}, f32[4,128,128]{2,1,0:T(8,128)S(1)}, u32[]{:S(2)}, u32[]{:S(2)}) collective-permute-start(f32[4,128,128]{2,1,0:T(8,128)S(1)} %get-tuple-element.30), channel_id=1, source_target_pairs={{0,1},{1,0},{2,3},{3,2},{4,5},{5,4},{6,7},{7,6},{8,9},{9,8},{10,11... | collective-permute-start | bytes 786440 | tf_op jit(solution)/shard_map/ppermute | solution.py:249
  10.4 5.5 %collective-permute-start.4 = (bf16[2,8,4096]{2,1,0:T(8,128)(2,1)S(1)}, bf16[2,8,4096]{2,1,0:T(8,128)(2,1)S(1)}, u32[]{:S(2)}, u32[]{:S(2)}) collective-permute-start(bf16[2,8,4096]{2,1,0:T(8,128)(2,1)S(1)} %shard_map.58.left_ref), channel_id=1, source_target_pairs={{0,4},{1,5},{2,6},{3,7},{4,0},{5,1},{6,2},{7,3},{8,12},{9,13},{10,... | collective-permute-start | bytes 393224 | tf_op jit(solution)/shard_map/ppermute | solution.py:249
  12.1 6.2 %collective-permute-start.2 = (bf16[4,160,128]{2,1,0:T(8,128)(2,1)S(1)}, bf16[4,160,128]{2,1,0:T(8,128)(2,1)S(1)}, u32[]{:S(2)}, u32[]{:S(2)}) collective-permute-start(bf16[4,160,128]{2,1,0:T(8,128)(2,1)S(1)} %shard_map.56), channel_id=1, source_target_pairs={{0,2},{1,3},{2,0},{3,1},{4,6},{5,7},{6,4},{7,5},{8,10},{9,11},{10,... | collective-permute-start | bytes 491528 | tf_op jit(solution)/shard_map/ppermute | solution.py:249
  15.9 7.8 %collective-permute-start.5 = (bf16[4,8,4096]{2,1,0:T(8,128)(2,1)S(1)}, bf16[4,8,4096]{2,1,0:T(8,128)(2,1)S(1)}, u32[]{:S(2)}, u32[]{:S(2)}) collective-permute-start(bf16[4,8,4096]{2,1,0:T(8,128)(2,1)S(1)} %shard_map.59.refs_0_), channel_id=1, source_target_pairs={{0,2},{1,3},{2,0},{3,1},{4,6},{5,7},{6,4},{7,5},{8,10},{9,11},{10,... | collective-permute-start | bytes 786440 | tf_op jit(solution)/shard_map/ppermute | solution.py:249
  17.5 6.2 %collective-permute-start.6 = (bf16[4,8,4096]{2,1,0:T(8,128)(2,1)S(1)}, bf16[4,8,4096]{2,1,0:T(8,128)(2,1)S(1)}, u32[]{:S(2)}, u32[]{:S(2)}) collective-permute-start(bf16[4,8,4096]{2,1,0:T(8,128)(2,1)S(1)} %shard_map.59.refs_0_), channel_id=1, source_target_pairs={{0,1},{1,0},{2,3},{3,2},{4,5},{5,4},{6,7},{7,6},{8,9},{9,8},{10,11... | collective-permute-start | bytes 786440 | tf_op jit(solution)/shard_map/ppermute | solution.py:249
  19.1 9.4 %all-to-all-start = ((bf16[4,128,128]{2,1,0:T(8,128)(2,1)}), bf16[4,128,128]{2,1,0:T(8,128)(2,1)S(1)}, u32[]{:S(2)}, u32[]{:S(2)}) async-start(bf16[4,128,128]{2,1,0:T(8,128)(2,1)} %get-tuple-element.35), calls=%async_computation | async-start | bytes 262144 | tf_op jit(solution)/shard_map/all_to_all | solution.py:270
  28.5 1.5 %collective-permute-start.7 = (bf16[4,8,4096]{2,1,0:T(8,128)(2,1)S(1)}, bf16[4,8,4096]{2,1,0:T(8,128)(2,1)S(1)}, u32[]{:S(2)}, u32[]{:S(2)}) collective-permute-start(bf16[4,8,4096]{2,1,0:T(8,128)(2,1)S(1)} %collective-permute-done.5.queries_ref), channel_id=1, source_target_pairs={{0,1},{1,0},{2,3},{3,2},{4,5},{5,4},{6,7},{7,6},{8,9},{9,8},{10,11... | collective-permute-start | bytes 786440 | tf_op jit(solution)/shard_map/ppermute | solution.py:249

commit v8 on v6

--- a/solution.py
+++ b/solution.py
@@ -9,7 +9,8 @@
 
 SEQ = 64
 VMEM_BYTES = 32 * 1024 * 1024
-AHEAD = 3
+AHEAD = 7
+CODE_SCALE = 2.0**-8
 LANES_BY_LANES = (((1,), (1,)), ((), ()))
 HBM_SPEC = pl.BlockSpec(memory_space=pltpu.HBM)
 VMEM_SPEC = pl.BlockSpec(memory_space=pltpu.VMEM)
@@ -60,7 +61,7 @@
     width = inputs.shape[1] // devices
     rank = proj_in_t.shape[0]
     low = jax.ShapeDtypeStruct((devices // 4, 2 * rank, width), jnp.float32)
-    chunks = [a.shape[0] // 256 if a.shape[0] % 256 == 0 else 1 for a in (inputs, out_grads)]
+    chunks = [a.shape[0] // rows if a.shape[0] % rows == 0 else 1 for a, rows in ((inputs, 128), (out_grads, 256))]
     return pl.pallas_call(
         project_kernel,
         out_shape=[low] * 4,
@@ -78,48 +79,60 @@
     )(*arrays)
 
 
-def put_split(out_ref, low):
-    rank = low.shape[0] // 2
-    low_in = low[:rank, :]
-    high = low_in.astype(jnp.bfloat16)
-    out_ref[:rank, :] = high
-    out_ref[rank : 2 * rank, :] = low[rank:, :].astype(jnp.bfloat16)
-    out_ref[2 * rank :, :] = (low_in - high.astype(jnp.float32)).astype(jnp.bfloat16)
-
-
-def get_split(ref):
-    rank = ref.shape[0] // 3
-    low_in = ref[:rank, :].astype(jnp.float32) + ref[2 * rank :, :].astype(jnp.float32)
-    return jnp.concatenate([low_in, ref[rank : 2 * rank, :].astype(jnp.float32)], axis=0)
+def put_coded(out_ref, low):
+    rows = low.shape[0]
+    rounded = low.astype(jnp.bfloat16)
+    out_ref[:rows, :] = rounded
+    rounded = rounded.astype(jnp.float32)
+    left = (low - rounded) / jnp.maximum(jnp.abs(rounded) * CODE_SCALE, 1e-30)
+    level = jnp.clip(jnp.floor(2.0 * left) + 2.0, 0.0, 3.0)
+    part = rows // 4
+    word = level[:part, :]
+    for index in range(1, 4):
+        word = word + 4.0**index * level[index * part : (index + 1) * part, :]
+    out_ref[rows:, :] = word.astype(jnp.bfloat16)
+
+
+def add_coded(total, ref):
+    part = ref.shape[0] // 5
+    word = ref[4 * part :, :].astype(jnp.float32)
+    parts = []
+    for index in reversed(range(4)):
+        level = jnp.floor(word * 0.25**index)
+        word = word - level * 4.0**index
+        rounded = ref[index * part : (index + 1) * part, :].astype(jnp.float32)
+        left = jnp.abs(rounded) * ((CODE_SCALE * 0.5) * level - CODE_SCALE * 0.75)
+        parts.append((slice(index * part, (index + 1) * part), total(index * part, part) + rounded + left))
+    return parts
 
 
 def add_given_kernel(kept_ref, came_ref, out_ref):
     for block in range(out_ref.shape[0]):
-        put_split(out_ref.at[block], kept_ref[block] + came_ref[block])
+        put_coded(out_ref.at[block], kept_ref[block] + came_ref[block])
 
 
 def add_given(kept, came):
     blocks, rows, width = kept.shape
     return pl.pallas_call(
         add_given_kernel,
-        out_shape=jax.ShapeDtypeStruct((blocks, rows // 2 * 3, width), jnp.bfloat16),
+        out_shape=jax.ShapeDtypeStruct((blocks, rows // 4 * 5, width), jnp.bfloat16),
         compiler_params=PARAMS,
     )(kept, came)
 
 
 def add_kept_kernel(kept_ref, came_ref, across_ref, *out_refs):
-    for block, out_ref in enumerate(out_refs):
-        total = kept_ref[block] + came_ref[block] + get_split(across_ref.at[block])
-        out_ref[...] = total.astype(out_ref.dtype)
-
-
-def add_kept(kept, came, across):
-    blocks, rows, width = kept.shape
-    wide = jax.ShapeDtypeStruct((rows, width), jnp.float32)
-    rounded = jax.ShapeDtypeStruct((rows, width), jnp.bfloat16)
+    for z, out_ref in enumerate(out_refs):
+        def here(first, rows):
+            return kept_ref[z, first : first + rows, :] + came_ref[z, first : first + rows, :]
+
+        for rows, total in add_coded(here, across_ref.at[z]):
+            out_ref[rows, :] = total.astype(out_ref.dtype)
+
+
+def add_kept(kept, came, across, types):
     return pl.pallas_call(
         add_kept_kernel,
-        out_shape=[wide if 2 * block < blocks else rounded for block in range(blocks)],
+        out_shape=[jax.ShapeDtypeStruct(kept.shape[1:], dtype) for dtype in types],
         compiler_params=PARAMS,
     )(kept, came, across)
 
@@ -248,14 +261,15 @@
     other_held = swap(held, core=1)
     across, came = together((across, came))
 
-    sums = add_kept(kept, came, across)
-    parts = list(sums)
+    types = [jnp.float32 if z < depth // 2 else jnp.bfloat16 for z in range(depth)]
+    parts = list(add_kept(kept, came, across, types))
     for z in list(range(depth // 2, depth)) + list(range(1, depth // 2)):
         parts[z] = swap(parts[z], chip=2 * z)
     came_held, other_held, parts = together((came_held, other_held, parts))
     other_came = swap(came_held, core=1)
     reach_y = [chip ^ 1 for chip in reach]
-    grads, scores = first_scores(parts, [held, other_held, came_held], [(0, reach), (1, reach), (0, reach_y)], rank)
+    held = [held, other_held, came_held]
+    grads, scores = first_scores(parts, held, [(0, reach), (1, reach), (0, reach_y)], rank)
     return last_scores(grads, scores, other_came, reach_y)
 
 

time: 29 us -> 37.9 us (1.31)
  waiting for transfers between devices: 8.37 us -> 18.4 us
  starting transfers between devices: 13.6 us -> 12.6 us
    ppermute x11, waiting for transfers between devices: 8.37 us -> 18.4 us  [swap(): lax.ppermute(array, 'ex', [(i, i ^ distance) for i in range(devices)])]
    ppermute x11, starting transfers between devices: 13.6 us -> 12.6 us  [swap(): lax.ppermute(array, 'ex', [(i, i ^ distance) for i in range(devices)])]
  transfers between devices with their start and end apart: 11 -> 11, of which waited for: 6 -> 5; matrix products, arithmetic and copies ran while one was open for 0% -> 0% of each run, Pallas kernels for 20% -> 15%
where the time goes in v8:
time: 37.9 us; the launch traced here: 37.8 us
  waiting for transfers between devices  18.4 us (49%)
  starting transfers between devices  12.6 us (33%)
  Pallas kernels  6.7 us (18%)
    ppermute x11, waiting for transfers between devices, swap(): lax.ppermute(array, 'ex', [(i, i ^ distance) for i in range(devices)])  18.4 us
    ppermute x11, starting transfers between devices, swap(): lax.ppermute(array, 'ex', [(i, i ^ distance) for i in range(devices)])  12.6 us
    pallas_call x1, Pallas kernels, project(): pl.pallas_call(project_kernel, out_shape=[low] * 4, in_specs=[HBM_SPEC] *...  4.83 us
    pallas_call x1, Pallas kernels, last_scores(): pl.pallas_call(functools.partial(last_score_kernel, chips), out_shape=jax...  0.98 us
  transfers between devices with their start and end apart: 11, of which 5 were waited for; matrix products, arithmetic and copies ran while one was open for 0% of the time, Pallas kernels for 15%

profile of v8, /device:TPU:0, one launch (start us, length us, event | category | flops | bytes accessed | tf_op | source)
XLA Modules:
  0.0 37.8 jit_solution(2051177552725239398)
XLA Ops:
  0.0 0.0 copy-start
  0.0 4.0 %collective-permute-start = (bf16[1,8,4096]{2,1,0:T(8,128)(2,1)}, bf16[1,8,4096]{2,1,0:T(8,128)(2,1)S(1)}, u32[]{:S(2)}, u32[]{:S(2)}) collective-permute-start(bf16[1,8,4096]{2,1,0:T(8,128)(2,1)} %bitcast.3), channel_id=1, source_target_pairs={{0,8},{1,9},{2,10},{3,11},{4,12},{5,13},{6,14},{7,15},{8,0},{9,1},... | collective-permute-start | bytes 196616 | tf_op jit(solution)/shard_map/ppermute | solution.py:245
  4.0 4.8 %shard_map.55 = (f32[4,128,128]{2,1,0:T(8,128)S(1)}, f32[4,128,128]{2,1,0:T(8,128)S(1)}, f32[4,128,128]{2,1,0:T(8,128)S(1)}, f32[4,128,128]{2,1,0:T(8,128)S(1)}) custom-call(bf16[512,2048]{1,0:T(8,128)(2,1)} %x_hbm.1, bf16[1792,2048]{1,0:T(8,128)(2,1)} %w_hbm.1, bf16[64,512]{1,0:T(8,128)(2,1)} %bitcast.6, bf16[64,1792]{1,0:T(8,128)(2,1)} %bitcast.5), custom_call_target="tpu_custom_call" | custom-call | flops 603979776 | bytes 9437184 | tf_op jit(solution)/shard_map/pallas_call | solution.py:65
  8.9 0.0 collective-permute-done.right_ref
  8.9 0.1 collective-permute-start.4
  9.0 0.0 copy-done
  9.0 1.6 %collective-permute-start.1 = (bf16[2,8,4096]{2,1,0:T(8,128)(2,1)S(1)}, bf16[2,8,4096]{2,1,0:T(8,128)(2,1)S(1)}, u32[]{:S(2)}, u32[]{:S(2)}) collective-permute-start(bf16[2,8,4096]{2,1,0:T(8,128)(2,1)S(1)} %shard_map.56.left_ref), channel_id=1, source_target_pairs={{0,4},{1,5},{2,6},{3,7},{4,0},{5,1},{6,2},{7,3},{8,12},{9,13},{10,... | collective-permute-start | bytes 393224 | tf_op jit(solution)/shard_map/ppermute | solution.py:245
  10.6 0.2 collective-permute-start.6
  10.8 4.1 %collective-permute-done.1.right_ref = bf16[2,8,4096]{2,1,0:T(8,128)(2,1)S(1)} collective-permute-done((bf16[2,8,4096]{2,1,0:T(8,128)(2,1)S(1)}, bf16[2,8,4096]{2,1,0:T(8,128)(2,1)S(1)}, u32[]{:S(2)}, u32[]{:S(2)}) %collective-permute-start.1) | collective-permute-done | bytes 131104 | tf_op jit(solution)/shard_map/ppermute | solution.py:245
  15.0 1.6 %collective-permute-start.2 = (bf16[4,8,4096]{2,1,0:T(8,128)(2,1)S(1)}, bf16[4,8,4096]{2,1,0:T(8,128)(2,1)S(1)}, u32[]{:S(2)}, u32[]{:S(2)}) collective-permute-start(bf16[4,8,4096]{2,1,0:T(8,128)(2,1)S(1)} %shard_map.57.refs_4_), channel_id=1, source_target_pairs={{0,2},{1,3},{2,0},{3,1},{4,6},{5,7},{6,4},{7,5},{8,10},{9,11},{10,... | collective-permute-start | bytes 786440 | tf_op jit(solution)/shard_map/ppermute | solution.py:245
  16.6 0.0 collective-permute-start.3
  16.6 0.0 collective-permute-done.4.came_ref
  16.6 0.1 shard_map.58
  16.7 0.6 %collective-permute-start.5 = (bf16[4,160,128]{2,1,0:T(8,128)(2,1)S(1)}, bf16[4,160,128]{2,1,0:T(8,128)(2,1)S(1)}, u32[]{:S(2)}, u32[]{:S(2)}) collective-permute-start(bf16[4,160,128]{2,1,0:T(8,128)(2,1)S(1)} %shard_map.58), channel_id=1, source_target_pairs={{0,2},{1,3},{2,0},{3,1},{4,6},{5,7},{6,4},{7,5},{8,10},{9,11},{10,... | collective-permute-start | bytes 491528 | tf_op jit(solution)/shard_map/ppermute | solution.py:245
  17.3 0.0 collective-permute-done.6.came_ref
  17.3 9.2 %collective-permute-done.5.across_ref = bf16[4,160,128]{2,1,0:T(8,128)(2,1)S(1)} collective-permute-done((bf16[4,160,128]{2,1,0:T(8,128)(2,1)S(1)}, bf16[4,160,128]{2,1,0:T(8,128)(2,1)S(1)}, u32[]{:S(2)}, u32[]{:S(2)}) %collective-permute-start.5) | collective-permute-done | bytes 163872 | tf_op jit(solution)/shard_map/ppermute | solution.py:245
  26.5 0.1 shard_map.59
  26.6 1.6 %collective-permute-start.7 = (f32[128,128]{1,0:T(8,128)S(1)}, f32[128,128]{1,0:T(8,128)S(1)}, u32[]{:S(2)}, u32[]{:S(2)}) collective-permute-start(f32[128,128]{1,0:T(8,128)S(1)} %get-tuple-element.40), channel_id=1, source_target_pairs={{0,4},{1,5},{2,6},{3,7},{4,0},{5,1},{6,2},{7,3},{8,12},{9,13},{10,... | collective-permute-start | bytes 196616 | tf_op jit(solution)/shard_map/ppermute | solution.py:245
  28.2 1.3 %collective-permute-start.8 = (bf16[128,128]{1,0:T(8,128)(2,1)S(1)}, bf16[128,128]{1,0:T(8,128)(2,1)S(1)}, u32[]{:S(2)}, u32[]{:S(2)}) collective-permute-start(bf16[128,128]{1,0:T(8,128)(2,1)S(1)} %get-tuple-element.41), channel_id=1, source_target_pairs={{0,8},{1,9},{2,10},{3,11},{4,12},{5,13},{6,14},{7,15},{8,0},{9,1},... | collective-permute-start | bytes 98312 | tf_op jit(solution)/shard_map/ppermute | solution.py:245
  29.6 1.5 %collective-permute-start.9 = (bf16[128,128]{1,0:T(8,128)(2,1)S(1)}, bf16[128,128]{1,0:T(8,128)(2,1)S(1)}, u32[]{:S(2)}, u32[]{:S(2)}) collective-permute-start(bf16[128,128]{1,0:T(8,128)(2,1)S(1)} %get-tuple-element.42), channel_id=1, source_target_pairs={{0,12},{1,13},{2,14},{3,15},{4,8},{5,9},{6,10},{7,11},{8,4},{9,5},... | collective-permute-start | bytes 98312 | tf_op jit(solution)/shard_map/ppermute | solution.py:245
  31.0 0.0 collective-permute-done.2.refs_6_
  31.0 0.0 collective-permute-done.3.refs_5_
  31.0 2.2 %collective-permute-done.8.refs_2_ = bf16[128,128]{1,0:T(8,128)(2,1)S(1)} collective-permute-done((bf16[128,128]{1,0:T(8,128)(2,1)S(1)}, bf16[128,128]{1,0:T(8,128)(2,1)S(1)}, u32[]{:S(2)}, u32[]{:S(2)}) %collective-permute-start.8) | collective-permute-done | bytes 32800 | tf_op jit(solution)/shard_map/ppermute | solution.py:245
  33.3 2.0 %collective-permute-done.9.refs_3_ = bf16[128,128]{1,0:T(8,128)(2,1)S(1)} collective-permute-done((bf16[128,128]{1,0:T(8,128)(2,1)S(1)}, bf16[128,128]{1,0:T(8,128)(2,1)S(1)}, u32[]{:S(2)}, u32[]{:S(2)}) %collective-permute-start.9) | collective-permute-done | bytes 32800 | tf_op jit(solution)/shard_map/ppermute | solution.py:245
  35.3 0.0 collective-permute-done.7.refs_1_
  35.3 0.0 collective-permute-start.10
  35.3 0.6 %shard_map.60 = (f32[2,32,128]{2,1,0:T(8,128)S(1)}, f32[2,8,2,8,128]{4,3,2,1,0:T(8,128)S(1)}) custom-call(f32[128,128]{1,0:T(8,128)S(1)} %get-tuple-element.43.refs_0_, f32[128,128]{1,0:T(8,128)S(1)} %collective-permute-done.7.refs_1_, bf16[128,128]{1,0:T(8,128)(2,1)S(1)} %collective-permute-done.8.refs_2_, ...), custom_call_target="tpu_custom_call" | custom-call | tf_op jit(solution)/shard_map/pallas_call | solution.py:215
  35.9 0.9 %collective-permute-done.10.queries_ref = bf16[4,8,4096]{2,1,0:T(8,128)(2,1)S(1)} collective-permute-done((bf16[4,8,4096]{2,1,0:T(8,128)(2,1)S(1)}, bf16[4,8,4096]{2,1,0:T(8,128)(2,1)S(1)}, u32[]{:S(2)}, u32[]{:S(2)}) %collective-permute-start.10) | collective-permute-done | bytes 262176 | tf_op jit(solution)/shard_map/ppermute | solution.py:245
  36.8 1.0 %shard_map.61 = f32[2,128]{1,0:T(2,128)} custom-call(f32[2,32,128]{2,1,0:T(8,128)S(1)} %get-tuple-element.49.grads_ref, f32[2,8,2,8,128]{4,3,2,1,0:T(8,128)S(1)} %get-tuple-element.50.before_ref, bf16[4,8,4096]{2,1,0:T(8,128)(2,1)S(1)} %collective-permute-done.10.queries_ref), custom_call_target="tpu_custom_call" | custom-call | tf_op jit(solution)/shard_map/pallas_call | solution.py:228
  (2 shorter events, 0.0 us)
Async XLA Ops:
  0.0 9.0 %copy-start = (bf16[8,4096]{1,0:T(8,128)(2,1)S(1)}, bf16[8,4096]{1,0:T(8,128)(2,1)}, u32[]{:S(2)}) copy-start(bf16[8,4096]{1,0:T(8,128)(2,1)} %param.9) | copy-start | bytes 196612
  0.0 8.9 %collective-permute-start = (bf16[1,8,4096]{2,1,0:T(8,128)(2,1)}, bf16[1,8,4096]{2,1,0:T(8,128)(2,1)S(1)}, u32[]{:S(2)}, u32[]{:S(2)}) collective-permute-start(bf16[1,8,4096]{2,1,0:T(8,128)(2,1)} %bitcast.3), channel_id=1, source_target_pairs={{0,8},{1,9},{2,10},{3,11},{4,12},{5,13},{6,14},{7,15},{8,0},{9,1},... | collective-permute-start | bytes 196616 | tf_op jit(solution)/shard_map/ppermute | solution.py:245
  8.9 7.7 %collective-permute-start.4 = (f32[4,128,128]{2,1,0:T(8,128)S(1)}, f32[4,128,128]{2,1,0:T(8,128)S(1)}, u32[]{:S(2)}, u32[]{:S(2)}) collective-permute-start(f32[4,128,128]{2,1,0:T(8,128)S(1)} %get-tuple-element.35), channel_id=1, source_target_pairs={{0,1},{1,0},{2,3},{3,2},{4,5},{5,4},{6,7},{7,6},{8,9},{9,8},{10,11... | collective-permute-start | bytes 786440 | tf_op jit(solution)/shard_map/ppermute | solution.py:245
  9.0 6.0 %collective-permute-start.1 = (bf16[2,8,4096]{2,1,0:T(8,128)(2,1)S(1)}, bf16[2,8,4096]{2,1,0:T(8,128)(2,1)S(1)}, u32[]{:S(2)}, u32[]{:S(2)}) collective-permute-start(bf16[2,8,4096]{2,1,0:T(8,128)(2,1)S(1)} %shard_map.56.left_ref), channel_id=1, source_target_pairs={{0,4},{1,5},{2,6},{3,7},{4,0},{5,1},{6,2},{7,3},{8,12},{9,13},{10,... | collective-permute-start | bytes 393224 | tf_op jit(solution)/shard_map/ppermute | solution.py:245
  10.6 6.6 %collective-permute-start.6 = (f32[4,128,128]{2,1,0:T(8,128)S(1)}, f32[4,128,128]{2,1,0:T(8,128)S(1)}, u32[]{:S(2)}, u32[]{:S(2)}) collective-permute-start(f32[4,128,128]{2,1,0:T(8,128)S(1)} %get-tuple-element.36), channel_id=1, source_target_pairs={{0,1},{1,0},{2,3},{3,2},{4,5},{5,4},{6,7},{7,6},{8,9},{9,8},{10,11... | collective-permute-start | bytes 786440 | tf_op jit(solution)/shard_map/ppermute | solution.py:245
  15.0 16.1 %collective-permute-start.2 = (bf16[4,8,4096]{2,1,0:T(8,128)(2,1)S(1)}, bf16[4,8,4096]{2,1,0:T(8,128)(2,1)S(1)}, u32[]{:S(2)}, u32[]{:S(2)}) collective-permute-start(bf16[4,8,4096]{2,1,0:T(8,128)(2,1)S(1)} %shard_map.57.refs_4_), channel_id=1, source_target_pairs={{0,2},{1,3},{2,0},{3,1},{4,6},{5,7},{6,4},{7,5},{8,10},{9,11},{10,... | collective-permute-start | bytes 786440 | tf_op jit(solution)/shard_map/ppermute | solution.py:245
  16.6 14.5 %collective-permute-start.3 = (bf16[4,8,4096]{2,1,0:T(8,128)(2,1)S(1)}, bf16[4,8,4096]{2,1,0:T(8,128)(2,1)S(1)}, u32[]{:S(2)}, u32[]{:S(2)}) collective-permute-start(bf16[4,8,4096]{2,1,0:T(8,128)(2,1)S(1)} %shard_map.57.refs_4_), channel_id=1, source_target_pairs={{0,1},{1,0},{2,3},{3,2},{4,5},{5,4},{6,7},{7,6},{8,9},{9,8},{10,11... | collective-permute-start | bytes 786440 | tf_op jit(solution)/shard_map/ppermute | solution.py:245
  16.7 9.8 %collective-permute-start.5 = (bf16[4,160,128]{2,1,0:T(8,128)(2,1)S(1)}, bf16[4,160,128]{2,1,0:T(8,128)(2,1)S(1)}, u32[]{:S(2)}, u32[]{:S(2)}) collective-permute-start(bf16[4,160,128]{2,1,0:T(8,128)(2,1)S(1)} %shard_map.58), channel_id=1, source_target_pairs={{0,2},{1,3},{2,0},{3,1},{4,6},{5,7},{6,4},{7,5},{8,10},{9,11},{10,... | collective-permute-start | bytes 491528 | tf_op jit(solution)/shard_map/ppermute | solution.py:245
  26.6 8.7 %collective-permute-start.7 = (f32[128,128]{1,0:T(8,128)S(1)}, f32[128,128]{1,0:T(8,128)S(1)}, u32[]{:S(2)}, u32[]{:S(2)}) collective-permute-start(f32[128,128]{1,0:T(8,128)S(1)} %get-tuple-element.40), channel_id=1, source_target_pairs={{0,4},{1,5},{2,6},{3,7},{4,0},{5,1},{6,2},{7,3},{8,12},{9,13},{10,... | collective-permute-start | bytes 196616 | tf_op jit(solution)/shard_map/ppermute | solution.py:245
  28.2 5.1 %collective-permute-start.8 = (bf16[128,128]{1,0:T(8,128)(2,1)S(1)}, bf16[128,128]{1,0:T(8,128)(2,1)S(1)}, u32[]{:S(2)}, u32[]{:S(2)}) collective-permute-start(bf16[128,128]{1,0:T(8,128)(2,1)S(1)} %get-tuple-element.41), channel_id=1, source_target_pairs={{0,8},{1,9},{2,10},{3,11},{4,12},{5,13},{6,14},{7,15},{8,0},{9,1},... | collective-permute-start | bytes 98312 | tf_op jit(solution)/shard_map/ppermute | solution.py:245
  29.6 5.7 %collective-permute-start.9 = (bf16[128,128]{1,0:T(8,128)(2,1)S(1)}, bf16[128,128]{1,0:T(8,128)(2,1)S(1)}, u32[]{:S(2)}, u32[]{:S(2)}) collective-permute-start(bf16[128,128]{1,0:T(8,128)(2,1)S(1)} %get-tuple-element.42), channel_id=1, source_target_pairs={{0,12},{1,13},{2,14},{3,15},{4,8},{5,9},{6,10},{7,11},{8,4},{9,5},... | collective-permute-start | bytes 98312 | tf_op jit(solution)/shard_map/ppermute | solution.py:245
  35.3 1.5 %collective-permute-start.10 = (bf16[4,8,4096]{2,1,0:T(8,128)(2,1)S(1)}, bf16[4,8,4096]{2,1,0:T(8,128)(2,1)S(1)}, u32[]{:S(2)}, u32[]{:S(2)}) collective-permute-start(bf16[4,8,4096]{2,1,0:T(8,128)(2,1)S(1)} %collective-permute-done.2.refs_6_), channel_id=1, source_target_pairs={{0,1},{1,0},{2,3},{3,2},{4,5},{5,4},{6,7},{7,6},{8,9},{9,8},{10,11... | collective-permute-start | bytes 786440 | tf_op jit(solution)/shard_map/ppermute | solution.py:245

commit v9 on v8

--- a/solution.py
+++ b/solution.py
@@ -10,6 +10,7 @@
 SEQ = 64
 VMEM_BYTES = 32 * 1024 * 1024
 AHEAD = 7
+NEAR_PAD = 64
 CODE_SCALE = 2.0**-8
 LANES_BY_LANES = (((1,), (1,)), ((), ()))
 HBM_SPEC = pl.BlockSpec(memory_space=pltpu.HBM)
@@ -130,9 +131,11 @@
 
 
 def add_kept(kept, came, across, types):
+    _, rows, width = kept.shape
+    heights = [rows if z == 0 or dtype == jnp.bfloat16 else rows + NEAR_PAD for z, dtype in enumerate(types)]
     return pl.pallas_call(
         add_kept_kernel,
-        out_shape=[jax.ShapeDtypeStruct(kept.shape[1:], dtype) for dtype in types],
+        out_shape=[jax.ShapeDtypeStruct((height, width), dtype) for height, dtype in zip(heights, types)],
         compiler_params=PARAMS,
     )(kept, came, across)
 
@@ -175,7 +178,7 @@
     core = lax.rem(lax.axis_index("ex"), 2)
     total = part_refs[0][...]
     for part_ref in part_refs[1:]:
-        total = total + part_ref[...].astype(jnp.float32)
+        total = total + part_ref[: 2 * rank, :].astype(jnp.float32)
     out_t_ref[...] = total[rank:, :]
     even = out_t_ref[pl.ds(0, rank // 2, stride=2), :]
     odd = out_t_ref[pl.ds(1, rank // 2, stride=2), :]

time: 37.9 us -> 28.4 us (0.75)
  waiting for transfers between devices: 18.4 us -> 7.87 us
  starting transfers between devices: 12.6 us -> 13.6 us
    ppermute x11, waiting for transfers between devices: 18.4 us -> 7.87 us  [swap(): lax.ppermute(array, 'ex', [(i, i ^ distance) for i in range(devices)])]
    ppermute x11, starting transfers between devices: 12.6 us -> 13.6 us  [swap(): lax.ppermute(array, 'ex', [(i, i ^ distance) for i in range(devices)])]
  transfers between devices with their start and end apart: 11 -> 11, of which waited for: 5 -> 6; matrix products, arithmetic and copies ran while one was open for 0% -> 0% of each run, Pallas kernels for 15% -> 20%
where the time goes in v9:
time: 28.4 us; the launch traced here: 28.2 us
  starting transfers between devices  13.6 us (48%)
  waiting for transfers between devices  7.87 us (28%)
  Pallas kernels  6.7 us (24%)
    ppermute x11, starting transfers between devices, swap(): lax.ppermute(array, 'ex', [(i, i ^ distance) for i in range(devices)])  13.6 us
    ppermute x11, waiting for transfers between devices, swap(): lax.ppermute(array, 'ex', [(i, i ^ distance) for i in range(devices)])  7.87 us
    pallas_call x1, Pallas kernels, project(): pl.pallas_call(project_kernel, out_shape=[low] * 4, in_specs=[HBM_SPEC] *...  4.83 us
    pallas_call x1, Pallas kernels, last_scores(): pl.pallas_call(functools.partial(last_score_kernel, chips), out_shape=jax...  0.98 us
    pallas_call x1, Pallas kernels, first_scores(): pl.pallas_call(functools.partial(first_score_kernel, len(parts), held), o...  0.64 us
  transfers between devices with their start and end apart: 11, of which 6 were waited for; matrix products, arithmetic and copies ran while one was open for 0% of the time, Pallas kernels for 20%

profile of v9, /device:TPU:0, one launch (start us, length us, event | category | flops | bytes accessed | tf_op | source)
XLA Modules:
  0.0 28.2 jit_solution(2409565913649141150)
XLA Ops:
  0.0 0.0 copy-start
  0.0 4.0 %collective-permute-start = (bf16[1,8,4096]{2,1,0:T(8,128)(2,1)}, bf16[1,8,4096]{2,1,0:T(8,128)(2,1)S(1)}, u32[]{:S(2)}, u32[]{:S(2)}) collective-permute-start(bf16[1,8,4096]{2,1,0:T(8,128)(2,1)} %bitcast.3), channel_id=1, source_target_pairs={{0,8},{1,9},{2,10},{3,11},{4,12},{5,13},{6,14},{7,15},{8,0},{9,1},... | collective-permute-start | bytes 196616 | tf_op jit(solution)/shard_map/ppermute | solution.py:248
  4.0 4.8 %shard_map.55 = (f32[4,128,128]{2,1,0:T(8,128)S(1)}, f32[4,128,128]{2,1,0:T(8,128)S(1)}, f32[4,128,128]{2,1,0:T(8,128)S(1)}, f32[4,128,128]{2,1,0:T(8,128)S(1)}) custom-call(bf16[512,2048]{1,0:T(8,128)(2,1)} %x_hbm.1, bf16[1792,2048]{1,0:T(8,128)(2,1)} %w_hbm.1, bf16[64,512]{1,0:T(8,128)(2,1)} %bitcast.6, bf16[64,1792]{1,0:T(8,128)(2,1)} %bitcast.5), custom_call_target="tpu_custom_call" | custom-call | flops 603979776 | bytes 9437184 | tf_op jit(solution)/shard_map/pallas_call | solution.py:66
  8.9 0.0 collective-permute-done.right_ref
  8.9 0.1 collective-permute-start.4
  9.0 0.0 copy-done
  9.0 1.6 %collective-permute-start.1 = (bf16[2,8,4096]{2,1,0:T(8,128)(2,1)S(1)}, bf16[2,8,4096]{2,1,0:T(8,128)(2,1)S(1)}, u32[]{:S(2)}, u32[]{:S(2)}) collective-permute-start(bf16[2,8,4096]{2,1,0:T(8,128)(2,1)S(1)} %shard_map.56.left_ref), channel_id=1, source_target_pairs={{0,4},{1,5},{2,6},{3,7},{4,0},{5,1},{6,2},{7,3},{8,12},{9,13},{10,... | collective-permute-start | bytes 393224 | tf_op jit(solution)/shard_map/ppermute | solution.py:248
  10.6 0.2 collective-permute-start.6
  10.8 0.0 collective-permute-done.4.came_ref
  10.8 0.1 shard_map.58
  11.0 1.6 %collective-permute-start.5 = (bf16[4,160,128]{2,1,0:T(8,128)(2,1)S(1)}, bf16[4,160,128]{2,1,0:T(8,128)(2,1)S(1)}, u32[]{:S(2)}, u32[]{:S(2)}) collective-permute-start(bf16[4,160,128]{2,1,0:T(8,128)(2,1)S(1)} %shard_map.58), channel_id=1, source_target_pairs={{0,2},{1,3},{2,0},{3,1},{4,6},{5,7},{6,4},{7,5},{8,10},{9,11},{10,... | collective-permute-start | bytes 491528 | tf_op jit(solution)/shard_map/ppermute | solution.py:248
  12.6 2.4 %collective-permute-done.1.right_ref = bf16[2,8,4096]{2,1,0:T(8,128)(2,1)S(1)} collective-permute-done((bf16[2,8,4096]{2,1,0:T(8,128)(2,1)S(1)}, bf16[2,8,4096]{2,1,0:T(8,128)(2,1)S(1)}, u32[]{:S(2)}, u32[]{:S(2)}) %collective-permute-start.1) | collective-permute-done | bytes 131104 | tf_op jit(solution)/shard_map/ppermute | solution.py:248
  15.0 1.6 %collective-permute-start.2 = (bf16[4,8,4096]{2,1,0:T(8,128)(2,1)S(1)}, bf16[4,8,4096]{2,1,0:T(8,128)(2,1)S(1)}, u32[]{:S(2)}, u32[]{:S(2)}) collective-permute-start(bf16[4,8,4096]{2,1,0:T(8,128)(2,1)S(1)} %shard_map.57.refs_4_), channel_id=1, source_target_pairs={{0,2},{1,3},{2,0},{3,1},{4,6},{5,7},{6,4},{7,5},{8,10},{9,11},{10,... | collective-permute-start | bytes 786440 | tf_op jit(solution)/shard_map/ppermute | solution.py:248
  16.6 0.0 collective-permute-start.3
  16.6 0.0 collective-permute-done.6.came_ref
  16.6 0.9 %collective-permute-done.5.across_ref = bf16[4,160,128]{2,1,0:T(8,128)(2,1)S(1)} collective-permute-done((bf16[4,160,128]{2,1,0:T(8,128)(2,1)S(1)}, bf16[4,160,128]{2,1,0:T(8,128)(2,1)S(1)}, u32[]{:S(2)}, u32[]{:S(2)}) %collective-permute-start.5) | collective-permute-done | bytes 163872 | tf_op jit(solution)/shard_map/ppermute | solution.py:248
  17.5 0.1 shard_map.59
  17.6 1.1 %collective-permute-start.7 = (f32[192,128]{1,0:T(8,128)S(1)}, f32[192,128]{1,0:T(8,128)S(1)}, u32[]{:S(2)}, u32[]{:S(2)}) collective-permute-start(f32[192,128]{1,0:T(8,128)S(1)} %get-tuple-element.40), channel_id=1, source_target_pairs={{0,4},{1,5},{2,6},{3,7},{4,0},{5,1},{6,2},{7,3},{8,12},{9,13},{10,... | collective-permute-start | bytes 294920 | tf_op jit(solution)/shard_map/ppermute | solution.py:248
  18.7 1.3 %collective-permute-start.8 = (bf16[128,128]{1,0:T(8,128)(2,1)S(1)}, bf16[128,128]{1,0:T(8,128)(2,1)S(1)}, u32[]{:S(2)}, u32[]{:S(2)}) collective-permute-start(bf16[128,128]{1,0:T(8,128)(2,1)S(1)} %get-tuple-element.41), channel_id=1, source_target_pairs={{0,8},{1,9},{2,10},{3,11},{4,12},{5,13},{6,14},{7,15},{8,0},{9,1},... | collective-permute-start | bytes 98312 | tf_op jit(solution)/shard_map/ppermute | solution.py:248
  20.0 2.1 %collective-permute-start.9 = (bf16[128,128]{1,0:T(8,128)(2,1)S(1)}, bf16[128,128]{1,0:T(8,128)(2,1)S(1)}, u32[]{:S(2)}, u32[]{:S(2)}) collective-permute-start(bf16[128,128]{1,0:T(8,128)(2,1)S(1)} %get-tuple-element.42), channel_id=1, source_target_pairs={{0,12},{1,13},{2,14},{3,15},{4,8},{5,9},{6,10},{7,11},{8,4},{9,5},... | collective-permute-start | bytes 98312 | tf_op jit(solution)/shard_map/ppermute | solution.py:248
  22.1 1.0 %collective-permute-done.2.refs_6_ = bf16[4,8,4096]{2,1,0:T(8,128)(2,1)S(1)} collective-permute-done((bf16[4,8,4096]{2,1,0:T(8,128)(2,1)S(1)}, bf16[4,8,4096]{2,1,0:T(8,128)(2,1)S(1)}, u32[]{:S(2)}, u32[]{:S(2)}) %collective-permute-start.2) | collective-permute-done | bytes 262176 | tf_op jit(solution)/shard_map/ppermute | solution.py:248
  23.1 0.0 collective-permute-done.3.refs_5_
  23.1 0.4 %collective-permute-done.8.refs_2_ = bf16[128,128]{1,0:T(8,128)(2,1)S(1)} collective-permute-done((bf16[128,128]{1,0:T(8,128)(2,1)S(1)}, bf16[128,128]{1,0:T(8,128)(2,1)S(1)}, u32[]{:S(2)}, u32[]{:S(2)}) %collective-permute-start.8) | collective-permute-done | bytes 32800 | tf_op jit(solution)/shard_map/ppermute | solution.py:248
  23.5 2.2 %collective-permute-done.9.refs_3_ = bf16[128,128]{1,0:T(8,128)(2,1)S(1)} collective-permute-done((bf16[128,128]{1,0:T(8,128)(2,1)S(1)}, bf16[128,128]{1,0:T(8,128)(2,1)S(1)}, u32[]{:S(2)}, u32[]{:S(2)}) %collective-permute-start.9) | collective-permute-done | bytes 32800 | tf_op jit(solution)/shard_map/ppermute | solution.py:248
  25.7 0.0 collective-permute-done.7.refs_1_
  25.7 0.0 collective-permute-start.10
  25.7 0.6 %shard_map.60 = (f32[2,32,128]{2,1,0:T(8,128)S(1)}, f32[2,8,2,8,128]{4,3,2,1,0:T(8,128)S(1)}) custom-call(f32[128,128]{1,0:T(8,128)S(1)} %get-tuple-element.43.refs_0_, f32[192,128]{1,0:T(8,128)S(1)} %collective-permute-done.7.refs_1_, bf16[128,128]{1,0:T(8,128)(2,1)S(1)} %collective-permute-done.8.refs_2_, ...), custom_call_target="tpu_custom_call" | custom-call | tf_op jit(solution)/shard_map/pallas_call | solution.py:218
  26.4 0.9 %collective-permute-done.10.queries_ref = bf16[4,8,4096]{2,1,0:T(8,128)(2,1)S(1)} collective-permute-done((bf16[4,8,4096]{2,1,0:T(8,128)(2,1)S(1)}, bf16[4,8,4096]{2,1,0:T(8,128)(2,1)S(1)}, u32[]{:S(2)}, u32[]{:S(2)}) %collective-permute-start.10) | collective-permute-done | bytes 262176 | tf_op jit(solution)/shard_map/ppermute | solution.py:248
  27.2 1.0 %shard_map.61 = f32[2,128]{1,0:T(2,128)} custom-call(f32[2,32,128]{2,1,0:T(8,128)S(1)} %get-tuple-element.49.grads_ref, f32[2,8,2,8,128]{4,3,2,1,0:T(8,128)S(1)} %get-tuple-element.50.before_ref, bf16[4,8,4096]{2,1,0:T(8,128)(2,1)S(1)} %collective-permute-done.10.queries_ref), custom_call_target="tpu_custom_call" | custom-call | tf_op jit(solution)/shard_map/pallas_call | solution.py:231
  (2 shorter events, 0.0 us)
Async XLA Ops:
  0.0 9.0 %copy-start = (bf16[8,4096]{1,0:T(8,128)(2,1)S(1)}, bf16[8,4096]{1,0:T(8,128)(2,1)}, u32[]{:S(2)}) copy-start(bf16[8,4096]{1,0:T(8,128)(2,1)} %param.9) | copy-start | bytes 196612
  0.0 8.9 %collective-permute-start = (bf16[1,8,4096]{2,1,0:T(8,128)(2,1)}, bf16[1,8,4096]{2,1,0:T(8,128)(2,1)S(1)}, u32[]{:S(2)}, u32[]{:S(2)}) collective-permute-start(bf16[1,8,4096]{2,1,0:T(8,128)(2,1)} %bitcast.3), channel_id=1, source_target_pairs={{0,8},{1,9},{2,10},{3,11},{4,12},{5,13},{6,14},{7,15},{8,0},{9,1},... | collective-permute-start | bytes 196616 | tf_op jit(solution)/shard_map/ppermute | solution.py:248
  8.9 2.0 %collective-permute-start.4 = (f32[4,128,128]{2,1,0:T(8,128)S(1)}, f32[4,128,128]{2,1,0:T(8,128)S(1)}, u32[]{:S(2)}, u32[]{:S(2)}) collective-permute-start(f32[4,128,128]{2,1,0:T(8,128)S(1)} %get-tuple-element.35), channel_id=1, source_target_pairs={{0,1},{1,0},{2,3},{3,2},{4,5},{5,4},{6,7},{7,6},{8,9},{9,8},{10,11... | collective-permute-start | bytes 786440 | tf_op jit(solution)/shard_map/ppermute | solution.py:248
  9.0 6.0 %collective-permute-start.1 = (bf16[2,8,4096]{2,1,0:T(8,128)(2,1)S(1)}, bf16[2,8,4096]{2,1,0:T(8,128)(2,1)S(1)}, u32[]{:S(2)}, u32[]{:S(2)}) collective-permute-start(bf16[2,8,4096]{2,1,0:T(8,128)(2,1)S(1)} %shard_map.56.left_ref), channel_id=1, source_target_pairs={{0,4},{1,5},{2,6},{3,7},{4,0},{5,1},{6,2},{7,3},{8,12},{9,13},{10,... | collective-permute-start | bytes 393224 | tf_op jit(solution)/shard_map/ppermute | solution.py:248
  10.6 5.9 %collective-permute-start.6 = (f32[4,128,128]{2,1,0:T(8,128)S(1)}, f32[4,128,128]{2,1,0:T(8,128)S(1)}, u32[]{:S(2)}, u32[]{:S(2)}) collective-permute-start(f32[4,128,128]{2,1,0:T(8,128)S(1)} %get-tuple-element.36), channel_id=1, source_target_pairs={{0,1},{1,0},{2,3},{3,2},{4,5},{5,4},{6,7},{7,6},{8,9},{9,8},{10,11... | collective-permute-start | bytes 786440 | tf_op jit(solution)/shard_map/ppermute | solution.py:248
  11.0 6.5 %collective-permute-start.5 = (bf16[4,160,128]{2,1,0:T(8,128)(2,1)S(1)}, bf16[4,160,128]{2,1,0:T(8,128)(2,1)S(1)}, u32[]{:S(2)}, u32[]{:S(2)}) collective-permute-start(bf16[4,160,128]{2,1,0:T(8,128)(2,1)S(1)} %shard_map.58), channel_id=1, source_target_pairs={{0,2},{1,3},{2,0},{3,1},{4,6},{5,7},{6,4},{7,5},{8,10},{9,11},{10,... | collective-permute-start | bytes 491528 | tf_op jit(solution)/shard_map/ppermute | solution.py:248
  15.0 8.1 %collective-permute-start.2 = (bf16[4,8,4096]{2,1,0:T(8,128)(2,1)S(1)}, bf16[4,8,4096]{2,1,0:T(8,128)(2,1)S(1)}, u32[]{:S(2)}, u32[]{:S(2)}) collective-permute-start(bf16[4,8,4096]{2,1,0:T(8,128)(2,1)S(1)} %shard_map.57.refs_4_), channel_id=1, source_target_pairs={{0,2},{1,3},{2,0},{3,1},{4,6},{5,7},{6,4},{7,5},{8,10},{9,11},{10,... | collective-permute-start | bytes 786440 | tf_op jit(solution)/shard_map/ppermute | solution.py:248
  16.6 6.5 %collective-permute-start.3 = (bf16[4,8,4096]{2,1,0:T(8,128)(2,1)S(1)}, bf16[4,8,4096]{2,1,0:T(8,128)(2,1)S(1)}, u32[]{:S(2)}, u32[]{:S(2)}) collective-permute-start(bf16[4,8,4096]{2,1,0:T(8,128)(2,1)S(1)} %shard_map.57.refs_4_), channel_id=1, source_target_pairs={{0,1},{1,0},{2,3},{3,2},{4,5},{5,4},{6,7},{7,6},{8,9},{9,8},{10,11... | collective-permute-start | bytes 786440 | tf_op jit(solution)/shard_map/ppermute | solution.py:248
  17.6 8.1 %collective-permute-start.7 = (f32[192,128]{1,0:T(8,128)S(1)}, f32[192,128]{1,0:T(8,128)S(1)}, u32[]{:S(2)}, u32[]{:S(2)}) collective-permute-start(f32[192,128]{1,0:T(8,128)S(1)} %get-tuple-element.40), channel_id=1, source_target_pairs={{0,4},{1,5},{2,6},{3,7},{4,0},{5,1},{6,2},{7,3},{8,12},{9,13},{10,... | collective-permute-start | bytes 294920 | tf_op jit(solution)/shard_map/ppermute | solution.py:248
  18.7 4.8 %collective-permute-start.8 = (bf16[128,128]{1,0:T(8,128)(2,1)S(1)}, bf16[128,128]{1,0:T(8,128)(2,1)S(1)}, u32[]{:S(2)}, u32[]{:S(2)}) collective-permute-start(bf16[128,128]{1,0:T(8,128)(2,1)S(1)} %get-tuple-element.41), channel_id=1, source_target_pairs={{0,8},{1,9},{2,10},{3,11},{4,12},{5,13},{6,14},{7,15},{8,0},{9,1},... | collective-permute-start | bytes 98312 | tf_op jit(solution)/shard_map/ppermute | solution.py:248
  20.0 5.7 %collective-permute-start.9 = (bf16[128,128]{1,0:T(8,128)(2,1)S(1)}, bf16[128,128]{1,0:T(8,128)(2,1)S(1)}, u32[]{:S(2)}, u32[]{:S(2)}) collective-permute-start(bf16[128,128]{1,0:T(8,128)(2,1)S(1)} %get-tuple-element.42), channel_id=1, source_target_pairs={{0,12},{1,13},{2,14},{3,15},{4,8},{5,9},{6,10},{7,11},{8,4},{9,5},... | collective-permute-start | bytes 98312 | tf_op jit(solution)/shard_map/ppermute | solution.py:248
  25.7 1.5 %collective-permute-start.10 = (bf16[4,8,4096]{2,1,0:T(8,128)(2,1)S(1)}, bf16[4,8,4096]{2,1,0:T(8,128)(2,1)S(1)}, u32[]{:S(2)}, u32[]{:S(2)}) collective-permute-start(bf16[4,8,4096]{2,1,0:T(8,128)(2,1)S(1)} %collective-permute-done.2.refs_6_), channel_id=1, source_target_pairs={{0,1},{1,0},{2,3},{3,2},{4,5},{5,4},{6,7},{7,6},{8,9},{9,8},{10,11... | collective-permute-start | bytes 786440 | tf_op jit(solution)/shard_map/ppermute | solution.py:248

commit v10 on v9

--- a/solution.py
+++ b/solution.py
@@ -19,7 +19,7 @@
 
 
 def project_kernel(x_hbm, w_hbm, p_in_hbm, p_out_hbm, *refs):
-    given_y, given_here, kept_y, kept_here, x_buf, w_buf, p_in, p_out, low, p_sems, x_sems, w_sems = refs
+    *given_y, given_here, kept_y, kept_here, x_buf, w_buf, p_in, p_out, low, p_sems, x_sems, w_sems = refs
     here = lax.axis_index("ex")
     core, chip = lax.rem(here, 2), lax.div(here, 2)
     depth = kept_y.shape[0]
@@ -48,12 +48,13 @@
             columns = slice(column, column + step)
             product = jnp.dot(matrix[:, part], buf[part, columns], preferred_element_type=jnp.float32)
             low[lines, columns] = product if first else low[lines, columns] + product
-    for flip, given_ref, kept_ref in ((1, given_y, kept_y), (0, given_here, kept_here)):
+    for flip, given_refs, kept_ref in ((1, given_y, kept_y), (0, [given_here], kept_here)):
         for z in range(depth):
             place = lax.bitwise_xor(chip, 2 * z + flip)
             both = low[:, pl.ds(pl.multiple_of(place * 2 * width, 2 * width), 2 * width)]
             left, right = both[:, :width], both[:, width:]
-            given_ref[z] = jnp.where(core == 0, right, left)
+            given_ref = given_refs[z * len(given_refs) // depth]
+            given_ref[z % given_ref.shape[0]] = jnp.where(core == 0, right, left)
             kept_ref[z] = jnp.where(core == 0, left, right)
 
 
@@ -62,12 +63,13 @@
     width = inputs.shape[1] // devices
     rank = proj_in_t.shape[0]
     low = jax.ShapeDtypeStruct((devices // 4, 2 * rank, width), jnp.float32)
+    half = jax.ShapeDtypeStruct((devices // 8, 2 * rank, width), jnp.float32)
     chunks = [a.shape[0] // rows if a.shape[0] % rows == 0 else 1 for a, rows in ((inputs, 128), (out_grads, 256))]
     return pl.pallas_call(
         project_kernel,
-        out_shape=[low] * 4,
+        out_shape=[half] * 2 + [low] * 3,
         in_specs=[HBM_SPEC] * 4,
-        out_specs=[VMEM_SPEC] * 4,
+        out_specs=[VMEM_SPEC] * 5,
         scratch_shapes=[pltpu.VMEM(a.shape, jnp.bfloat16) for a in arrays]
         + [pltpu.VMEM((2 * rank, inputs.shape[1]), jnp.float32), pltpu.SemaphoreType.DMA((2,))]
         + [pltpu.SemaphoreType.DMA((count,)) for count in chunks],
@@ -107,9 +109,11 @@
     return parts
 
 
-def add_given_kernel(kept_ref, came_ref, out_ref):
+def add_given_kernel(kept_ref, *refs):
+    *came_refs, out_ref = refs
+    half = came_refs[0].shape[0]
     for block in range(out_ref.shape[0]):
-        put_coded(out_ref.at[block], kept_ref[block] + came_ref[block])
+        put_coded(out_ref.at[block], kept_ref[block] + came_refs[block // half][block % half])
 
 
 def add_given(kept, came):
@@ -118,7 +122,7 @@
         add_given_kernel,
         out_shape=jax.ShapeDtypeStruct((blocks, rows // 4 * 5, width), jnp.bfloat16),
         compiler_params=PARAMS,
-    )(kept, came)
+    )(kept, *came)
 
 
 def add_kept_kernel(kept_ref, came_ref, across_ref, *out_refs):
@@ -199,16 +203,13 @@
     sums_ref[...] = before_ref[...]
     add_scores(queries_ref, chips, lax.rem(core + 1, 2), grads_ref, sums_ref)
     examples, *rows, lanes = sums_ref.shape
-    ones = jnp.ones((8, lanes), jnp.float32)
+    sums = sums_ref[...].reshape(examples * out_ref.shape[1], lanes)
+    high = sums.astype(jnp.bfloat16)
+    low = (sums - high.astype(jnp.float32)).astype(jnp.bfloat16)
+    ones = jnp.ones((16, lanes), jnp.bfloat16)
+    row = sum(lax.dot_general(ones, part, LANES_BY_LANES, preferred_element_type=jnp.float32) for part in (high, low))
     for n in range(examples):
-        row = lax.dot_general(
-            ones,
-            sums_ref[n].reshape(out_ref.shape[1], lanes),
-            LANES_BY_LANES,
-            precision=lax.Precision.HIGHEST,
-            preferred_element_type=jnp.float32,
-        )
-        out_ref[n : n + 1, :] = row[0:1, :]
+        out_ref[n : n + 1, :] = row[0:1, n * out_ref.shape[1] : (n + 1) * out_ref.shape[1]]
 
 
 def first_scores(parts, queries, held, rank):
@@ -251,9 +252,8 @@
     held, reach = queries[None], [0]
     came_held = swap(held, chip=steps[0])
     lows = project(inputs, out_grads, proj_in.T, proj_out.T, devices)
-    came_held, lows = together((came_held, lows))
-    given_y, given, kept_y, kept = lows
-    came_y = swap(given_y, core=1)
+    *given_y, given, kept_y, kept = lows
+    came_y = [swap(array, core=1) for array in given_y]
     came = swap(given, core=1)
     for last, step in zip(steps, steps[1:-1]):
         held, reach = stack(held, came_held), reach + [chip ^ last for chip in reach]

time: 28.4 us -> 28.2 us (level)
  starting transfers between devices: 13.6 us -> 13 us
  waiting for transfers between devices: 7.87 us -> 8.36 us
    ppermute x11 -> x12, starting transfers between devices: 13.6 us -> 13 us  [swap(): lax.ppermute(array, 'ex', [(i, i ^ distance) for i in range(devices)])]
    ppermute x11 -> x12, waiting for transfers between devices: 7.87 us -> 8.36 us  [swap(): lax.ppermute(array, 'ex', [(i, i ^ distance) for i in range(devices)])]
  transfers between devices with their start and end apart: 11 -> 12, of which waited for: 6 -> 5; matrix products, arithmetic and copies ran while one was open for 0% -> 0% of each run, Pallas kernels for 20% -> 20%
where the time goes in v10:
time: 28.2 us; the launch traced here: 28 us
  starting transfers between devices  13 us (46%)
  waiting for transfers between devices  8.36 us (30%)
  Pallas kernels  6.54 us (23%)
    ppermute x12, starting transfers between devices, swap(): lax.ppermute(array, 'ex', [(i, i ^ distance) for i in range(devices)])  13 us
    ppermute x12, waiting for transfers between devices, swap(): lax.ppermute(array, 'ex', [(i, i ^ distance) for i in range(devices)])  8.36 us
    pallas_call x1, Pallas kernels, project(): pl.pallas_call(project_kernel, out_shape=[half] * 2 + [low] * 3, in_specs...  4.83 us
    pallas_call x1, Pallas kernels, last_scores(): pl.pallas_call(functools.partial(last_score_kernel, chips), out_shape=jax...  0.81 us
    pallas_call x1, Pallas kernels, first_scores(): pl.pallas_call(functools.partial(first_score_kernel, len(parts), held), o...  0.64 us
  transfers between devices with their start and end apart: 12, of which 5 were waited for; matrix products, arithmetic and copies ran while one was open for 0% of the time, Pallas kernels for 20%

profile of v10, /device:TPU:0, one launch (start us, length us, event | category | flops | bytes accessed | tf_op | source)
XLA Modules:
  0.0 28.0 jit_solution(11074591316683747764)
XLA Ops:
  0.0 0.0 copy-start
  0.0 4.0 %collective-permute-start = (bf16[1,8,4096]{2,1,0:T(8,128)(2,1)}, bf16[1,8,4096]{2,1,0:T(8,128)(2,1)S(1)}, u32[]{:S(2)}, u32[]{:S(2)}) collective-permute-start(bf16[1,8,4096]{2,1,0:T(8,128)(2,1)} %bitcast.3), channel_id=1, source_target_pairs={{0,8},{1,9},{2,10},{3,11},{4,12},{5,13},{6,14},{7,15},{8,0},{9,1},... | collective-permute-start | bytes 196616 | tf_op jit(solution)/shard_map/ppermute | solution.py:249
  4.0 4.8 %shard_map.57 = (f32[2,128,128]{2,1,0:T(8,128)S(1)}, f32[2,128,128]{2,1,0:T(8,128)S(1)}, f32[4,128,128]{2,1,0:T(8,128)S(1)}, f32[4,128,128]{2,1,0:T(8,128)S(1)}, f32[4,128,128]{2,1,0:T(8,128)S(1)}) custom-call(bf16[512,2048]{1,0:T(8,128)(2,1)} %x_hbm.1, bf16[1792,2048]{1,0:T(8,128)(2,1)} %w_hbm.1, bf16[64,512]{1,0:T(8,128)(2,1)} %bitcast.6, ...), custom_call_target="tpu_custom_call" | custom-call | flops 603979776 | bytes 9437184 | tf_op jit(solution)/shard_map/pallas_call | solution.py:68
  8.9 0.1 collective-permute-start.4
  9.0 0.5 %collective-permute-start.5 = (f32[2,128,128]{2,1,0:T(8,128)S(1)}, f32[2,128,128]{2,1,0:T(8,128)S(1)}, u32[]{:S(2)}, u32[]{:S(2)}) collective-permute-start(f32[2,128,128]{2,1,0:T(8,128)S(1)} %get-tuple-element.27), channel_id=1, source_target_pairs={{0,1},{1,0},{2,3},{3,2},{4,5},{5,4},{6,7},{7,6},{8,9},{9,8},{10,11... | collective-permute-start | bytes 393224 | tf_op jit(solution)/shard_map/ppermute | solution.py:249
  9.4 0.0 collective-permute-done.right_ref
  9.5 0.0 copy-done
  9.5 1.6 %collective-permute-start.1 = (bf16[2,8,4096]{2,1,0:T(8,128)(2,1)S(1)}, bf16[2,8,4096]{2,1,0:T(8,128)(2,1)S(1)}, u32[]{:S(2)}, u32[]{:S(2)}) collective-permute-start(bf16[2,8,4096]{2,1,0:T(8,128)(2,1)S(1)} %shard_map.55.left_ref), channel_id=1, source_target_pairs={{0,4},{1,5},{2,6},{3,7},{4,0},{5,1},{6,2},{7,3},{8,12},{9,13},{10,... | collective-permute-start | bytes 393224 | tf_op jit(solution)/shard_map/ppermute | solution.py:249
  11.1 0.0 collective-permute-start.7
  11.1 0.0 collective-permute-done.4.refs_0_
  11.1 0.0 collective-permute-done.5.refs_1_
  11.1 0.1 shard_map.58
  11.3 1.6 %collective-permute-start.6 = (bf16[4,160,128]{2,1,0:T(8,128)(2,1)S(1)}, bf16[4,160,128]{2,1,0:T(8,128)(2,1)S(1)}, u32[]{:S(2)}, u32[]{:S(2)}) collective-permute-start(bf16[4,160,128]{2,1,0:T(8,128)(2,1)S(1)} %shard_map.58), channel_id=1, source_target_pairs={{0,2},{1,3},{2,0},{3,1},{4,6},{5,7},{6,4},{7,5},{8,10},{9,11},{10,... | collective-permute-start | bytes 491528 | tf_op jit(solution)/shard_map/ppermute | solution.py:249
  12.8 2.2 %collective-permute-done.1.right_ref = bf16[2,8,4096]{2,1,0:T(8,128)(2,1)S(1)} collective-permute-done((bf16[2,8,4096]{2,1,0:T(8,128)(2,1)S(1)}, bf16[2,8,4096]{2,1,0:T(8,128)(2,1)S(1)}, u32[]{:S(2)}, u32[]{:S(2)}) %collective-permute-start.1) | collective-permute-done | bytes 131104 | tf_op jit(solution)/shard_map/ppermute | solution.py:249
  15.0 1.6 %collective-permute-start.2 = (bf16[4,8,4096]{2,1,0:T(8,128)(2,1)S(1)}, bf16[4,8,4096]{2,1,0:T(8,128)(2,1)S(1)}, u32[]{:S(2)}, u32[]{:S(2)}) collective-permute-start(bf16[4,8,4096]{2,1,0:T(8,128)(2,1)S(1)} %shard_map.56.refs_4_), channel_id=1, source_target_pairs={{0,2},{1,3},{2,0},{3,1},{4,6},{5,7},{6,4},{7,5},{8,10},{9,11},{10,... | collective-permute-start | bytes 786440 | tf_op jit(solution)/shard_map/ppermute | solution.py:249
  16.6 0.0 collective-permute-start.3
  16.6 0.0 collective-permute-done.7.came_ref
  16.6 1.7 %collective-permute-done.6.across_ref = bf16[4,160,128]{2,1,0:T(8,128)(2,1)S(1)} collective-permute-done((bf16[4,160,128]{2,1,0:T(8,128)(2,1)S(1)}, bf16[4,160,128]{2,1,0:T(8,128)(2,1)S(1)}, u32[]{:S(2)}, u32[]{:S(2)}) %collective-permute-start.6) | collective-permute-done | bytes 163872 | tf_op jit(solution)/shard_map/ppermute | solution.py:249
  18.3 0.1 shard_map.59
  18.4 0.5 %collective-permute-start.8 = (f32[192,128]{1,0:T(8,128)S(1)}, f32[192,128]{1,0:T(8,128)S(1)}, u32[]{:S(2)}, u32[]{:S(2)}) collective-permute-start(f32[192,128]{1,0:T(8,128)S(1)} %get-tuple-element.32), channel_id=1, source_target_pairs={{0,4},{1,5},{2,6},{3,7},{4,0},{5,1},{6,2},{7,3},{8,12},{9,13},{10,... | collective-permute-start | bytes 294920 | tf_op jit(solution)/shard_map/ppermute | solution.py:249
  18.9 1.8 %collective-permute-start.10 = (bf16[128,128]{1,0:T(8,128)(2,1)S(1)}, bf16[128,128]{1,0:T(8,128)(2,1)S(1)}, u32[]{:S(2)}, u32[]{:S(2)}) collective-permute-start(bf16[128,128]{1,0:T(8,128)(2,1)S(1)} %get-tuple-element.34), channel_id=1, source_target_pairs={{0,12},{1,13},{2,14},{3,15},{4,8},{5,9},{6,10},{7,11},{8,4},{9,5},... | collective-permute-start | bytes 98312 | tf_op jit(solution)/shard_map/ppermute | solution.py:249
  20.8 1.2 %collective-permute-start.9 = (bf16[128,128]{1,0:T(8,128)(2,1)S(1)}, bf16[128,128]{1,0:T(8,128)(2,1)S(1)}, u32[]{:S(2)}, u32[]{:S(2)}) collective-permute-start(bf16[128,128]{1,0:T(8,128)(2,1)S(1)} %get-tuple-element.33), channel_id=1, source_target_pairs={{0,8},{1,9},{2,10},{3,11},{4,12},{5,13},{6,14},{7,15},{8,0},{9,1},... | collective-permute-start | bytes 98312 | tf_op jit(solution)/shard_map/ppermute | solution.py:249
  22.0 2.7 %collective-permute-done.10.refs_3_ = bf16[128,128]{1,0:T(8,128)(2,1)S(1)} collective-permute-done((bf16[128,128]{1,0:T(8,128)(2,1)S(1)}, bf16[128,128]{1,0:T(8,128)(2,1)S(1)}, u32[]{:S(2)}, u32[]{:S(2)}) %collective-permute-start.10) | collective-permute-done | bytes 32800 | tf_op jit(solution)/shard_map/ppermute | solution.py:249
  24.7 0.9 %collective-permute-done.9.refs_2_ = bf16[128,128]{1,0:T(8,128)(2,1)S(1)} collective-permute-done((bf16[128,128]{1,0:T(8,128)(2,1)S(1)}, bf16[128,128]{1,0:T(8,128)(2,1)S(1)}, u32[]{:S(2)}, u32[]{:S(2)}) %collective-permute-start.9) | collective-permute-done | bytes 32800 | tf_op jit(solution)/shard_map/ppermute | solution.py:249
  25.6 0.0 collective-permute-done.8.refs_1_
  25.6 0.0 collective-permute-done.2.refs_6_
  25.6 0.0 collective-permute-done.3.refs_5_
  25.6 0.1 collective-permute-start.11
  25.7 0.6 %shard_map.60 = (f32[2,32,128]{2,1,0:T(8,128)S(1)}, f32[2,8,2,8,128]{4,3,2,1,0:T(8,128)S(1)}) custom-call(f32[128,128]{1,0:T(8,128)S(1)} %get-tuple-element.35.refs_0_, f32[192,128]{1,0:T(8,128)S(1)} %collective-permute-done.8.refs_1_, bf16[128,128]{1,0:T(8,128)(2,1)S(1)} %collective-permute-done.9.refs_2_, ...), custom_call_target="tpu_custom_call" | custom-call | tf_op jit(solution)/shard_map/pallas_call | solution.py:219
  26.3 0.9 %collective-permute-done.11.queries_ref = bf16[4,8,4096]{2,1,0:T(8,128)(2,1)S(1)} collective-permute-done((bf16[4,8,4096]{2,1,0:T(8,128)(2,1)S(1)}, bf16[4,8,4096]{2,1,0:T(8,128)(2,1)S(1)}, u32[]{:S(2)}, u32[]{:S(2)}) %collective-permute-start.11) | collective-permute-done | bytes 262176 | tf_op jit(solution)/shard_map/ppermute | solution.py:249
  27.2 0.8 %shard_map.61 = f32[2,128]{1,0:T(2,128)} custom-call(f32[2,32,128]{2,1,0:T(8,128)S(1)} %get-tuple-element.41.grads_ref, f32[2,8,2,8,128]{4,3,2,1,0:T(8,128)S(1)} %get-tuple-element.42.before_ref, bf16[4,8,4096]{2,1,0:T(8,128)(2,1)S(1)} %collective-permute-done.11.queries_ref), custom_call_target="tpu_custom_call" | custom-call | tf_op jit(solution)/shard_map/pallas_call | solution.py:232
  (2 shorter events, 0.0 us)
Async XLA Ops:
  0.0 9.5 %copy-start = (bf16[8,4096]{1,0:T(8,128)(2,1)S(1)}, bf16[8,4096]{1,0:T(8,128)(2,1)}, u32[]{:S(2)}) copy-start(bf16[8,4096]{1,0:T(8,128)(2,1)} %param.9) | copy-start | bytes 196612
  0.0 9.4 %collective-permute-start = (bf16[1,8,4096]{2,1,0:T(8,128)(2,1)}, bf16[1,8,4096]{2,1,0:T(8,128)(2,1)S(1)}, u32[]{:S(2)}, u32[]{:S(2)}) collective-permute-start(bf16[1,8,4096]{2,1,0:T(8,128)(2,1)} %bitcast.3), channel_id=1, source_target_pairs={{0,8},{1,9},{2,10},{3,11},{4,12},{5,13},{6,14},{7,15},{8,0},{9,1},... | collective-permute-start | bytes 196616 | tf_op jit(solution)/shard_map/ppermute | solution.py:249
  8.9 2.2 %collective-permute-start.4 = (f32[2,128,128]{2,1,0:T(8,128)S(1)}, f32[2,128,128]{2,1,0:T(8,128)S(1)}, u32[]{:S(2)}, u32[]{:S(2)}) collective-permute-start(f32[2,128,128]{2,1,0:T(8,128)S(1)} %get-tuple-element.26), channel_id=1, source_target_pairs={{0,1},{1,0},{2,3},{3,2},{4,5},{5,4},{6,7},{7,6},{8,9},{9,8},{10,11... | collective-permute-start | bytes 393224 | tf_op jit(solution)/shard_map/ppermute | solution.py:249
  9.0 2.2 %collective-permute-start.5 = (f32[2,128,128]{2,1,0:T(8,128)S(1)}, f32[2,128,128]{2,1,0:T(8,128)S(1)}, u32[]{:S(2)}, u32[]{:S(2)}) collective-permute-start(f32[2,128,128]{2,1,0:T(8,128)S(1)} %get-tuple-element.27), channel_id=1, source_target_pairs={{0,1},{1,0},{2,3},{3,2},{4,5},{5,4},{6,7},{7,6},{8,9},{9,8},{10,11... | collective-permute-start | bytes 393224 | tf_op jit(solution)/shard_map/ppermute | solution.py:249
  9.5 5.5 %collective-permute-start.1 = (bf16[2,8,4096]{2,1,0:T(8,128)(2,1)S(1)}, bf16[2,8,4096]{2,1,0:T(8,128)(2,1)S(1)}, u32[]{:S(2)}, u32[]{:S(2)}) collective-permute-start(bf16[2,8,4096]{2,1,0:T(8,128)(2,1)S(1)} %shard_map.55.left_ref), channel_id=1, source_target_pairs={{0,4},{1,5},{2,6},{3,7},{4,0},{5,1},{6,2},{7,3},{8,12},{9,13},{10,... | collective-permute-start | bytes 393224 | tf_op jit(solution)/shard_map/ppermute | solution.py:249
  11.1 5.5 %collective-permute-start.7 = (f32[4,128,128]{2,1,0:T(8,128)S(1)}, f32[4,128,128]{2,1,0:T(8,128)S(1)}, u32[]{:S(2)}, u32[]{:S(2)}) collective-permute-start(f32[4,128,128]{2,1,0:T(8,128)S(1)} %get-tuple-element.28), channel_id=1, source_target_pairs={{0,1},{1,0},{2,3},{3,2},{4,5},{5,4},{6,7},{7,6},{8,9},{9,8},{10,11... | collective-permute-start | bytes 786440 | tf_op jit(solution)/shard_map/ppermute | solution.py:249
  11.3 7.1 %collective-permute-start.6 = (bf16[4,160,128]{2,1,0:T(8,128)(2,1)S(1)}, bf16[4,160,128]{2,1,0:T(8,128)(2,1)S(1)}, u32[]{:S(2)}, u32[]{:S(2)}) collective-permute-start(bf16[4,160,128]{2,1,0:T(8,128)(2,1)S(1)} %shard_map.58), channel_id=1, source_target_pairs={{0,2},{1,3},{2,0},{3,1},{4,6},{5,7},{6,4},{7,5},{8,10},{9,11},{10,... | collective-permute-start | bytes 491528 | tf_op jit(solution)/shard_map/ppermute | solution.py:249
  15.0 10.6 %collective-permute-start.2 = (bf16[4,8,4096]{2,1,0:T(8,128)(2,1)S(1)}, bf16[4,8,4096]{2,1,0:T(8,128)(2,1)S(1)}, u32[]{:S(2)}, u32[]{:S(2)}) collective-permute-start(bf16[4,8,4096]{2,1,0:T(8,128)(2,1)S(1)} %shard_map.56.refs_4_), channel_id=1, source_target_pairs={{0,2},{1,3},{2,0},{3,1},{4,6},{5,7},{6,4},{7,5},{8,10},{9,11},{10,... | collective-permute-start | bytes 786440 | tf_op jit(solution)/shard_map/ppermute | solution.py:249
  16.6 9.0 %collective-permute-start.3 = (bf16[4,8,4096]{2,1,0:T(8,128)(2,1)S(1)}, bf16[4,8,4096]{2,1,0:T(8,128)(2,1)S(1)}, u32[]{:S(2)}, u32[]{:S(2)}) collective-permute-start(bf16[4,8,4096]{2,1,0:T(8,128)(2,1)S(1)} %shard_map.56.refs_4_), channel_id=1, source_target_pairs={{0,1},{1,0},{2,3},{3,2},{4,5},{5,4},{6,7},{7,6},{8,9},{9,8},{10,11... | collective-permute-start | bytes 786440 | tf_op jit(solution)/shard_map/ppermute | solution.py:249
  18.4 7.2 %collective-permute-start.8 = (f32[192,128]{1,0:T(8,128)S(1)}, f32[192,128]{1,0:T(8,128)S(1)}, u32[]{:S(2)}, u32[]{:S(2)}) collective-permute-start(f32[192,128]{1,0:T(8,128)S(1)} %get-tuple-element.32), channel_id=1, source_target_pairs={{0,4},{1,5},{2,6},{3,7},{4,0},{5,1},{6,2},{7,3},{8,12},{9,13},{10,... | collective-permute-start | bytes 294920 | tf_op jit(solution)/shard_map/ppermute | solution.py:249
  18.9 5.8 %collective-permute-start.10 = (bf16[128,128]{1,0:T(8,128)(2,1)S(1)}, bf16[128,128]{1,0:T(8,128)(2,1)S(1)}, u32[]{:S(2)}, u32[]{:S(2)}) collective-permute-start(bf16[128,128]{1,0:T(8,128)(2,1)S(1)} %get-tuple-element.34), channel_id=1, source_target_pairs={{0,12},{1,13},{2,14},{3,15},{4,8},{5,9},{6,10},{7,11},{8,4},{9,5},... | collective-permute-start | bytes 98312 | tf_op jit(solution)/shard_map/ppermute | solution.py:249
  20.8 4.8 %collective-permute-start.9 = (bf16[128,128]{1,0:T(8,128)(2,1)S(1)}, bf16[128,128]{1,0:T(8,128)(2,1)S(1)}, u32[]{:S(2)}, u32[]{:S(2)}) collective-permute-start(bf16[128,128]{1,0:T(8,128)(2,1)S(1)} %get-tuple-element.33), channel_id=1, source_target_pairs={{0,8},{1,9},{2,10},{3,11},{4,12},{5,13},{6,14},{7,15},{8,0},{9,1},... | collective-permute-start | bytes 98312 | tf_op jit(solution)/shard_map/ppermute | solution.py:249
  25.6 1.6 %collective-permute-start.11 = (bf16[4,8,4096]{2,1,0:T(8,128)(2,1)S(1)}, bf16[4,8,4096]{2,1,0:T(8,128)(2,1)S(1)}, u32[]{:S(2)}, u32[]{:S(2)}) collective-permute-start(bf16[4,8,4096]{2,1,0:T(8,128)(2,1)S(1)} %collective-permute-done.2.refs_6_), channel_id=1, source_target_pairs={{0,1},{1,0},{2,3},{3,2},{4,5},{5,4},{6,7},{7,6},{8,9},{9,8},{10,11... | collective-permute-start | bytes 786440 | tf_op jit(solution)/shard_map/ppermute | solution.py:249

commit v11 on v10

--- a/solution.py
+++ b/solution.py
@@ -9,8 +9,8 @@
 
 SEQ = 64
 VMEM_BYTES = 32 * 1024 * 1024
-AHEAD = 7
 NEAR_PAD = 64
+LOADED_ROWS = 256
 CODE_SCALE = 2.0**-8
 LANES_BY_LANES = (((1,), (1,)), ((), ()))
 HBM_SPEC = pl.BlockSpec(memory_space=pltpu.HBM)
@@ -18,68 +18,93 @@
 PARAMS = pltpu.CompilerParams(vmem_limit_bytes=VMEM_BYTES)
 
 
-def project_kernel(x_hbm, w_hbm, p_in_hbm, p_out_hbm, *refs):
-    *given_y, given_here, kept_y, kept_here, x_buf, w_buf, p_in, p_out, low, p_sems, x_sems, w_sems = refs
-    here = lax.axis_index("ex")
-    core, chip = lax.rem(here, 2), lax.div(here, 2)
-    depth = kept_y.shape[0]
-    rank, width = kept_y.shape[1] // 2, kept_y.shape[2]
+def project_loaded_kernel(x_hbm, w_hbm, p_in_hbm, p_out_hbm, low_in_ref, low_out_ref, x_buf, w_buf, p_in, p_out, sems, p_sems):
     matrices = [
         pltpu.make_async_copy(p_in_hbm, p_in, p_sems.at[0]),
         pltpu.make_async_copy(p_out_hbm, p_out, p_sems.at[1]),
     ]
     chunks = []
-    for top, hbm, buf, sems, matrix in ((0, x_hbm, x_buf, x_sems, p_in), (rank, w_hbm, w_buf, w_sems, p_out)):
-        rows = buf.shape[0] // sems.shape[0]
-        for chunk in range(sems.shape[0]):
-            part = pl.ds(chunk * rows, rows)
-            copy = pltpu.make_async_copy(hbm.at[part, :], buf.at[part, :], sems.at[chunk])
-            chunks.append((slice(top, top + rank), part, buf, matrix, copy, chunk == 0))
-    for copy in matrices + [chunk[4] for chunk in chunks[:AHEAD]]:
+    for hbm, buf, matrix, low_ref in ((x_hbm, x_buf, p_in, low_in_ref), (w_hbm, w_buf, p_out, low_out_ref)):
+        count = buf.shape[0] // LOADED_ROWS if buf.shape[0] % LOADED_ROWS == 0 else 1
+        for chunk in range(count):
+            part = pl.ds(chunk * (buf.shape[0] // count), buf.shape[0] // count)
+            copy = pltpu.make_async_copy(hbm.at[part, :], buf.at[part, :], sems.at[len(chunks)])
+            chunks.append((part, buf, matrix, low_ref, copy, chunk == 0))
+    for copy in matrices + [chunk[4] for chunk in chunks]:
         copy.start()
     for copy in matrices:
         copy.wait()
-    step = min(1024, low.shape[1])
-    for index, (lines, part, buf, matrix, copy, first) in enumerate(chunks):
+    step = min(1024, low_in_ref.shape[1])
+    for part, buf, matrix, low_ref, copy, first in chunks:
         copy.wait()
-        if index + AHEAD < len(chunks):
-            chunks[index + AHEAD][4].start()
-        for column in range(0, low.shape[1], step):
+        for column in range(0, low_ref.shape[1], step):
             columns = slice(column, column + step)
             product = jnp.dot(matrix[:, part], buf[part, columns], preferred_element_type=jnp.float32)
-            low[lines, columns] = product if first else low[lines, columns] + product
+            low_ref[:, columns] = product if first else low_ref[:, columns] + product
+
+
+def project_loaded(inputs, out_grads, proj_in_t, proj_out_t, rows):
+    arrays = [pltpu.with_memory_space_constraint(a, pltpu.HBM) for a in (inputs, out_grads, proj_in_t, proj_out_t)]
+    rank, tokens = proj_in_t.shape[0], inputs.shape[1]
+    chunks = sum(a // LOADED_ROWS if a % LOADED_ROWS == 0 else 1 for a in (inputs.shape[0], rows))
+    return pl.pallas_call(
+        project_loaded_kernel,
+        out_shape=[jax.ShapeDtypeStruct((rank, tokens), jnp.float32)] * 2,
+        in_specs=[HBM_SPEC] * 4,
+        out_specs=[VMEM_SPEC] * 2,
+        scratch_shapes=[
+            pltpu.VMEM(inputs.shape, jnp.bfloat16),
+            pltpu.VMEM((rows, tokens), jnp.bfloat16),
+            pltpu.VMEM(proj_in_t.shape, jnp.bfloat16),
+            pltpu.VMEM(proj_out_t.shape, jnp.bfloat16),
+            pltpu.SemaphoreType.DMA((chunks,)),
+            pltpu.SemaphoreType.DMA((2,)),
+        ],
+        compiler_params=PARAMS,
+        cost_estimate=pl.CostEstimate(
+            flops=2 * rank * (inputs.shape[0] + rows) * tokens,
+            bytes_accessed=2 * (inputs.shape[0] + rows) * tokens,
+            transcendentals=0,
+        ),
+    )(*arrays)
+
+
+def project_kernel(done, low_in_ref, low_out_ref, p_ref, w_ref, *refs):
+    *given_y, given_here, kept_y, kept_here = refs
+    here = lax.axis_index("ex")
+    core, chip = lax.rem(here, 2), lax.div(here, 2)
+    depth = kept_y.shape[0]
+    rank, width = kept_y.shape[1] // 2, kept_y.shape[2]
     for flip, given_refs, kept_ref in ((1, given_y, kept_y), (0, [given_here], kept_here)):
         for z in range(depth):
             place = lax.bitwise_xor(chip, 2 * z + flip)
-            both = low[:, pl.ds(pl.multiple_of(place * 2 * width, 2 * width), 2 * width)]
-            left, right = both[:, :width], both[:, width:]
+            columns = pl.ds(pl.multiple_of(place * 2 * width, 2 * width), 2 * width)
+            low_out = jnp.dot(p_ref[:, done:], w_ref[done:, columns], preferred_element_type=jnp.float32)
+            low_out = low_out + low_out_ref[:, columns]
             given_ref = given_refs[z * len(given_refs) // depth]
-            given_ref[z % given_ref.shape[0]] = jnp.where(core == 0, right, left)
-            kept_ref[z] = jnp.where(core == 0, left, right)
+            for lines, low in ((slice(0, rank), low_in_ref[:, columns]), (slice(rank, 2 * rank), low_out)):
+                left, right = low[:, :width], low[:, width:]
+                given_ref[z % given_ref.shape[0], lines, :] = jnp.where(core == 0, right, left)
+                kept_ref[z, lines, :] = jnp.where(core == 0, left, right)
 
 
 def project(inputs, out_grads, proj_in_t, proj_out_t, devices):
-    arrays = [pltpu.with_memory_space_constraint(a, pltpu.HBM) for a in (inputs, out_grads, proj_in_t, proj_out_t)]
-    width = inputs.shape[1] // devices
-    rank = proj_in_t.shape[0]
+    rank, width = proj_in_t.shape[0], inputs.shape[1] // devices
+    units = out_grads.shape[0]
+    rows = 2 * LOADED_ROWS if units % LOADED_ROWS == 0 else 16
+    lows = project_loaded(inputs, out_grads, proj_in_t, proj_out_t, rows)
     low = jax.ShapeDtypeStruct((devices // 4, 2 * rank, width), jnp.float32)
     half = jax.ShapeDtypeStruct((devices // 8, 2 * rank, width), jnp.float32)
-    chunks = [a.shape[0] // rows if a.shape[0] % rows == 0 else 1 for a, rows in ((inputs, 128), (out_grads, 256))]
-    return pl.pallas_call(
-        project_kernel,
+    return pl.pallas_call(
+        functools.partial(project_kernel, rows),
         out_shape=[half] * 2 + [low] * 3,
-        in_specs=[HBM_SPEC] * 4,
+        in_specs=[VMEM_SPEC] * 4,
         out_specs=[VMEM_SPEC] * 5,
-        scratch_shapes=[pltpu.VMEM(a.shape, jnp.bfloat16) for a in arrays]
-        + [pltpu.VMEM((2 * rank, inputs.shape[1]), jnp.float32), pltpu.SemaphoreType.DMA((2,))]
-        + [pltpu.SemaphoreType.DMA((count,)) for count in chunks],
         compiler_params=PARAMS,
         cost_estimate=pl.CostEstimate(
-            flops=2 * rank * (inputs.size + out_grads.size),
-            bytes_accessed=2 * (inputs.size + out_grads.size),
-            transcendentals=0,
+            flops=2 * rank * out_grads.size, bytes_accessed=2 * out_grads.size, transcendentals=0
         ),
-    )(*arrays)
+    )(*lows, proj_out_t, out_grads)
 
 
 def put_coded(out_ref, low):

time: 28.2 us -> 28.2 us (level)
  waiting for transfers between devices: 8.36 us -> 9.07 us
  Pallas kernels: 6.54 us -> 5.83 us
    ppermute x12, waiting for transfers between devices: 8.36 us -> 9.07 us  [swap(): lax.ppermute(array, 'ex', [(i, i ^ distance) for i in range(devices)])]
    pallas_call x1 -> x2, Pallas kernels: 4.83 us -> 4.11 us  [the longest x1 2.98 us: project_loaded(): pl.pallas_call(project_loaded_kernel, out_shape=[jax.ShapeDtypeStruct((ra...]
  transfers between devices with their start and end apart: 12 -> 12, of which waited for: 5 -> 5; matrix products, arithmetic and copies ran while one was open for 0% -> 0% of each run, Pallas kernels for 20% -> 18%
where the time goes in v11:
time: 28.2 us; the launch traced here: 28.1 us
  starting transfers between devices  13.1 us (46%)
  waiting for transfers between devices  9.07 us (32%)
  Pallas kernels  5.83 us (21%)
    ppermute x12, starting transfers between devices, swap(): lax.ppermute(array, 'ex', [(i, i ^ distance) for i in range(devices)])  13.1 us
    ppermute x12, waiting for transfers between devices, swap(): lax.ppermute(array, 'ex', [(i, i ^ distance) for i in range(devices)])  9.07 us
    pallas_call x1, Pallas kernels, project_loaded(): pl.pallas_call(project_loaded_kernel, out_shape=[jax.ShapeDtypeStruct((ra...  2.98 us
    pallas_call x1, Pallas kernels, project(): pl.pallas_call(functools.partial(project_kernel, rows), out_shape=[half]...  1.13 us
    pallas_call x1, Pallas kernels, last_scores(): pl.pallas_call(functools.partial(last_score_kernel, chips), out_shape=jax...  0.81 us
    pallas_call x1, Pallas kernels, first_scores(): pl.pallas_call(functools.partial(first_score_kernel, len(parts), held), o...  0.64 us
  transfers between devices with their start and end apart: 12, of which 5 were waited for; matrix products, arithmetic and copies ran while one was open for 0% of the time, Pallas kernels for 18%

profile of v11, /device:TPU:0, one launch (start us, length us, event | category | flops | bytes accessed | tf_op | source)
XLA Modules:
  0.0 28.1 jit_solution(5594694156340482073)
XLA Ops:
  0.0 0.0 copy-start.1
  0.0 0.0 copy-start
  0.0 4.0 %collective-permute-start = (bf16[1,8,4096]{2,1,0:T(8,128)(2,1)}, bf16[1,8,4096]{2,1,0:T(8,128)(2,1)S(1)}, u32[]{:S(2)}, u32[]{:S(2)}) collective-permute-start(bf16[1,8,4096]{2,1,0:T(8,128)(2,1)} %bitcast.5), channel_id=1, source_target_pairs={{0,8},{1,9},{2,10},{3,11},{4,12},{5,13},{6,14},{7,15},{8,0},{9,1},... | collective-permute-start | bytes 196616 | tf_op jit(solution)/shard_map/ppermute | solution.py:274
  4.0 0.0 copy-start.2
  4.0 3.0 %shard_map.57 = (f32[64,2048]{1,0:T(8,128)S(1)}, f32[64,2048]{1,0:T(8,128)S(1)}) custom-call(bf16[512,2048]{1,0:T(8,128)(2,1)} %x_hbm.1, bf16[1792,2048]{1,0:T(8,128)(2,1)} %w_ref.1, bf16[64,512]{1,0:T(8,128)(2,1)} %bitcast.7, bf16[64,1792]{1,0:T(8,128)(2,1)} %bitcast.3), custom_call_target="tpu_custom_call" | custom-call | flops 268435456 | bytes 4194304 | tf_op jit(solution)/shard_map/pallas_call | solution.py:50
  7.0 0.0 copy-done.1
  7.0 0.0 copy-done
  7.1 1.1 %shard_map.58 = (f32[2,128,128]{2,1,0:T(8,128)S(1)}, f32[2,128,128]{2,1,0:T(8,128)S(1)}, f32[4,128,128]{2,1,0:T(8,128)S(1)}, f32[4,128,128]{2,1,0:T(8,128)S(1)}, f32[4,128,128]{2,1,0:T(8,128)S(1)}) custom-call(f32[64,2048]{1,0:T(8,128)S(1)} %get-tuple-element.26.low_in_ref, f32[64,2048]{1,0:T(8,128)S(1)} %get-tuple-element.27.low_out_ref, ...), custom_call_target="tpu_custom_call" | custom-call | flops 469762048 | bytes 7340032 | tf_op jit(solution)/shard_map/pallas_call | solution.py:98
  8.2 0.1 collective-permute-start.4
  8.3 0.5 %collective-permute-start.5 = (f32[2,128,128]{2,1,0:T(8,128)S(1)}, f32[2,128,128]{2,1,0:T(8,128)S(1)}, u32[]{:S(2)}, u32[]{:S(2)}) collective-permute-start(f32[2,128,128]{2,1,0:T(8,128)S(1)} %get-tuple-element.31), channel_id=1, source_target_pairs={{0,1},{1,0},{2,3},{3,2},{4,5},{5,4},{6,7},{7,6},{8,9},{9,8},{10,11... | collective-permute-start | bytes 393224 | tf_op jit(solution)/shard_map/ppermute | solution.py:274
  8.8 0.0 collective-permute-done.right_ref
  8.8 0.0 copy-done.2
  8.8 1.6 %collective-permute-start.1 = (bf16[2,8,4096]{2,1,0:T(8,128)(2,1)S(1)}, bf16[2,8,4096]{2,1,0:T(8,128)(2,1)S(1)}, u32[]{:S(2)}, u32[]{:S(2)}) collective-permute-start(bf16[2,8,4096]{2,1,0:T(8,128)(2,1)S(1)} %shard_map.55.left_ref), channel_id=1, source_target_pairs={{0,4},{1,5},{2,6},{3,7},{4,0},{5,1},{6,2},{7,3},{8,12},{9,13},{10,... | collective-permute-start | bytes 393224 | tf_op jit(solution)/shard_map/ppermute | solution.py:274
  10.4 0.0 collective-permute-start.7
  10.4 0.0 collective-permute-done.4.refs_0_
  10.4 0.0 collective-permute-done.5.refs_1_
  10.4 0.1 shard_map.59
  10.6 1.6 %collective-permute-start.6 = (bf16[4,160,128]{2,1,0:T(8,128)(2,1)S(1)}, bf16[4,160,128]{2,1,0:T(8,128)(2,1)S(1)}, u32[]{:S(2)}, u32[]{:S(2)}) collective-permute-start(bf16[4,160,128]{2,1,0:T(8,128)(2,1)S(1)} %shard_map.59), channel_id=1, source_target_pairs={{0,2},{1,3},{2,0},{3,1},{4,6},{5,7},{6,4},{7,5},{8,10},{9,11},{10,... | collective-permute-start | bytes 491528 | tf_op jit(solution)/shard_map/ppermute | solution.py:274
  12.2 2.2 %collective-permute-done.1.right_ref = bf16[2,8,4096]{2,1,0:T(8,128)(2,1)S(1)} collective-permute-done((bf16[2,8,4096]{2,1,0:T(8,128)(2,1)S(1)}, bf16[2,8,4096]{2,1,0:T(8,128)(2,1)S(1)}, u32[]{:S(2)}, u32[]{:S(2)}) %collective-permute-start.1) | collective-permute-done | bytes 131104 | tf_op jit(solution)/shard_map/ppermute | solution.py:274
  14.4 1.6 %collective-permute-start.2 = (bf16[4,8,4096]{2,1,0:T(8,128)(2,1)S(1)}, bf16[4,8,4096]{2,1,0:T(8,128)(2,1)S(1)}, u32[]{:S(2)}, u32[]{:S(2)}) collective-permute-start(bf16[4,8,4096]{2,1,0:T(8,128)(2,1)S(1)} %shard_map.56.refs_4_), channel_id=1, source_target_pairs={{0,2},{1,3},{2,0},{3,1},{4,6},{5,7},{6,4},{7,5},{8,10},{9,11},{10,... | collective-permute-start | bytes 786440 | tf_op jit(solution)/shard_map/ppermute | solution.py:274
  15.9 0.0 collective-permute-start.3
  16.0 0.0 collective-permute-done.7.came_ref
  16.0 1.7 %collective-permute-done.6.across_ref = bf16[4,160,128]{2,1,0:T(8,128)(2,1)S(1)} collective-permute-done((bf16[4,160,128]{2,1,0:T(8,128)(2,1)S(1)}, bf16[4,160,128]{2,1,0:T(8,128)(2,1)S(1)}, u32[]{:S(2)}, u32[]{:S(2)}) %collective-permute-start.6) | collective-permute-done | bytes 163872 | tf_op jit(solution)/shard_map/ppermute | solution.py:274
  17.6 0.1 shard_map.60
  17.8 0.5 %collective-permute-start.8 = (f32[192,128]{1,0:T(8,128)S(1)}, f32[192,128]{1,0:T(8,128)S(1)}, u32[]{:S(2)}, u32[]{:S(2)}) collective-permute-start(f32[192,128]{1,0:T(8,128)S(1)} %get-tuple-element.36), channel_id=1, source_target_pairs={{0,4},{1,5},{2,6},{3,7},{4,0},{5,1},{6,2},{7,3},{8,12},{9,13},{10,... | collective-permute-start | bytes 294920 | tf_op jit(solution)/shard_map/ppermute | solution.py:274
  18.3 2.6 %collective-permute-start.10 = (bf16[128,128]{1,0:T(8,128)(2,1)S(1)}, bf16[128,128]{1,0:T(8,128)(2,1)S(1)}, u32[]{:S(2)}, u32[]{:S(2)}) collective-permute-start(bf16[128,128]{1,0:T(8,128)(2,1)S(1)} %get-tuple-element.38), channel_id=1, source_target_pairs={{0,12},{1,13},{2,14},{3,15},{4,8},{5,9},{6,10},{7,11},{8,4},{9,5},... | collective-permute-start | bytes 98312 | tf_op jit(solution)/shard_map/ppermute | solution.py:274
  20.8 0.5 %collective-permute-start.9 = (bf16[128,128]{1,0:T(8,128)(2,1)S(1)}, bf16[128,128]{1,0:T(8,128)(2,1)S(1)}, u32[]{:S(2)}, u32[]{:S(2)}) collective-permute-start(bf16[128,128]{1,0:T(8,128)(2,1)S(1)} %get-tuple-element.37), channel_id=1, source_target_pairs={{0,8},{1,9},{2,10},{3,11},{4,12},{5,13},{6,14},{7,15},{8,0},{9,1},... | collective-permute-start | bytes 98312 | tf_op jit(solution)/shard_map/ppermute | solution.py:274
  21.3 3.1 %collective-permute-done.10.refs_3_ = bf16[128,128]{1,0:T(8,128)(2,1)S(1)} collective-permute-done((bf16[128,128]{1,0:T(8,128)(2,1)S(1)}, bf16[128,128]{1,0:T(8,128)(2,1)S(1)}, u32[]{:S(2)}, u32[]{:S(2)}) %collective-permute-start.10) | collective-permute-done | bytes 32800 | tf_op jit(solution)/shard_map/ppermute | solution.py:274
  24.4 1.2 %collective-permute-done.9.refs_2_ = bf16[128,128]{1,0:T(8,128)(2,1)S(1)} collective-permute-done((bf16[128,128]{1,0:T(8,128)(2,1)S(1)}, bf16[128,128]{1,0:T(8,128)(2,1)S(1)}, u32[]{:S(2)}, u32[]{:S(2)}) %collective-permute-start.9) | collective-permute-done | bytes 32800 | tf_op jit(solution)/shard_map/ppermute | solution.py:274
  25.6 0.0 collective-permute-done.8.refs_1_
  25.6 0.0 collective-permute-done.2.refs_6_
  25.6 0.0 collective-permute-done.3.refs_5_
  25.7 0.1 collective-permute-start.11
  25.7 0.6 %shard_map.61 = (f32[2,32,128]{2,1,0:T(8,128)S(1)}, f32[2,8,2,8,128]{4,3,2,1,0:T(8,128)S(1)}) custom-call(f32[128,128]{1,0:T(8,128)S(1)} %get-tuple-element.39.refs_0_, f32[192,128]{1,0:T(8,128)S(1)} %collective-permute-done.8.refs_1_, bf16[128,128]{1,0:T(8,128)(2,1)S(1)} %collective-permute-done.9.refs_2_, ...), custom_call_target="tpu_custom_call" | custom-call | tf_op jit(solution)/shard_map/pallas_call | solution.py:244
  26.4 0.9 %collective-permute-done.11.queries_ref = bf16[4,8,4096]{2,1,0:T(8,128)(2,1)S(1)} collective-permute-done((bf16[4,8,4096]{2,1,0:T(8,128)(2,1)S(1)}, bf16[4,8,4096]{2,1,0:T(8,128)(2,1)S(1)}, u32[]{:S(2)}, u32[]{:S(2)}) %collective-permute-start.11) | collective-permute-done | bytes 262176 | tf_op jit(solution)/shard_map/ppermute | solution.py:274
  27.3 0.8 %shard_map.62 = f32[2,128]{1,0:T(2,128)} custom-call(f32[2,32,128]{2,1,0:T(8,128)S(1)} %get-tuple-element.45.grads_ref, f32[2,8,2,8,128]{4,3,2,1,0:T(8,128)S(1)} %get-tuple-element.46.before_ref, bf16[4,8,4096]{2,1,0:T(8,128)(2,1)S(1)} %collective-permute-done.11.queries_ref), custom_call_target="tpu_custom_call" | custom-call | tf_op jit(solution)/shard_map/pallas_call | solution.py:257
  (2 shorter events, 0.0 us)
Async XLA Ops:
  0.0 7.0 %copy-start.1 = (bf16[1792,64]{0,1:T(8,128)(2,1)S(1)}, bf16[1792,64]{0,1:T(8,128)(2,1)}, u32[]{:S(2)}) copy-start(bf16[1792,64]{0,1:T(8,128)(2,1)} %param.8) | copy-start | bytes 688132
  0.0 7.0 %copy-start = (bf16[1792,2048]{1,0:T(8,128)(2,1)S(1)}, bf16[1792,2048]{1,0:T(8,128)(2,1)}, u32[]{:S(2)}) copy-start(bf16[1792,2048]{1,0:T(8,128)(2,1)} %w_ref.1) | copy-start | bytes 22020100
  0.0 8.8 %collective-permute-start = (bf16[1,8,4096]{2,1,0:T(8,128)(2,1)}, bf16[1,8,4096]{2,1,0:T(8,128)(2,1)S(1)}, u32[]{:S(2)}, u32[]{:S(2)}) collective-permute-start(bf16[1,8,4096]{2,1,0:T(8,128)(2,1)} %bitcast.5), channel_id=1, source_target_pairs={{0,8},{1,9},{2,10},{3,11},{4,12},{5,13},{6,14},{7,15},{8,0},{9,1},... | collective-permute-start | bytes 196616 | tf_op jit(solution)/shard_map/ppermute | solution.py:274
  4.0 4.7 %copy-start.2 = (bf16[8,4096]{1,0:T(8,128)(2,1)S(1)}, bf16[8,4096]{1,0:T(8,128)(2,1)}, u32[]{:S(2)}) copy-start(bf16[8,4096]{1,0:T(8,128)(2,1)} %param.9) | copy-start | bytes 196612
  8.2 2.2 %collective-permute-start.4 = (f32[2,128,128]{2,1,0:T(8,128)S(1)}, f32[2,128,128]{2,1,0:T(8,128)S(1)}, u32[]{:S(2)}, u32[]{:S(2)}) collective-permute-start(f32[2,128,128]{2,1,0:T(8,128)S(1)} %get-tuple-element.30), channel_id=1, source_target_pairs={{0,1},{1,0},{2,3},{3,2},{4,5},{5,4},{6,7},{7,6},{8,9},{9,8},{10,11... | collective-permute-start | bytes 393224 | tf_op jit(solution)/shard_map/ppermute | solution.py:274
  8.3 2.2 %collective-permute-start.5 = (f32[2,128,128]{2,1,0:T(8,128)S(1)}, f32[2,128,128]{2,1,0:T(8,128)S(1)}, u32[]{:S(2)}, u32[]{:S(2)}) collective-permute-start(f32[2,128,128]{2,1,0:T(8,128)S(1)} %get-tuple-element.31), channel_id=1, source_target_pairs={{0,1},{1,0},{2,3},{3,2},{4,5},{5,4},{6,7},{7,6},{8,9},{9,8},{10,11... | collective-permute-start | bytes 393224 | tf_op jit(solution)/shard_map/ppermute | solution.py:274
  8.8 5.5 %collective-permute-start.1 = (bf16[2,8,4096]{2,1,0:T(8,128)(2,1)S(1)}, bf16[2,8,4096]{2,1,0:T(8,128)(2,1)S(1)}, u32[]{:S(2)}, u32[]{:S(2)}) collective-permute-start(bf16[2,8,4096]{2,1,0:T(8,128)(2,1)S(1)} %shard_map.55.left_ref), channel_id=1, source_target_pairs={{0,4},{1,5},{2,6},{3,7},{4,0},{5,1},{6,2},{7,3},{8,12},{9,13},{10,... | collective-permute-start | bytes 393224 | tf_op jit(solution)/shard_map/ppermute | solution.py:274
  10.4 5.5 %collective-permute-start.7 = (f32[4,128,128]{2,1,0:T(8,128)S(1)}, f32[4,128,128]{2,1,0:T(8,128)S(1)}, u32[]{:S(2)}, u32[]{:S(2)}) collective-permute-start(f32[4,128,128]{2,1,0:T(8,128)S(1)} %get-tuple-element.32), channel_id=1, source_target_pairs={{0,1},{1,0},{2,3},{3,2},{4,5},{5,4},{6,7},{7,6},{8,9},{9,8},{10,11... | collective-permute-start | bytes 786440 | tf_op jit(solution)/shard_map/ppermute | solution.py:274
  10.6 7.1 %collective-permute-start.6 = (bf16[4,160,128]{2,1,0:T(8,128)(2,1)S(1)}, bf16[4,160,128]{2,1,0:T(8,128)(2,1)S(1)}, u32[]{:S(2)}, u32[]{:S(2)}) collective-permute-start(bf16[4,160,128]{2,1,0:T(8,128)(2,1)S(1)} %shard_map.59), channel_id=1, source_target_pairs={{0,2},{1,3},{2,0},{3,1},{4,6},{5,7},{6,4},{7,5},{8,10},{9,11},{10,... | collective-permute-start | bytes 491528 | tf_op jit(solution)/shard_map/ppermute | solution.py:274
  14.4 11.3 %collective-permute-start.2 = (bf16[4,8,4096]{2,1,0:T(8,128)(2,1)S(1)}, bf16[4,8,4096]{2,1,0:T(8,128)(2,1)S(1)}, u32[]{:S(2)}, u32[]{:S(2)}) collective-permute-start(bf16[4,8,4096]{2,1,0:T(8,128)(2,1)S(1)} %shard_map.56.refs_4_), channel_id=1, source_target_pairs={{0,2},{1,3},{2,0},{3,1},{4,6},{5,7},{6,4},{7,5},{8,10},{9,11},{10,... | collective-permute-start | bytes 786440 | tf_op jit(solution)/shard_map/ppermute | solution.py:274
  15.9 9.7 %collective-permute-start.3 = (bf16[4,8,4096]{2,1,0:T(8,128)(2,1)S(1)}, bf16[4,8,4096]{2,1,0:T(8,128)(2,1)S(1)}, u32[]{:S(2)}, u32[]{:S(2)}) collective-permute-start(bf16[4,8,4096]{2,1,0:T(8,128)(2,1)S(1)} %shard_map.56.refs_4_), channel_id=1, source_target_pairs={{0,1},{1,0},{2,3},{3,2},{4,5},{5,4},{6,7},{7,6},{8,9},{9,8},{10,11... | collective-permute-start | bytes 786440 | tf_op jit(solution)/shard_map/ppermute | solution.py:274
  17.8 7.9 %collective-permute-start.8 = (f32[192,128]{1,0:T(8,128)S(1)}, f32[192,128]{1,0:T(8,128)S(1)}, u32[]{:S(2)}, u32[]{:S(2)}) collective-permute-start(f32[192,128]{1,0:T(8,128)S(1)} %get-tuple-element.36), channel_id=1, source_target_pairs={{0,4},{1,5},{2,6},{3,7},{4,0},{5,1},{6,2},{7,3},{8,12},{9,13},{10,... | collective-permute-start | bytes 294920 | tf_op jit(solution)/shard_map/ppermute | solution.py:274
  18.3 6.2 %collective-permute-start.10 = (bf16[128,128]{1,0:T(8,128)(2,1)S(1)}, bf16[128,128]{1,0:T(8,128)(2,1)S(1)}, u32[]{:S(2)}, u32[]{:S(2)}) collective-permute-start(bf16[128,128]{1,0:T(8,128)(2,1)S(1)} %get-tuple-element.38), channel_id=1, source_target_pairs={{0,12},{1,13},{2,14},{3,15},{4,8},{5,9},{6,10},{7,11},{8,4},{9,5},... | collective-permute-start | bytes 98312 | tf_op jit(solution)/shard_map/ppermute | solution.py:274
  20.8 4.8 %collective-permute-start.9 = (bf16[128,128]{1,0:T(8,128)(2,1)S(1)}, bf16[128,128]{1,0:T(8,128)(2,1)S(1)}, u32[]{:S(2)}, u32[]{:S(2)}) collective-permute-start(bf16[128,128]{1,0:T(8,128)(2,1)S(1)} %get-tuple-element.37), channel_id=1, source_target_pairs={{0,8},{1,9},{2,10},{3,11},{4,12},{5,13},{6,14},{7,15},{8,0},{9,1},... | collective-permute-start | bytes 98312 | tf_op jit(solution)/shard_map/ppermute | solution.py:274
  25.7 1.6 %collective-permute-start.11 = (bf16[4,8,4096]{2,1,0:T(8,128)(2,1)S(1)}, bf16[4,8,4096]{2,1,0:T(8,128)(2,1)S(1)}, u32[]{:S(2)}, u32[]{:S(2)}) collective-permute-start(bf16[4,8,4096]{2,1,0:T(8,128)(2,1)S(1)} %collective-permute-done.2.refs_6_), channel_id=1, source_target_pairs={{0,1},{1,0},{2,3},{3,2},{4,5},{5,4},{6,7},{7,6},{8,9},{9,8},{10,11... | collective-permute-start | bytes 786440 | tf_op jit(solution)/shard_map/ppermute | solution.py:274

commit v12 on v11

--- a/solution.py
+++ b/solution.py
@@ -10,7 +10,7 @@
 SEQ = 64
 VMEM_BYTES = 32 * 1024 * 1024
 NEAR_PAD = 64
-LOADED_ROWS = 256
+LOADED_ROWS = 128
 CODE_SCALE = 2.0**-8
 LANES_BY_LANES = (((1,), (1,)), ((), ()))
 HBM_SPEC = pl.BlockSpec(memory_space=pltpu.HBM)
@@ -21,7 +21,7 @@
 def project_loaded_kernel(x_hbm, w_hbm, p_in_hbm, p_out_hbm, low_in_ref, low_out_ref, x_buf, w_buf, p_in, p_out, sems, p_sems):
     matrices = [
         pltpu.make_async_copy(p_in_hbm, p_in, p_sems.at[0]),
-        pltpu.make_async_copy(p_out_hbm, p_out, p_sems.at[1]),
+        pltpu.make_async_copy(p_out_hbm.at[:, pl.ds(0, p_out.shape[1])], p_out, p_sems.at[1]),
     ]
     chunks = []
     for hbm, buf, matrix, low_ref in ((x_hbm, x_buf, p_in, low_in_ref), (w_hbm, w_buf, p_out, low_out_ref)):
@@ -56,7 +56,7 @@
             pltpu.VMEM(inputs.shape, jnp.bfloat16),
             pltpu.VMEM((rows, tokens), jnp.bfloat16),
             pltpu.VMEM(proj_in_t.shape, jnp.bfloat16),
-            pltpu.VMEM(proj_out_t.shape, jnp.bfloat16),
+            pltpu.VMEM((rank, max(rows, 128)), jnp.bfloat16),
             pltpu.SemaphoreType.DMA((chunks,)),
             pltpu.SemaphoreType.DMA((2,)),
         ],
@@ -91,7 +91,7 @@
 def project(inputs, out_grads, proj_in_t, proj_out_t, devices):
     rank, width = proj_in_t.shape[0], inputs.shape[1] // devices
     units = out_grads.shape[0]
-    rows = 2 * LOADED_ROWS if units % LOADED_ROWS == 0 else 16
+    rows = LOADED_ROWS if units % LOADED_ROWS == 0 else 16
     lows = project_loaded(inputs, out_grads, proj_in_t, proj_out_t, rows)
     low = jax.ShapeDtypeStruct((devices // 4, 2 * rank, width), jnp.float32)
     half = jax.ShapeDtypeStruct((devices // 8, 2 * rank, width), jnp.float32)

time: 28.2 us -> 28.2 us (level)
  Pallas kernels: 5.83 us -> 5.37 us
  waiting for transfers between devices: 9.07 us -> 9.49 us
    pallas_call x1, Pallas kernels: 2.98 us -> 2.22 us  [project_loaded(): pl.pallas_call(project_loaded_kernel, out_shape=[jax.ShapeDtypeStruct((ra...]
    ppermute x12, waiting for transfers between devices: 9.07 us -> 9.49 us  [swap(): lax.ppermute(array, 'ex', [(i, i ^ distance) for i in range(devices)])]
    pallas_call x1, Pallas kernels: 1.13 us -> 1.43 us  [project(): pl.pallas_call(functools.partial(project_kernel, rows), out_shape=[half]...]
  transfers between devices with their start and end apart: 12 -> 12, of which waited for: 5 -> 5; matrix products, arithmetic and copies ran while one was open for 0% -> 0% of each run, Pallas kernels for 18% -> 16%
where the time goes in v12:
time: 28.2 us; the launch traced here: 28 us
  starting transfers between devices  13.1 us (46%)
  waiting for transfers between devices  9.49 us (34%)
  Pallas kernels  5.37 us (19%)
    ppermute x12, starting transfers between devices, swap(): lax.ppermute(array, 'ex', [(i, i ^ distance) for i in range(devices)])  13.1 us
    ppermute x12, waiting for transfers between devices, swap(): lax.ppermute(array, 'ex', [(i, i ^ distance) for i in range(devices)])  9.49 us
    pallas_call x1, Pallas kernels, project_loaded(): pl.pallas_call(project_loaded_kernel, out_shape=[jax.ShapeDtypeStruct((ra...  2.22 us
    pallas_call x1, Pallas kernels, project(): pl.pallas_call(functools.partial(project_kernel, rows), out_shape=[half]...  1.43 us
    pallas_call x1, Pallas kernels, last_scores(): pl.pallas_call(functools.partial(last_score_kernel, chips), out_shape=jax...  0.81 us
    pallas_call x1, Pallas kernels, first_scores(): pl.pallas_call(functools.partial(first_score_kernel, len(parts), held), o...  0.64 us
  transfers between devices with their start and end apart: 12, of which 5 were waited for; matrix products, arithmetic and copies ran while one was open for 0% of the time, Pallas kernels for 16%

profile of v12, /device:TPU:0, one launch (start us, length us, event | category | flops | bytes accessed | tf_op | source)
XLA Modules:
  0.0 28.0 jit_solution(9983709133214936578)
XLA Ops:
  0.0 0.0 copy-start.1
  0.0 0.0 copy-start
  0.0 4.0 %collective-permute-start = (bf16[1,8,4096]{2,1,0:T(8,128)(2,1)}, bf16[1,8,4096]{2,1,0:T(8,128)(2,1)S(1)}, u32[]{:S(2)}, u32[]{:S(2)}) collective-permute-start(bf16[1,8,4096]{2,1,0:T(8,128)(2,1)} %bitcast.5), channel_id=1, source_target_pairs={{0,8},{1,9},{2,10},{3,11},{4,12},{5,13},{6,14},{7,15},{8,0},{9,1},... | collective-permute-start | bytes 196616 | tf_op jit(solution)/shard_map/ppermute | solution.py:274
  4.0 0.0 copy-start.2
  4.0 2.2 %shard_map.57 = (f32[64,2048]{1,0:T(8,128)S(1)}, f32[64,2048]{1,0:T(8,128)S(1)}) custom-call(bf16[512,2048]{1,0:T(8,128)(2,1)} %x_hbm.1, bf16[1792,2048]{1,0:T(8,128)(2,1)} %w_ref.1, bf16[64,512]{1,0:T(8,128)(2,1)} %bitcast.7, bf16[64,1792]{1,0:T(8,128)(2,1)} %bitcast.3), custom_call_target="tpu_custom_call" | custom-call | flops 167772160 | bytes 2621440 | tf_op jit(solution)/shard_map/pallas_call | solution.py:50
  6.3 0.0 copy-done.1
  6.3 0.0 copy-done
  6.3 1.4 %shard_map.58 = (f32[2,128,128]{2,1,0:T(8,128)S(1)}, f32[2,128,128]{2,1,0:T(8,128)S(1)}, f32[4,128,128]{2,1,0:T(8,128)S(1)}, f32[4,128,128]{2,1,0:T(8,128)S(1)}, f32[4,128,128]{2,1,0:T(8,128)S(1)}) custom-call(f32[64,2048]{1,0:T(8,128)S(1)} %get-tuple-element.26.low_in_ref, f32[64,2048]{1,0:T(8,128)S(1)} %get-tuple-element.27.low_out_ref, ...), custom_call_target="tpu_custom_call" | custom-call | flops 469762048 | bytes 7340032 | tf_op jit(solution)/shard_map/pallas_call | solution.py:98
  7.7 0.1 collective-permute-start.4
  7.8 0.5 %collective-permute-start.5 = (f32[2,128,128]{2,1,0:T(8,128)S(1)}, f32[2,128,128]{2,1,0:T(8,128)S(1)}, u32[]{:S(2)}, u32[]{:S(2)}) collective-permute-start(f32[2,128,128]{2,1,0:T(8,128)S(1)} %get-tuple-element.31), channel_id=1, source_target_pairs={{0,1},{1,0},{2,3},{3,2},{4,5},{5,4},{6,7},{7,6},{8,9},{9,8},{10,11... | collective-permute-start | bytes 393224 | tf_op jit(solution)/shard_map/ppermute | solution.py:274
  8.3 0.0 collective-permute-done.right_ref
  8.3 0.0 copy-done.2
  8.3 1.6 %collective-permute-start.1 = (bf16[2,8,4096]{2,1,0:T(8,128)(2,1)S(1)}, bf16[2,8,4096]{2,1,0:T(8,128)(2,1)S(1)}, u32[]{:S(2)}, u32[]{:S(2)}) collective-permute-start(bf16[2,8,4096]{2,1,0:T(8,128)(2,1)S(1)} %shard_map.55.left_ref), channel_id=1, source_target_pairs={{0,4},{1,5},{2,6},{3,7},{4,0},{5,1},{6,2},{7,3},{8,12},{9,13},{10,... | collective-permute-start | bytes 393224 | tf_op jit(solution)/shard_map/ppermute | solution.py:274
  10.0 0.0 collective-permute-start.7
  10.0 0.0 collective-permute-done.4.refs_0_
  10.0 0.0 collective-permute-done.5.refs_1_
  10.0 0.1 shard_map.59
  10.1 1.6 %collective-permute-start.6 = (bf16[4,160,128]{2,1,0:T(8,128)(2,1)S(1)}, bf16[4,160,128]{2,1,0:T(8,128)(2,1)S(1)}, u32[]{:S(2)}, u32[]{:S(2)}) collective-permute-start(bf16[4,160,128]{2,1,0:T(8,128)(2,1)S(1)} %shard_map.59), channel_id=1, source_target_pairs={{0,2},{1,3},{2,0},{3,1},{4,6},{5,7},{6,4},{7,5},{8,10},{9,11},{10,... | collective-permute-start | bytes 491528 | tf_op jit(solution)/shard_map/ppermute | solution.py:274
  11.7 2.2 %collective-permute-done.1.right_ref = bf16[2,8,4096]{2,1,0:T(8,128)(2,1)S(1)} collective-permute-done((bf16[2,8,4096]{2,1,0:T(8,128)(2,1)S(1)}, bf16[2,8,4096]{2,1,0:T(8,128)(2,1)S(1)}, u32[]{:S(2)}, u32[]{:S(2)}) %collective-permute-start.1) | collective-permute-done | bytes 131104 | tf_op jit(solution)/shard_map/ppermute | solution.py:274
  13.9 1.6 %collective-permute-start.2 = (bf16[4,8,4096]{2,1,0:T(8,128)(2,1)S(1)}, bf16[4,8,4096]{2,1,0:T(8,128)(2,1)S(1)}, u32[]{:S(2)}, u32[]{:S(2)}) collective-permute-start(bf16[4,8,4096]{2,1,0:T(8,128)(2,1)S(1)} %shard_map.56.refs_4_), channel_id=1, source_target_pairs={{0,2},{1,3},{2,0},{3,1},{4,6},{5,7},{6,4},{7,5},{8,10},{9,11},{10,... | collective-permute-start | bytes 786440 | tf_op jit(solution)/shard_map/ppermute | solution.py:274
  15.5 0.0 collective-permute-start.3
  15.5 0.0 collective-permute-done.7.came_ref
  15.5 1.7 %collective-permute-done.6.across_ref = bf16[4,160,128]{2,1,0:T(8,128)(2,1)S(1)} collective-permute-done((bf16[4,160,128]{2,1,0:T(8,128)(2,1)S(1)}, bf16[4,160,128]{2,1,0:T(8,128)(2,1)S(1)}, u32[]{:S(2)}, u32[]{:S(2)}) %collective-permute-start.6) | collective-permute-done | bytes 163872 | tf_op jit(solution)/shard_map/ppermute | solution.py:274
  17.2 0.1 shard_map.60
  17.3 0.5 %collective-permute-start.8 = (f32[192,128]{1,0:T(8,128)S(1)}, f32[192,128]{1,0:T(8,128)S(1)}, u32[]{:S(2)}, u32[]{:S(2)}) collective-permute-start(f32[192,128]{1,0:T(8,128)S(1)} %get-tuple-element.36), channel_id=1, source_target_pairs={{0,4},{1,5},{2,6},{3,7},{4,0},{5,1},{6,2},{7,3},{8,12},{9,13},{10,... | collective-permute-start | bytes 294920 | tf_op jit(solution)/shard_map/ppermute | solution.py:274
  17.8 3.0 %collective-permute-start.10 = (bf16[128,128]{1,0:T(8,128)(2,1)S(1)}, bf16[128,128]{1,0:T(8,128)(2,1)S(1)}, u32[]{:S(2)}, u32[]{:S(2)}) collective-permute-start(bf16[128,128]{1,0:T(8,128)(2,1)S(1)} %get-tuple-element.38), channel_id=1, source_target_pairs={{0,12},{1,13},{2,14},{3,15},{4,8},{5,9},{6,10},{7,11},{8,4},{9,5},... | collective-permute-start | bytes 98312 | tf_op jit(solution)/shard_map/ppermute | solution.py:274
  20.8 0.1 collective-permute-start.9
  20.8 3.2 %collective-permute-done.10.refs_3_ = bf16[128,128]{1,0:T(8,128)(2,1)S(1)} collective-permute-done((bf16[128,128]{1,0:T(8,128)(2,1)S(1)}, bf16[128,128]{1,0:T(8,128)(2,1)S(1)}, u32[]{:S(2)}, u32[]{:S(2)}) %collective-permute-start.10) | collective-permute-done | bytes 32800 | tf_op jit(solution)/shard_map/ppermute | solution.py:274
  24.1 1.5 %collective-permute-done.9.refs_2_ = bf16[128,128]{1,0:T(8,128)(2,1)S(1)} collective-permute-done((bf16[128,128]{1,0:T(8,128)(2,1)S(1)}, bf16[128,128]{1,0:T(8,128)(2,1)S(1)}, u32[]{:S(2)}, u32[]{:S(2)}) %collective-permute-start.9) | collective-permute-done | bytes 32800 | tf_op jit(solution)/shard_map/ppermute | solution.py:274
  25.6 0.0 collective-permute-done.8.refs_1_
  25.6 0.0 collective-permute-done.2.refs_6_
  25.6 0.0 collective-permute-done.3.refs_5_
  25.6 0.1 collective-permute-start.11
  25.7 0.6 %shard_map.61 = (f32[2,32,128]{2,1,0:T(8,128)S(1)}, f32[2,8,2,8,128]{4,3,2,1,0:T(8,128)S(1)}) custom-call(f32[128,128]{1,0:T(8,128)S(1)} %get-tuple-element.39.refs_0_, f32[192,128]{1,0:T(8,128)S(1)} %collective-permute-done.8.refs_1_, bf16[128,128]{1,0:T(8,128)(2,1)S(1)} %collective-permute-done.9.refs_2_, ...), custom_call_target="tpu_custom_call" | custom-call | tf_op jit(solution)/shard_map/pallas_call | solution.py:244
  26.3 0.9 %collective-permute-done.11.queries_ref = bf16[4,8,4096]{2,1,0:T(8,128)(2,1)S(1)} collective-permute-done((bf16[4,8,4096]{2,1,0:T(8,128)(2,1)S(1)}, bf16[4,8,4096]{2,1,0:T(8,128)(2,1)S(1)}, u32[]{:S(2)}, u32[]{:S(2)}) %collective-permute-start.11) | collective-permute-done | bytes 262176 | tf_op jit(solution)/shard_map/ppermute | solution.py:274
  27.2 0.8 %shard_map.62 = f32[2,128]{1,0:T(2,128)} custom-call(f32[2,32,128]{2,1,0:T(8,128)S(1)} %get-tuple-element.45.grads_ref, f32[2,8,2,8,128]{4,3,2,1,0:T(8,128)S(1)} %get-tuple-element.46.before_ref, bf16[4,8,4096]{2,1,0:T(8,128)(2,1)S(1)} %collective-permute-done.11.queries_ref), custom_call_target="tpu_custom_call" | custom-call | tf_op jit(solution)/shard_map/pallas_call | solution.py:257
  (2 shorter events, 0.0 us)
Async XLA Ops:
  0.0 6.3 %copy-start.1 = (bf16[1792,64]{0,1:T(8,128)(2,1)S(1)}, bf16[1792,64]{0,1:T(8,128)(2,1)}, u32[]{:S(2)}) copy-start(bf16[1792,64]{0,1:T(8,128)(2,1)} %param.8) | copy-start | bytes 688132
  0.0 6.3 %copy-start = (bf16[1792,2048]{1,0:T(8,128)(2,1)S(1)}, bf16[1792,2048]{1,0:T(8,128)(2,1)}, u32[]{:S(2)}) copy-start(bf16[1792,2048]{1,0:T(8,128)(2,1)} %w_ref.1) | copy-start | bytes 22020100
  0.0 8.3 %collective-permute-start = (bf16[1,8,4096]{2,1,0:T(8,128)(2,1)}, bf16[1,8,4096]{2,1,0:T(8,128)(2,1)S(1)}, u32[]{:S(2)}, u32[]{:S(2)}) collective-permute-start(bf16[1,8,4096]{2,1,0:T(8,128)(2,1)} %bitcast.5), channel_id=1, source_target_pairs={{0,8},{1,9},{2,10},{3,11},{4,12},{5,13},{6,14},{7,15},{8,0},{9,1},... | collective-permute-start | bytes 196616 | tf_op jit(solution)/shard_map/ppermute | solution.py:274
  4.0 4.3 %copy-start.2 = (bf16[8,4096]{1,0:T(8,128)(2,1)S(1)}, bf16[8,4096]{1,0:T(8,128)(2,1)}, u32[]{:S(2)}) copy-start(bf16[8,4096]{1,0:T(8,128)(2,1)} %param.9) | copy-start | bytes 196612
  7.7 2.2 %collective-permute-start.4 = (f32[2,128,128]{2,1,0:T(8,128)S(1)}, f32[2,128,128]{2,1,0:T(8,128)S(1)}, u32[]{:S(2)}, u32[]{:S(2)}) collective-permute-start(f32[2,128,128]{2,1,0:T(8,128)S(1)} %get-tuple-element.30), channel_id=1, source_target_pairs={{0,1},{1,0},{2,3},{3,2},{4,5},{5,4},{6,7},{7,6},{8,9},{9,8},{10,11... | collective-permute-start | bytes 393224 | tf_op jit(solution)/shard_map/ppermute | solution.py:274
  7.8 2.2 %collective-permute-start.5 = (f32[2,128,128]{2,1,0:T(8,128)S(1)}, f32[2,128,128]{2,1,0:T(8,128)S(1)}, u32[]{:S(2)}, u32[]{:S(2)}) collective-permute-start(f32[2,128,128]{2,1,0:T(8,128)S(1)} %get-tuple-element.31), channel_id=1, source_target_pairs={{0,1},{1,0},{2,3},{3,2},{4,5},{5,4},{6,7},{7,6},{8,9},{9,8},{10,11... | collective-permute-start | bytes 393224 | tf_op jit(solution)/shard_map/ppermute | solution.py:274
  8.3 5.5 %collective-permute-start.1 = (bf16[2,8,4096]{2,1,0:T(8,128)(2,1)S(1)}, bf16[2,8,4096]{2,1,0:T(8,128)(2,1)S(1)}, u32[]{:S(2)}, u32[]{:S(2)}) collective-permute-start(bf16[2,8,4096]{2,1,0:T(8,128)(2,1)S(1)} %shard_map.55.left_ref), channel_id=1, source_target_pairs={{0,4},{1,5},{2,6},{3,7},{4,0},{5,1},{6,2},{7,3},{8,12},{9,13},{10,... | collective-permute-start | bytes 393224 | tf_op jit(solution)/shard_map/ppermute | solution.py:274
  10.0 5.5 %collective-permute-start.7 = (f32[4,128,128]{2,1,0:T(8,128)S(1)}, f32[4,128,128]{2,1,0:T(8,128)S(1)}, u32[]{:S(2)}, u32[]{:S(2)}) collective-permute-start(f32[4,128,128]{2,1,0:T(8,128)S(1)} %get-tuple-element.32), channel_id=1, source_target_pairs={{0,1},{1,0},{2,3},{3,2},{4,5},{5,4},{6,7},{7,6},{8,9},{9,8},{10,11... | collective-permute-start | bytes 786440 | tf_op jit(solution)/shard_map/ppermute | solution.py:274
  10.1 7.1 %collective-permute-start.6 = (bf16[4,160,128]{2,1,0:T(8,128)(2,1)S(1)}, bf16[4,160,128]{2,1,0:T(8,128)(2,1)S(1)}, u32[]{:S(2)}, u32[]{:S(2)}) collective-permute-start(bf16[4,160,128]{2,1,0:T(8,128)(2,1)S(1)} %shard_map.59), channel_id=1, source_target_pairs={{0,2},{1,3},{2,0},{3,1},{4,6},{5,7},{6,4},{7,5},{8,10},{9,11},{10,... | collective-permute-start | bytes 491528 | tf_op jit(solution)/shard_map/ppermute | solution.py:274
  13.9 11.7 %collective-permute-start.2 = (bf16[4,8,4096]{2,1,0:T(8,128)(2,1)S(1)}, bf16[4,8,4096]{2,1,0:T(8,128)(2,1)S(1)}, u32[]{:S(2)}, u32[]{:S(2)}) collective-permute-start(bf16[4,8,4096]{2,1,0:T(8,128)(2,1)S(1)} %shard_map.56.refs_4_), channel_id=1, source_target_pairs={{0,2},{1,3},{2,0},{3,1},{4,6},{5,7},{6,4},{7,5},{8,10},{9,11},{10,... | collective-permute-start | bytes 786440 | tf_op jit(solution)/shard_map/ppermute | solution.py:274
  15.5 10.1 %collective-permute-start.3 = (bf16[4,8,4096]{2,1,0:T(8,128)(2,1)S(1)}, bf16[4,8,4096]{2,1,0:T(8,128)(2,1)S(1)}, u32[]{:S(2)}, u32[]{:S(2)}) collective-permute-start(bf16[4,8,4096]{2,1,0:T(8,128)(2,1)S(1)} %shard_map.56.refs_4_), channel_id=1, source_target_pairs={{0,1},{1,0},{2,3},{3,2},{4,5},{5,4},{6,7},{7,6},{8,9},{9,8},{10,11... | collective-permute-start | bytes 786440 | tf_op jit(solution)/shard_map/ppermute | solution.py:274
  17.3 8.3 %collective-permute-start.8 = (f32[192,128]{1,0:T(8,128)S(1)}, f32[192,128]{1,0:T(8,128)S(1)}, u32[]{:S(2)}, u32[]{:S(2)}) collective-permute-start(f32[192,128]{1,0:T(8,128)S(1)} %get-tuple-element.36), channel_id=1, source_target_pairs={{0,4},{1,5},{2,6},{3,7},{4,0},{5,1},{6,2},{7,3},{8,12},{9,13},{10,... | collective-permute-start | bytes 294920 | tf_op jit(solution)/shard_map/ppermute | solution.py:274
  17.8 6.3 %collective-permute-start.10 = (bf16[128,128]{1,0:T(8,128)(2,1)S(1)}, bf16[128,128]{1,0:T(8,128)(2,1)S(1)}, u32[]{:S(2)}, u32[]{:S(2)}) collective-permute-start(bf16[128,128]{1,0:T(8,128)(2,1)S(1)} %get-tuple-element.38), channel_id=1, source_target_pairs={{0,12},{1,13},{2,14},{3,15},{4,8},{5,9},{6,10},{7,11},{8,4},{9,5},... | collective-permute-start | bytes 98312 | tf_op jit(solution)/shard_map/ppermute | solution.py:274
  20.8 4.8 %collective-permute-start.9 = (bf16[128,128]{1,0:T(8,128)(2,1)S(1)}, bf16[128,128]{1,0:T(8,128)(2,1)S(1)}, u32[]{:S(2)}, u32[]{:S(2)}) collective-permute-start(bf16[128,128]{1,0:T(8,128)(2,1)S(1)} %get-tuple-element.37), channel_id=1, source_target_pairs={{0,8},{1,9},{2,10},{3,11},{4,12},{5,13},{6,14},{7,15},{8,0},{9,1},... | collective-permute-start | bytes 98312 | tf_op jit(solution)/shard_map/ppermute | solution.py:274
  25.6 1.6 %collective-permute-start.11 = (bf16[4,8,4096]{2,1,0:T(8,128)(2,1)S(1)}, bf16[4,8,4096]{2,1,0:T(8,128)(2,1)S(1)}, u32[]{:S(2)}, u32[]{:S(2)}) collective-permute-start(bf16[4,8,4096]{2,1,0:T(8,128)(2,1)S(1)} %collective-permute-done.2.refs_6_), channel_id=1, source_target_pairs={{0,1},{1,0},{2,3},{3,2},{4,5},{5,4},{6,7},{7,6},{8,9},{9,8},{10,11... | collective-permute-start | bytes 786440 | tf_op jit(solution)/shard_map/ppermute | solution.py:274

commit v13 on v12

--- a/solution.py
+++ b/solution.py
@@ -9,9 +9,9 @@
 
 SEQ = 64
 VMEM_BYTES = 32 * 1024 * 1024
-NEAR_PAD = 64
+NEAR_PAD = 96
 LOADED_ROWS = 128
-CODE_SCALE = 2.0**-8
+LEFT_OVER = 0.36 * 2.0**-8
 LANES_BY_LANES = (((1,), (1,)), ((), ()))
 HBM_SPEC = pl.BlockSpec(memory_space=pltpu.HBM)
 VMEM_SPEC = pl.BlockSpec(memory_space=pltpu.VMEM)
@@ -70,12 +70,13 @@
 
 
 def project_kernel(done, low_in_ref, low_out_ref, p_ref, w_ref, *refs):
-    *given_y, given_here, kept_y, kept_here = refs
+    *given, kept_y, kept_here = refs
+    given_y, given_here = given[:-1], given[-1:]
     here = lax.axis_index("ex")
     core, chip = lax.rem(here, 2), lax.div(here, 2)
     depth = kept_y.shape[0]
     rank, width = kept_y.shape[1] // 2, kept_y.shape[2]
-    for flip, given_refs, kept_ref in ((1, given_y, kept_y), (0, [given_here], kept_here)):
+    for flip, given_refs, kept_ref in ((1, given_y, kept_y), (0, given_here, kept_here)):
         for z in range(depth):
             place = lax.bitwise_xor(chip, 2 * z + flip)
             columns = pl.ds(pl.multiple_of(place * 2 * width, 2 * width), 2 * width)
@@ -111,25 +112,23 @@
     rows = low.shape[0]
     rounded = low.astype(jnp.bfloat16)
     out_ref[:rows, :] = rounded
-    rounded = rounded.astype(jnp.float32)
-    left = (low - rounded) / jnp.maximum(jnp.abs(rounded) * CODE_SCALE, 1e-30)
-    level = jnp.clip(jnp.floor(2.0 * left) + 2.0, 0.0, 3.0)
-    part = rows // 4
-    word = level[:part, :]
-    for index in range(1, 4):
-        word = word + 4.0**index * level[index * part : (index + 1) * part, :]
+    above = jnp.where(low > rounded.astype(jnp.float32), 1.0, 0.0)
+    part = rows // 8
+    word = above[:part, :]
+    for index in range(1, 8):
+        word = word + 2.0**index * above[index * part : (index + 1) * part, :]
     out_ref[rows:, :] = word.astype(jnp.bfloat16)
 
 
 def add_coded(total, ref):
-    part = ref.shape[0] // 5
-    word = ref[4 * part :, :].astype(jnp.float32)
+    part = ref.shape[0] // 9
+    word = ref[8 * part :, :].astype(jnp.float32)
     parts = []
-    for index in reversed(range(4)):
-        level = jnp.floor(word * 0.25**index)
-        word = word - level * 4.0**index
+    for index in reversed(range(8)):
+        above = jnp.floor(word * 0.5**index)
+        word = word - above * 2.0**index
         rounded = ref[index * part : (index + 1) * part, :].astype(jnp.float32)
-        left = jnp.abs(rounded) * ((CODE_SCALE * 0.5) * level - CODE_SCALE * 0.75)
+        left = jnp.abs(rounded) * ((2.0 * LEFT_OVER) * above - LEFT_OVER)
         parts.append((slice(index * part, (index + 1) * part), total(index * part, part) + rounded + left))
     return parts
 
@@ -145,7 +144,7 @@
     blocks, rows, width = kept.shape
     return pl.pallas_call(
         add_given_kernel,
-        out_shape=jax.ShapeDtypeStruct((blocks, rows // 4 * 5, width), jnp.bfloat16),
+        out_shape=jax.ShapeDtypeStruct((blocks, rows // 8 * 9, width), jnp.bfloat16),
         compiler_params=PARAMS,
     )(kept, *came)
 

time: 28.2 us -> 27.7 us (0.982)
  waiting for transfers between devices: 9.49 us -> 9.14 us
    ppermute x12, waiting for transfers between devices: 9.49 us -> 9.14 us  [swap(): lax.ppermute(array, 'ex', [(i, i ^ distance) for i in range(devices)])]
where the time goes in v13:
time: 27.7 us; the launch traced here: 27.6 us
  starting transfers between devices  13.1 us (47%)
  waiting for transfers between devices  9.14 us (33%)
  Pallas kernels  5.31 us (19%)
    ppermute x12, starting transfers between devices, swap(): lax.ppermute(array, 'ex', [(i, i ^ distance) for i in range(devices)])  13.1 us
    ppermute x12, waiting for transfers between devices, swap(): lax.ppermute(array, 'ex', [(i, i ^ distance) for i in range(devices)])  9.14 us
    pallas_call x1, Pallas kernels, project_loaded(): pl.pallas_call(project_loaded_kernel, out_shape=[jax.ShapeDtypeStruct((ra...  2.22 us
    pallas_call x1, Pallas kernels, project(): pl.pallas_call(functools.partial(project_kernel, rows), out_shape=[half]...  1.43 us
    pallas_call x1, Pallas kernels, last_scores(): pl.pallas_call(functools.partial(last_score_kernel, chips), out_shape=jax...  0.81 us
    pallas_call x1, Pallas kernels, first_scores(): pl.pallas_call(functools.partial(first_score_kernel, len(parts), held), o...  0.64 us
  transfers between devices with their start and end apart: 12, of which 5 were waited for; matrix products, arithmetic and copies ran while one was open for 0% of the time, Pallas kernels for 16%

profile of v13, /device:TPU:0, one launch (start us, length us, event | category | flops | bytes accessed | tf_op | source)
XLA Modules:
  0.0 27.6 jit_solution(15639541656808474885)
XLA Ops:
  0.0 0.0 copy-start.1
  0.0 0.0 copy-start
  0.0 4.0 %collective-permute-start = (bf16[1,8,4096]{2,1,0:T(8,128)(2,1)}, bf16[1,8,4096]{2,1,0:T(8,128)(2,1)S(1)}, u32[]{:S(2)}, u32[]{:S(2)}) collective-permute-start(bf16[1,8,4096]{2,1,0:T(8,128)(2,1)} %bitcast.5), channel_id=1, source_target_pairs={{0,8},{1,9},{2,10},{3,11},{4,12},{5,13},{6,14},{7,15},{8,0},{9,1},... | collective-permute-start | bytes 196616 | tf_op jit(solution)/shard_map/ppermute | solution.py:273
  4.0 0.0 copy-start.2
  4.0 2.2 %shard_map.57 = (f32[64,2048]{1,0:T(8,128)S(1)}, f32[64,2048]{1,0:T(8,128)S(1)}) custom-call(bf16[512,2048]{1,0:T(8,128)(2,1)} %x_hbm.1, bf16[1792,2048]{1,0:T(8,128)(2,1)} %w_ref.1, bf16[64,512]{1,0:T(8,128)(2,1)} %bitcast.7, bf16[64,1792]{1,0:T(8,128)(2,1)} %bitcast.3), custom_call_target="tpu_custom_call" | custom-call | flops 167772160 | bytes 2621440 | tf_op jit(solution)/shard_map/pallas_call | solution.py:50
  6.3 0.0 copy-done.1
  6.3 0.0 copy-done
  6.3 1.4 %shard_map.58 = (f32[2,128,128]{2,1,0:T(8,128)S(1)}, f32[2,128,128]{2,1,0:T(8,128)S(1)}, f32[4,128,128]{2,1,0:T(8,128)S(1)}, f32[4,128,128]{2,1,0:T(8,128)S(1)}, f32[4,128,128]{2,1,0:T(8,128)S(1)}) custom-call(f32[64,2048]{1,0:T(8,128)S(1)} %get-tuple-element.26.low_in_ref, f32[64,2048]{1,0:T(8,128)S(1)} %get-tuple-element.27.low_out_ref, ...), custom_call_target="tpu_custom_call" | custom-call | flops 469762048 | bytes 7340032 | tf_op jit(solution)/shard_map/pallas_call | solution.py:99
  7.7 0.1 collective-permute-start.4
  7.8 0.5 %collective-permute-start.5 = (f32[2,128,128]{2,1,0:T(8,128)S(1)}, f32[2,128,128]{2,1,0:T(8,128)S(1)}, u32[]{:S(2)}, u32[]{:S(2)}) collective-permute-start(f32[2,128,128]{2,1,0:T(8,128)S(1)} %get-tuple-element.31), channel_id=1, source_target_pairs={{0,1},{1,0},{2,3},{3,2},{4,5},{5,4},{6,7},{7,6},{8,9},{9,8},{10,11... | collective-permute-start | bytes 393224 | tf_op jit(solution)/shard_map/ppermute | solution.py:273
  8.3 0.0 collective-permute-done.right_ref
  8.3 0.0 copy-done.2
  8.3 1.6 %collective-permute-start.1 = (bf16[2,8,4096]{2,1,0:T(8,128)(2,1)S(1)}, bf16[2,8,4096]{2,1,0:T(8,128)(2,1)S(1)}, u32[]{:S(2)}, u32[]{:S(2)}) collective-permute-start(bf16[2,8,4096]{2,1,0:T(8,128)(2,1)S(1)} %shard_map.55.left_ref), channel_id=1, source_target_pairs={{0,4},{1,5},{2,6},{3,7},{4,0},{5,1},{6,2},{7,3},{8,12},{9,13},{10,... | collective-permute-start | bytes 393224 | tf_op jit(solution)/shard_map/ppermute | solution.py:273
  10.0 0.0 collective-permute-start.7
  10.0 0.0 collective-permute-done.4.refs_0_
  10.0 0.0 collective-permute-done.5.refs_1_
  10.0 0.1 shard_map.59
  10.0 1.6 %collective-permute-start.6 = (bf16[4,144,128]{2,1,0:T(8,128)(2,1)S(1)}, bf16[4,144,128]{2,1,0:T(8,128)(2,1)S(1)}, u32[]{:S(2)}, u32[]{:S(2)}) collective-permute-start(bf16[4,144,128]{2,1,0:T(8,128)(2,1)S(1)} %shard_map.59), channel_id=1, source_target_pairs={{0,2},{1,3},{2,0},{3,1},{4,6},{5,7},{6,4},{7,5},{8,10},{9,11},{10,... | collective-permute-start | bytes 442376 | tf_op jit(solution)/shard_map/ppermute | solution.py:273
  11.6 2.2 %collective-permute-done.1.right_ref = bf16[2,8,4096]{2,1,0:T(8,128)(2,1)S(1)} collective-permute-done((bf16[2,8,4096]{2,1,0:T(8,128)(2,1)S(1)}, bf16[2,8,4096]{2,1,0:T(8,128)(2,1)S(1)}, u32[]{:S(2)}, u32[]{:S(2)}) %collective-permute-start.1) | collective-permute-done | bytes 131104 | tf_op jit(solution)/shard_map/ppermute | solution.py:273
  13.9 1.6 %collective-permute-start.2 = (bf16[4,8,4096]{2,1,0:T(8,128)(2,1)S(1)}, bf16[4,8,4096]{2,1,0:T(8,128)(2,1)S(1)}, u32[]{:S(2)}, u32[]{:S(2)}) collective-permute-start(bf16[4,8,4096]{2,1,0:T(8,128)(2,1)S(1)} %shard_map.56.refs_4_), channel_id=1, source_target_pairs={{0,2},{1,3},{2,0},{3,1},{4,6},{5,7},{6,4},{7,5},{8,10},{9,11},{10,... | collective-permute-start | bytes 786440 | tf_op jit(solution)/shard_map/ppermute | solution.py:273
  15.5 0.0 collective-permute-start.3
  15.5 0.0 collective-permute-done.7.came_ref
  15.5 1.2 %collective-permute-done.6.across_ref = bf16[4,144,128]{2,1,0:T(8,128)(2,1)S(1)} collective-permute-done((bf16[4,144,128]{2,1,0:T(8,128)(2,1)S(1)}, bf16[4,144,128]{2,1,0:T(8,128)(2,1)S(1)}, u32[]{:S(2)}, u32[]{:S(2)}) %collective-permute-start.6) | collective-permute-done | bytes 147488 | tf_op jit(solution)/shard_map/ppermute | solution.py:273
  16.8 0.1 shard_map.60
  16.9 0.4 %collective-permute-start.8 = (f32[224,128]{1,0:T(8,128)S(1)}, f32[224,128]{1,0:T(8,128)S(1)}, u32[]{:S(2)}, u32[]{:S(2)}) collective-permute-start(f32[224,128]{1,0:T(8,128)S(1)} %get-tuple-element.36), channel_id=1, source_target_pairs={{0,4},{1,5},{2,6},{3,7},{4,0},{5,1},{6,2},{7,3},{8,12},{9,13},{10,... | collective-permute-start | bytes 344072 | tf_op jit(solution)/shard_map/ppermute | solution.py:273
  17.3 3.1 %collective-permute-start.10 = (bf16[128,128]{1,0:T(8,128)(2,1)S(1)}, bf16[128,128]{1,0:T(8,128)(2,1)S(1)}, u32[]{:S(2)}, u32[]{:S(2)}) collective-permute-start(bf16[128,128]{1,0:T(8,128)(2,1)S(1)} %get-tuple-element.38), channel_id=1, source_target_pairs={{0,12},{1,13},{2,14},{3,15},{4,8},{5,9},{6,10},{7,11},{8,4},{9,5},... | collective-permute-start | bytes 98312 | tf_op jit(solution)/shard_map/ppermute | solution.py:273
  20.4 0.1 collective-permute-start.9
  20.4 3.7 %collective-permute-done.10.refs_3_ = bf16[128,128]{1,0:T(8,128)(2,1)S(1)} collective-permute-done((bf16[128,128]{1,0:T(8,128)(2,1)S(1)}, bf16[128,128]{1,0:T(8,128)(2,1)S(1)}, u32[]{:S(2)}, u32[]{:S(2)}) %collective-permute-start.10) | collective-permute-done | bytes 32800 | tf_op jit(solution)/shard_map/ppermute | solution.py:273
  24.2 1.0 %collective-permute-done.9.refs_2_ = bf16[128,128]{1,0:T(8,128)(2,1)S(1)} collective-permute-done((bf16[128,128]{1,0:T(8,128)(2,1)S(1)}, bf16[128,128]{1,0:T(8,128)(2,1)S(1)}, u32[]{:S(2)}, u32[]{:S(2)}) %collective-permute-start.9) | collective-permute-done | bytes 32800 | tf_op jit(solution)/shard_map/ppermute | solution.py:273
  25.2 0.0 collective-permute-done.8.refs_1_
  25.2 0.0 collective-permute-done.2.refs_6_
  25.2 0.0 collective-permute-done.3.refs_5_
  25.2 0.1 collective-permute-start.11
  25.3 0.6 %shard_map.61 = (f32[2,32,128]{2,1,0:T(8,128)S(1)}, f32[2,8,2,8,128]{4,3,2,1,0:T(8,128)S(1)}) custom-call(f32[128,128]{1,0:T(8,128)S(1)} %get-tuple-element.39.refs_0_, f32[224,128]{1,0:T(8,128)S(1)} %collective-permute-done.8.refs_1_, bf16[128,128]{1,0:T(8,128)(2,1)S(1)} %collective-permute-done.9.refs_2_, ...), custom_call_target="tpu_custom_call" | custom-call | tf_op jit(solution)/shard_map/pallas_call | solution.py:243
  25.9 0.9 %collective-permute-done.11.queries_ref = bf16[4,8,4096]{2,1,0:T(8,128)(2,1)S(1)} collective-permute-done((bf16[4,8,4096]{2,1,0:T(8,128)(2,1)S(1)}, bf16[4,8,4096]{2,1,0:T(8,128)(2,1)S(1)}, u32[]{:S(2)}, u32[]{:S(2)}) %collective-permute-start.11) | collective-permute-done | bytes 262176 | tf_op jit(solution)/shard_map/ppermute | solution.py:273
  26.8 0.8 %shard_map.62 = f32[2,128]{1,0:T(2,128)} custom-call(f32[2,32,128]{2,1,0:T(8,128)S(1)} %get-tuple-element.45.grads_ref, f32[2,8,2,8,128]{4,3,2,1,0:T(8,128)S(1)} %get-tuple-element.46.before_ref, bf16[4,8,4096]{2,1,0:T(8,128)(2,1)S(1)} %collective-permute-done.11.queries_ref), custom_call_target="tpu_custom_call" | custom-call | tf_op jit(solution)/shard_map/pallas_call | solution.py:256
  (2 shorter events, 0.0 us)
Async XLA Ops:
  0.0 6.3 %copy-start.1 = (bf16[1792,64]{0,1:T(8,128)(2,1)S(1)}, bf16[1792,64]{0,1:T(8,128)(2,1)}, u32[]{:S(2)}) copy-start(bf16[1792,64]{0,1:T(8,128)(2,1)} %param.8) | copy-start | bytes 688132
  0.0 6.3 %copy-start = (bf16[1792,2048]{1,0:T(8,128)(2,1)S(1)}, bf16[1792,2048]{1,0:T(8,128)(2,1)}, u32[]{:S(2)}) copy-start(bf16[1792,2048]{1,0:T(8,128)(2,1)} %w_ref.1) | copy-start | bytes 22020100
  0.0 8.3 %collective-permute-start = (bf16[1,8,4096]{2,1,0:T(8,128)(2,1)}, bf16[1,8,4096]{2,1,0:T(8,128)(2,1)S(1)}, u32[]{:S(2)}, u32[]{:S(2)}) collective-permute-start(bf16[1,8,4096]{2,1,0:T(8,128)(2,1)} %bitcast.5), channel_id=1, source_target_pairs={{0,8},{1,9},{2,10},{3,11},{4,12},{5,13},{6,14},{7,15},{8,0},{9,1},... | collective-permute-start | bytes 196616 | tf_op jit(solution)/shard_map/ppermute | solution.py:273
  4.0 4.3 %copy-start.2 = (bf16[8,4096]{1,0:T(8,128)(2,1)S(1)}, bf16[8,4096]{1,0:T(8,128)(2,1)}, u32[]{:S(2)}) copy-start(bf16[8,4096]{1,0:T(8,128)(2,1)} %param.9) | copy-start | bytes 196612
  7.7 2.2 %collective-permute-start.4 = (f32[2,128,128]{2,1,0:T(8,128)S(1)}, f32[2,128,128]{2,1,0:T(8,128)S(1)}, u32[]{:S(2)}, u32[]{:S(2)}) collective-permute-start(f32[2,128,128]{2,1,0:T(8,128)S(1)} %get-tuple-element.30), channel_id=1, source_target_pairs={{0,1},{1,0},{2,3},{3,2},{4,5},{5,4},{6,7},{7,6},{8,9},{9,8},{10,11... | collective-permute-start | bytes 393224 | tf_op jit(solution)/shard_map/ppermute | solution.py:273
  7.8 2.2 %collective-permute-start.5 = (f32[2,128,128]{2,1,0:T(8,128)S(1)}, f32[2,128,128]{2,1,0:T(8,128)S(1)}, u32[]{:S(2)}, u32[]{:S(2)}) collective-permute-start(f32[2,128,128]{2,1,0:T(8,128)S(1)} %get-tuple-element.31), channel_id=1, source_target_pairs={{0,1},{1,0},{2,3},{3,2},{4,5},{5,4},{6,7},{7,6},{8,9},{9,8},{10,11... | collective-permute-start | bytes 393224 | tf_op jit(solution)/shard_map/ppermute | solution.py:273
  8.3 5.5 %collective-permute-start.1 = (bf16[2,8,4096]{2,1,0:T(8,128)(2,1)S(1)}, bf16[2,8,4096]{2,1,0:T(8,128)(2,1)S(1)}, u32[]{:S(2)}, u32[]{:S(2)}) collective-permute-start(bf16[2,8,4096]{2,1,0:T(8,128)(2,1)S(1)} %shard_map.55.left_ref), channel_id=1, source_target_pairs={{0,4},{1,5},{2,6},{3,7},{4,0},{5,1},{6,2},{7,3},{8,12},{9,13},{10,... | collective-permute-start | bytes 393224 | tf_op jit(solution)/shard_map/ppermute | solution.py:273
  10.0 5.5 %collective-permute-start.7 = (f32[4,128,128]{2,1,0:T(8,128)S(1)}, f32[4,128,128]{2,1,0:T(8,128)S(1)}, u32[]{:S(2)}, u32[]{:S(2)}) collective-permute-start(f32[4,128,128]{2,1,0:T(8,128)S(1)} %get-tuple-element.32), channel_id=1, source_target_pairs={{0,1},{1,0},{2,3},{3,2},{4,5},{5,4},{6,7},{7,6},{8,9},{9,8},{10,11... | collective-permute-start | bytes 786440 | tf_op jit(solution)/shard_map/ppermute | solution.py:273
  10.0 6.7 %collective-permute-start.6 = (bf16[4,144,128]{2,1,0:T(8,128)(2,1)S(1)}, bf16[4,144,128]{2,1,0:T(8,128)(2,1)S(1)}, u32[]{:S(2)}, u32[]{:S(2)}) collective-permute-start(bf16[4,144,128]{2,1,0:T(8,128)(2,1)S(1)} %shard_map.59), channel_id=1, source_target_pairs={{0,2},{1,3},{2,0},{3,1},{4,6},{5,7},{6,4},{7,5},{8,10},{9,11},{10,... | collective-permute-start | bytes 442376 | tf_op jit(solution)/shard_map/ppermute | solution.py:273
  13.9 11.3 %collective-permute-start.2 = (bf16[4,8,4096]{2,1,0:T(8,128)(2,1)S(1)}, bf16[4,8,4096]{2,1,0:T(8,128)(2,1)S(1)}, u32[]{:S(2)}, u32[]{:S(2)}) collective-permute-start(bf16[4,8,4096]{2,1,0:T(8,128)(2,1)S(1)} %shard_map.56.refs_4_), channel_id=1, source_target_pairs={{0,2},{1,3},{2,0},{3,1},{4,6},{5,7},{6,4},{7,5},{8,10},{9,11},{10,... | collective-permute-start | bytes 786440 | tf_op jit(solution)/shard_map/ppermute | solution.py:273
  15.5 9.7 %collective-permute-start.3 = (bf16[4,8,4096]{2,1,0:T(8,128)(2,1)S(1)}, bf16[4,8,4096]{2,1,0:T(8,128)(2,1)S(1)}, u32[]{:S(2)}, u32[]{:S(2)}) collective-permute-start(bf16[4,8,4096]{2,1,0:T(8,128)(2,1)S(1)} %shard_map.56.refs_4_), channel_id=1, source_target_pairs={{0,1},{1,0},{2,3},{3,2},{4,5},{5,4},{6,7},{7,6},{8,9},{9,8},{10,11... | collective-permute-start | bytes 786440 | tf_op jit(solution)/shard_map/ppermute | solution.py:273
  16.9 8.3 %collective-permute-start.8 = (f32[224,128]{1,0:T(8,128)S(1)}, f32[224,128]{1,0:T(8,128)S(1)}, u32[]{:S(2)}, u32[]{:S(2)}) collective-permute-start(f32[224,128]{1,0:T(8,128)S(1)} %get-tuple-element.36), channel_id=1, source_target_pairs={{0,4},{1,5},{2,6},{3,7},{4,0},{5,1},{6,2},{7,3},{8,12},{9,13},{10,... | collective-permute-start | bytes 344072 | tf_op jit(solution)/shard_map/ppermute | solution.py:273
  17.3 6.9 %collective-permute-start.10 = (bf16[128,128]{1,0:T(8,128)(2,1)S(1)}, bf16[128,128]{1,0:T(8,128)(2,1)S(1)}, u32[]{:S(2)}, u32[]{:S(2)}) collective-permute-start(bf16[128,128]{1,0:T(8,128)(2,1)S(1)} %get-tuple-element.38), channel_id=1, source_target_pairs={{0,12},{1,13},{2,14},{3,15},{4,8},{5,9},{6,10},{7,11},{8,4},{9,5},... | collective-permute-start | bytes 98312 | tf_op jit(solution)/shard_map/ppermute | solution.py:273
  20.4 4.8 %collective-permute-start.9 = (bf16[128,128]{1,0:T(8,128)(2,1)S(1)}, bf16[128,128]{1,0:T(8,128)(2,1)S(1)}, u32[]{:S(2)}, u32[]{:S(2)}) collective-permute-start(bf16[128,128]{1,0:T(8,128)(2,1)S(1)} %get-tuple-element.37), channel_id=1, source_target_pairs={{0,8},{1,9},{2,10},{3,11},{4,12},{5,13},{6,14},{7,15},{8,0},{9,1},... | collective-permute-start | bytes 98312 | tf_op jit(solution)/shard_map/ppermute | solution.py:273
  25.2 1.6 %collective-permute-start.11 = (bf16[4,8,4096]{2,1,0:T(8,128)(2,1)S(1)}, bf16[4,8,4096]{2,1,0:T(8,128)(2,1)S(1)}, u32[]{:S(2)}, u32[]{:S(2)}) collective-permute-start(bf16[4,8,4096]{2,1,0:T(8,128)(2,1)S(1)} %collective-permute-done.2.refs_6_), channel_id=1, source_target_pairs={{0,1},{1,0},{2,3},{3,2},{4,5},{5,4},{6,7},{7,6},{8,9},{9,8},{10,11... | collective-permute-start | bytes 786440 | tf_op jit(solution)/shard_map/ppermute | solution.py:273

commit v14 on v13

--- a/solution.py
+++ b/solution.py
@@ -9,7 +9,6 @@
 
 SEQ = 64
 VMEM_BYTES = 32 * 1024 * 1024
-NEAR_PAD = 96
 LOADED_ROWS = 128
 LEFT_OVER = 0.36 * 2.0**-8
 LANES_BY_LANES = (((1,), (1,)), ((), ()))
@@ -159,11 +158,9 @@
 
 
 def add_kept(kept, came, across, types):
-    _, rows, width = kept.shape
-    heights = [rows if z == 0 or dtype == jnp.bfloat16 else rows + NEAR_PAD for z, dtype in enumerate(types)]
     return pl.pallas_call(
         add_kept_kernel,
-        out_shape=[jax.ShapeDtypeStruct((height, width), dtype) for height, dtype in zip(heights, types)],
+        out_shape=[jax.ShapeDtypeStruct(kept.shape[1:], dtype) for dtype in types],
         compiler_params=PARAMS,
     )(kept, came, across)
 
@@ -206,7 +203,7 @@
     core = lax.rem(lax.axis_index("ex"), 2)
     total = part_refs[0][...]
     for part_ref in part_refs[1:]:
-        total = total + part_ref[: 2 * rank, :].astype(jnp.float32)
+        total = total + part_ref[...].astype(jnp.float32)
     out_t_ref[...] = total[rank:, :]
     even = out_t_ref[pl.ds(0, rank // 2, stride=2), :]
     odd = out_t_ref[pl.ds(1, rank // 2, stride=2), :]
@@ -283,20 +280,25 @@
         held, reach = stack(held, came_held), reach + [chip ^ last for chip in reach]
         came_held = swap(held, chip=step)
     across = swap(add_given(kept_y, came_y), chip=1)
-    held, reach = stack(held, came_held), reach + [chip ^ steps[-2] for chip in reach]
+    early, early_reach = held, reach
+    late, late_reach = came_held, [chip ^ steps[-2] for chip in reach]
+    held, reach = stack(early, late), early_reach + late_reach
     came_held = swap(held, chip=1)
-    other_held = swap(held, core=1)
-    across, came = together((across, came))
+    other_early = swap(early, core=1)
+    across, came, other_early = together((across, came, other_early))
 
     types = [jnp.float32 if z < depth // 2 else jnp.bfloat16 for z in range(depth)]
     parts = list(add_kept(kept, came, across, types))
+    late, parts = together((late, parts))
+    other_late = swap(late, core=1)
     for z in list(range(depth // 2, depth)) + list(range(1, depth // 2)):
         parts[z] = swap(parts[z], chip=2 * z)
-    came_held, other_held, parts = together((came_held, other_held, parts))
+    came_held, other_late, parts = together((came_held, other_late, parts))
     other_came = swap(came_held, core=1)
     reach_y = [chip ^ 1 for chip in reach]
-    held = [held, other_held, came_held]
-    grads, scores = first_scores(parts, held, [(0, reach), (1, reach), (0, reach_y)], rank)
+    queries = [held, other_early, other_late, came_held]
+    reaches = [(0, reach), (1, early_reach), (1, late_reach), (0, reach_y)]
+    grads, scores = first_scores(parts, queries, reaches, rank)
     return last_scores(grads, scores, other_came, reach_y)
 
 

time: 27.7 us -> 27.8 us (level)
  starting transfers between devices: 13.1 us -> 14.1 us
  waiting for transfers between devices: 9.14 us -> 8.17 us
    ppermute x12 -> x13, starting transfers between devices: 13.1 us -> 14.1 us  [swap(): lax.ppermute(array, 'ex', [(i, i ^ distance) for i in range(devices)])]
    ppermute x12 -> x13, waiting for transfers between devices: 9.14 us -> 8.17 us  [swap(): lax.ppermute(array, 'ex', [(i, i ^ distance) for i in range(devices)])]
  transfers between devices with their start and end apart: 12 -> 13, of which waited for: 5 -> 5; matrix products, arithmetic and copies ran while one was open for 0% -> 0% of each run, Pallas kernels for 16% -> 16%
where the time goes in v14:
time: 27.8 us; the launch traced here: 27.7 us
  starting transfers between devices  14.1 us (51%)
  waiting for transfers between devices  8.17 us (29%)
  Pallas kernels  5.31 us (19%)
    ppermute x13, starting transfers between devices, swap(): lax.ppermute(array, 'ex', [(i, i ^ distance) for i in range(devices)])  14.1 us
    ppermute x13, waiting for transfers between devices, swap(): lax.ppermute(array, 'ex', [(i, i ^ distance) for i in range(devices)])  8.17 us
    pallas_call x1, Pallas kernels, project_loaded(): pl.pallas_call(project_loaded_kernel, out_shape=[jax.ShapeDtypeStruct((ra...  2.22 us
    pallas_call x1, Pallas kernels, project(): pl.pallas_call(functools.partial(project_kernel, rows), out_shape=[half]...  1.43 us
    pallas_call x1, Pallas kernels, last_scores(): pl.pallas_call(functools.partial(last_score_kernel, chips), out_shape=jax...  0.81 us
    pallas_call x1, Pallas kernels, first_scores(): pl.pallas_call(functools.partial(first_score_kernel, len(parts), held), o...  0.64 us
  transfers between devices with their start and end apart: 13, of which 5 were waited for; matrix products, arithmetic and copies ran while one was open for 0% of the time, Pallas kernels for 16%

profile of v14, /device:TPU:0, one launch (start us, length us, event | category | flops | bytes accessed | tf_op | source)
XLA Modules:
  0.0 27.7 jit_solution(15204815690153271102)
XLA Ops:
  0.0 0.0 copy-start.1
  0.0 0.0 copy-start
  0.0 4.0 %collective-permute-start = (bf16[1,8,4096]{2,1,0:T(8,128)(2,1)}, bf16[1,8,4096]{2,1,0:T(8,128)(2,1)S(1)}, u32[]{:S(2)}, u32[]{:S(2)}) collective-permute-start(bf16[1,8,4096]{2,1,0:T(8,128)(2,1)} %bitcast.5), channel_id=1, source_target_pairs={{0,8},{1,9},{2,10},{3,11},{4,12},{5,13},{6,14},{7,15},{8,0},{9,1},... | collective-permute-start | bytes 196616 | tf_op jit(solution)/shard_map/ppermute | solution.py:270
  4.0 0.0 copy-start.2
  4.0 2.2 %shard_map.57 = (f32[64,2048]{1,0:T(8,128)S(1)}, f32[64,2048]{1,0:T(8,128)S(1)}) custom-call(bf16[512,2048]{1,0:T(8,128)(2,1)} %x_hbm.1, bf16[1792,2048]{1,0:T(8,128)(2,1)} %w_ref.1, bf16[64,512]{1,0:T(8,128)(2,1)} %bitcast.7, bf16[64,1792]{1,0:T(8,128)(2,1)} %bitcast.3), custom_call_target="tpu_custom_call" | custom-call | flops 167772160 | bytes 2621440 | tf_op jit(solution)/shard_map/pallas_call | solution.py:49
  6.3 0.0 copy-done.1
  6.3 0.0 copy-done
  6.3 1.4 %shard_map.58 = (f32[2,128,128]{2,1,0:T(8,128)S(1)}, f32[2,128,128]{2,1,0:T(8,128)S(1)}, f32[4,128,128]{2,1,0:T(8,128)S(1)}, f32[4,128,128]{2,1,0:T(8,128)S(1)}, f32[4,128,128]{2,1,0:T(8,128)S(1)}) custom-call(f32[64,2048]{1,0:T(8,128)S(1)} %get-tuple-element.32.low_in_ref, f32[64,2048]{1,0:T(8,128)S(1)} %get-tuple-element.33.low_out_ref, ...), custom_call_target="tpu_custom_call" | custom-call | flops 469762048 | bytes 7340032 | tf_op jit(solution)/shard_map/pallas_call | solution.py:98
  7.7 0.1 collective-permute-start.3
  7.8 0.5 %collective-permute-start.4 = (f32[2,128,128]{2,1,0:T(8,128)S(1)}, f32[2,128,128]{2,1,0:T(8,128)S(1)}, u32[]{:S(2)}, u32[]{:S(2)}) collective-permute-start(f32[2,128,128]{2,1,0:T(8,128)S(1)} %get-tuple-element.37), channel_id=1, source_target_pairs={{0,1},{1,0},{2,3},{3,2},{4,5},{5,4},{6,7},{7,6},{8,9},{9,8},{10,11... | collective-permute-start | bytes 393224 | tf_op jit(solution)/shard_map/ppermute | solution.py:270
  8.3 0.1 collective-permute-start.6
  8.4 0.0 collective-permute-done.right_ref
  8.4 0.0 copy-done.2
  8.4 1.6 %collective-permute-start.1 = (bf16[2,8,4096]{2,1,0:T(8,128)(2,1)S(1)}, bf16[2,8,4096]{2,1,0:T(8,128)(2,1)S(1)}, u32[]{:S(2)}, u32[]{:S(2)}) collective-permute-start(bf16[2,8,4096]{2,1,0:T(8,128)(2,1)S(1)} %shard_map.55.left_ref), channel_id=1, source_target_pairs={{0,4},{1,5},{2,6},{3,7},{4,0},{5,1},{6,2},{7,3},{8,12},{9,13},{10,... | collective-permute-start | bytes 393224 | tf_op jit(solution)/shard_map/ppermute | solution.py:270
  10.0 0.0 collective-permute-done.3.refs_0_
  10.0 0.0 collective-permute-done.4.refs_1_
  10.0 0.1 shard_map.59
  10.1 1.6 %collective-permute-start.5 = (bf16[4,144,128]{2,1,0:T(8,128)(2,1)S(1)}, bf16[4,144,128]{2,1,0:T(8,128)(2,1)S(1)}, u32[]{:S(2)}, u32[]{:S(2)}) collective-permute-start(bf16[4,144,128]{2,1,0:T(8,128)(2,1)S(1)} %shard_map.59), channel_id=1, source_target_pairs={{0,2},{1,3},{2,0},{3,1},{4,6},{5,7},{6,4},{7,5},{8,10},{9,11},{10,... | collective-permute-start | bytes 442376 | tf_op jit(solution)/shard_map/ppermute | solution.py:270
  11.7 0.0 collective-permute-start.7
  11.7 2.6 %collective-permute-done.1.right_ref = bf16[2,8,4096]{2,1,0:T(8,128)(2,1)S(1)} collective-permute-done((bf16[2,8,4096]{2,1,0:T(8,128)(2,1)S(1)}, bf16[2,8,4096]{2,1,0:T(8,128)(2,1)S(1)}, u32[]{:S(2)}, u32[]{:S(2)}) %collective-permute-start.1) | collective-permute-done | bytes 131104 | tf_op jit(solution)/shard_map/ppermute | solution.py:270
  14.3 1.6 %collective-permute-start.2 = (bf16[4,8,4096]{2,1,0:T(8,128)(2,1)S(1)}, bf16[4,8,4096]{2,1,0:T(8,128)(2,1)S(1)}, u32[]{:S(2)}, u32[]{:S(2)}) collective-permute-start(bf16[4,8,4096]{2,1,0:T(8,128)(2,1)S(1)} %shard_map.56.refs_4_), channel_id=1, source_target_pairs={{0,2},{1,3},{2,0},{3,1},{4,6},{5,7},{6,4},{7,5},{8,10},{9,11},{10,... | collective-permute-start | bytes 786440 | tf_op jit(solution)/shard_map/ppermute | solution.py:270
  15.9 0.0 collective-permute-done.7.refs_5_
  15.9 0.0 collective-permute-done.6.came_ref
  15.9 0.1 collective-permute-done.5.across_ref
  16.1 0.1 shard_map.60
  16.2 0.1 collective-permute-start.8
  16.3 1.5 %collective-permute-start.9 = (f32[128,128]{1,0:T(8,128)S(1)}, f32[128,128]{1,0:T(8,128)S(1)}, u32[]{:S(2)}, u32[]{:S(2)}) collective-permute-start(f32[128,128]{1,0:T(8,128)S(1)} %get-tuple-element.47), channel_id=1, source_target_pairs={{0,4},{1,5},{2,6},{3,7},{4,0},{5,1},{6,2},{7,3},{8,12},{9,13},{10,... | collective-permute-start | bytes 196616 | tf_op jit(solution)/shard_map/ppermute | solution.py:270
  17.8 1.8 %collective-permute-start.10 = (bf16[128,128]{1,0:T(8,128)(2,1)S(1)}, bf16[128,128]{1,0:T(8,128)(2,1)S(1)}, u32[]{:S(2)}, u32[]{:S(2)}) collective-permute-start(bf16[128,128]{1,0:T(8,128)(2,1)S(1)} %get-tuple-element.48), channel_id=1, source_target_pairs={{0,8},{1,9},{2,10},{3,11},{4,12},{5,13},{6,14},{7,15},{8,0},{9,1},... | collective-permute-start | bytes 98312 | tf_op jit(solution)/shard_map/ppermute | solution.py:270
  19.5 1.2 %collective-permute-start.11 = (bf16[128,128]{1,0:T(8,128)(2,1)S(1)}, bf16[128,128]{1,0:T(8,128)(2,1)S(1)}, u32[]{:S(2)}, u32[]{:S(2)}) collective-permute-start(bf16[128,128]{1,0:T(8,128)(2,1)S(1)} %get-tuple-element.49), channel_id=1, source_target_pairs={{0,12},{1,13},{2,14},{3,15},{4,8},{5,9},{6,10},{7,11},{8,4},{9,5},... | collective-permute-start | bytes 98312 | tf_op jit(solution)/shard_map/ppermute | solution.py:270
  20.7 2.5 %collective-permute-done.10.refs_2_ = bf16[128,128]{1,0:T(8,128)(2,1)S(1)} collective-permute-done((bf16[128,128]{1,0:T(8,128)(2,1)S(1)}, bf16[128,128]{1,0:T(8,128)(2,1)S(1)}, u32[]{:S(2)}, u32[]{:S(2)}) %collective-permute-start.10) | collective-permute-done | bytes 32800 | tf_op jit(solution)/shard_map/ppermute | solution.py:270
  23.2 2.0 %collective-permute-done.11.refs_3_ = bf16[128,128]{1,0:T(8,128)(2,1)S(1)} collective-permute-done((bf16[128,128]{1,0:T(8,128)(2,1)S(1)}, bf16[128,128]{1,0:T(8,128)(2,1)S(1)}, u32[]{:S(2)}, u32[]{:S(2)}) %collective-permute-start.11) | collective-permute-done | bytes 32800 | tf_op jit(solution)/shard_map/ppermute | solution.py:270
  25.3 0.0 collective-permute-done.9.refs_1_
  25.3 0.0 collective-permute-done.8.refs_6_
  25.3 0.0 collective-permute-done.2.refs_7_
  25.3 0.1 collective-permute-start.12
  25.3 0.6 %shard_map.61 = (f32[2,32,128]{2,1,0:T(8,128)S(1)}, f32[2,8,2,8,128]{4,3,2,1,0:T(8,128)S(1)}) custom-call(f32[128,128]{1,0:T(8,128)S(1)} %get-tuple-element.50.refs_0_, f32[128,128]{1,0:T(8,128)S(1)} %collective-permute-done.9.refs_1_, bf16[128,128]{1,0:T(8,128)(2,1)S(1)} %collective-permute-done.10.refs_2_, ...), custom_call_target="tpu_custom_call" | custom-call | tf_op jit(solution)/shard_map/pallas_call | solution.py:240
  26.0 0.9 %collective-permute-done.12.queries_ref = bf16[4,8,4096]{2,1,0:T(8,128)(2,1)S(1)} collective-permute-done((bf16[4,8,4096]{2,1,0:T(8,128)(2,1)S(1)}, bf16[4,8,4096]{2,1,0:T(8,128)(2,1)S(1)}, u32[]{:S(2)}, u32[]{:S(2)}) %collective-permute-start.12) | collective-permute-done | bytes 262176 | tf_op jit(solution)/shard_map/ppermute | solution.py:270
  26.9 0.8 %shard_map.62 = f32[2,128]{1,0:T(2,128)} custom-call(f32[2,32,128]{2,1,0:T(8,128)S(1)} %get-tuple-element.57.grads_ref, f32[2,8,2,8,128]{4,3,2,1,0:T(8,128)S(1)} %get-tuple-element.58.before_ref, bf16[4,8,4096]{2,1,0:T(8,128)(2,1)S(1)} %collective-permute-done.12.queries_ref), custom_call_target="tpu_custom_call" | custom-call | tf_op jit(solution)/shard_map/pallas_call | solution.py:253
  (2 shorter events, 0.0 us)
Async XLA Ops:
  0.0 6.3 %copy-start.1 = (bf16[1792,64]{0,1:T(8,128)(2,1)S(1)}, bf16[1792,64]{0,1:T(8,128)(2,1)}, u32[]{:S(2)}) copy-start(bf16[1792,64]{0,1:T(8,128)(2,1)} %param.8) | copy-start | bytes 688132
  0.0 6.3 %copy-start = (bf16[1792,2048]{1,0:T(8,128)(2,1)S(1)}, bf16[1792,2048]{1,0:T(8,128)(2,1)}, u32[]{:S(2)}) copy-start(bf16[1792,2048]{1,0:T(8,128)(2,1)} %w_ref.1) | copy-start | bytes 22020100
  0.0 8.4 %collective-permute-start = (bf16[1,8,4096]{2,1,0:T(8,128)(2,1)}, bf16[1,8,4096]{2,1,0:T(8,128)(2,1)S(1)}, u32[]{:S(2)}, u32[]{:S(2)}) collective-permute-start(bf16[1,8,4096]{2,1,0:T(8,128)(2,1)} %bitcast.5), channel_id=1, source_target_pairs={{0,8},{1,9},{2,10},{3,11},{4,12},{5,13},{6,14},{7,15},{8,0},{9,1},... | collective-permute-start | bytes 196616 | tf_op jit(solution)/shard_map/ppermute | solution.py:270
  4.0 4.4 %copy-start.2 = (bf16[8,4096]{1,0:T(8,128)(2,1)S(1)}, bf16[8,4096]{1,0:T(8,128)(2,1)}, u32[]{:S(2)}) copy-start(bf16[8,4096]{1,0:T(8,128)(2,1)} %param.9) | copy-start | bytes 196612
  7.7 2.3 %collective-permute-start.3 = (f32[2,128,128]{2,1,0:T(8,128)S(1)}, f32[2,128,128]{2,1,0:T(8,128)S(1)}, u32[]{:S(2)}, u32[]{:S(2)}) collective-permute-start(f32[2,128,128]{2,1,0:T(8,128)S(1)} %get-tuple-element.36), channel_id=1, source_target_pairs={{0,1},{1,0},{2,3},{3,2},{4,5},{5,4},{6,7},{7,6},{8,9},{9,8},{10,11... | collective-permute-start | bytes 393224 | tf_op jit(solution)/shard_map/ppermute | solution.py:270
  7.8 2.2 %collective-permute-start.4 = (f32[2,128,128]{2,1,0:T(8,128)S(1)}, f32[2,128,128]{2,1,0:T(8,128)S(1)}, u32[]{:S(2)}, u32[]{:S(2)}) collective-permute-start(f32[2,128,128]{2,1,0:T(8,128)S(1)} %get-tuple-element.37), channel_id=1, source_target_pairs={{0,1},{1,0},{2,3},{3,2},{4,5},{5,4},{6,7},{7,6},{8,9},{9,8},{10,11... | collective-permute-start | bytes 393224 | tf_op jit(solution)/shard_map/ppermute | solution.py:270
  8.3 7.6 %collective-permute-start.6 = (f32[4,128,128]{2,1,0:T(8,128)S(1)}, f32[4,128,128]{2,1,0:T(8,128)S(1)}, u32[]{:S(2)}, u32[]{:S(2)}) collective-permute-start(f32[4,128,128]{2,1,0:T(8,128)S(1)} %get-tuple-element.38), channel_id=1, source_target_pairs={{0,1},{1,0},{2,3},{3,2},{4,5},{5,4},{6,7},{7,6},{8,9},{9,8},{10,11... | collective-permute-start | bytes 786440 | tf_op jit(solution)/shard_map/ppermute | solution.py:270
  8.4 5.9 %collective-permute-start.1 = (bf16[2,8,4096]{2,1,0:T(8,128)(2,1)S(1)}, bf16[2,8,4096]{2,1,0:T(8,128)(2,1)S(1)}, u32[]{:S(2)}, u32[]{:S(2)}) collective-permute-start(bf16[2,8,4096]{2,1,0:T(8,128)(2,1)S(1)} %shard_map.55.left_ref), channel_id=1, source_target_pairs={{0,4},{1,5},{2,6},{3,7},{4,0},{5,1},{6,2},{7,3},{8,12},{9,13},{10,... | collective-permute-start | bytes 393224 | tf_op jit(solution)/shard_map/ppermute | solution.py:270
  10.1 6.0 %collective-permute-start.5 = (bf16[4,144,128]{2,1,0:T(8,128)(2,1)S(1)}, bf16[4,144,128]{2,1,0:T(8,128)(2,1)S(1)}, u32[]{:S(2)}, u32[]{:S(2)}) collective-permute-start(bf16[4,144,128]{2,1,0:T(8,128)(2,1)S(1)} %shard_map.59), channel_id=1, source_target_pairs={{0,2},{1,3},{2,0},{3,1},{4,6},{5,7},{6,4},{7,5},{8,10},{9,11},{10,... | collective-permute-start | bytes 442376 | tf_op jit(solution)/shard_map/ppermute | solution.py:270
  11.7 4.2 %collective-permute-start.7 = (bf16[2,8,4096]{2,1,0:T(8,128)(2,1)S(1)}, bf16[2,8,4096]{2,1,0:T(8,128)(2,1)S(1)}, u32[]{:S(2)}, u32[]{:S(2)}) collective-permute-start(bf16[2,8,4096]{2,1,0:T(8,128)(2,1)S(1)} %shard_map.55.left_ref), channel_id=1, source_target_pairs={{0,1},{1,0},{2,3},{3,2},{4,5},{5,4},{6,7},{7,6},{8,9},{9,8},{10,11... | collective-permute-start | bytes 393224 | tf_op jit(solution)/shard_map/ppermute | solution.py:270
  14.3 10.9 %collective-permute-start.2 = (bf16[4,8,4096]{2,1,0:T(8,128)(2,1)S(1)}, bf16[4,8,4096]{2,1,0:T(8,128)(2,1)S(1)}, u32[]{:S(2)}, u32[]{:S(2)}) collective-permute-start(bf16[4,8,4096]{2,1,0:T(8,128)(2,1)S(1)} %shard_map.56.refs_4_), channel_id=1, source_target_pairs={{0,2},{1,3},{2,0},{3,1},{4,6},{5,7},{6,4},{7,5},{8,10},{9,11},{10,... | collective-permute-start | bytes 786440 | tf_op jit(solution)/shard_map/ppermute | solution.py:270
  16.2 9.0 %collective-permute-start.8 = (bf16[2,8,4096]{2,1,0:T(8,128)(2,1)S(1)}, bf16[2,8,4096]{2,1,0:T(8,128)(2,1)S(1)}, u32[]{:S(2)}, u32[]{:S(2)}) collective-permute-start(bf16[2,8,4096]{2,1,0:T(8,128)(2,1)S(1)} %collective-permute-done.1.right_ref), channel_id=1, source_target_pairs={{0,1},{1,0},{2,3},{3,2},{4,5},{5,4},{6,7},{7,6},{8,9},{9,8},{10,11... | collective-permute-start | bytes 393224 | tf_op jit(solution)/shard_map/ppermute | solution.py:270
  16.3 9.0 %collective-permute-start.9 = (f32[128,128]{1,0:T(8,128)S(1)}, f32[128,128]{1,0:T(8,128)S(1)}, u32[]{:S(2)}, u32[]{:S(2)}) collective-permute-start(f32[128,128]{1,0:T(8,128)S(1)} %get-tuple-element.47), channel_id=1, source_target_pairs={{0,4},{1,5},{2,6},{3,7},{4,0},{5,1},{6,2},{7,3},{8,12},{9,13},{10,... | collective-permute-start | bytes 196616 | tf_op jit(solution)/shard_map/ppermute | solution.py:270
  17.8 5.4 %collective-permute-start.10 = (bf16[128,128]{1,0:T(8,128)(2,1)S(1)}, bf16[128,128]{1,0:T(8,128)(2,1)S(1)}, u32[]{:S(2)}, u32[]{:S(2)}) collective-permute-start(bf16[128,128]{1,0:T(8,128)(2,1)S(1)} %get-tuple-element.48), channel_id=1, source_target_pairs={{0,8},{1,9},{2,10},{3,11},{4,12},{5,13},{6,14},{7,15},{8,0},{9,1},... | collective-permute-start | bytes 98312 | tf_op jit(solution)/shard_map/ppermute | solution.py:270
  19.5 5.7 %collective-permute-start.11 = (bf16[128,128]{1,0:T(8,128)(2,1)S(1)}, bf16[128,128]{1,0:T(8,128)(2,1)S(1)}, u32[]{:S(2)}, u32[]{:S(2)}) collective-permute-start(bf16[128,128]{1,0:T(8,128)(2,1)S(1)} %get-tuple-element.49), channel_id=1, source_target_pairs={{0,12},{1,13},{2,14},{3,15},{4,8},{5,9},{6,10},{7,11},{8,4},{9,5},... | collective-permute-start | bytes 98312 | tf_op jit(solution)/shard_map/ppermute | solution.py:270
  25.3 1.6 %collective-permute-start.12 = (bf16[4,8,4096]{2,1,0:T(8,128)(2,1)S(1)}, bf16[4,8,4096]{2,1,0:T(8,128)(2,1)S(1)}, u32[]{:S(2)}, u32[]{:S(2)}) collective-permute-start(bf16[4,8,4096]{2,1,0:T(8,128)(2,1)S(1)} %collective-permute-done.2.refs_7_), channel_id=1, source_target_pairs={{0,1},{1,0},{2,3},{3,2},{4,5},{5,4},{6,7},{7,6},{8,9},{9,8},{10,11... | collective-permute-start | bytes 786440 | tf_op jit(solution)/shard_map/ppermute | solution.py:270

commit v15 on v14

--- a/solution.py
+++ b/solution.py
@@ -153,14 +153,22 @@
         def here(first, rows):
             return kept_ref[z, first : first + rows, :] + came_ref[z, first : first + rows, :]
 
-        for rows, total in add_coded(here, across_ref.at[z]):
+        sums = add_coded(here, across_ref.at[z])
+        if out_ref.shape[0] != kept_ref.shape[1]:
+            put_coded(out_ref, jnp.concatenate([total for _, total in reversed(sums)], axis=0))
+            continue
+        for rows, total in sums:
             out_ref[rows, :] = total.astype(out_ref.dtype)
 
 
-def add_kept(kept, came, across, types):
+def add_kept(kept, came, across):
+    depth, rows, width = kept.shape
+    own = jax.ShapeDtypeStruct((rows, width), jnp.float32)
+    near = jax.ShapeDtypeStruct((rows // 8 * 9, width), jnp.bfloat16)
+    far = jax.ShapeDtypeStruct((rows, width), jnp.bfloat16)
     return pl.pallas_call(
         add_kept_kernel,
-        out_shape=[jax.ShapeDtypeStruct(kept.shape[1:], dtype) for dtype in types],
+        out_shape=[own] + [near] * (depth // 2 - 1) + [far] * (depth // 2),
         compiler_params=PARAMS,
     )(kept, came, across)
 
@@ -198,18 +206,21 @@
 
 def first_score_kernel(parts_count, held, *refs):
     part_refs, query_refs = refs[:parts_count], refs[parts_count : parts_count + len(held)]
-    grads_ref, sums_ref, out_t_ref = refs[parts_count + len(held) :]
-    rank, tokens = out_t_ref.shape
+    grads_ref, sums_ref, total_ref = refs[parts_count + len(held) :]
+    rank, tokens = total_ref.shape[0] // 2, total_ref.shape[1]
     core = lax.rem(lax.axis_index("ex"), 2)
-    total = part_refs[0][...]
+    total_ref[...] = part_refs[0][...]
     for part_ref in part_refs[1:]:
-        total = total + part_ref[...].astype(jnp.float32)
-    out_t_ref[...] = total[rank:, :]
-    even = out_t_ref[pl.ds(0, rank // 2, stride=2), :]
-    odd = out_t_ref[pl.ds(1, rank // 2, stride=2), :]
+        if part_ref.shape[0] == 2 * rank:
+            total_ref[...] += part_ref[...].astype(jnp.float32)
+        else:
+            for rows, total in add_coded(lambda first, count: total_ref[first : first + count, :], part_ref):
+                total_ref[rows, :] = total
+    even = total_ref[pl.ds(rank, rank // 2, stride=2), :]
+    odd = total_ref[pl.ds(rank + 1, rank // 2, stride=2), :]
     token = lax.broadcasted_iota(jnp.int32, (rank, tokens), 1)
     for n in range(tokens // SEQ):
-        mine = jnp.where((token >= n * SEQ) & (token < (n + 1) * SEQ), total[:rank, :], 0.0)
+        mine = jnp.where((token >= n * SEQ) & (token < (n + 1) * SEQ), total_ref[:rank, :], 0.0)
         for side, rows in enumerate((even, odd)):
             grads_ref[n, :, side * rank : (side + 1) * rank] = lax.dot_general(
                 rows, mine, LANES_BY_LANES, precision=lax.Precision.HIGHEST, preferred_element_type=jnp.float32
@@ -243,7 +254,7 @@
             jax.ShapeDtypeStruct((examples, rank // 2, 2 * rank), jnp.float32),
             jax.ShapeDtypeStruct((examples, chips, 2, queries[0].shape[1], 2 * rank), jnp.float32),
         ],
-        scratch_shapes=[pltpu.VMEM((rank, tokens), jnp.float32)],
+        scratch_shapes=[pltpu.VMEM((2 * rank, tokens), jnp.float32)],
         compiler_params=PARAMS,
     )(*parts, *queries)
 
@@ -287,8 +298,7 @@
     other_early = swap(early, core=1)
     across, came, other_early = together((across, came, other_early))
 
-    types = [jnp.float32 if z < depth // 2 else jnp.bfloat16 for z in range(depth)]
-    parts = list(add_kept(kept, came, across, types))
+    parts = list(add_kept(kept, came, across))
     late, parts = together((late, parts))
     other_late = swap(late, core=1)
     for z in list(range(depth // 2, depth)) + list(range(1, depth // 2)):

time: 27.8 us -> 27.8 us (level)
  no operation moved by 1% of the time
where the time goes in v15:
time: 27.8 us; the launch traced here: 27.7 us
  starting transfers between devices  14.1 us (51%)
  waiting for transfers between devices  8.12 us (29%)
  Pallas kernels  5.36 us (19%)
    ppermute x13, starting transfers between devices, swap(): lax.ppermute(array, 'ex', [(i, i ^ distance) for i in range(devices)])  14.1 us
    ppermute x13, waiting for transfers between devices, swap(): lax.ppermute(array, 'ex', [(i, i ^ distance) for i in range(devices)])  8.12 us
    pallas_call x1, Pallas kernels, project_loaded(): pl.pallas_call(project_loaded_kernel, out_shape=[jax.ShapeDtypeStruct((ra...  2.22 us
    pallas_call x1, Pallas kernels, project(): pl.pallas_call(functools.partial(project_kernel, rows), out_shape=[half]...  1.43 us
    pallas_call x1, Pallas kernels, last_scores(): pl.pallas_call(functools.partial(last_score_kernel, chips), out_shape=jax...  0.81 us
    pallas_call x1, Pallas kernels, first_scores(): pl.pallas_call(functools.partial(first_score_kernel, len(parts), held), o...  0.68 us
  transfers between devices with their start and end apart: 13, of which 5 were waited for; matrix products, arithmetic and copies ran while one was open for 0% of the time, Pallas kernels for 16%

profile of v15, /device:TPU:0, one launch (start us, length us, event | category | flops | bytes accessed | tf_op | source)
XLA Modules:
  0.0 27.7 jit_solution(5450294304019074686)
XLA Ops:
  0.0 0.0 copy-start.1
  0.0 0.0 copy-start
  0.0 4.0 %collective-permute-start = (bf16[1,8,4096]{2,1,0:T(8,128)(2,1)}, bf16[1,8,4096]{2,1,0:T(8,128)(2,1)S(1)}, u32[]{:S(2)}, u32[]{:S(2)}) collective-permute-start(bf16[1,8,4096]{2,1,0:T(8,128)(2,1)} %bitcast.5), channel_id=1, source_target_pairs={{0,8},{1,9},{2,10},{3,11},{4,12},{5,13},{6,14},{7,15},{8,0},{9,1},... | collective-permute-start | bytes 196616 | tf_op jit(solution)/shard_map/ppermute | solution.py:281
  4.0 0.0 copy-start.2
  4.0 2.2 %shard_map.57 = (f32[64,2048]{1,0:T(8,128)S(1)}, f32[64,2048]{1,0:T(8,128)S(1)}) custom-call(bf16[512,2048]{1,0:T(8,128)(2,1)} %x_hbm.1, bf16[1792,2048]{1,0:T(8,128)(2,1)} %w_ref.1, bf16[64,512]{1,0:T(8,128)(2,1)} %bitcast.7, bf16[64,1792]{1,0:T(8,128)(2,1)} %bitcast.3), custom_call_target="tpu_custom_call" | custom-call | flops 167772160 | bytes 2621440 | tf_op jit(solution)/shard_map/pallas_call | solution.py:49
  6.3 0.0 copy-done.1
  6.3 0.0 copy-done
  6.3 1.4 %shard_map.58 = (f32[2,128,128]{2,1,0:T(8,128)S(1)}, f32[2,128,128]{2,1,0:T(8,128)S(1)}, f32[4,128,128]{2,1,0:T(8,128)S(1)}, f32[4,128,128]{2,1,0:T(8,128)S(1)}, f32[4,128,128]{2,1,0:T(8,128)S(1)}) custom-call(f32[64,2048]{1,0:T(8,128)S(1)} %get-tuple-element.32.low_in_ref, f32[64,2048]{1,0:T(8,128)S(1)} %get-tuple-element.33.low_out_ref, ...), custom_call_target="tpu_custom_call" | custom-call | flops 469762048 | bytes 7340032 | tf_op jit(solution)/shard_map/pallas_call | solution.py:98
  7.7 0.1 collective-permute-start.3
  7.8 0.5 %collective-permute-start.4 = (f32[2,128,128]{2,1,0:T(8,128)S(1)}, f32[2,128,128]{2,1,0:T(8,128)S(1)}, u32[]{:S(2)}, u32[]{:S(2)}) collective-permute-start(f32[2,128,128]{2,1,0:T(8,128)S(1)} %get-tuple-element.37), channel_id=1, source_target_pairs={{0,1},{1,0},{2,3},{3,2},{4,5},{5,4},{6,7},{7,6},{8,9},{9,8},{10,11... | collective-permute-start | bytes 393224 | tf_op jit(solution)/shard_map/ppermute | solution.py:281
  8.3 0.1 collective-permute-start.6
  8.4 0.0 collective-permute-done.right_ref
  8.4 0.0 copy-done.2
  8.4 1.6 %collective-permute-start.1 = (bf16[2,8,4096]{2,1,0:T(8,128)(2,1)S(1)}, bf16[2,8,4096]{2,1,0:T(8,128)(2,1)S(1)}, u32[]{:S(2)}, u32[]{:S(2)}) collective-permute-start(bf16[2,8,4096]{2,1,0:T(8,128)(2,1)S(1)} %shard_map.55.left_ref), channel_id=1, source_target_pairs={{0,4},{1,5},{2,6},{3,7},{4,0},{5,1},{6,2},{7,3},{8,12},{9,13},{10,... | collective-permute-start | bytes 393224 | tf_op jit(solution)/shard_map/ppermute | solution.py:281
  10.0 0.0 collective-permute-done.3.refs_0_
  10.0 0.0 collective-permute-done.4.refs_1_
  10.0 0.1 shard_map.59
  10.1 1.6 %collective-permute-start.5 = (bf16[4,144,128]{2,1,0:T(8,128)(2,1)S(1)}, bf16[4,144,128]{2,1,0:T(8,128)(2,1)S(1)}, u32[]{:S(2)}, u32[]{:S(2)}) collective-permute-start(bf16[4,144,128]{2,1,0:T(8,128)(2,1)S(1)} %shard_map.59), channel_id=1, source_target_pairs={{0,2},{1,3},{2,0},{3,1},{4,6},{5,7},{6,4},{7,5},{8,10},{9,11},{10,... | collective-permute-start | bytes 442376 | tf_op jit(solution)/shard_map/ppermute | solution.py:281
  11.7 0.0 collective-permute-start.7
  11.7 2.6 %collective-permute-done.1.right_ref = bf16[2,8,4096]{2,1,0:T(8,128)(2,1)S(1)} collective-permute-done((bf16[2,8,4096]{2,1,0:T(8,128)(2,1)S(1)}, bf16[2,8,4096]{2,1,0:T(8,128)(2,1)S(1)}, u32[]{:S(2)}, u32[]{:S(2)}) %collective-permute-start.1) | collective-permute-done | bytes 131104 | tf_op jit(solution)/shard_map/ppermute | solution.py:281
  14.3 1.6 %collective-permute-start.2 = (bf16[4,8,4096]{2,1,0:T(8,128)(2,1)S(1)}, bf16[4,8,4096]{2,1,0:T(8,128)(2,1)S(1)}, u32[]{:S(2)}, u32[]{:S(2)}) collective-permute-start(bf16[4,8,4096]{2,1,0:T(8,128)(2,1)S(1)} %shard_map.56.refs_4_), channel_id=1, source_target_pairs={{0,2},{1,3},{2,0},{3,1},{4,6},{5,7},{6,4},{7,5},{8,10},{9,11},{10,... | collective-permute-start | bytes 786440 | tf_op jit(solution)/shard_map/ppermute | solution.py:281
  15.9 0.0 collective-permute-done.7.refs_5_
  15.9 0.0 collective-permute-done.6.came_ref
  15.9 0.1 collective-permute-done.5.across_ref
  16.1 0.1 shard_map.60
  16.2 0.1 collective-permute-start.8
  16.3 1.5 %collective-permute-start.9 = (bf16[144,128]{1,0:T(8,128)(2,1)S(1)}, bf16[144,128]{1,0:T(8,128)(2,1)S(1)}, u32[]{:S(2)}, u32[]{:S(2)}) collective-permute-start(bf16[144,128]{1,0:T(8,128)(2,1)S(1)} %get-tuple-element.47), channel_id=1, source_target_pairs={{0,4},{1,5},{2,6},{3,7},{4,0},{5,1},{6,2},{7,3},{8,12},{9,13},{10,... | collective-permute-start | bytes 110600 | tf_op jit(solution)/shard_map/ppermute | solution.py:281
  17.8 1.8 %collective-permute-start.10 = (bf16[128,128]{1,0:T(8,128)(2,1)S(1)}, bf16[128,128]{1,0:T(8,128)(2,1)S(1)}, u32[]{:S(2)}, u32[]{:S(2)}) collective-permute-start(bf16[128,128]{1,0:T(8,128)(2,1)S(1)} %get-tuple-element.48), channel_id=1, source_target_pairs={{0,8},{1,9},{2,10},{3,11},{4,12},{5,13},{6,14},{7,15},{8,0},{9,1},... | collective-permute-start | bytes 98312 | tf_op jit(solution)/shard_map/ppermute | solution.py:281
  19.5 1.2 %collective-permute-start.11 = (bf16[128,128]{1,0:T(8,128)(2,1)S(1)}, bf16[128,128]{1,0:T(8,128)(2,1)S(1)}, u32[]{:S(2)}, u32[]{:S(2)}) collective-permute-start(bf16[128,128]{1,0:T(8,128)(2,1)S(1)} %get-tuple-element.49), channel_id=1, source_target_pairs={{0,12},{1,13},{2,14},{3,15},{4,8},{5,9},{6,10},{7,11},{8,4},{9,5},... | collective-permute-start | bytes 98312 | tf_op jit(solution)/shard_map/ppermute | solution.py:281
  20.8 2.5 %collective-permute-done.10.refs_2_ = bf16[128,128]{1,0:T(8,128)(2,1)S(1)} collective-permute-done((bf16[128,128]{1,0:T(8,128)(2,1)S(1)}, bf16[128,128]{1,0:T(8,128)(2,1)S(1)}, u32[]{:S(2)}, u32[]{:S(2)}) %collective-permute-start.10) | collective-permute-done | bytes 32800 | tf_op jit(solution)/shard_map/ppermute | solution.py:281
  23.2 2.1 %collective-permute-done.11.refs_3_ = bf16[128,128]{1,0:T(8,128)(2,1)S(1)} collective-permute-done((bf16[128,128]{1,0:T(8,128)(2,1)S(1)}, bf16[128,128]{1,0:T(8,128)(2,1)S(1)}, u32[]{:S(2)}, u32[]{:S(2)}) %collective-permute-start.11) | collective-permute-done | bytes 32800 | tf_op jit(solution)/shard_map/ppermute | solution.py:281
  25.3 0.0 collective-permute-done.9.refs_1_
  25.3 0.0 collective-permute-done.8.refs_6_
  25.3 0.0 collective-permute-done.2.refs_7_
  25.3 0.1 collective-permute-start.12
  25.4 0.7 %shard_map.61 = (f32[2,32,128]{2,1,0:T(8,128)S(1)}, f32[2,8,2,8,128]{4,3,2,1,0:T(8,128)S(1)}) custom-call(f32[128,128]{1,0:T(8,128)S(1)} %get-tuple-element.50.refs_0_, bf16[144,128]{1,0:T(8,128)(2,1)S(1)} %collective-permute-done.9.refs_1_, bf16[128,128]{1,0:T(8,128)(2,1)S(1)} %collective-permute-done.10.refs_2_, ...), custom_call_target="tpu_custom_call" | custom-call | tf_op jit(solution)/shard_map/pallas_call | solution.py:251
  26.0 0.8 %collective-permute-done.12.queries_ref = bf16[4,8,4096]{2,1,0:T(8,128)(2,1)S(1)} collective-permute-done((bf16[4,8,4096]{2,1,0:T(8,128)(2,1)S(1)}, bf16[4,8,4096]{2,1,0:T(8,128)(2,1)S(1)}, u32[]{:S(2)}, u32[]{:S(2)}) %collective-permute-start.12) | collective-permute-done | bytes 262176 | tf_op jit(solution)/shard_map/ppermute | solution.py:281
  26.9 0.8 %shard_map.62 = f32[2,128]{1,0:T(2,128)} custom-call(f32[2,32,128]{2,1,0:T(8,128)S(1)} %get-tuple-element.57.grads_ref, f32[2,8,2,8,128]{4,3,2,1,0:T(8,128)S(1)} %get-tuple-element.58.before_ref, bf16[4,8,4096]{2,1,0:T(8,128)(2,1)S(1)} %collective-permute-done.12.queries_ref), custom_call_target="tpu_custom_call" | custom-call | tf_op jit(solution)/shard_map/pallas_call | solution.py:264
  (2 shorter events, 0.0 us)
Async XLA Ops:
  0.0 6.3 %copy-start.1 = (bf16[1792,64]{0,1:T(8,128)(2,1)S(1)}, bf16[1792,64]{0,1:T(8,128)(2,1)}, u32[]{:S(2)}) copy-start(bf16[1792,64]{0,1:T(8,128)(2,1)} %param.8) | copy-start | bytes 688132
  0.0 6.3 %copy-start = (bf16[1792,2048]{1,0:T(8,128)(2,1)S(1)}, bf16[1792,2048]{1,0:T(8,128)(2,1)}, u32[]{:S(2)}) copy-start(bf16[1792,2048]{1,0:T(8,128)(2,1)} %w_ref.1) | copy-start | bytes 22020100
  0.0 8.4 %collective-permute-start = (bf16[1,8,4096]{2,1,0:T(8,128)(2,1)}, bf16[1,8,4096]{2,1,0:T(8,128)(2,1)S(1)}, u32[]{:S(2)}, u32[]{:S(2)}) collective-permute-start(bf16[1,8,4096]{2,1,0:T(8,128)(2,1)} %bitcast.5), channel_id=1, source_target_pairs={{0,8},{1,9},{2,10},{3,11},{4,12},{5,13},{6,14},{7,15},{8,0},{9,1},... | collective-permute-start | bytes 196616 | tf_op jit(solution)/shard_map/ppermute | solution.py:281
  4.0 4.4 %copy-start.2 = (bf16[8,4096]{1,0:T(8,128)(2,1)S(1)}, bf16[8,4096]{1,0:T(8,128)(2,1)}, u32[]{:S(2)}) copy-start(bf16[8,4096]{1,0:T(8,128)(2,1)} %param.9) | copy-start | bytes 196612
  7.7 2.3 %collective-permute-start.3 = (f32[2,128,128]{2,1,0:T(8,128)S(1)}, f32[2,128,128]{2,1,0:T(8,128)S(1)}, u32[]{:S(2)}, u32[]{:S(2)}) collective-permute-start(f32[2,128,128]{2,1,0:T(8,128)S(1)} %get-tuple-element.36), channel_id=1, source_target_pairs={{0,1},{1,0},{2,3},{3,2},{4,5},{5,4},{6,7},{7,6},{8,9},{9,8},{10,11... | collective-permute-start | bytes 393224 | tf_op jit(solution)/shard_map/ppermute | solution.py:281
  7.8 2.2 %collective-permute-start.4 = (f32[2,128,128]{2,1,0:T(8,128)S(1)}, f32[2,128,128]{2,1,0:T(8,128)S(1)}, u32[]{:S(2)}, u32[]{:S(2)}) collective-permute-start(f32[2,128,128]{2,1,0:T(8,128)S(1)} %get-tuple-element.37), channel_id=1, source_target_pairs={{0,1},{1,0},{2,3},{3,2},{4,5},{5,4},{6,7},{7,6},{8,9},{9,8},{10,11... | collective-permute-start | bytes 393224 | tf_op jit(solution)/shard_map/ppermute | solution.py:281
  8.3 7.6 %collective-permute-start.6 = (f32[4,128,128]{2,1,0:T(8,128)S(1)}, f32[4,128,128]{2,1,0:T(8,128)S(1)}, u32[]{:S(2)}, u32[]{:S(2)}) collective-permute-start(f32[4,128,128]{2,1,0:T(8,128)S(1)} %get-tuple-element.38), channel_id=1, source_target_pairs={{0,1},{1,0},{2,3},{3,2},{4,5},{5,4},{6,7},{7,6},{8,9},{9,8},{10,11... | collective-permute-start | bytes 786440 | tf_op jit(solution)/shard_map/ppermute | solution.py:281
  8.4 5.9 %collective-permute-start.1 = (bf16[2,8,4096]{2,1,0:T(8,128)(2,1)S(1)}, bf16[2,8,4096]{2,1,0:T(8,128)(2,1)S(1)}, u32[]{:S(2)}, u32[]{:S(2)}) collective-permute-start(bf16[2,8,4096]{2,1,0:T(8,128)(2,1)S(1)} %shard_map.55.left_ref), channel_id=1, source_target_pairs={{0,4},{1,5},{2,6},{3,7},{4,0},{5,1},{6,2},{7,3},{8,12},{9,13},{10,... | collective-permute-start | bytes 393224 | tf_op jit(solution)/shard_map/ppermute | solution.py:281
  10.1 6.0 %collective-permute-start.5 = (bf16[4,144,128]{2,1,0:T(8,128)(2,1)S(1)}, bf16[4,144,128]{2,1,0:T(8,128)(2,1)S(1)}, u32[]{:S(2)}, u32[]{:S(2)}) collective-permute-start(bf16[4,144,128]{2,1,0:T(8,128)(2,1)S(1)} %shard_map.59), channel_id=1, source_target_pairs={{0,2},{1,3},{2,0},{3,1},{4,6},{5,7},{6,4},{7,5},{8,10},{9,11},{10,... | collective-permute-start | bytes 442376 | tf_op jit(solution)/shard_map/ppermute | solution.py:281
  11.7 4.2 %collective-permute-start.7 = (bf16[2,8,4096]{2,1,0:T(8,128)(2,1)S(1)}, bf16[2,8,4096]{2,1,0:T(8,128)(2,1)S(1)}, u32[]{:S(2)}, u32[]{:S(2)}) collective-permute-start(bf16[2,8,4096]{2,1,0:T(8,128)(2,1)S(1)} %shard_map.55.left_ref), channel_id=1, source_target_pairs={{0,1},{1,0},{2,3},{3,2},{4,5},{5,4},{6,7},{7,6},{8,9},{9,8},{10,11... | collective-permute-start | bytes 393224 | tf_op jit(solution)/shard_map/ppermute | solution.py:281
  14.3 10.9 %collective-permute-start.2 = (bf16[4,8,4096]{2,1,0:T(8,128)(2,1)S(1)}, bf16[4,8,4096]{2,1,0:T(8,128)(2,1)S(1)}, u32[]{:S(2)}, u32[]{:S(2)}) collective-permute-start(bf16[4,8,4096]{2,1,0:T(8,128)(2,1)S(1)} %shard_map.56.refs_4_), channel_id=1, source_target_pairs={{0,2},{1,3},{2,0},{3,1},{4,6},{5,7},{6,4},{7,5},{8,10},{9,11},{10,... | collective-permute-start | bytes 786440 | tf_op jit(solution)/shard_map/ppermute | solution.py:281
  16.2 9.0 %collective-permute-start.8 = (bf16[2,8,4096]{2,1,0:T(8,128)(2,1)S(1)}, bf16[2,8,4096]{2,1,0:T(8,128)(2,1)S(1)}, u32[]{:S(2)}, u32[]{:S(2)}) collective-permute-start(bf16[2,8,4096]{2,1,0:T(8,128)(2,1)S(1)} %collective-permute-done.1.right_ref), channel_id=1, source_target_pairs={{0,1},{1,0},{2,3},{3,2},{4,5},{5,4},{6,7},{7,6},{8,9},{9,8},{10,11... | collective-permute-start | bytes 393224 | tf_op jit(solution)/shard_map/ppermute | solution.py:281
  16.3 9.0 %collective-permute-start.9 = (bf16[144,128]{1,0:T(8,128)(2,1)S(1)}, bf16[144,128]{1,0:T(8,128)(2,1)S(1)}, u32[]{:S(2)}, u32[]{:S(2)}) collective-permute-start(bf16[144,128]{1,0:T(8,128)(2,1)S(1)} %get-tuple-element.47), channel_id=1, source_target_pairs={{0,4},{1,5},{2,6},{3,7},{4,0},{5,1},{6,2},{7,3},{8,12},{9,13},{10,... | collective-permute-start | bytes 110600 | tf_op jit(solution)/shard_map/ppermute | solution.py:281
  17.8 5.4 %collective-permute-start.10 = (bf16[128,128]{1,0:T(8,128)(2,1)S(1)}, bf16[128,128]{1,0:T(8,128)(2,1)S(1)}, u32[]{:S(2)}, u32[]{:S(2)}) collective-permute-start(bf16[128,128]{1,0:T(8,128)(2,1)S(1)} %get-tuple-element.48), channel_id=1, source_target_pairs={{0,8},{1,9},{2,10},{3,11},{4,12},{5,13},{6,14},{7,15},{8,0},{9,1},... | collective-permute-start | bytes 98312 | tf_op jit(solution)/shard_map/ppermute | solution.py:281
  19.5 5.7 %collective-permute-start.11 = (bf16[128,128]{1,0:T(8,128)(2,1)S(1)}, bf16[128,128]{1,0:T(8,128)(2,1)S(1)}, u32[]{:S(2)}, u32[]{:S(2)}) collective-permute-start(bf16[128,128]{1,0:T(8,128)(2,1)S(1)} %get-tuple-element.49), channel_id=1, source_target_pairs={{0,12},{1,13},{2,14},{3,15},{4,8},{5,9},{6,10},{7,11},{8,4},{9,5},... | collective-permute-start | bytes 98312 | tf_op jit(solution)/shard_map/ppermute | solution.py:281
  25.3 1.6 %collective-permute-start.12 = (bf16[4,8,4096]{2,1,0:T(8,128)(2,1)S(1)}, bf16[4,8,4096]{2,1,0:T(8,128)(2,1)S(1)}, u32[]{:S(2)}, u32[]{:S(2)}) collective-permute-start(bf16[4,8,4096]{2,1,0:T(8,128)(2,1)S(1)} %collective-permute-done.2.refs_7_), channel_id=1, source_target_pairs={{0,1},{1,0},{2,3},{3,2},{4,5},{5,4},{6,7},{7,6},{8,9},{9,8},{10,11... | collective-permute-start | bytes 786440 | tf_op jit(solution)/shard_map/ppermute | solution.py:281

commit v16 on v15

--- a/solution.py
+++ b/solution.py
@@ -148,27 +148,26 @@
     )(kept, *came)
 
 
-def add_kept_kernel(kept_ref, came_ref, across_ref, *out_refs):
-    for z, out_ref in enumerate(out_refs):
+def add_kept_kernel(kept_ref, came_ref, across_ref, own_ref, *out_refs):
+    for z in range(len(out_refs) + 1):
         def here(first, rows):
             return kept_ref[z, first : first + rows, :] + came_ref[z, first : first + rows, :]
 
         sums = add_coded(here, across_ref.at[z])
-        if out_ref.shape[0] != kept_ref.shape[1]:
-            put_coded(out_ref, jnp.concatenate([total for _, total in reversed(sums)], axis=0))
-            continue
-        for rows, total in sums:
-            out_ref[rows, :] = total.astype(out_ref.dtype)
+        if z == 0:
+            for rows, total in sums:
+                own_ref[rows, :] = total
+        else:
+            put_coded(out_refs[len(out_refs) - z], jnp.concatenate([total for _, total in reversed(sums)], axis=0))
 
 
 def add_kept(kept, came, across):
     depth, rows, width = kept.shape
     own = jax.ShapeDtypeStruct((rows, width), jnp.float32)
-    near = jax.ShapeDtypeStruct((rows // 8 * 9, width), jnp.bfloat16)
-    far = jax.ShapeDtypeStruct((rows, width), jnp.bfloat16)
+    coded = jax.ShapeDtypeStruct((rows // 8 * 9, width), jnp.bfloat16)
     return pl.pallas_call(
         add_kept_kernel,
-        out_shape=[own] + [near] * (depth // 2 - 1) + [far] * (depth // 2),
+        out_shape=[own] + [coded] * (depth - 1),
         compiler_params=PARAMS,
     )(kept, came, across)
 
@@ -211,11 +210,8 @@
     core = lax.rem(lax.axis_index("ex"), 2)
     total_ref[...] = part_refs[0][...]
     for part_ref in part_refs[1:]:
-        if part_ref.shape[0] == 2 * rank:
-            total_ref[...] += part_ref[...].astype(jnp.float32)
-        else:
-            for rows, total in add_coded(lambda first, count: total_ref[first : first + count, :], part_ref):
-                total_ref[rows, :] = total
+        for rows, total in add_coded(lambda first, count: total_ref[first : first + count, :], part_ref):
+            total_ref[rows, :] = total
     even = total_ref[pl.ds(rank, rank // 2, stride=2), :]
     odd = total_ref[pl.ds(rank + 1, rank // 2, stride=2), :]
     token = lax.broadcasted_iota(jnp.int32, (rank, tokens), 1)
@@ -301,8 +297,7 @@
     parts = list(add_kept(kept, came, across))
     late, parts = together((late, parts))
     other_late = swap(late, core=1)
-    for z in list(range(depth // 2, depth)) + list(range(1, depth // 2)):
-        parts[z] = swap(parts[z], chip=2 * z)
+    parts[1:] = [swap(part, chip=2 * z) for z, part in zip(reversed(range(1, depth)), parts[1:])]
     came_held, other_late, parts = together((came_held, other_late, parts))
     other_came = swap(came_held, core=1)
     reach_y = [chip ^ 1 for chip in reach]

time: 27.8 us -> 27.8 us (level)
  transfers between devices with their start and end apart: 13 -> 13, of which waited for: 5 -> 6; matrix products, arithmetic and copies ran while one was open for 0% -> 0% of each run, Pallas kernels for 16% -> 17%
where the time goes in v16:
time: 27.8 us; the launch traced here: 27.7 us
  starting transfers between devices  14 us (50%)
  waiting for transfers between devices  8.15 us (29%)
  Pallas kernels  5.41 us (19%)
    ppermute x13, starting transfers between devices, swap(): lax.ppermute(array, 'ex', [(i, i ^ distance) for i in range(devices)])  14 us
    ppermute x13, waiting for transfers between devices, swap(): lax.ppermute(array, 'ex', [(i, i ^ distance) for i in range(devices)])  8.15 us
    pallas_call x1, Pallas kernels, project_loaded(): pl.pallas_call(project_loaded_kernel, out_shape=[jax.ShapeDtypeStruct((ra...  2.22 us
    pallas_call x1, Pallas kernels, project(): pl.pallas_call(functools.partial(project_kernel, rows), out_shape=[half]...  1.43 us
    pallas_call x1, Pallas kernels, last_scores(): pl.pallas_call(functools.partial(last_score_kernel, chips), out_shape=jax...  0.82 us
    pallas_call x1, Pallas kernels, first_scores(): pl.pallas_call(functools.partial(first_score_kernel, len(parts), held), o...  0.7 us
  transfers between devices with their start and end apart: 13, of which 6 were waited for; matrix products, arithmetic and copies ran while one was open for 0% of the time, Pallas kernels for 17%

profile of v16, /device:TPU:0, one launch (start us, length us, event | category | flops | bytes accessed | tf_op | source)
XLA Modules:
  0.0 27.7 jit_solution(16398737968660121407)
XLA Ops:
  0.0 0.0 copy-start.1
  0.0 0.0 copy-start
  0.0 4.0 %collective-permute-start = (bf16[1,8,4096]{2,1,0:T(8,128)(2,1)}, bf16[1,8,4096]{2,1,0:T(8,128)(2,1)S(1)}, u32[]{:S(2)}, u32[]{:S(2)}) collective-permute-start(bf16[1,8,4096]{2,1,0:T(8,128)(2,1)} %bitcast.5), channel_id=1, source_target_pairs={{0,8},{1,9},{2,10},{3,11},{4,12},{5,13},{6,14},{7,15},{8,0},{9,1},... | collective-permute-start | bytes 196616 | tf_op jit(solution)/shard_map/ppermute | solution.py:277
  4.0 0.0 copy-start.2
  4.0 2.2 %shard_map.57 = (f32[64,2048]{1,0:T(8,128)S(1)}, f32[64,2048]{1,0:T(8,128)S(1)}) custom-call(bf16[512,2048]{1,0:T(8,128)(2,1)} %x_hbm.1, bf16[1792,2048]{1,0:T(8,128)(2,1)} %w_ref.1, bf16[64,512]{1,0:T(8,128)(2,1)} %bitcast.7, bf16[64,1792]{1,0:T(8,128)(2,1)} %bitcast.3), custom_call_target="tpu_custom_call" | custom-call | flops 167772160 | bytes 2621440 | tf_op jit(solution)/shard_map/pallas_call | solution.py:49
  6.3 0.0 copy-done.1
  6.3 0.0 copy-done
  6.3 1.4 %shard_map.58 = (f32[2,128,128]{2,1,0:T(8,128)S(1)}, f32[2,128,128]{2,1,0:T(8,128)S(1)}, f32[4,128,128]{2,1,0:T(8,128)S(1)}, f32[4,128,128]{2,1,0:T(8,128)S(1)}, f32[4,128,128]{2,1,0:T(8,128)S(1)}) custom-call(f32[64,2048]{1,0:T(8,128)S(1)} %get-tuple-element.32.low_in_ref, f32[64,2048]{1,0:T(8,128)S(1)} %get-tuple-element.33.low_out_ref, ...), custom_call_target="tpu_custom_call" | custom-call | flops 469762048 | bytes 7340032 | tf_op jit(solution)/shard_map/pallas_call | solution.py:98
  7.7 0.1 collective-permute-start.3
  7.8 0.5 %collective-permute-start.4 = (f32[2,128,128]{2,1,0:T(8,128)S(1)}, f32[2,128,128]{2,1,0:T(8,128)S(1)}, u32[]{:S(2)}, u32[]{:S(2)}) collective-permute-start(f32[2,128,128]{2,1,0:T(8,128)S(1)} %get-tuple-element.37), channel_id=1, source_target_pairs={{0,1},{1,0},{2,3},{3,2},{4,5},{5,4},{6,7},{7,6},{8,9},{9,8},{10,11... | collective-permute-start | bytes 393224 | tf_op jit(solution)/shard_map/ppermute | solution.py:277
  8.3 0.1 collective-permute-start.6
  8.4 0.0 collective-permute-done.right_ref
  8.4 0.0 copy-done.2
  8.4 1.6 %collective-permute-start.1 = (bf16[2,8,4096]{2,1,0:T(8,128)(2,1)S(1)}, bf16[2,8,4096]{2,1,0:T(8,128)(2,1)S(1)}, u32[]{:S(2)}, u32[]{:S(2)}) collective-permute-start(bf16[2,8,4096]{2,1,0:T(8,128)(2,1)S(1)} %shard_map.55.left_ref), channel_id=1, source_target_pairs={{0,4},{1,5},{2,6},{3,7},{4,0},{5,1},{6,2},{7,3},{8,12},{9,13},{10,... | collective-permute-start | bytes 393224 | tf_op jit(solution)/shard_map/ppermute | solution.py:277
  10.0 0.0 collective-permute-done.3.refs_0_
  10.0 0.0 collective-permute-done.4.refs_1_
  10.0 0.1 shard_map.59
  10.1 1.6 %collective-permute-start.5 = (bf16[4,144,128]{2,1,0:T(8,128)(2,1)S(1)}, bf16[4,144,128]{2,1,0:T(8,128)(2,1)S(1)}, u32[]{:S(2)}, u32[]{:S(2)}) collective-permute-start(bf16[4,144,128]{2,1,0:T(8,128)(2,1)S(1)} %shard_map.59), channel_id=1, source_target_pairs={{0,2},{1,3},{2,0},{3,1},{4,6},{5,7},{6,4},{7,5},{8,10},{9,11},{10,... | collective-permute-start | bytes 442376 | tf_op jit(solution)/shard_map/ppermute | solution.py:277
  11.7 0.0 collective-permute-start.7
  11.7 2.6 %collective-permute-done.1.right_ref = bf16[2,8,4096]{2,1,0:T(8,128)(2,1)S(1)} collective-permute-done((bf16[2,8,4096]{2,1,0:T(8,128)(2,1)S(1)}, bf16[2,8,4096]{2,1,0:T(8,128)(2,1)S(1)}, u32[]{:S(2)}, u32[]{:S(2)}) %collective-permute-start.1) | collective-permute-done | bytes 131104 | tf_op jit(solution)/shard_map/ppermute | solution.py:277
  14.3 1.6 %collective-permute-start.2 = (bf16[4,8,4096]{2,1,0:T(8,128)(2,1)S(1)}, bf16[4,8,4096]{2,1,0:T(8,128)(2,1)S(1)}, u32[]{:S(2)}, u32[]{:S(2)}) collective-permute-start(bf16[4,8,4096]{2,1,0:T(8,128)(2,1)S(1)} %shard_map.56.refs_4_), channel_id=1, source_target_pairs={{0,2},{1,3},{2,0},{3,1},{4,6},{5,7},{6,4},{7,5},{8,10},{9,11},{10,... | collective-permute-start | bytes 786440 | tf_op jit(solution)/shard_map/ppermute | solution.py:277
  15.9 0.0 collective-permute-done.7.refs_5_
  15.9 0.0 collective-permute-done.6.came_ref
  15.9 0.1 collective-permute-done.5.across_ref
  16.1 0.1 shard_map.60
  16.2 0.1 collective-permute-start.8
  16.3 1.8 %collective-permute-start.10 = (bf16[144,128]{1,0:T(8,128)(2,1)S(1)}, bf16[144,128]{1,0:T(8,128)(2,1)S(1)}, u32[]{:S(2)}, u32[]{:S(2)}) collective-permute-start(bf16[144,128]{1,0:T(8,128)(2,1)S(1)} %get-tuple-element.48), channel_id=1, source_target_pairs={{0,8},{1,9},{2,10},{3,11},{4,12},{5,13},{6,14},{7,15},{8,0},{9,1},... | collective-permute-start | bytes 110600 | tf_op jit(solution)/shard_map/ppermute | solution.py:277
  18.1 1.4 %collective-permute-start.11 = (bf16[144,128]{1,0:T(8,128)(2,1)S(1)}, bf16[144,128]{1,0:T(8,128)(2,1)S(1)}, u32[]{:S(2)}, u32[]{:S(2)}) collective-permute-start(bf16[144,128]{1,0:T(8,128)(2,1)S(1)} %get-tuple-element.49), channel_id=1, source_target_pairs={{0,4},{1,5},{2,6},{3,7},{4,0},{5,1},{6,2},{7,3},{8,12},{9,13},{10,... | collective-permute-start | bytes 110600 | tf_op jit(solution)/shard_map/ppermute | solution.py:277
  19.6 1.2 %collective-permute-start.9 = (bf16[144,128]{1,0:T(8,128)(2,1)S(1)}, bf16[144,128]{1,0:T(8,128)(2,1)S(1)}, u32[]{:S(2)}, u32[]{:S(2)}) collective-permute-start(bf16[144,128]{1,0:T(8,128)(2,1)S(1)} %get-tuple-element.47), channel_id=1, source_target_pairs={{0,12},{1,13},{2,14},{3,15},{4,8},{5,9},{6,10},{7,11},{8,4},{9,5},... | collective-permute-start | bytes 110600 | tf_op jit(solution)/shard_map/ppermute | solution.py:277
  20.8 0.5 %collective-permute-done.10.refs_2_ = bf16[144,128]{1,0:T(8,128)(2,1)S(1)} collective-permute-done((bf16[144,128]{1,0:T(8,128)(2,1)S(1)}, bf16[144,128]{1,0:T(8,128)(2,1)S(1)}, u32[]{:S(2)}, u32[]{:S(2)}) %collective-permute-start.10) | collective-permute-done | bytes 36896 | tf_op jit(solution)/shard_map/ppermute | solution.py:277
  21.3 0.8 %collective-permute-done.11.refs_3_ = bf16[144,128]{1,0:T(8,128)(2,1)S(1)} collective-permute-done((bf16[144,128]{1,0:T(8,128)(2,1)S(1)}, bf16[144,128]{1,0:T(8,128)(2,1)S(1)}, u32[]{:S(2)}, u32[]{:S(2)}) %collective-permute-start.11) | collective-permute-done | bytes 36896 | tf_op jit(solution)/shard_map/ppermute | solution.py:277
  22.1 3.2 %collective-permute-done.9.refs_1_ = bf16[144,128]{1,0:T(8,128)(2,1)S(1)} collective-permute-done((bf16[144,128]{1,0:T(8,128)(2,1)S(1)}, bf16[144,128]{1,0:T(8,128)(2,1)S(1)}, u32[]{:S(2)}, u32[]{:S(2)}) %collective-permute-start.9) | collective-permute-done | bytes 36896 | tf_op jit(solution)/shard_map/ppermute | solution.py:277
  25.3 0.0 collective-permute-done.8.refs_6_
  25.3 0.0 collective-permute-done.2.refs_7_
  25.3 0.0 collective-permute-start.12
  25.3 0.7 %shard_map.61 = (f32[2,32,128]{2,1,0:T(8,128)S(1)}, f32[2,8,2,8,128]{4,3,2,1,0:T(8,128)S(1)}) custom-call(f32[128,128]{1,0:T(8,128)S(1)} %get-tuple-element.50.refs_0_, bf16[144,128]{1,0:T(8,128)(2,1)S(1)} %collective-permute-done.9.refs_1_, bf16[144,128]{1,0:T(8,128)(2,1)S(1)} %collective-permute-done.10.refs_2_, ...), custom_call_target="tpu_custom_call" | custom-call | tf_op jit(solution)/shard_map/pallas_call | solution.py:247
  26.0 0.8 %collective-permute-done.12.queries_ref = bf16[4,8,4096]{2,1,0:T(8,128)(2,1)S(1)} collective-permute-done((bf16[4,8,4096]{2,1,0:T(8,128)(2,1)S(1)}, bf16[4,8,4096]{2,1,0:T(8,128)(2,1)S(1)}, u32[]{:S(2)}, u32[]{:S(2)}) %collective-permute-start.12) | collective-permute-done | bytes 262176 | tf_op jit(solution)/shard_map/ppermute | solution.py:277
  26.9 0.8 %shard_map.62 = f32[2,128]{1,0:T(2,128)} custom-call(f32[2,32,128]{2,1,0:T(8,128)S(1)} %get-tuple-element.57.grads_ref, f32[2,8,2,8,128]{4,3,2,1,0:T(8,128)S(1)} %get-tuple-element.58.before_ref, bf16[4,8,4096]{2,1,0:T(8,128)(2,1)S(1)} %collective-permute-done.12.queries_ref), custom_call_target="tpu_custom_call" | custom-call | tf_op jit(solution)/shard_map/pallas_call | solution.py:260
  (2 shorter events, 0.0 us)
Async XLA Ops:
  0.0 6.3 %copy-start.1 = (bf16[1792,64]{0,1:T(8,128)(2,1)S(1)}, bf16[1792,64]{0,1:T(8,128)(2,1)}, u32[]{:S(2)}) copy-start(bf16[1792,64]{0,1:T(8,128)(2,1)} %param.8) | copy-start | bytes 688132
  0.0 6.3 %copy-start = (bf16[1792,2048]{1,0:T(8,128)(2,1)S(1)}, bf16[1792,2048]{1,0:T(8,128)(2,1)}, u32[]{:S(2)}) copy-start(bf16[1792,2048]{1,0:T(8,128)(2,1)} %w_ref.1) | copy-start | bytes 22020100
  0.0 8.4 %collective-permute-start = (bf16[1,8,4096]{2,1,0:T(8,128)(2,1)}, bf16[1,8,4096]{2,1,0:T(8,128)(2,1)S(1)}, u32[]{:S(2)}, u32[]{:S(2)}) collective-permute-start(bf16[1,8,4096]{2,1,0:T(8,128)(2,1)} %bitcast.5), channel_id=1, source_target_pairs={{0,8},{1,9},{2,10},{3,11},{4,12},{5,13},{6,14},{7,15},{8,0},{9,1},... | collective-permute-start | bytes 196616 | tf_op jit(solution)/shard_map/ppermute | solution.py:277
  4.0 4.4 %copy-start.2 = (bf16[8,4096]{1,0:T(8,128)(2,1)S(1)}, bf16[8,4096]{1,0:T(8,128)(2,1)}, u32[]{:S(2)}) copy-start(bf16[8,4096]{1,0:T(8,128)(2,1)} %param.9) | copy-start | bytes 196612
  7.7 2.3 %collective-permute-start.3 = (f32[2,128,128]{2,1,0:T(8,128)S(1)}, f32[2,128,128]{2,1,0:T(8,128)S(1)}, u32[]{:S(2)}, u32[]{:S(2)}) collective-permute-start(f32[2,128,128]{2,1,0:T(8,128)S(1)} %get-tuple-element.36), channel_id=1, source_target_pairs={{0,1},{1,0},{2,3},{3,2},{4,5},{5,4},{6,7},{7,6},{8,9},{9,8},{10,11... | collective-permute-start | bytes 393224 | tf_op jit(solution)/shard_map/ppermute | solution.py:277
  7.8 2.2 %collective-permute-start.4 = (f32[2,128,128]{2,1,0:T(8,128)S(1)}, f32[2,128,128]{2,1,0:T(8,128)S(1)}, u32[]{:S(2)}, u32[]{:S(2)}) collective-permute-start(f32[2,128,128]{2,1,0:T(8,128)S(1)} %get-tuple-element.37), channel_id=1, source_target_pairs={{0,1},{1,0},{2,3},{3,2},{4,5},{5,4},{6,7},{7,6},{8,9},{9,8},{10,11... | collective-permute-start | bytes 393224 | tf_op jit(solution)/shard_map/ppermute | solution.py:277
  8.3 7.6 %collective-permute-start.6 = (f32[4,128,128]{2,1,0:T(8,128)S(1)}, f32[4,128,128]{2,1,0:T(8,128)S(1)}, u32[]{:S(2)}, u32[]{:S(2)}) collective-permute-start(f32[4,128,128]{2,1,0:T(8,128)S(1)} %get-tuple-element.38), channel_id=1, source_target_pairs={{0,1},{1,0},{2,3},{3,2},{4,5},{5,4},{6,7},{7,6},{8,9},{9,8},{10,11... | collective-permute-start | bytes 786440 | tf_op jit(solution)/shard_map/ppermute | solution.py:277
  8.4 5.9 %collective-permute-start.1 = (bf16[2,8,4096]{2,1,0:T(8,128)(2,1)S(1)}, bf16[2,8,4096]{2,1,0:T(8,128)(2,1)S(1)}, u32[]{:S(2)}, u32[]{:S(2)}) collective-permute-start(bf16[2,8,4096]{2,1,0:T(8,128)(2,1)S(1)} %shard_map.55.left_ref), channel_id=1, source_target_pairs={{0,4},{1,5},{2,6},{3,7},{4,0},{5,1},{6,2},{7,3},{8,12},{9,13},{10,... | collective-permute-start | bytes 393224 | tf_op jit(solution)/shard_map/ppermute | solution.py:277
  10.1 6.0 %collective-permute-start.5 = (bf16[4,144,128]{2,1,0:T(8,128)(2,1)S(1)}, bf16[4,144,128]{2,1,0:T(8,128)(2,1)S(1)}, u32[]{:S(2)}, u32[]{:S(2)}) collective-permute-start(bf16[4,144,128]{2,1,0:T(8,128)(2,1)S(1)} %shard_map.59), channel_id=1, source_target_pairs={{0,2},{1,3},{2,0},{3,1},{4,6},{5,7},{6,4},{7,5},{8,10},{9,11},{10,... | collective-permute-start | bytes 442376 | tf_op jit(solution)/shard_map/ppermute | solution.py:277
  11.7 4.2 %collective-permute-start.7 = (bf16[2,8,4096]{2,1,0:T(8,128)(2,1)S(1)}, bf16[2,8,4096]{2,1,0:T(8,128)(2,1)S(1)}, u32[]{:S(2)}, u32[]{:S(2)}) collective-permute-start(bf16[2,8,4096]{2,1,0:T(8,128)(2,1)S(1)} %shard_map.55.left_ref), channel_id=1, source_target_pairs={{0,1},{1,0},{2,3},{3,2},{4,5},{5,4},{6,7},{7,6},{8,9},{9,8},{10,11... | collective-permute-start | bytes 393224 | tf_op jit(solution)/shard_map/ppermute | solution.py:277
  14.3 11.0 %collective-permute-start.2 = (bf16[4,8,4096]{2,1,0:T(8,128)(2,1)S(1)}, bf16[4,8,4096]{2,1,0:T(8,128)(2,1)S(1)}, u32[]{:S(2)}, u32[]{:S(2)}) collective-permute-start(bf16[4,8,4096]{2,1,0:T(8,128)(2,1)S(1)} %shard_map.56.refs_4_), channel_id=1, source_target_pairs={{0,2},{1,3},{2,0},{3,1},{4,6},{5,7},{6,4},{7,5},{8,10},{9,11},{10,... | collective-permute-start | bytes 786440 | tf_op jit(solution)/shard_map/ppermute | solution.py:277
  16.2 9.1 %collective-permute-start.8 = (bf16[2,8,4096]{2,1,0:T(8,128)(2,1)S(1)}, bf16[2,8,4096]{2,1,0:T(8,128)(2,1)S(1)}, u32[]{:S(2)}, u32[]{:S(2)}) collective-permute-start(bf16[2,8,4096]{2,1,0:T(8,128)(2,1)S(1)} %collective-permute-done.1.right_ref), channel_id=1, source_target_pairs={{0,1},{1,0},{2,3},{3,2},{4,5},{5,4},{6,7},{7,6},{8,9},{9,8},{10,11... | collective-permute-start | bytes 393224 | tf_op jit(solution)/shard_map/ppermute | solution.py:277
  16.3 5.0 %collective-permute-start.10 = (bf16[144,128]{1,0:T(8,128)(2,1)S(1)}, bf16[144,128]{1,0:T(8,128)(2,1)S(1)}, u32[]{:S(2)}, u32[]{:S(2)}) collective-permute-start(bf16[144,128]{1,0:T(8,128)(2,1)S(1)} %get-tuple-element.48), channel_id=1, source_target_pairs={{0,8},{1,9},{2,10},{3,11},{4,12},{5,13},{6,14},{7,15},{8,0},{9,1},... | collective-permute-start | bytes 110600 | tf_op jit(solution)/shard_map/ppermute | solution.py:277
  18.1 4.0 %collective-permute-start.11 = (bf16[144,128]{1,0:T(8,128)(2,1)S(1)}, bf16[144,128]{1,0:T(8,128)(2,1)S(1)}, u32[]{:S(2)}, u32[]{:S(2)}) collective-permute-start(bf16[144,128]{1,0:T(8,128)(2,1)S(1)} %get-tuple-element.49), channel_id=1, source_target_pairs={{0,4},{1,5},{2,6},{3,7},{4,0},{5,1},{6,2},{7,3},{8,12},{9,13},{10,... | collective-permute-start | bytes 110600 | tf_op jit(solution)/shard_map/ppermute | solution.py:277
  19.6 5.8 %collective-permute-start.9 = (bf16[144,128]{1,0:T(8,128)(2,1)S(1)}, bf16[144,128]{1,0:T(8,128)(2,1)S(1)}, u32[]{:S(2)}, u32[]{:S(2)}) collective-permute-start(bf16[144,128]{1,0:T(8,128)(2,1)S(1)} %get-tuple-element.47), channel_id=1, source_target_pairs={{0,12},{1,13},{2,14},{3,15},{4,8},{5,9},{6,10},{7,11},{8,4},{9,5},... | collective-permute-start | bytes 110600 | tf_op jit(solution)/shard_map/ppermute | solution.py:277
  25.3 1.5 %collective-permute-start.12 = (bf16[4,8,4096]{2,1,0:T(8,128)(2,1)S(1)}, bf16[4,8,4096]{2,1,0:T(8,128)(2,1)S(1)}, u32[]{:S(2)}, u32[]{:S(2)}) collective-permute-start(bf16[4,8,4096]{2,1,0:T(8,128)(2,1)S(1)} %collective-permute-done.2.refs_7_), channel_id=1, source_target_pairs={{0,1},{1,0},{2,3},{3,2},{4,5},{5,4},{6,7},{7,6},{8,9},{9,8},{10,11... | collective-permute-start | bytes 786440 | tf_op jit(solution)/shard_map/ppermute | solution.py:277

commit v17 on v16

--- a/solution.py
+++ b/solution.py
@@ -10,6 +10,7 @@
 SEQ = 64
 VMEM_BYTES = 32 * 1024 * 1024
 LOADED_ROWS = 128
+PLAIN = 2
 LEFT_OVER = 0.36 * 2.0**-8
 LANES_BY_LANES = (((1,), (1,)), ((), ()))
 HBM_SPEC = pl.BlockSpec(memory_space=pltpu.HBM)
@@ -157,6 +158,9 @@
         if z == 0:
             for rows, total in sums:
                 own_ref[rows, :] = total
+        elif z <= PLAIN:
+            for rows, total in sums:
+                out_refs[len(out_refs) - z][rows, :] = total.astype(jnp.bfloat16)
         else:
             put_coded(out_refs[len(out_refs) - z], jnp.concatenate([total for _, total in reversed(sums)], axis=0))
 
@@ -164,10 +168,10 @@
 def add_kept(kept, came, across):
     depth, rows, width = kept.shape
     own = jax.ShapeDtypeStruct((rows, width), jnp.float32)
-    coded = jax.ShapeDtypeStruct((rows // 8 * 9, width), jnp.bfloat16)
+    heights = [rows if z <= PLAIN else rows // 8 * 9 for z in reversed(range(1, depth))]
     return pl.pallas_call(
         add_kept_kernel,
-        out_shape=[own] + [coded] * (depth - 1),
+        out_shape=[own] + [jax.ShapeDtypeStruct((height, width), jnp.bfloat16) for height in heights],
         compiler_params=PARAMS,
     )(kept, came, across)
 
@@ -210,6 +214,9 @@
     core = lax.rem(lax.axis_index("ex"), 2)
     total_ref[...] = part_refs[0][...]
     for part_ref in part_refs[1:]:
+        if part_ref.shape[0] == 2 * rank:
+            total_ref[...] += part_ref[...].astype(jnp.float32)
+            continue
         for rows, total in add_coded(lambda first, count: total_ref[first : first + count, :], part_ref):
             total_ref[rows, :] = total
     even = total_ref[pl.ds(rank, rank // 2, stride=2), :]

time: 27.8 us -> 26.4 us (0.950)
  waiting for transfers between devices: 8.15 us -> 6.72 us
    ppermute x13, waiting for transfers between devices: 8.15 us -> 6.72 us  [swap(): lax.ppermute(array, 'ex', [(i, i ^ distance) for i in range(devices)])]
  transfers between devices with their start and end apart: 13 -> 13, of which waited for: 6 -> 4; matrix products, arithmetic and copies ran while one was open for 0% -> 0% of each run, Pallas kernels for 17% -> 17%
where the time goes in v17:
time: 26.4 us; the launch traced here: 26.3 us
  starting transfers between devices  14.1 us (53%)
  waiting for transfers between devices  6.72 us (25%)
  Pallas kernels  5.36 us (20%)
    ppermute x13, starting transfers between devices, swap(): lax.ppermute(array, 'ex', [(i, i ^ distance) for i in range(devices)])  14.1 us
    ppermute x13, waiting for transfers between devices, swap(): lax.ppermute(array, 'ex', [(i, i ^ distance) for i in range(devices)])  6.72 us
    pallas_call x1, Pallas kernels, project_loaded(): pl.pallas_call(project_loaded_kernel, out_shape=[jax.ShapeDtypeStruct((ra...  2.22 us
    pallas_call x1, Pallas kernels, project(): pl.pallas_call(functools.partial(project_kernel, rows), out_shape=[half]...  1.43 us
    pallas_call x1, Pallas kernels, last_scores(): pl.pallas_call(functools.partial(last_score_kernel, chips), out_shape=jax...  0.81 us
    pallas_call x1, Pallas kernels, first_scores(): pl.pallas_call(functools.partial(first_score_kernel, len(parts), held), o...  0.68 us
  transfers between devices with their start and end apart: 13, of which 4 were waited for; matrix products, arithmetic and copies ran while one was open for 0% of the time, Pallas kernels for 17%

profile of v17, /device:TPU:0, one launch (start us, length us, event | category | flops | bytes accessed | tf_op | source)
XLA Modules:
  0.0 26.3 jit_solution(14443582018980851357)
XLA Ops:
  0.0 0.0 copy-start.1
  0.0 0.0 copy-start
  0.0 4.0 %collective-permute-start = (bf16[1,8,4096]{2,1,0:T(8,128)(2,1)}, bf16[1,8,4096]{2,1,0:T(8,128)(2,1)S(1)}, u32[]{:S(2)}, u32[]{:S(2)}) collective-permute-start(bf16[1,8,4096]{2,1,0:T(8,128)(2,1)} %bitcast.5), channel_id=1, source_target_pairs={{0,8},{1,9},{2,10},{3,11},{4,12},{5,13},{6,14},{7,15},{8,0},{9,1},... | collective-permute-start | bytes 196616 | tf_op jit(solution)/shard_map/ppermute | solution.py:284
  4.0 0.0 copy-start.2
  4.0 2.2 %shard_map.57 = (f32[64,2048]{1,0:T(8,128)S(1)}, f32[64,2048]{1,0:T(8,128)S(1)}) custom-call(bf16[512,2048]{1,0:T(8,128)(2,1)} %x_hbm.1, bf16[1792,2048]{1,0:T(8,128)(2,1)} %w_ref.1, bf16[64,512]{1,0:T(8,128)(2,1)} %bitcast.7, bf16[64,1792]{1,0:T(8,128)(2,1)} %bitcast.3), custom_call_target="tpu_custom_call" | custom-call | flops 167772160 | bytes 2621440 | tf_op jit(solution)/shard_map/pallas_call | solution.py:50
  6.3 0.0 copy-done.1
  6.3 0.0 copy-done
  6.3 1.4 %shard_map.58 = (f32[2,128,128]{2,1,0:T(8,128)S(1)}, f32[2,128,128]{2,1,0:T(8,128)S(1)}, f32[4,128,128]{2,1,0:T(8,128)S(1)}, f32[4,128,128]{2,1,0:T(8,128)S(1)}, f32[4,128,128]{2,1,0:T(8,128)S(1)}) custom-call(f32[64,2048]{1,0:T(8,128)S(1)} %get-tuple-element.32.low_in_ref, f32[64,2048]{1,0:T(8,128)S(1)} %get-tuple-element.33.low_out_ref, ...), custom_call_target="tpu_custom_call" | custom-call | flops 469762048 | bytes 7340032 | tf_op jit(solution)/shard_map/pallas_call | solution.py:99
  7.7 0.1 collective-permute-start.3
  7.8 0.5 %collective-permute-start.4 = (f32[2,128,128]{2,1,0:T(8,128)S(1)}, f32[2,128,128]{2,1,0:T(8,128)S(1)}, u32[]{:S(2)}, u32[]{:S(2)}) collective-permute-start(f32[2,128,128]{2,1,0:T(8,128)S(1)} %get-tuple-element.37), channel_id=1, source_target_pairs={{0,1},{1,0},{2,3},{3,2},{4,5},{5,4},{6,7},{7,6},{8,9},{9,8},{10,11... | collective-permute-start | bytes 393224 | tf_op jit(solution)/shard_map/ppermute | solution.py:284
  8.3 0.1 collective-permute-start.6
  8.4 0.0 collective-permute-done.right_ref
  8.4 0.0 copy-done.2
  8.4 1.6 %collective-permute-start.1 = (bf16[2,8,4096]{2,1,0:T(8,128)(2,1)S(1)}, bf16[2,8,4096]{2,1,0:T(8,128)(2,1)S(1)}, u32[]{:S(2)}, u32[]{:S(2)}) collective-permute-start(bf16[2,8,4096]{2,1,0:T(8,128)(2,1)S(1)} %shard_map.55.left_ref), channel_id=1, source_target_pairs={{0,4},{1,5},{2,6},{3,7},{4,0},{5,1},{6,2},{7,3},{8,12},{9,13},{10,... | collective-permute-start | bytes 393224 | tf_op jit(solution)/shard_map/ppermute | solution.py:284
  10.0 0.0 collective-permute-done.3.refs_0_
  10.0 0.0 collective-permute-done.4.refs_1_
  10.0 0.1 shard_map.59
  10.1 1.6 %collective-permute-start.5 = (bf16[4,144,128]{2,1,0:T(8,128)(2,1)S(1)}, bf16[4,144,128]{2,1,0:T(8,128)(2,1)S(1)}, u32[]{:S(2)}, u32[]{:S(2)}) collective-permute-start(bf16[4,144,128]{2,1,0:T(8,128)(2,1)S(1)} %shard_map.59), channel_id=1, source_target_pairs={{0,2},{1,3},{2,0},{3,1},{4,6},{5,7},{6,4},{7,5},{8,10},{9,11},{10,... | collective-permute-start | bytes 442376 | tf_op jit(solution)/shard_map/ppermute | solution.py:284
  11.7 0.0 collective-permute-start.7
  11.7 2.6 %collective-permute-done.1.right_ref = bf16[2,8,4096]{2,1,0:T(8,128)(2,1)S(1)} collective-permute-done((bf16[2,8,4096]{2,1,0:T(8,128)(2,1)S(1)}, bf16[2,8,4096]{2,1,0:T(8,128)(2,1)S(1)}, u32[]{:S(2)}, u32[]{:S(2)}) %collective-permute-start.1) | collective-permute-done | bytes 131104 | tf_op jit(solution)/shard_map/ppermute | solution.py:284
  14.3 1.6 %collective-permute-start.2 = (bf16[4,8,4096]{2,1,0:T(8,128)(2,1)S(1)}, bf16[4,8,4096]{2,1,0:T(8,128)(2,1)S(1)}, u32[]{:S(2)}, u32[]{:S(2)}) collective-permute-start(bf16[4,8,4096]{2,1,0:T(8,128)(2,1)S(1)} %shard_map.56.refs_4_), channel_id=1, source_target_pairs={{0,2},{1,3},{2,0},{3,1},{4,6},{5,7},{6,4},{7,5},{8,10},{9,11},{10,... | collective-permute-start | bytes 786440 | tf_op jit(solution)/shard_map/ppermute | solution.py:284
  15.9 0.0 collective-permute-done.7.refs_5_
  15.9 0.0 collective-permute-done.6.came_ref
  15.9 0.1 collective-permute-done.5.across_ref
  16.1 0.1 shard_map.60
  16.2 0.1 collective-permute-start.8
  16.3 2.7 %collective-permute-start.9 = (bf16[144,128]{1,0:T(8,128)(2,1)S(1)}, bf16[144,128]{1,0:T(8,128)(2,1)S(1)}, u32[]{:S(2)}, u32[]{:S(2)}) collective-permute-start(bf16[144,128]{1,0:T(8,128)(2,1)S(1)} %get-tuple-element.47), channel_id=1, source_target_pairs={{0,12},{1,13},{2,14},{3,15},{4,8},{5,9},{6,10},{7,11},{8,4},{9,5},... | collective-permute-start | bytes 110600 | tf_op jit(solution)/shard_map/ppermute | solution.py:284
  19.0 0.3 %collective-permute-start.10 = (bf16[128,128]{1,0:T(8,128)(2,1)S(1)}, bf16[128,128]{1,0:T(8,128)(2,1)S(1)}, u32[]{:S(2)}, u32[]{:S(2)}) collective-permute-start(bf16[128,128]{1,0:T(8,128)(2,1)S(1)} %get-tuple-element.48), channel_id=1, source_target_pairs={{0,8},{1,9},{2,10},{3,11},{4,12},{5,13},{6,14},{7,15},{8,0},{9,1},... | collective-permute-start | bytes 98312 | tf_op jit(solution)/shard_map/ppermute | solution.py:284
  19.3 1.5 %collective-permute-start.11 = (bf16[128,128]{1,0:T(8,128)(2,1)S(1)}, bf16[128,128]{1,0:T(8,128)(2,1)S(1)}, u32[]{:S(2)}, u32[]{:S(2)}) collective-permute-start(bf16[128,128]{1,0:T(8,128)(2,1)S(1)} %get-tuple-element.49), channel_id=1, source_target_pairs={{0,4},{1,5},{2,6},{3,7},{4,0},{5,1},{6,2},{7,3},{8,12},{9,13},{10,... | collective-permute-start | bytes 98312 | tf_op jit(solution)/shard_map/ppermute | solution.py:284
  20.8 3.1 %collective-permute-done.10.refs_2_ = bf16[128,128]{1,0:T(8,128)(2,1)S(1)} collective-permute-done((bf16[128,128]{1,0:T(8,128)(2,1)S(1)}, bf16[128,128]{1,0:T(8,128)(2,1)S(1)}, u32[]{:S(2)}, u32[]{:S(2)}) %collective-permute-start.10) | collective-permute-done | bytes 32800 | tf_op jit(solution)/shard_map/ppermute | solution.py:284
  23.8 0.0 collective-permute-done.11.refs_3_
  23.9 0.0 collective-permute-done.9.refs_1_
  23.9 0.0 collective-permute-done.8.refs_6_
  23.9 0.0 collective-permute-done.2.refs_7_
  23.9 0.1 collective-permute-start.12
  23.9 0.7 %shard_map.61 = (f32[2,32,128]{2,1,0:T(8,128)S(1)}, f32[2,8,2,8,128]{4,3,2,1,0:T(8,128)S(1)}) custom-call(f32[128,128]{1,0:T(8,128)S(1)} %get-tuple-element.50.refs_0_, bf16[144,128]{1,0:T(8,128)(2,1)S(1)} %collective-permute-done.9.refs_1_, bf16[128,128]{1,0:T(8,128)(2,1)S(1)} %collective-permute-done.10.refs_2_, ...), custom_call_target="tpu_custom_call" | custom-call | tf_op jit(solution)/shard_map/pallas_call | solution.py:254
  24.6 0.8 %collective-permute-done.12.queries_ref = bf16[4,8,4096]{2,1,0:T(8,128)(2,1)S(1)} collective-permute-done((bf16[4,8,4096]{2,1,0:T(8,128)(2,1)S(1)}, bf16[4,8,4096]{2,1,0:T(8,128)(2,1)S(1)}, u32[]{:S(2)}, u32[]{:S(2)}) %collective-permute-start.12) | collective-permute-done | bytes 262176 | tf_op jit(solution)/shard_map/ppermute | solution.py:284
  25.5 0.8 %shard_map.62 = f32[2,128]{1,0:T(2,128)} custom-call(f32[2,32,128]{2,1,0:T(8,128)S(1)} %get-tuple-element.57.grads_ref, f32[2,8,2,8,128]{4,3,2,1,0:T(8,128)S(1)} %get-tuple-element.58.before_ref, bf16[4,8,4096]{2,1,0:T(8,128)(2,1)S(1)} %collective-permute-done.12.queries_ref), custom_call_target="tpu_custom_call" | custom-call | tf_op jit(solution)/shard_map/pallas_call | solution.py:267
  (2 shorter events, 0.0 us)
Async XLA Ops:
  0.0 6.3 %copy-start.1 = (bf16[1792,64]{0,1:T(8,128)(2,1)S(1)}, bf16[1792,64]{0,1:T(8,128)(2,1)}, u32[]{:S(2)}) copy-start(bf16[1792,64]{0,1:T(8,128)(2,1)} %param.8) | copy-start | bytes 688132
  0.0 6.3 %copy-start = (bf16[1792,2048]{1,0:T(8,128)(2,1)S(1)}, bf16[1792,2048]{1,0:T(8,128)(2,1)}, u32[]{:S(2)}) copy-start(bf16[1792,2048]{1,0:T(8,128)(2,1)} %w_ref.1) | copy-start | bytes 22020100
  0.0 8.4 %collective-permute-start = (bf16[1,8,4096]{2,1,0:T(8,128)(2,1)}, bf16[1,8,4096]{2,1,0:T(8,128)(2,1)S(1)}, u32[]{:S(2)}, u32[]{:S(2)}) collective-permute-start(bf16[1,8,4096]{2,1,0:T(8,128)(2,1)} %bitcast.5), channel_id=1, source_target_pairs={{0,8},{1,9},{2,10},{3,11},{4,12},{5,13},{6,14},{7,15},{8,0},{9,1},... | collective-permute-start | bytes 196616 | tf_op jit(solution)/shard_map/ppermute | solution.py:284
  4.0 4.4 %copy-start.2 = (bf16[8,4096]{1,0:T(8,128)(2,1)S(1)}, bf16[8,4096]{1,0:T(8,128)(2,1)}, u32[]{:S(2)}) copy-start(bf16[8,4096]{1,0:T(8,128)(2,1)} %param.9) | copy-start | bytes 196612
  7.7 2.3 %collective-permute-start.3 = (f32[2,128,128]{2,1,0:T(8,128)S(1)}, f32[2,128,128]{2,1,0:T(8,128)S(1)}, u32[]{:S(2)}, u32[]{:S(2)}) collective-permute-start(f32[2,128,128]{2,1,0:T(8,128)S(1)} %get-tuple-element.36), channel_id=1, source_target_pairs={{0,1},{1,0},{2,3},{3,2},{4,5},{5,4},{6,7},{7,6},{8,9},{9,8},{10,11... | collective-permute-start | bytes 393224 | tf_op jit(solution)/shard_map/ppermute | solution.py:284
  7.8 2.2 %collective-permute-start.4 = (f32[2,128,128]{2,1,0:T(8,128)S(1)}, f32[2,128,128]{2,1,0:T(8,128)S(1)}, u32[]{:S(2)}, u32[]{:S(2)}) collective-permute-start(f32[2,128,128]{2,1,0:T(8,128)S(1)} %get-tuple-element.37), channel_id=1, source_target_pairs={{0,1},{1,0},{2,3},{3,2},{4,5},{5,4},{6,7},{7,6},{8,9},{9,8},{10,11... | collective-permute-start | bytes 393224 | tf_op jit(solution)/shard_map/ppermute | solution.py:284
  8.3 7.6 %collective-permute-start.6 = (f32[4,128,128]{2,1,0:T(8,128)S(1)}, f32[4,128,128]{2,1,0:T(8,128)S(1)}, u32[]{:S(2)}, u32[]{:S(2)}) collective-permute-start(f32[4,128,128]{2,1,0:T(8,128)S(1)} %get-tuple-element.38), channel_id=1, source_target_pairs={{0,1},{1,0},{2,3},{3,2},{4,5},{5,4},{6,7},{7,6},{8,9},{9,8},{10,11... | collective-permute-start | bytes 786440 | tf_op jit(solution)/shard_map/ppermute | solution.py:284
  8.4 5.9 %collective-permute-start.1 = (bf16[2,8,4096]{2,1,0:T(8,128)(2,1)S(1)}, bf16[2,8,4096]{2,1,0:T(8,128)(2,1)S(1)}, u32[]{:S(2)}, u32[]{:S(2)}) collective-permute-start(bf16[2,8,4096]{2,1,0:T(8,128)(2,1)S(1)} %shard_map.55.left_ref), channel_id=1, source_target_pairs={{0,4},{1,5},{2,6},{3,7},{4,0},{5,1},{6,2},{7,3},{8,12},{9,13},{10,... | collective-permute-start | bytes 393224 | tf_op jit(solution)/shard_map/ppermute | solution.py:284
  10.1 6.0 %collective-permute-start.5 = (bf16[4,144,128]{2,1,0:T(8,128)(2,1)S(1)}, bf16[4,144,128]{2,1,0:T(8,128)(2,1)S(1)}, u32[]{:S(2)}, u32[]{:S(2)}) collective-permute-start(bf16[4,144,128]{2,1,0:T(8,128)(2,1)S(1)} %shard_map.59), channel_id=1, source_target_pairs={{0,2},{1,3},{2,0},{3,1},{4,6},{5,7},{6,4},{7,5},{8,10},{9,11},{10,... | collective-permute-start | bytes 442376 | tf_op jit(solution)/shard_map/ppermute | solution.py:284
  11.7 4.2 %collective-permute-start.7 = (bf16[2,8,4096]{2,1,0:T(8,128)(2,1)S(1)}, bf16[2,8,4096]{2,1,0:T(8,128)(2,1)S(1)}, u32[]{:S(2)}, u32[]{:S(2)}) collective-permute-start(bf16[2,8,4096]{2,1,0:T(8,128)(2,1)S(1)} %shard_map.55.left_ref), channel_id=1, source_target_pairs={{0,1},{1,0},{2,3},{3,2},{4,5},{5,4},{6,7},{7,6},{8,9},{9,8},{10,11... | collective-permute-start | bytes 393224 | tf_op jit(solution)/shard_map/ppermute | solution.py:284
  14.3 9.5 %collective-permute-start.2 = (bf16[4,8,4096]{2,1,0:T(8,128)(2,1)S(1)}, bf16[4,8,4096]{2,1,0:T(8,128)(2,1)S(1)}, u32[]{:S(2)}, u32[]{:S(2)}) collective-permute-start(bf16[4,8,4096]{2,1,0:T(8,128)(2,1)S(1)} %shard_map.56.refs_4_), channel_id=1, source_target_pairs={{0,2},{1,3},{2,0},{3,1},{4,6},{5,7},{6,4},{7,5},{8,10},{9,11},{10,... | collective-permute-start | bytes 786440 | tf_op jit(solution)/shard_map/ppermute | solution.py:284
  16.2 7.6 %collective-permute-start.8 = (bf16[2,8,4096]{2,1,0:T(8,128)(2,1)S(1)}, bf16[2,8,4096]{2,1,0:T(8,128)(2,1)S(1)}, u32[]{:S(2)}, u32[]{:S(2)}) collective-permute-start(bf16[2,8,4096]{2,1,0:T(8,128)(2,1)S(1)} %collective-permute-done.1.right_ref), channel_id=1, source_target_pairs={{0,1},{1,0},{2,3},{3,2},{4,5},{5,4},{6,7},{7,6},{8,9},{9,8},{10,11... | collective-permute-start | bytes 393224 | tf_op jit(solution)/shard_map/ppermute | solution.py:284
  16.3 7.6 %collective-permute-start.9 = (bf16[144,128]{1,0:T(8,128)(2,1)S(1)}, bf16[144,128]{1,0:T(8,128)(2,1)S(1)}, u32[]{:S(2)}, u32[]{:S(2)}) collective-permute-start(bf16[144,128]{1,0:T(8,128)(2,1)S(1)} %get-tuple-element.47), channel_id=1, source_target_pairs={{0,12},{1,13},{2,14},{3,15},{4,8},{5,9},{6,10},{7,11},{8,4},{9,5},... | collective-permute-start | bytes 110600 | tf_op jit(solution)/shard_map/ppermute | solution.py:284
  19.0 4.9 %collective-permute-start.10 = (bf16[128,128]{1,0:T(8,128)(2,1)S(1)}, bf16[128,128]{1,0:T(8,128)(2,1)S(1)}, u32[]{:S(2)}, u32[]{:S(2)}) collective-permute-start(bf16[128,128]{1,0:T(8,128)(2,1)S(1)} %get-tuple-element.48), channel_id=1, source_target_pairs={{0,8},{1,9},{2,10},{3,11},{4,12},{5,13},{6,14},{7,15},{8,0},{9,1},... | collective-permute-start | bytes 98312 | tf_op jit(solution)/shard_map/ppermute | solution.py:284
  19.3 4.6 %collective-permute-start.11 = (bf16[128,128]{1,0:T(8,128)(2,1)S(1)}, bf16[128,128]{1,0:T(8,128)(2,1)S(1)}, u32[]{:S(2)}, u32[]{:S(2)}) collective-permute-start(bf16[128,128]{1,0:T(8,128)(2,1)S(1)} %get-tuple-element.49), channel_id=1, source_target_pairs={{0,4},{1,5},{2,6},{3,7},{4,0},{5,1},{6,2},{7,3},{8,12},{9,13},{10,... | collective-permute-start | bytes 98312 | tf_op jit(solution)/shard_map/ppermute | solution.py:284
  23.9 1.6 %collective-permute-start.12 = (bf16[4,8,4096]{2,1,0:T(8,128)(2,1)S(1)}, bf16[4,8,4096]{2,1,0:T(8,128)(2,1)S(1)}, u32[]{:S(2)}, u32[]{:S(2)}) collective-permute-start(bf16[4,8,4096]{2,1,0:T(8,128)(2,1)S(1)} %collective-permute-done.2.refs_7_), channel_id=1, source_target_pairs={{0,1},{1,0},{2,3},{3,2},{4,5},{5,4},{6,7},{7,6},{8,9},{9,8},{10,11... | collective-permute-start | bytes 786440 | tf_op jit(solution)/shard_map/ppermute | solution.py:284

commit v18 on v17

--- a/solution.py
+++ b/solution.py
@@ -69,24 +69,22 @@
     )(*arrays)
 
 
-def project_kernel(done, low_in_ref, low_out_ref, p_ref, w_ref, *refs):
-    *given, kept_y, kept_here = refs
-    given_y, given_here = given[:-1], given[-1:]
+def project_kernel(done, flip, low_in_ref, low_out_ref, p_ref, w_ref, *refs):
+    *given_refs, kept_ref = refs
     here = lax.axis_index("ex")
     core, chip = lax.rem(here, 2), lax.div(here, 2)
-    depth = kept_y.shape[0]
-    rank, width = kept_y.shape[1] // 2, kept_y.shape[2]
-    for flip, given_refs, kept_ref in ((1, given_y, kept_y), (0, given_here, kept_here)):
-        for z in range(depth):
-            place = lax.bitwise_xor(chip, 2 * z + flip)
-            columns = pl.ds(pl.multiple_of(place * 2 * width, 2 * width), 2 * width)
-            low_out = jnp.dot(p_ref[:, done:], w_ref[done:, columns], preferred_element_type=jnp.float32)
-            low_out = low_out + low_out_ref[:, columns]
-            given_ref = given_refs[z * len(given_refs) // depth]
-            for lines, low in ((slice(0, rank), low_in_ref[:, columns]), (slice(rank, 2 * rank), low_out)):
-                left, right = low[:, :width], low[:, width:]
-                given_ref[z % given_ref.shape[0], lines, :] = jnp.where(core == 0, right, left)
-                kept_ref[z, lines, :] = jnp.where(core == 0, left, right)
+    depth = kept_ref.shape[0]
+    rank, width = kept_ref.shape[1] // 2, kept_ref.shape[2]
+    for z in range(depth):
+        place = lax.bitwise_xor(chip, 2 * z + flip)
+        columns = pl.ds(pl.multiple_of(place * 2 * width, 2 * width), 2 * width)
+        low_out = jnp.dot(p_ref[:, done:], w_ref[done:, columns], preferred_element_type=jnp.float32)
+        low_out = low_out + low_out_ref[:, columns]
+        given_ref = given_refs[z * len(given_refs) // depth]
+        for lines, low in ((slice(0, rank), low_in_ref[:, columns]), (slice(rank, 2 * rank), low_out)):
+            left, right = low[:, :width], low[:, width:]
+            given_ref[z % given_ref.shape[0], lines, :] = jnp.where(core == 0, right, left)
+            kept_ref[z, lines, :] = jnp.where(core == 0, left, right)
 
 
 def project(inputs, out_grads, proj_in_t, proj_out_t, devices):
@@ -94,18 +92,23 @@
     units = out_grads.shape[0]
     rows = LOADED_ROWS if units % LOADED_ROWS == 0 else 16
     lows = project_loaded(inputs, out_grads, proj_in_t, proj_out_t, rows)
-    low = jax.ShapeDtypeStruct((devices // 4, 2 * rank, width), jnp.float32)
-    half = jax.ShapeDtypeStruct((devices // 8, 2 * rank, width), jnp.float32)
-    return pl.pallas_call(
-        functools.partial(project_kernel, rows),
-        out_shape=[half] * 2 + [low] * 3,
-        in_specs=[VMEM_SPEC] * 4,
-        out_specs=[VMEM_SPEC] * 5,
-        compiler_params=PARAMS,
-        cost_estimate=pl.CostEstimate(
-            flops=2 * rank * out_grads.size, bytes_accessed=2 * out_grads.size, transcendentals=0
-        ),
-    )(*lows, proj_out_t, out_grads)
+
+    def part(flip, given_count):
+        low = jax.ShapeDtypeStruct((devices // 4, 2 * rank, width), jnp.float32)
+        given = jax.ShapeDtypeStruct((devices // 4 // given_count, 2 * rank, width), jnp.float32)
+        *given, kept = pl.pallas_call(
+            functools.partial(project_kernel, rows, flip),
+            out_shape=[given] * given_count + [low],
+            in_specs=[VMEM_SPEC] * 4,
+            out_specs=[VMEM_SPEC] * (given_count + 1),
+            compiler_params=PARAMS,
+            cost_estimate=pl.CostEstimate(
+                flops=rank * out_grads.size, bytes_accessed=out_grads.size, transcendentals=0
+            ),
+        )(*lows, proj_out_t, out_grads)
+        return given, kept
+
+    return part(1, 2), part(0, 1)
 
 
 def put_coded(out_ref, low):
@@ -286,10 +289,9 @@
     steps = [1 << bit for bit in reversed(range(chips.bit_length() - 1))]
     held, reach = queries[None], [0]
     came_held = swap(held, chip=steps[0])
-    lows = project(inputs, out_grads, proj_in.T, proj_out.T, devices)
-    *given_y, given, kept_y, kept = lows
+    (given_y, kept_y), (given, kept) = project(inputs, out_grads, proj_in.T, proj_out.T, devices)
     came_y = [swap(array, core=1) for array in given_y]
-    came = swap(given, core=1)
+    came = swap(given[0], core=1)
     for last, step in zip(steps, steps[1:-1]):
         held, reach = stack(held, came_held), reach + [chip ^ last for chip in reach]
         came_held = swap(held, chip=step)

time: 26.4 us -> 26.6 us (level)
    pallas_call x1 -> x2, Pallas kernels: 1.43 us -> 1.54 us  [part(): pl.pallas_call(functools.partial(project_kernel, rows, flip), out_shape=[...]
  transfers between devices with their start and end apart: 13 -> 13, of which waited for: 4 -> 4; matrix products, arithmetic and copies ran while one was open for 0% -> 0% of each run, Pallas kernels for 17% -> 18%
where the time goes in v18:
time: 26.6 us; the launch traced here: 26.5 us
  starting transfers between devices  14.2 us (53%)
  waiting for transfers between devices  6.71 us (25%)
  Pallas kernels  5.48 us (21%)
    ppermute x13, starting transfers between devices, swap(): lax.ppermute(array, 'ex', [(i, i ^ distance) for i in range(devices)])  14.2 us
    ppermute x13, waiting for transfers between devices, swap(): lax.ppermute(array, 'ex', [(i, i ^ distance) for i in range(devices)])  6.71 us
    pallas_call x1, Pallas kernels, project_loaded(): pl.pallas_call(project_loaded_kernel, out_shape=[jax.ShapeDtypeStruct((ra...  2.23 us
    pallas_call x2, Pallas kernels, part(): pl.pallas_call(functools.partial(project_kernel, rows, flip), out_shape=[...  1.54 us
    pallas_call x1, Pallas kernels, last_scores(): pl.pallas_call(functools.partial(last_score_kernel, chips), out_shape=jax...  0.81 us
    pallas_call x1, Pallas kernels, first_scores(): pl.pallas_call(functools.partial(first_score_kernel, len(parts), held), o...  0.68 us
  transfers between devices with their start and end apart: 13, of which 4 were waited for; matrix products, arithmetic and copies ran while one was open for 0% of the time, Pallas kernels for 18%

profile of v18, /device:TPU:0, one launch (start us, length us, event | category | flops | bytes accessed | tf_op | source)
XLA Modules:
  0.0 26.5 jit_solution(17018201299369969880)
XLA Ops:
  0.0 0.0 copy-start.1
  0.0 0.0 copy-start
  0.0 4.0 %collective-permute-start = (bf16[1,8,4096]{2,1,0:T(8,128)(2,1)}, bf16[1,8,4096]{2,1,0:T(8,128)(2,1)S(1)}, u32[]{:S(2)}, u32[]{:S(2)}) collective-permute-start(bf16[1,8,4096]{2,1,0:T(8,128)(2,1)} %bitcast.6), channel_id=1, source_target_pairs={{0,8},{1,9},{2,10},{3,11},{4,12},{5,13},{6,14},{7,15},{8,0},{9,1},... | collective-permute-start | bytes 196616 | tf_op jit(solution)/shard_map/ppermute | solution.py:287
  4.0 2.2 %shard_map.57 = (f32[64,2048]{1,0:T(8,128)S(1)}, f32[64,2048]{1,0:T(8,128)S(1)}) custom-call(bf16[512,2048]{1,0:T(8,128)(2,1)} %x_hbm.1, bf16[1792,2048]{1,0:T(8,128)(2,1)} %w_ref.3, bf16[64,512]{1,0:T(8,128)(2,1)} %bitcast.8, bf16[64,1792]{1,0:T(8,128)(2,1)} %bitcast.3), custom_call_target="tpu_custom_call" | custom-call | flops 167772160 | bytes 2621440 | tf_op jit(solution)/shard_map/pallas_call | solution.py:50
  6.3 0.0 copy-done.1
  6.3 0.0 copy-done
  6.3 0.0 copy-start.2
  6.3 0.8 %shard_map.59 = (f32[2,128,128]{2,1,0:T(8,128)S(1)}, f32[2,128,128]{2,1,0:T(8,128)S(1)}, f32[4,128,128]{2,1,0:T(8,128)S(1)}) custom-call(f32[64,2048]{1,0:T(8,128)S(1)} %get-tuple-element.32.low_in_ref, f32[64,2048]{1,0:T(8,128)S(1)} %get-tuple-element.33.low_out_ref, bf16[64,1792]{1,0:T(8,128)(2,1)S(1)} %bitcast.4, bf16[1792,2048]{1,0:T(8,128)(2,1)S(1)} %copy-done), custom_call_target="tpu_custom_call" | custom-call | flops 234881024 | bytes 3670016 | tf_op jit(solution)/shard_map/pallas_call | solution.py:99
  7.1 0.1 collective-permute-start.3
  7.2 0.5 %collective-permute-start.4 = (f32[2,128,128]{2,1,0:T(8,128)S(1)}, f32[2,128,128]{2,1,0:T(8,128)S(1)}, u32[]{:S(2)}, u32[]{:S(2)}) collective-permute-start(f32[2,128,128]{2,1,0:T(8,128)S(1)} %get-tuple-element.37), channel_id=1, source_target_pairs={{0,1},{1,0},{2,3},{3,2},{4,5},{5,4},{6,7},{7,6},{8,9},{9,8},{10,11... | collective-permute-start | bytes 393224 | tf_op jit(solution)/shard_map/ppermute | solution.py:287
  7.7 0.8 %shard_map.58 = (f32[4,128,128]{2,1,0:T(8,128)S(1)}, f32[4,128,128]{2,1,0:T(8,128)S(1)}) custom-call(f32[64,2048]{1,0:T(8,128)S(1)} %get-tuple-element.32.low_in_ref, f32[64,2048]{1,0:T(8,128)S(1)} %get-tuple-element.33.low_out_ref, bf16[64,1792]{1,0:T(8,128)(2,1)S(1)} %bitcast.5, bf16[1792,2048]{1,0:T(8,128)(2,1)S(1)} %copy-done), custom_call_target="tpu_custom_call" | custom-call | flops 234881024 | bytes 3670016 | tf_op jit(solution)/shard_map/pallas_call | solution.py:99
  8.4 0.1 collective-permute-start.6
  8.6 0.0 collective-permute-done.right_ref
  8.6 0.0 copy-done.2
  8.6 1.6 %collective-permute-start.1 = (bf16[2,8,4096]{2,1,0:T(8,128)(2,1)S(1)}, bf16[2,8,4096]{2,1,0:T(8,128)(2,1)S(1)}, u32[]{:S(2)}, u32[]{:S(2)}) collective-permute-start(bf16[2,8,4096]{2,1,0:T(8,128)(2,1)S(1)} %shard_map.55.left_ref), channel_id=1, source_target_pairs={{0,4},{1,5},{2,6},{3,7},{4,0},{5,1},{6,2},{7,3},{8,12},{9,13},{10,... | collective-permute-start | bytes 393224 | tf_op jit(solution)/shard_map/ppermute | solution.py:287
  10.2 0.0 collective-permute-done.3.refs_0_
  10.2 0.0 collective-permute-done.4.refs_1_
  10.2 0.1 shard_map.60
  10.3 1.6 %collective-permute-start.5 = (bf16[4,144,128]{2,1,0:T(8,128)(2,1)S(1)}, bf16[4,144,128]{2,1,0:T(8,128)(2,1)S(1)}, u32[]{:S(2)}, u32[]{:S(2)}) collective-permute-start(bf16[4,144,128]{2,1,0:T(8,128)(2,1)S(1)} %shard_map.60), channel_id=1, source_target_pairs={{0,2},{1,3},{2,0},{3,1},{4,6},{5,7},{6,4},{7,5},{8,10},{9,11},{10,... | collective-permute-start | bytes 442376 | tf_op jit(solution)/shard_map/ppermute | solution.py:287
  11.9 0.0 collective-permute-start.7
  11.9 2.6 %collective-permute-done.1.right_ref = bf16[2,8,4096]{2,1,0:T(8,128)(2,1)S(1)} collective-permute-done((bf16[2,8,4096]{2,1,0:T(8,128)(2,1)S(1)}, bf16[2,8,4096]{2,1,0:T(8,128)(2,1)S(1)}, u32[]{:S(2)}, u32[]{:S(2)}) %collective-permute-start.1) | collective-permute-done | bytes 131104 | tf_op jit(solution)/shard_map/ppermute | solution.py:287
  14.5 1.6 %collective-permute-start.2 = (bf16[4,8,4096]{2,1,0:T(8,128)(2,1)S(1)}, bf16[4,8,4096]{2,1,0:T(8,128)(2,1)S(1)}, u32[]{:S(2)}, u32[]{:S(2)}) collective-permute-start(bf16[4,8,4096]{2,1,0:T(8,128)(2,1)S(1)} %shard_map.56.refs_4_), channel_id=1, source_target_pairs={{0,2},{1,3},{2,0},{3,1},{4,6},{5,7},{6,4},{7,5},{8,10},{9,11},{10,... | collective-permute-start | bytes 786440 | tf_op jit(solution)/shard_map/ppermute | solution.py:287
  16.1 0.0 collective-permute-done.7.refs_5_
  16.1 0.0 collective-permute-done.6.came_ref
  16.1 0.2 collective-permute-done.5.across_ref
  16.3 0.1 shard_map.61
  16.4 0.1 collective-permute-start.8
  16.5 2.7 %collective-permute-start.9 = (bf16[144,128]{1,0:T(8,128)(2,1)S(1)}, bf16[144,128]{1,0:T(8,128)(2,1)S(1)}, u32[]{:S(2)}, u32[]{:S(2)}) collective-permute-start(bf16[144,128]{1,0:T(8,128)(2,1)S(1)} %get-tuple-element.47), channel_id=1, source_target_pairs={{0,12},{1,13},{2,14},{3,15},{4,8},{5,9},{6,10},{7,11},{8,4},{9,5},... | collective-permute-start | bytes 110600 | tf_op jit(solution)/shard_map/ppermute | solution.py:287
  19.2 0.3 %collective-permute-start.10 = (bf16[128,128]{1,0:T(8,128)(2,1)S(1)}, bf16[128,128]{1,0:T(8,128)(2,1)S(1)}, u32[]{:S(2)}, u32[]{:S(2)}) collective-permute-start(bf16[128,128]{1,0:T(8,128)(2,1)S(1)} %get-tuple-element.48), channel_id=1, source_target_pairs={{0,8},{1,9},{2,10},{3,11},{4,12},{5,13},{6,14},{7,15},{8,0},{9,1},... | collective-permute-start | bytes 98312 | tf_op jit(solution)/shard_map/ppermute | solution.py:287
  19.4 1.5 %collective-permute-start.11 = (bf16[128,128]{1,0:T(8,128)(2,1)S(1)}, bf16[128,128]{1,0:T(8,128)(2,1)S(1)}, u32[]{:S(2)}, u32[]{:S(2)}) collective-permute-start(bf16[128,128]{1,0:T(8,128)(2,1)S(1)} %get-tuple-element.49), channel_id=1, source_target_pairs={{0,4},{1,5},{2,6},{3,7},{4,0},{5,1},{6,2},{7,3},{8,12},{9,13},{10,... | collective-permute-start | bytes 98312 | tf_op jit(solution)/shard_map/ppermute | solution.py:287
  21.0 3.1 %collective-permute-done.10.refs_2_ = bf16[128,128]{1,0:T(8,128)(2,1)S(1)} collective-permute-done((bf16[128,128]{1,0:T(8,128)(2,1)S(1)}, bf16[128,128]{1,0:T(8,128)(2,1)S(1)}, u32[]{:S(2)}, u32[]{:S(2)}) %collective-permute-start.10) | collective-permute-done | bytes 32800 | tf_op jit(solution)/shard_map/ppermute | solution.py:287
  24.0 0.0 collective-permute-done.11.refs_3_
  24.0 0.0 collective-permute-done.9.refs_1_
  24.0 0.0 collective-permute-done.8.refs_6_
  24.1 0.0 collective-permute-done.2.refs_7_
  24.1 0.1 collective-permute-start.12
  24.1 0.7 %shard_map.62 = (f32[2,32,128]{2,1,0:T(8,128)S(1)}, f32[2,8,2,8,128]{4,3,2,1,0:T(8,128)S(1)}) custom-call(f32[128,128]{1,0:T(8,128)S(1)} %get-tuple-element.50.refs_0_, bf16[144,128]{1,0:T(8,128)(2,1)S(1)} %collective-permute-done.9.refs_1_, bf16[128,128]{1,0:T(8,128)(2,1)S(1)} %collective-permute-done.10.refs_2_, ...), custom_call_target="tpu_custom_call" | custom-call | tf_op jit(solution)/shard_map/pallas_call | solution.py:257
  24.8 0.8 %collective-permute-done.12.queries_ref = bf16[4,8,4096]{2,1,0:T(8,128)(2,1)S(1)} collective-permute-done((bf16[4,8,4096]{2,1,0:T(8,128)(2,1)S(1)}, bf16[4,8,4096]{2,1,0:T(8,128)(2,1)S(1)}, u32[]{:S(2)}, u32[]{:S(2)}) %collective-permute-start.12) | collective-permute-done | bytes 262176 | tf_op jit(solution)/shard_map/ppermute | solution.py:287
  25.7 0.8 %shard_map.63 = f32[2,128]{1,0:T(2,128)} custom-call(f32[2,32,128]{2,1,0:T(8,128)S(1)} %get-tuple-element.57.grads_ref, f32[2,8,2,8,128]{4,3,2,1,0:T(8,128)S(1)} %get-tuple-element.58.before_ref, bf16[4,8,4096]{2,1,0:T(8,128)(2,1)S(1)} %collective-permute-done.12.queries_ref), custom_call_target="tpu_custom_call" | custom-call | tf_op jit(solution)/shard_map/pallas_call | solution.py:270
  (2 shorter events, 0.0 us)
Async XLA Ops:
  0.0 6.3 %copy-start.1 = (bf16[1792,64]{0,1:T(8,128)(2,1)S(1)}, bf16[1792,64]{0,1:T(8,128)(2,1)}, u32[]{:S(2)}) copy-start(bf16[1792,64]{0,1:T(8,128)(2,1)} %param.8) | copy-start | bytes 688132
  0.0 6.3 %copy-start = (bf16[1792,2048]{1,0:T(8,128)(2,1)S(1)}, bf16[1792,2048]{1,0:T(8,128)(2,1)}, u32[]{:S(2)}) copy-start(bf16[1792,2048]{1,0:T(8,128)(2,1)} %w_ref.3) | copy-start | bytes 22020100
  0.0 8.6 %collective-permute-start = (bf16[1,8,4096]{2,1,0:T(8,128)(2,1)}, bf16[1,8,4096]{2,1,0:T(8,128)(2,1)S(1)}, u32[]{:S(2)}, u32[]{:S(2)}) collective-permute-start(bf16[1,8,4096]{2,1,0:T(8,128)(2,1)} %bitcast.6), channel_id=1, source_target_pairs={{0,8},{1,9},{2,10},{3,11},{4,12},{5,13},{6,14},{7,15},{8,0},{9,1},... | collective-permute-start | bytes 196616 | tf_op jit(solution)/shard_map/ppermute | solution.py:287
  6.3 2.3 %copy-start.2 = (bf16[8,4096]{1,0:T(8,128)(2,1)S(1)}, bf16[8,4096]{1,0:T(8,128)(2,1)}, u32[]{:S(2)}) copy-start(bf16[8,4096]{1,0:T(8,128)(2,1)} %param.9) | copy-start | bytes 196612
  7.1 3.1 %collective-permute-start.3 = (f32[2,128,128]{2,1,0:T(8,128)S(1)}, f32[2,128,128]{2,1,0:T(8,128)S(1)}, u32[]{:S(2)}, u32[]{:S(2)}) collective-permute-start(f32[2,128,128]{2,1,0:T(8,128)S(1)} %get-tuple-element.36), channel_id=1, source_target_pairs={{0,1},{1,0},{2,3},{3,2},{4,5},{5,4},{6,7},{7,6},{8,9},{9,8},{10,11... | collective-permute-start | bytes 393224 | tf_op jit(solution)/shard_map/ppermute | solution.py:287
  7.2 3.1 %collective-permute-start.4 = (f32[2,128,128]{2,1,0:T(8,128)S(1)}, f32[2,128,128]{2,1,0:T(8,128)S(1)}, u32[]{:S(2)}, u32[]{:S(2)}) collective-permute-start(f32[2,128,128]{2,1,0:T(8,128)S(1)} %get-tuple-element.37), channel_id=1, source_target_pairs={{0,1},{1,0},{2,3},{3,2},{4,5},{5,4},{6,7},{7,6},{8,9},{9,8},{10,11... | collective-permute-start | bytes 393224 | tf_op jit(solution)/shard_map/ppermute | solution.py:287
  8.4 7.7 %collective-permute-start.6 = (f32[4,128,128]{2,1,0:T(8,128)S(1)}, f32[4,128,128]{2,1,0:T(8,128)S(1)}, u32[]{:S(2)}, u32[]{:S(2)}) collective-permute-start(f32[4,128,128]{2,1,0:T(8,128)S(1)} %get-tuple-element.38), channel_id=1, source_target_pairs={{0,1},{1,0},{2,3},{3,2},{4,5},{5,4},{6,7},{7,6},{8,9},{9,8},{10,11... | collective-permute-start | bytes 786440 | tf_op jit(solution)/shard_map/ppermute | solution.py:287
  8.6 5.9 %collective-permute-start.1 = (bf16[2,8,4096]{2,1,0:T(8,128)(2,1)S(1)}, bf16[2,8,4096]{2,1,0:T(8,128)(2,1)S(1)}, u32[]{:S(2)}, u32[]{:S(2)}) collective-permute-start(bf16[2,8,4096]{2,1,0:T(8,128)(2,1)S(1)} %shard_map.55.left_ref), channel_id=1, source_target_pairs={{0,4},{1,5},{2,6},{3,7},{4,0},{5,1},{6,2},{7,3},{8,12},{9,13},{10,... | collective-permute-start | bytes 393224 | tf_op jit(solution)/shard_map/ppermute | solution.py:287
  10.3 6.0 %collective-permute-start.5 = (bf16[4,144,128]{2,1,0:T(8,128)(2,1)S(1)}, bf16[4,144,128]{2,1,0:T(8,128)(2,1)S(1)}, u32[]{:S(2)}, u32[]{:S(2)}) collective-permute-start(bf16[4,144,128]{2,1,0:T(8,128)(2,1)S(1)} %shard_map.60), channel_id=1, source_target_pairs={{0,2},{1,3},{2,0},{3,1},{4,6},{5,7},{6,4},{7,5},{8,10},{9,11},{10,... | collective-permute-start | bytes 442376 | tf_op jit(solution)/shard_map/ppermute | solution.py:287
  11.9 4.2 %collective-permute-start.7 = (bf16[2,8,4096]{2,1,0:T(8,128)(2,1)S(1)}, bf16[2,8,4096]{2,1,0:T(8,128)(2,1)S(1)}, u32[]{:S(2)}, u32[]{:S(2)}) collective-permute-start(bf16[2,8,4096]{2,1,0:T(8,128)(2,1)S(1)} %shard_map.55.left_ref), channel_id=1, source_target_pairs={{0,1},{1,0},{2,3},{3,2},{4,5},{5,4},{6,7},{7,6},{8,9},{9,8},{10,11... | collective-permute-start | bytes 393224 | tf_op jit(solution)/shard_map/ppermute | solution.py:287
  14.5 9.5 %collective-permute-start.2 = (bf16[4,8,4096]{2,1,0:T(8,128)(2,1)S(1)}, bf16[4,8,4096]{2,1,0:T(8,128)(2,1)S(1)}, u32[]{:S(2)}, u32[]{:S(2)}) collective-permute-start(bf16[4,8,4096]{2,1,0:T(8,128)(2,1)S(1)} %shard_map.56.refs_4_), channel_id=1, source_target_pairs={{0,2},{1,3},{2,0},{3,1},{4,6},{5,7},{6,4},{7,5},{8,10},{9,11},{10,... | collective-permute-start | bytes 786440 | tf_op jit(solution)/shard_map/ppermute | solution.py:287
  16.4 7.6 %collective-permute-start.8 = (bf16[2,8,4096]{2,1,0:T(8,128)(2,1)S(1)}, bf16[2,8,4096]{2,1,0:T(8,128)(2,1)S(1)}, u32[]{:S(2)}, u32[]{:S(2)}) collective-permute-start(bf16[2,8,4096]{2,1,0:T(8,128)(2,1)S(1)} %collective-permute-done.1.right_ref), channel_id=1, source_target_pairs={{0,1},{1,0},{2,3},{3,2},{4,5},{5,4},{6,7},{7,6},{8,9},{9,8},{10,11... | collective-permute-start | bytes 393224 | tf_op jit(solution)/shard_map/ppermute | solution.py:287
  16.5 7.5 %collective-permute-start.9 = (bf16[144,128]{1,0:T(8,128)(2,1)S(1)}, bf16[144,128]{1,0:T(8,128)(2,1)S(1)}, u32[]{:S(2)}, u32[]{:S(2)}) collective-permute-start(bf16[144,128]{1,0:T(8,128)(2,1)S(1)} %get-tuple-element.47), channel_id=1, source_target_pairs={{0,12},{1,13},{2,14},{3,15},{4,8},{5,9},{6,10},{7,11},{8,4},{9,5},... | collective-permute-start | bytes 110600 | tf_op jit(solution)/shard_map/ppermute | solution.py:287
  19.2 4.9 %collective-permute-start.10 = (bf16[128,128]{1,0:T(8,128)(2,1)S(1)}, bf16[128,128]{1,0:T(8,128)(2,1)S(1)}, u32[]{:S(2)}, u32[]{:S(2)}) collective-permute-start(bf16[128,128]{1,0:T(8,128)(2,1)S(1)} %get-tuple-element.48), channel_id=1, source_target_pairs={{0,8},{1,9},{2,10},{3,11},{4,12},{5,13},{6,14},{7,15},{8,0},{9,1},... | collective-permute-start | bytes 98312 | tf_op jit(solution)/shard_map/ppermute | solution.py:287
  19.4 4.6 %collective-permute-start.11 = (bf16[128,128]{1,0:T(8,128)(2,1)S(1)}, bf16[128,128]{1,0:T(8,128)(2,1)S(1)}, u32[]{:S(2)}, u32[]{:S(2)}) collective-permute-start(bf16[128,128]{1,0:T(8,128)(2,1)S(1)} %get-tuple-element.49), channel_id=1, source_target_pairs={{0,4},{1,5},{2,6},{3,7},{4,0},{5,1},{6,2},{7,3},{8,12},{9,13},{10,... | collective-permute-start | bytes 98312 | tf_op jit(solution)/shard_map/ppermute | solution.py:287
  24.1 1.6 %collective-permute-start.12 = (bf16[4,8,4096]{2,1,0:T(8,128)(2,1)S(1)}, bf16[4,8,4096]{2,1,0:T(8,128)(2,1)S(1)}, u32[]{:S(2)}, u32[]{:S(2)}) collective-permute-start(bf16[4,8,4096]{2,1,0:T(8,128)(2,1)S(1)} %collective-permute-done.2.refs_7_), channel_id=1, source_target_pairs={{0,1},{1,0},{2,3},{3,2},{4,5},{5,4},{6,7},{7,6},{8,9},{9,8},{10,11... | collective-permute-start | bytes 786440 | tf_op jit(solution)/shard_map/ppermute | solution.py:287

commit v19 on v18

--- a/solution.py
+++ b/solution.py
@@ -177,6 +177,17 @@
         out_shape=[own] + [jax.ShapeDtypeStruct((height, width), jnp.bfloat16) for height in heights],
         compiler_params=PARAMS,
     )(kept, came, across)
+
+
+def halves_kernel(in_ref, *out_refs):
+    half = out_refs[0].shape[0]
+    for index, out_ref in enumerate(out_refs):
+        out_ref[...] = in_ref[index * half : (index + 1) * half]
+
+
+def halves(array):
+    half = jax.ShapeDtypeStruct((array.shape[0] // 2,) + array.shape[1:], array.dtype)
+    return pl.pallas_call(halves_kernel, out_shape=[half] * 2, compiler_params=PARAMS)(array)
 
 
 def stack_kernel(left_ref, right_ref, out_ref):
@@ -236,16 +247,19 @@
         add_scores(queries_ref, chips, lax.rem(core + other, 2), grads_ref, sums_ref)
 
 
-def last_score_kernel(chips, grads_ref, before_ref, queries_ref, out_ref, sums_ref):
+def last_score_kernel(chips, grads_ref, before_ref, first_ref, second_ref, out_ref, sums_ref):
     core = lax.rem(lax.axis_index("ex"), 2)
     sums_ref[...] = before_ref[...]
-    add_scores(queries_ref, chips, lax.rem(core + 1, 2), grads_ref, sums_ref)
+    half = len(chips) // 2
+    for queries_ref, reach in ((first_ref, chips[:half]), (second_ref, chips[half:])):
+        add_scores(queries_ref, reach, lax.rem(core + 1, 2), grads_ref, sums_ref)
     examples, *rows, lanes = sums_ref.shape
     sums = sums_ref[...].reshape(examples * out_ref.shape[1], lanes)
     high = sums.astype(jnp.bfloat16)
     low = (sums - high.astype(jnp.float32)).astype(jnp.bfloat16)
-    ones = jnp.ones((16, lanes), jnp.bfloat16)
-    row = sum(lax.dot_general(ones, part, LANES_BY_LANES, preferred_element_type=jnp.float32) for part in (high, low))
+    ones = jnp.ones((16, 2 * lanes), jnp.bfloat16)
+    both = jnp.concatenate([high, low], axis=1)
+    row = lax.dot_general(ones, both, LANES_BY_LANES, preferred_element_type=jnp.float32)
     for n in range(examples):
         out_ref[n : n + 1, :] = row[0:1, n * out_ref.shape[1] : (n + 1) * out_ref.shape[1]]
 
@@ -265,14 +279,14 @@
     )(*parts, *queries)
 
 
-def last_scores(grads, sums, queries, chips):
+def last_scores(grads, sums, first, second, chips):
     examples, all_chips, cores, held, _ = sums.shape
     return pl.pallas_call(
         functools.partial(last_score_kernel, chips),
         out_shape=jax.ShapeDtypeStruct((examples, all_chips * cores * held), jnp.float32),
         scratch_shapes=[pltpu.VMEM(sums.shape, jnp.float32)],
         compiler_params=PARAMS,
-    )(grads, sums, queries)
+    )(grads, sums, first, second)
 
 
 def shards(inputs, out_grads, proj_in, proj_out, queries):
@@ -308,12 +322,12 @@
     other_late = swap(late, core=1)
     parts[1:] = [swap(part, chip=2 * z) for z, part in zip(reversed(range(1, depth)), parts[1:])]
     came_held, other_late, parts = together((came_held, other_late, parts))
-    other_came = swap(came_held, core=1)
+    other_came = [swap(half, core=1) for half in halves(came_held)]
     reach_y = [chip ^ 1 for chip in reach]
     queries = [held, other_early, other_late, came_held]
     reaches = [(0, reach), (1, early_reach), (1, late_reach), (0, reach_y)]
     grads, scores = first_scores(parts, queries, reaches, rank)
-    return last_scores(grads, scores, other_came, reach_y)
+    return last_scores(grads, scores, *other_came, reach_y)
 
 
 def solution(mesh):

time: 26.6 us -> 26.7 us (level)
  starting transfers between devices: 14.2 us -> 14.7 us
  waiting for transfers between devices: 6.71 us -> 6.22 us
    ppermute x13 -> x14, starting transfers between devices: 14.2 us -> 14.7 us  [swap(): lax.ppermute(array, 'ex', [(i, i ^ distance) for i in range(devices)])]
    ppermute x13 -> x14, waiting for transfers between devices: 6.71 us -> 6.22 us  [swap(): lax.ppermute(array, 'ex', [(i, i ^ distance) for i in range(devices)])]
  transfers between devices with their start and end apart: 13 -> 14, of which waited for: 4 -> 5; matrix products, arithmetic and copies ran while one was open for 0% -> 0% of each run, Pallas kernels for 18% -> 18%
where the time goes in v19:
time: 26.7 us; the launch traced here: 26.5 us
  starting transfers between devices  14.7 us (55%)
  waiting for transfers between devices  6.22 us (23%)
  Pallas kernels  5.53 us (21%)
    ppermute x14, starting transfers between devices, swap(): lax.ppermute(array, 'ex', [(i, i ^ distance) for i in range(devices)])  14.7 us
    ppermute x14, waiting for transfers between devices, swap(): lax.ppermute(array, 'ex', [(i, i ^ distance) for i in range(devices)])  6.22 us
    pallas_call x1, Pallas kernels, project_loaded(): pl.pallas_call(project_loaded_kernel, out_shape=[jax.ShapeDtypeStruct((ra...  2.23 us
    pallas_call x2, Pallas kernels, part(): pl.pallas_call(functools.partial(project_kernel, rows, flip), out_shape=[...  1.54 us
    pallas_call x1, Pallas kernels, last_scores(): pl.pallas_call(functools.partial(last_score_kernel, chips), out_shape=jax...  0.85 us
    pallas_call x1, Pallas kernels, first_scores(): pl.pallas_call(functools.partial(first_score_kernel, len(parts), held), o...  0.68 us
  transfers between devices with their start and end apart: 14, of which 5 were waited for; matrix products, arithmetic and copies ran while one was open for 0% of the time, Pallas kernels for 18%

profile of v19, /device:TPU:0, one launch (start us, length us, event | category | flops | bytes accessed | tf_op | source)
XLA Modules:
  0.0 26.5 jit_solution(6612324761385945618)
XLA Ops:
  0.0 0.0 copy-start.1
  0.0 0.0 copy-start
  0.0 4.0 %collective-permute-start = (bf16[1,8,4096]{2,1,0:T(8,128)(2,1)}, bf16[1,8,4096]{2,1,0:T(8,128)(2,1)S(1)}, u32[]{:S(2)}, u32[]{:S(2)}) collective-permute-start(bf16[1,8,4096]{2,1,0:T(8,128)(2,1)} %bitcast.6), channel_id=1, source_target_pairs={{0,8},{1,9},{2,10},{3,11},{4,12},{5,13},{6,14},{7,15},{8,0},{9,1},... | collective-permute-start | bytes 196616 | tf_op jit(solution)/shard_map/ppermute | solution.py:301
  4.0 2.2 %shard_map.57 = (f32[64,2048]{1,0:T(8,128)S(1)}, f32[64,2048]{1,0:T(8,128)S(1)}) custom-call(bf16[512,2048]{1,0:T(8,128)(2,1)} %x_hbm.1, bf16[1792,2048]{1,0:T(8,128)(2,1)} %w_ref.3, bf16[64,512]{1,0:T(8,128)(2,1)} %bitcast.8, bf16[64,1792]{1,0:T(8,128)(2,1)} %bitcast.3), custom_call_target="tpu_custom_call" | custom-call | flops 167772160 | bytes 2621440 | tf_op jit(solution)/shard_map/pallas_call | solution.py:50
  6.3 0.0 copy-done.1
  6.3 0.0 copy-done
  6.3 0.0 copy-start.2
  6.3 0.8 %shard_map.59 = (f32[2,128,128]{2,1,0:T(8,128)S(1)}, f32[2,128,128]{2,1,0:T(8,128)S(1)}, f32[4,128,128]{2,1,0:T(8,128)S(1)}) custom-call(f32[64,2048]{1,0:T(8,128)S(1)} %get-tuple-element.34.low_in_ref, f32[64,2048]{1,0:T(8,128)S(1)} %get-tuple-element.35.low_out_ref, bf16[64,1792]{1,0:T(8,128)(2,1)S(1)} %bitcast.4, bf16[1792,2048]{1,0:T(8,128)(2,1)S(1)} %copy-done), custom_call_target="tpu_custom_call" | custom-call | flops 234881024 | bytes 3670016 | tf_op jit(solution)/shard_map/pallas_call | solution.py:99
  7.1 0.1 collective-permute-start.3
  7.2 0.5 %collective-permute-start.4 = (f32[2,128,128]{2,1,0:T(8,128)S(1)}, f32[2,128,128]{2,1,0:T(8,128)S(1)}, u32[]{:S(2)}, u32[]{:S(2)}) collective-permute-start(f32[2,128,128]{2,1,0:T(8,128)S(1)} %get-tuple-element.39), channel_id=1, source_target_pairs={{0,1},{1,0},{2,3},{3,2},{4,5},{5,4},{6,7},{7,6},{8,9},{9,8},{10,11... | collective-permute-start | bytes 393224 | tf_op jit(solution)/shard_map/ppermute | solution.py:301
  7.7 0.8 %shard_map.58 = (f32[4,128,128]{2,1,0:T(8,128)S(1)}, f32[4,128,128]{2,1,0:T(8,128)S(1)}) custom-call(f32[64,2048]{1,0:T(8,128)S(1)} %get-tuple-element.34.low_in_ref, f32[64,2048]{1,0:T(8,128)S(1)} %get-tuple-element.35.low_out_ref, bf16[64,1792]{1,0:T(8,128)(2,1)S(1)} %bitcast.5, bf16[1792,2048]{1,0:T(8,128)(2,1)S(1)} %copy-done), custom_call_target="tpu_custom_call" | custom-call | flops 234881024 | bytes 3670016 | tf_op jit(solution)/shard_map/pallas_call | solution.py:99
  8.4 0.1 collective-permute-start.6
  8.6 0.0 collective-permute-done.right_ref
  8.6 0.0 copy-done.2
  8.6 1.6 %collective-permute-start.1 = (bf16[2,8,4096]{2,1,0:T(8,128)(2,1)S(1)}, bf16[2,8,4096]{2,1,0:T(8,128)(2,1)S(1)}, u32[]{:S(2)}, u32[]{:S(2)}) collective-permute-start(bf16[2,8,4096]{2,1,0:T(8,128)(2,1)S(1)} %shard_map.55.left_ref), channel_id=1, source_target_pairs={{0,4},{1,5},{2,6},{3,7},{4,0},{5,1},{6,2},{7,3},{8,12},{9,13},{10,... | collective-permute-start | bytes 393224 | tf_op jit(solution)/shard_map/ppermute | solution.py:301
  10.2 0.0 collective-permute-done.3.refs_0_
  10.2 0.0 collective-permute-done.4.refs_1_
  10.2 0.1 shard_map.60
  10.3 1.6 %collective-permute-start.5 = (bf16[4,144,128]{2,1,0:T(8,128)(2,1)S(1)}, bf16[4,144,128]{2,1,0:T(8,128)(2,1)S(1)}, u32[]{:S(2)}, u32[]{:S(2)}) collective-permute-start(bf16[4,144,128]{2,1,0:T(8,128)(2,1)S(1)} %shard_map.60), channel_id=1, source_target_pairs={{0,2},{1,3},{2,0},{3,1},{4,6},{5,7},{6,4},{7,5},{8,10},{9,11},{10,... | collective-permute-start | bytes 442376 | tf_op jit(solution)/shard_map/ppermute | solution.py:301
  11.9 0.0 collective-permute-start.7
  11.9 2.6 %collective-permute-done.1.right_ref = bf16[2,8,4096]{2,1,0:T(8,128)(2,1)S(1)} collective-permute-done((bf16[2,8,4096]{2,1,0:T(8,128)(2,1)S(1)}, bf16[2,8,4096]{2,1,0:T(8,128)(2,1)S(1)}, u32[]{:S(2)}, u32[]{:S(2)}) %collective-permute-start.1) | collective-permute-done | bytes 131104 | tf_op jit(solution)/shard_map/ppermute | solution.py:301
  14.5 1.6 %collective-permute-start.2 = (bf16[4,8,4096]{2,1,0:T(8,128)(2,1)S(1)}, bf16[4,8,4096]{2,1,0:T(8,128)(2,1)S(1)}, u32[]{:S(2)}, u32[]{:S(2)}) collective-permute-start(bf16[4,8,4096]{2,1,0:T(8,128)(2,1)S(1)} %shard_map.56.refs_4_), channel_id=1, source_target_pairs={{0,2},{1,3},{2,0},{3,1},{4,6},{5,7},{6,4},{7,5},{8,10},{9,11},{10,... | collective-permute-start | bytes 786440 | tf_op jit(solution)/shard_map/ppermute | solution.py:301
  16.1 0.0 collective-permute-done.7.refs_5_
  16.1 0.0 collective-permute-done.6.came_ref
  16.1 0.2 collective-permute-done.5.across_ref
  16.3 0.1 shard_map.61
  16.4 0.1 collective-permute-start.8
  16.5 2.7 %collective-permute-start.9 = (bf16[144,128]{1,0:T(8,128)(2,1)S(1)}, bf16[144,128]{1,0:T(8,128)(2,1)S(1)}, u32[]{:S(2)}, u32[]{:S(2)}) collective-permute-start(bf16[144,128]{1,0:T(8,128)(2,1)S(1)} %get-tuple-element.49), channel_id=1, source_target_pairs={{0,12},{1,13},{2,14},{3,15},{4,8},{5,9},{6,10},{7,11},{8,4},{9,5},... | collective-permute-start | bytes 110600 | tf_op jit(solution)/shard_map/ppermute | solution.py:301
  19.2 0.3 %collective-permute-start.10 = (bf16[128,128]{1,0:T(8,128)(2,1)S(1)}, bf16[128,128]{1,0:T(8,128)(2,1)S(1)}, u32[]{:S(2)}, u32[]{:S(2)}) collective-permute-start(bf16[128,128]{1,0:T(8,128)(2,1)S(1)} %get-tuple-element.50), channel_id=1, source_target_pairs={{0,8},{1,9},{2,10},{3,11},{4,12},{5,13},{6,14},{7,15},{8,0},{9,1},... | collective-permute-start | bytes 98312 | tf_op jit(solution)/shard_map/ppermute | solution.py:301
  19.4 1.5 %collective-permute-start.11 = (bf16[128,128]{1,0:T(8,128)(2,1)S(1)}, bf16[128,128]{1,0:T(8,128)(2,1)S(1)}, u32[]{:S(2)}, u32[]{:S(2)}) collective-permute-start(bf16[128,128]{1,0:T(8,128)(2,1)S(1)} %get-tuple-element.51), channel_id=1, source_target_pairs={{0,4},{1,5},{2,6},{3,7},{4,0},{5,1},{6,2},{7,3},{8,12},{9,13},{10,... | collective-permute-start | bytes 98312 | tf_op jit(solution)/shard_map/ppermute | solution.py:301
  21.0 3.1 %collective-permute-done.10.refs_2_ = bf16[128,128]{1,0:T(8,128)(2,1)S(1)} collective-permute-done((bf16[128,128]{1,0:T(8,128)(2,1)S(1)}, bf16[128,128]{1,0:T(8,128)(2,1)S(1)}, u32[]{:S(2)}, u32[]{:S(2)}) %collective-permute-start.10) | collective-permute-done | bytes 32800 | tf_op jit(solution)/shard_map/ppermute | solution.py:301
  24.0 0.0 collective-permute-done.11.refs_3_
  24.0 0.0 collective-permute-done.9.refs_1_
  24.1 0.0 collective-permute-done.8.refs_6_
  24.1 0.0 collective-permute-done.2.refs_7_.in_ref
  24.1 0.1 collective-permute-start.12
  24.2 0.5 %collective-permute-start.13 = (bf16[2,8,4096]{2,1,0:T(8,128)(2,1)S(1)}, bf16[2,8,4096]{2,1,0:T(8,128)(2,1)S(1)}, u32[]{:S(2)}, u32[]{:S(2)}) collective-permute-start(bf16[2,8,4096]{2,1,0:T(8,128)(2,1)S(1)} %get-tuple-element.62), channel_id=1, source_target_pairs={{0,1},{1,0},{2,3},{3,2},{4,5},{5,4},{6,7},{7,6},{8,9},{9,8},{10,11... | collective-permute-start | bytes 393224 | tf_op jit(solution)/shard_map/ppermute | solution.py:301
  24.7 0.7 %shard_map.62 = (f32[2,32,128]{2,1,0:T(8,128)S(1)}, f32[2,8,2,8,128]{4,3,2,1,0:T(8,128)S(1)}) custom-call(f32[128,128]{1,0:T(8,128)S(1)} %get-tuple-element.52.refs_0_, bf16[144,128]{1,0:T(8,128)(2,1)S(1)} %collective-permute-done.9.refs_1_, bf16[128,128]{1,0:T(8,128)(2,1)S(1)} %collective-permute-done.10.refs_2_, ...), custom_call_target="tpu_custom_call" | custom-call | tf_op jit(solution)/shard_map/pallas_call | solution.py:271
  25.3 0.2 collective-permute-done.12.first_ref
  25.5 0.2 collective-permute-done.13.second_ref
  25.7 0.8 %shard_map.64 = f32[2,128]{1,0:T(2,128)} custom-call(f32[2,32,128]{2,1,0:T(8,128)S(1)} %get-tuple-element.59.grads_ref, f32[2,8,2,8,128]{4,3,2,1,0:T(8,128)S(1)} %get-tuple-element.60.before_ref, bf16[2,8,4096]{2,1,0:T(8,128)(2,1)S(1)} %collective-permute-done.12.first_ref, bf16[2,8,4096]{2,1,0:T(8,128)(2,1)S(1)} %collective-permute-done.13.second_ref), custom_call_target="tpu_custom_call" | custom-call | tf_op jit(solution)/shard_map/pallas_call | solution.py:284
  (3 shorter events, 0.0 us)
Async XLA Ops:
  0.0 6.3 %copy-start.1 = (bf16[1792,64]{0,1:T(8,128)(2,1)S(1)}, bf16[1792,64]{0,1:T(8,128)(2,1)}, u32[]{:S(2)}) copy-start(bf16[1792,64]{0,1:T(8,128)(2,1)} %param.8) | copy-start | bytes 688132
  0.0 6.3 %copy-start = (bf16[1792,2048]{1,0:T(8,128)(2,1)S(1)}, bf16[1792,2048]{1,0:T(8,128)(2,1)}, u32[]{:S(2)}) copy-start(bf16[1792,2048]{1,0:T(8,128)(2,1)} %w_ref.3) | copy-start | bytes 22020100
  0.0 8.6 %collective-permute-start = (bf16[1,8,4096]{2,1,0:T(8,128)(2,1)}, bf16[1,8,4096]{2,1,0:T(8,128)(2,1)S(1)}, u32[]{:S(2)}, u32[]{:S(2)}) collective-permute-start(bf16[1,8,4096]{2,1,0:T(8,128)(2,1)} %bitcast.6), channel_id=1, source_target_pairs={{0,8},{1,9},{2,10},{3,11},{4,12},{5,13},{6,14},{7,15},{8,0},{9,1},... | collective-permute-start | bytes 196616 | tf_op jit(solution)/shard_map/ppermute | solution.py:301
  6.3 2.3 %copy-start.2 = (bf16[8,4096]{1,0:T(8,128)(2,1)S(1)}, bf16[8,4096]{1,0:T(8,128)(2,1)}, u32[]{:S(2)}) copy-start(bf16[8,4096]{1,0:T(8,128)(2,1)} %param.9) | copy-start | bytes 196612
  7.1 3.1 %collective-permute-start.3 = (f32[2,128,128]{2,1,0:T(8,128)S(1)}, f32[2,128,128]{2,1,0:T(8,128)S(1)}, u32[]{:S(2)}, u32[]{:S(2)}) collective-permute-start(f32[2,128,128]{2,1,0:T(8,128)S(1)} %get-tuple-element.38), channel_id=1, source_target_pairs={{0,1},{1,0},{2,3},{3,2},{4,5},{5,4},{6,7},{7,6},{8,9},{9,8},{10,11... | collective-permute-start | bytes 393224 | tf_op jit(solution)/shard_map/ppermute | solution.py:301
  7.2 3.1 %collective-permute-start.4 = (f32[2,128,128]{2,1,0:T(8,128)S(1)}, f32[2,128,128]{2,1,0:T(8,128)S(1)}, u32[]{:S(2)}, u32[]{:S(2)}) collective-permute-start(f32[2,128,128]{2,1,0:T(8,128)S(1)} %get-tuple-element.39), channel_id=1, source_target_pairs={{0,1},{1,0},{2,3},{3,2},{4,5},{5,4},{6,7},{7,6},{8,9},{9,8},{10,11... | collective-permute-start | bytes 393224 | tf_op jit(solution)/shard_map/ppermute | solution.py:301
  8.4 7.7 %collective-permute-start.6 = (f32[4,128,128]{2,1,0:T(8,128)S(1)}, f32[4,128,128]{2,1,0:T(8,128)S(1)}, u32[]{:S(2)}, u32[]{:S(2)}) collective-permute-start(f32[4,128,128]{2,1,0:T(8,128)S(1)} %get-tuple-element.40), channel_id=1, source_target_pairs={{0,1},{1,0},{2,3},{3,2},{4,5},{5,4},{6,7},{7,6},{8,9},{9,8},{10,11... | collective-permute-start | bytes 786440 | tf_op jit(solution)/shard_map/ppermute | solution.py:301
  8.6 5.9 %collective-permute-start.1 = (bf16[2,8,4096]{2,1,0:T(8,128)(2,1)S(1)}, bf16[2,8,4096]{2,1,0:T(8,128)(2,1)S(1)}, u32[]{:S(2)}, u32[]{:S(2)}) collective-permute-start(bf16[2,8,4096]{2,1,0:T(8,128)(2,1)S(1)} %shard_map.55.left_ref), channel_id=1, source_target_pairs={{0,4},{1,5},{2,6},{3,7},{4,0},{5,1},{6,2},{7,3},{8,12},{9,13},{10,... | collective-permute-start | bytes 393224 | tf_op jit(solution)/shard_map/ppermute | solution.py:301
  10.3 6.0 %collective-permute-start.5 = (bf16[4,144,128]{2,1,0:T(8,128)(2,1)S(1)}, bf16[4,144,128]{2,1,0:T(8,128)(2,1)S(1)}, u32[]{:S(2)}, u32[]{:S(2)}) collective-permute-start(bf16[4,144,128]{2,1,0:T(8,128)(2,1)S(1)} %shard_map.60), channel_id=1, source_target_pairs={{0,2},{1,3},{2,0},{3,1},{4,6},{5,7},{6,4},{7,5},{8,10},{9,11},{10,... | collective-permute-start | bytes 442376 | tf_op jit(solution)/shard_map/ppermute | solution.py:301
  11.9 4.2 %collective-permute-start.7 = (bf16[2,8,4096]{2,1,0:T(8,128)(2,1)S(1)}, bf16[2,8,4096]{2,1,0:T(8,128)(2,1)S(1)}, u32[]{:S(2)}, u32[]{:S(2)}) collective-permute-start(bf16[2,8,4096]{2,1,0:T(8,128)(2,1)S(1)} %shard_map.55.left_ref), channel_id=1, source_target_pairs={{0,1},{1,0},{2,3},{3,2},{4,5},{5,4},{6,7},{7,6},{8,9},{9,8},{10,11... | collective-permute-start | bytes 393224 | tf_op jit(solution)/shard_map/ppermute | solution.py:301
  14.5 9.5 %collective-permute-start.2 = (bf16[4,8,4096]{2,1,0:T(8,128)(2,1)S(1)}, bf16[4,8,4096]{2,1,0:T(8,128)(2,1)S(1)}, u32[]{:S(2)}, u32[]{:S(2)}) collective-permute-start(bf16[4,8,4096]{2,1,0:T(8,128)(2,1)S(1)} %shard_map.56.refs_4_), channel_id=1, source_target_pairs={{0,2},{1,3},{2,0},{3,1},{4,6},{5,7},{6,4},{7,5},{8,10},{9,11},{10,... | collective-permute-start | bytes 786440 | tf_op jit(solution)/shard_map/ppermute | solution.py:301
  16.4 7.6 %collective-permute-start.8 = (bf16[2,8,4096]{2,1,0:T(8,128)(2,1)S(1)}, bf16[2,8,4096]{2,1,0:T(8,128)(2,1)S(1)}, u32[]{:S(2)}, u32[]{:S(2)}) collective-permute-start(bf16[2,8,4096]{2,1,0:T(8,128)(2,1)S(1)} %collective-permute-done.1.right_ref), channel_id=1, source_target_pairs={{0,1},{1,0},{2,3},{3,2},{4,5},{5,4},{6,7},{7,6},{8,9},{9,8},{10,11... | collective-permute-start | bytes 393224 | tf_op jit(solution)/shard_map/ppermute | solution.py:301
  16.5 7.5 %collective-permute-start.9 = (bf16[144,128]{1,0:T(8,128)(2,1)S(1)}, bf16[144,128]{1,0:T(8,128)(2,1)S(1)}, u32[]{:S(2)}, u32[]{:S(2)}) collective-permute-start(bf16[144,128]{1,0:T(8,128)(2,1)S(1)} %get-tuple-element.49), channel_id=1, source_target_pairs={{0,12},{1,13},{2,14},{3,15},{4,8},{5,9},{6,10},{7,11},{8,4},{9,5},... | collective-permute-start | bytes 110600 | tf_op jit(solution)/shard_map/ppermute | solution.py:301
  19.2 4.9 %collective-permute-start.10 = (bf16[128,128]{1,0:T(8,128)(2,1)S(1)}, bf16[128,128]{1,0:T(8,128)(2,1)S(1)}, u32[]{:S(2)}, u32[]{:S(2)}) collective-permute-start(bf16[128,128]{1,0:T(8,128)(2,1)S(1)} %get-tuple-element.50), channel_id=1, source_target_pairs={{0,8},{1,9},{2,10},{3,11},{4,12},{5,13},{6,14},{7,15},{8,0},{9,1},... | collective-permute-start | bytes 98312 | tf_op jit(solution)/shard_map/ppermute | solution.py:301
  19.4 4.6 %collective-permute-start.11 = (bf16[128,128]{1,0:T(8,128)(2,1)S(1)}, bf16[128,128]{1,0:T(8,128)(2,1)S(1)}, u32[]{:S(2)}, u32[]{:S(2)}) collective-permute-start(bf16[128,128]{1,0:T(8,128)(2,1)S(1)} %get-tuple-element.51), channel_id=1, source_target_pairs={{0,4},{1,5},{2,6},{3,7},{4,0},{5,1},{6,2},{7,3},{8,12},{9,13},{10,... | collective-permute-start | bytes 98312 | tf_op jit(solution)/shard_map/ppermute | solution.py:301
  24.1 1.4 %collective-permute-start.12 = (bf16[2,8,4096]{2,1,0:T(8,128)(2,1)S(1)}, bf16[2,8,4096]{2,1,0:T(8,128)(2,1)S(1)}, u32[]{:S(2)}, u32[]{:S(2)}) collective-permute-start(bf16[2,8,4096]{2,1,0:T(8,128)(2,1)S(1)} %get-tuple-element.61), channel_id=1, source_target_pairs={{0,1},{1,0},{2,3},{3,2},{4,5},{5,4},{6,7},{7,6},{8,9},{9,8},{10,11... | collective-permute-start | bytes 393224 | tf_op jit(solution)/shard_map/ppermute | solution.py:301
  24.2 1.5 %collective-permute-start.13 = (bf16[2,8,4096]{2,1,0:T(8,128)(2,1)S(1)}, bf16[2,8,4096]{2,1,0:T(8,128)(2,1)S(1)}, u32[]{:S(2)}, u32[]{:S(2)}) collective-permute-start(bf16[2,8,4096]{2,1,0:T(8,128)(2,1)S(1)} %get-tuple-element.62), channel_id=1, source_target_pairs={{0,1},{1,0},{2,3},{3,2},{4,5},{5,4},{6,7},{7,6},{8,9},{9,8},{10,11... | collective-permute-start | bytes 393224 | tf_op jit(solution)/shard_map/ppermute | solution.py:301

commit v20 on v16

--- a/solution.py
+++ b/solution.py
@@ -10,6 +10,7 @@
 SEQ = 64
 VMEM_BYTES = 32 * 1024 * 1024
 LOADED_ROWS = 128
+FAR_PAD = 16
 LEFT_OVER = 0.36 * 2.0**-8
 LANES_BY_LANES = (((1,), (1,)), ((), ()))
 HBM_SPEC = pl.BlockSpec(memory_space=pltpu.HBM)
@@ -116,12 +117,12 @@
     word = above[:part, :]
     for index in range(1, 8):
         word = word + 2.0**index * above[index * part : (index + 1) * part, :]
-    out_ref[rows:, :] = word.astype(jnp.bfloat16)
-
-
-def add_coded(total, ref):
-    part = ref.shape[0] // 9
-    word = ref[8 * part :, :].astype(jnp.float32)
+    out_ref[rows : rows + part, :] = word.astype(jnp.bfloat16)
+
+
+def add_coded(total, rows, ref):
+    part = rows // 8
+    word = ref[rows : rows + part, :].astype(jnp.float32)
     parts = []
     for index in reversed(range(8)):
         above = jnp.floor(word * 0.5**index)
@@ -153,7 +154,7 @@
         def here(first, rows):
             return kept_ref[z, first : first + rows, :] + came_ref[z, first : first + rows, :]
 
-        sums = add_coded(here, across_ref.at[z])
+        sums = add_coded(here, kept_ref.shape[1], across_ref.at[z])
         if z == 0:
             for rows, total in sums:
                 own_ref[rows, :] = total
@@ -164,10 +165,10 @@
 def add_kept(kept, came, across):
     depth, rows, width = kept.shape
     own = jax.ShapeDtypeStruct((rows, width), jnp.float32)
-    coded = jax.ShapeDtypeStruct((rows // 8 * 9, width), jnp.bfloat16)
+    heights = [rows // 8 * 9 + (FAR_PAD if z > 2 else 0) for z in reversed(range(1, depth))]
     return pl.pallas_call(
         add_kept_kernel,
-        out_shape=[own] + [coded] * (depth - 1),
+        out_shape=[own] + [jax.ShapeDtypeStruct((height, width), jnp.bfloat16) for height in heights],
         compiler_params=PARAMS,
     )(kept, came, across)
 
@@ -210,7 +211,7 @@
     core = lax.rem(lax.axis_index("ex"), 2)
     total_ref[...] = part_refs[0][...]
     for part_ref in part_refs[1:]:
-        for rows, total in add_coded(lambda first, count: total_ref[first : first + count, :], part_ref):
+        for rows, total in add_coded(lambda first, count: total_ref[first : first + count, :], 2 * rank, part_ref):
             total_ref[rows, :] = total
     even = total_ref[pl.ds(rank, rank // 2, stride=2), :]
     odd = total_ref[pl.ds(rank + 1, rank // 2, stride=2), :]

time: 27.8 us -> 26.6 us (0.957)
  waiting for transfers between devices: 8.15 us -> 6.83 us
    ppermute x13, waiting for transfers between devices: 8.15 us -> 6.83 us  [swap(): lax.ppermute(array, 'ex', [(i, i ^ distance) for i in range(devices)])]
  transfers between devices with their start and end apart: 13 -> 13, of which waited for: 6 -> 5; matrix products, arithmetic and copies ran while one was open for 0% -> 0% of each run, Pallas kernels for 17% -> 17%
where the time goes in v20:
time: 26.6 us; the launch traced here: 26.4 us
  starting transfers between devices  14.1 us (53%)
  waiting for transfers between devices  6.83 us (26%)
  Pallas kernels  5.4 us (20%)
    ppermute x13, starting transfers between devices, swap(): lax.ppermute(array, 'ex', [(i, i ^ distance) for i in range(devices)])  14.1 us
    ppermute x13, waiting for transfers between devices, swap(): lax.ppermute(array, 'ex', [(i, i ^ distance) for i in range(devices)])  6.83 us
    pallas_call x1, Pallas kernels, project_loaded(): pl.pallas_call(project_loaded_kernel, out_shape=[jax.ShapeDtypeStruct((ra...  2.22 us
    pallas_call x1, Pallas kernels, project(): pl.pallas_call(functools.partial(project_kernel, rows), out_shape=[half]...  1.43 us
    pallas_call x1, Pallas kernels, last_scores(): pl.pallas_call(functools.partial(last_score_kernel, chips), out_shape=jax...  0.81 us
    pallas_call x1, Pallas kernels, first_scores(): pl.pallas_call(functools.partial(first_score_kernel, len(parts), held), o...  0.7 us
  transfers between devices with their start and end apart: 13, of which 5 were waited for; matrix products, arithmetic and copies ran while one was open for 0% of the time, Pallas kernels for 17%

profile of v20, /device:TPU:0, one launch (start us, length us, event | category | flops | bytes accessed | tf_op | source)
XLA Modules:
  0.0 26.4 jit_solution(9809208144622490401)
XLA Ops:
  0.0 0.0 copy-start.1
  0.0 0.0 copy-start
  0.0 4.0 %collective-permute-start = (bf16[1,8,4096]{2,1,0:T(8,128)(2,1)}, bf16[1,8,4096]{2,1,0:T(8,128)(2,1)S(1)}, u32[]{:S(2)}, u32[]{:S(2)}) collective-permute-start(bf16[1,8,4096]{2,1,0:T(8,128)(2,1)} %bitcast.5), channel_id=1, source_target_pairs={{0,8},{1,9},{2,10},{3,11},{4,12},{5,13},{6,14},{7,15},{8,0},{9,1},... | collective-permute-start | bytes 196616 | tf_op jit(solution)/shard_map/ppermute | solution.py:278
  4.0 0.0 copy-start.2
  4.0 2.2 %shard_map.57 = (f32[64,2048]{1,0:T(8,128)S(1)}, f32[64,2048]{1,0:T(8,128)S(1)}) custom-call(bf16[512,2048]{1,0:T(8,128)(2,1)} %x_hbm.1, bf16[1792,2048]{1,0:T(8,128)(2,1)} %w_ref.1, bf16[64,512]{1,0:T(8,128)(2,1)} %bitcast.7, bf16[64,1792]{1,0:T(8,128)(2,1)} %bitcast.3), custom_call_target="tpu_custom_call" | custom-call | flops 167772160 | bytes 2621440 | tf_op jit(solution)/shard_map/pallas_call | solution.py:50
  6.3 0.0 copy-done.1
  6.3 0.0 copy-done
  6.3 1.4 %shard_map.58 = (f32[2,128,128]{2,1,0:T(8,128)S(1)}, f32[2,128,128]{2,1,0:T(8,128)S(1)}, f32[4,128,128]{2,1,0:T(8,128)S(1)}, f32[4,128,128]{2,1,0:T(8,128)S(1)}, f32[4,128,128]{2,1,0:T(8,128)S(1)}) custom-call(f32[64,2048]{1,0:T(8,128)S(1)} %get-tuple-element.32.low_in_ref, f32[64,2048]{1,0:T(8,128)S(1)} %get-tuple-element.33.low_out_ref, ...), custom_call_target="tpu_custom_call" | custom-call | flops 469762048 | bytes 7340032 | tf_op jit(solution)/shard_map/pallas_call | solution.py:99
  7.7 0.1 collective-permute-start.3
  7.8 0.5 %collective-permute-start.4 = (f32[2,128,128]{2,1,0:T(8,128)S(1)}, f32[2,128,128]{2,1,0:T(8,128)S(1)}, u32[]{:S(2)}, u32[]{:S(2)}) collective-permute-start(f32[2,128,128]{2,1,0:T(8,128)S(1)} %get-tuple-element.37), channel_id=1, source_target_pairs={{0,1},{1,0},{2,3},{3,2},{4,5},{5,4},{6,7},{7,6},{8,9},{9,8},{10,11... | collective-permute-start | bytes 393224 | tf_op jit(solution)/shard_map/ppermute | solution.py:278
  8.3 0.1 collective-permute-start.6
  8.4 0.0 collective-permute-done.right_ref
  8.4 0.0 copy-done.2
  8.4 1.6 %collective-permute-start.1 = (bf16[2,8,4096]{2,1,0:T(8,128)(2,1)S(1)}, bf16[2,8,4096]{2,1,0:T(8,128)(2,1)S(1)}, u32[]{:S(2)}, u32[]{:S(2)}) collective-permute-start(bf16[2,8,4096]{2,1,0:T(8,128)(2,1)S(1)} %shard_map.55.left_ref), channel_id=1, source_target_pairs={{0,4},{1,5},{2,6},{3,7},{4,0},{5,1},{6,2},{7,3},{8,12},{9,13},{10,... | collective-permute-start | bytes 393224 | tf_op jit(solution)/shard_map/ppermute | solution.py:278
  10.0 0.0 collective-permute-done.3.refs_0_
  10.0 0.0 collective-permute-done.4.refs_1_
  10.0 0.1 shard_map.59
  10.1 1.6 %collective-permute-start.5 = (bf16[4,144,128]{2,1,0:T(8,128)(2,1)S(1)}, bf16[4,144,128]{2,1,0:T(8,128)(2,1)S(1)}, u32[]{:S(2)}, u32[]{:S(2)}) collective-permute-start(bf16[4,144,128]{2,1,0:T(8,128)(2,1)S(1)} %shard_map.59), channel_id=1, source_target_pairs={{0,2},{1,3},{2,0},{3,1},{4,6},{5,7},{6,4},{7,5},{8,10},{9,11},{10,... | collective-permute-start | bytes 442376 | tf_op jit(solution)/shard_map/ppermute | solution.py:278
  11.7 0.0 collective-permute-start.7
  11.7 2.6 %collective-permute-done.1.right_ref = bf16[2,8,4096]{2,1,0:T(8,128)(2,1)S(1)} collective-permute-done((bf16[2,8,4096]{2,1,0:T(8,128)(2,1)S(1)}, bf16[2,8,4096]{2,1,0:T(8,128)(2,1)S(1)}, u32[]{:S(2)}, u32[]{:S(2)}) %collective-permute-start.1) | collective-permute-done | bytes 131104 | tf_op jit(solution)/shard_map/ppermute | solution.py:278
  14.3 1.6 %collective-permute-start.2 = (bf16[4,8,4096]{2,1,0:T(8,128)(2,1)S(1)}, bf16[4,8,4096]{2,1,0:T(8,128)(2,1)S(1)}, u32[]{:S(2)}, u32[]{:S(2)}) collective-permute-start(bf16[4,8,4096]{2,1,0:T(8,128)(2,1)S(1)} %shard_map.56.refs_4_), channel_id=1, source_target_pairs={{0,2},{1,3},{2,0},{3,1},{4,6},{5,7},{6,4},{7,5},{8,10},{9,11},{10,... | collective-permute-start | bytes 786440 | tf_op jit(solution)/shard_map/ppermute | solution.py:278
  15.9 0.0 collective-permute-done.7.refs_5_
  15.9 0.0 collective-permute-done.6.came_ref
  15.9 0.1 collective-permute-done.5.across_ref
  16.1 0.1 shard_map.60
  16.2 0.1 collective-permute-start.8
  16.3 2.7 %collective-permute-start.9 = (bf16[160,128]{1,0:T(8,128)(2,1)S(1)}, bf16[160,128]{1,0:T(8,128)(2,1)S(1)}, u32[]{:S(2)}, u32[]{:S(2)}) collective-permute-start(bf16[160,128]{1,0:T(8,128)(2,1)S(1)} %get-tuple-element.47), channel_id=1, source_target_pairs={{0,12},{1,13},{2,14},{3,15},{4,8},{5,9},{6,10},{7,11},{8,4},{9,5},... | collective-permute-start | bytes 122888 | tf_op jit(solution)/shard_map/ppermute | solution.py:278
  19.0 0.3 %collective-permute-start.10 = (bf16[144,128]{1,0:T(8,128)(2,1)S(1)}, bf16[144,128]{1,0:T(8,128)(2,1)S(1)}, u32[]{:S(2)}, u32[]{:S(2)}) collective-permute-start(bf16[144,128]{1,0:T(8,128)(2,1)S(1)} %get-tuple-element.48), channel_id=1, source_target_pairs={{0,8},{1,9},{2,10},{3,11},{4,12},{5,13},{6,14},{7,15},{8,0},{9,1},... | collective-permute-start | bytes 110600 | tf_op jit(solution)/shard_map/ppermute | solution.py:278
  19.3 1.5 %collective-permute-start.11 = (bf16[144,128]{1,0:T(8,128)(2,1)S(1)}, bf16[144,128]{1,0:T(8,128)(2,1)S(1)}, u32[]{:S(2)}, u32[]{:S(2)}) collective-permute-start(bf16[144,128]{1,0:T(8,128)(2,1)S(1)} %get-tuple-element.49), channel_id=1, source_target_pairs={{0,4},{1,5},{2,6},{3,7},{4,0},{5,1},{6,2},{7,3},{8,12},{9,13},{10,... | collective-permute-start | bytes 110600 | tf_op jit(solution)/shard_map/ppermute | solution.py:278
  20.8 3.1 %collective-permute-done.10.refs_2_ = bf16[144,128]{1,0:T(8,128)(2,1)S(1)} collective-permute-done((bf16[144,128]{1,0:T(8,128)(2,1)S(1)}, bf16[144,128]{1,0:T(8,128)(2,1)S(1)}, u32[]{:S(2)}, u32[]{:S(2)}) %collective-permute-start.10) | collective-permute-done | bytes 36896 | tf_op jit(solution)/shard_map/ppermute | solution.py:278
  23.9 0.1 collective-permute-done.11.refs_3_
  24.0 0.0 collective-permute-done.9.refs_1_
  24.0 0.0 collective-permute-done.8.refs_6_
  24.0 0.0 collective-permute-done.2.refs_7_
  24.0 0.1 collective-permute-start.12
  24.1 0.7 %shard_map.61 = (f32[2,32,128]{2,1,0:T(8,128)S(1)}, f32[2,8,2,8,128]{4,3,2,1,0:T(8,128)S(1)}) custom-call(f32[128,128]{1,0:T(8,128)S(1)} %get-tuple-element.50.refs_0_, bf16[160,128]{1,0:T(8,128)(2,1)S(1)} %collective-permute-done.9.refs_1_, bf16[144,128]{1,0:T(8,128)(2,1)S(1)} %collective-permute-done.10.refs_2_, ...), custom_call_target="tpu_custom_call" | custom-call | tf_op jit(solution)/shard_map/pallas_call | solution.py:248
  24.8 0.8 %collective-permute-done.12.queries_ref = bf16[4,8,4096]{2,1,0:T(8,128)(2,1)S(1)} collective-permute-done((bf16[4,8,4096]{2,1,0:T(8,128)(2,1)S(1)}, bf16[4,8,4096]{2,1,0:T(8,128)(2,1)S(1)}, u32[]{:S(2)}, u32[]{:S(2)}) %collective-permute-start.12) | collective-permute-done | bytes 262176 | tf_op jit(solution)/shard_map/ppermute | solution.py:278
  25.6 0.8 %shard_map.62 = f32[2,128]{1,0:T(2,128)} custom-call(f32[2,32,128]{2,1,0:T(8,128)S(1)} %get-tuple-element.57.grads_ref, f32[2,8,2,8,128]{4,3,2,1,0:T(8,128)S(1)} %get-tuple-element.58.before_ref, bf16[4,8,4096]{2,1,0:T(8,128)(2,1)S(1)} %collective-permute-done.12.queries_ref), custom_call_target="tpu_custom_call" | custom-call | tf_op jit(solution)/shard_map/pallas_call | solution.py:261
  (2 shorter events, 0.0 us)
Async XLA Ops:
  0.0 6.3 %copy-start.1 = (bf16[1792,64]{0,1:T(8,128)(2,1)S(1)}, bf16[1792,64]{0,1:T(8,128)(2,1)}, u32[]{:S(2)}) copy-start(bf16[1792,64]{0,1:T(8,128)(2,1)} %param.8) | copy-start | bytes 688132
  0.0 6.3 %copy-start = (bf16[1792,2048]{1,0:T(8,128)(2,1)S(1)}, bf16[1792,2048]{1,0:T(8,128)(2,1)}, u32[]{:S(2)}) copy-start(bf16[1792,2048]{1,0:T(8,128)(2,1)} %w_ref.1) | copy-start | bytes 22020100
  0.0 8.4 %collective-permute-start = (bf16[1,8,4096]{2,1,0:T(8,128)(2,1)}, bf16[1,8,4096]{2,1,0:T(8,128)(2,1)S(1)}, u32[]{:S(2)}, u32[]{:S(2)}) collective-permute-start(bf16[1,8,4096]{2,1,0:T(8,128)(2,1)} %bitcast.5), channel_id=1, source_target_pairs={{0,8},{1,9},{2,10},{3,11},{4,12},{5,13},{6,14},{7,15},{8,0},{9,1},... | collective-permute-start | bytes 196616 | tf_op jit(solution)/shard_map/ppermute | solution.py:278
  4.0 4.4 %copy-start.2 = (bf16[8,4096]{1,0:T(8,128)(2,1)S(1)}, bf16[8,4096]{1,0:T(8,128)(2,1)}, u32[]{:S(2)}) copy-start(bf16[8,4096]{1,0:T(8,128)(2,1)} %param.9) | copy-start | bytes 196612
  7.7 2.3 %collective-permute-start.3 = (f32[2,128,128]{2,1,0:T(8,128)S(1)}, f32[2,128,128]{2,1,0:T(8,128)S(1)}, u32[]{:S(2)}, u32[]{:S(2)}) collective-permute-start(f32[2,128,128]{2,1,0:T(8,128)S(1)} %get-tuple-element.36), channel_id=1, source_target_pairs={{0,1},{1,0},{2,3},{3,2},{4,5},{5,4},{6,7},{7,6},{8,9},{9,8},{10,11... | collective-permute-start | bytes 393224 | tf_op jit(solution)/shard_map/ppermute | solution.py:278
  7.8 2.2 %collective-permute-start.4 = (f32[2,128,128]{2,1,0:T(8,128)S(1)}, f32[2,128,128]{2,1,0:T(8,128)S(1)}, u32[]{:S(2)}, u32[]{:S(2)}) collective-permute-start(f32[2,128,128]{2,1,0:T(8,128)S(1)} %get-tuple-element.37), channel_id=1, source_target_pairs={{0,1},{1,0},{2,3},{3,2},{4,5},{5,4},{6,7},{7,6},{8,9},{9,8},{10,11... | collective-permute-start | bytes 393224 | tf_op jit(solution)/shard_map/ppermute | solution.py:278
  8.3 7.6 %collective-permute-start.6 = (f32[4,128,128]{2,1,0:T(8,128)S(1)}, f32[4,128,128]{2,1,0:T(8,128)S(1)}, u32[]{:S(2)}, u32[]{:S(2)}) collective-permute-start(f32[4,128,128]{2,1,0:T(8,128)S(1)} %get-tuple-element.38), channel_id=1, source_target_pairs={{0,1},{1,0},{2,3},{3,2},{4,5},{5,4},{6,7},{7,6},{8,9},{9,8},{10,11... | collective-permute-start | bytes 786440 | tf_op jit(solution)/shard_map/ppermute | solution.py:278
  8.4 5.9 %collective-permute-start.1 = (bf16[2,8,4096]{2,1,0:T(8,128)(2,1)S(1)}, bf16[2,8,4096]{2,1,0:T(8,128)(2,1)S(1)}, u32[]{:S(2)}, u32[]{:S(2)}) collective-permute-start(bf16[2,8,4096]{2,1,0:T(8,128)(2,1)S(1)} %shard_map.55.left_ref), channel_id=1, source_target_pairs={{0,4},{1,5},{2,6},{3,7},{4,0},{5,1},{6,2},{7,3},{8,12},{9,13},{10,... | collective-permute-start | bytes 393224 | tf_op jit(solution)/shard_map/ppermute | solution.py:278
  10.1 6.0 %collective-permute-start.5 = (bf16[4,144,128]{2,1,0:T(8,128)(2,1)S(1)}, bf16[4,144,128]{2,1,0:T(8,128)(2,1)S(1)}, u32[]{:S(2)}, u32[]{:S(2)}) collective-permute-start(bf16[4,144,128]{2,1,0:T(8,128)(2,1)S(1)} %shard_map.59), channel_id=1, source_target_pairs={{0,2},{1,3},{2,0},{3,1},{4,6},{5,7},{6,4},{7,5},{8,10},{9,11},{10,... | collective-permute-start | bytes 442376 | tf_op jit(solution)/shard_map/ppermute | solution.py:278
  11.7 4.2 %collective-permute-start.7 = (bf16[2,8,4096]{2,1,0:T(8,128)(2,1)S(1)}, bf16[2,8,4096]{2,1,0:T(8,128)(2,1)S(1)}, u32[]{:S(2)}, u32[]{:S(2)}) collective-permute-start(bf16[2,8,4096]{2,1,0:T(8,128)(2,1)S(1)} %shard_map.55.left_ref), channel_id=1, source_target_pairs={{0,1},{1,0},{2,3},{3,2},{4,5},{5,4},{6,7},{7,6},{8,9},{9,8},{10,11... | collective-permute-start | bytes 393224 | tf_op jit(solution)/shard_map/ppermute | solution.py:278
  14.3 9.7 %collective-permute-start.2 = (bf16[4,8,4096]{2,1,0:T(8,128)(2,1)S(1)}, bf16[4,8,4096]{2,1,0:T(8,128)(2,1)S(1)}, u32[]{:S(2)}, u32[]{:S(2)}) collective-permute-start(bf16[4,8,4096]{2,1,0:T(8,128)(2,1)S(1)} %shard_map.56.refs_4_), channel_id=1, source_target_pairs={{0,2},{1,3},{2,0},{3,1},{4,6},{5,7},{6,4},{7,5},{8,10},{9,11},{10,... | collective-permute-start | bytes 786440 | tf_op jit(solution)/shard_map/ppermute | solution.py:278
  16.2 7.8 %collective-permute-start.8 = (bf16[2,8,4096]{2,1,0:T(8,128)(2,1)S(1)}, bf16[2,8,4096]{2,1,0:T(8,128)(2,1)S(1)}, u32[]{:S(2)}, u32[]{:S(2)}) collective-permute-start(bf16[2,8,4096]{2,1,0:T(8,128)(2,1)S(1)} %collective-permute-done.1.right_ref), channel_id=1, source_target_pairs={{0,1},{1,0},{2,3},{3,2},{4,5},{5,4},{6,7},{7,6},{8,9},{9,8},{10,11... | collective-permute-start | bytes 393224 | tf_op jit(solution)/shard_map/ppermute | solution.py:278
  16.3 7.7 %collective-permute-start.9 = (bf16[160,128]{1,0:T(8,128)(2,1)S(1)}, bf16[160,128]{1,0:T(8,128)(2,1)S(1)}, u32[]{:S(2)}, u32[]{:S(2)}) collective-permute-start(bf16[160,128]{1,0:T(8,128)(2,1)S(1)} %get-tuple-element.47), channel_id=1, source_target_pairs={{0,12},{1,13},{2,14},{3,15},{4,8},{5,9},{6,10},{7,11},{8,4},{9,5},... | collective-permute-start | bytes 122888 | tf_op jit(solution)/shard_map/ppermute | solution.py:278
  19.0 4.9 %collective-permute-start.10 = (bf16[144,128]{1,0:T(8,128)(2,1)S(1)}, bf16[144,128]{1,0:T(8,128)(2,1)S(1)}, u32[]{:S(2)}, u32[]{:S(2)}) collective-permute-start(bf16[144,128]{1,0:T(8,128)(2,1)S(1)} %get-tuple-element.48), channel_id=1, source_target_pairs={{0,8},{1,9},{2,10},{3,11},{4,12},{5,13},{6,14},{7,15},{8,0},{9,1},... | collective-permute-start | bytes 110600 | tf_op jit(solution)/shard_map/ppermute | solution.py:278
  19.3 4.7 %collective-permute-start.11 = (bf16[144,128]{1,0:T(8,128)(2,1)S(1)}, bf16[144,128]{1,0:T(8,128)(2,1)S(1)}, u32[]{:S(2)}, u32[]{:S(2)}) collective-permute-start(bf16[144,128]{1,0:T(8,128)(2,1)S(1)} %get-tuple-element.49), channel_id=1, source_target_pairs={{0,4},{1,5},{2,6},{3,7},{4,0},{5,1},{6,2},{7,3},{8,12},{9,13},{10,... | collective-permute-start | bytes 110600 | tf_op jit(solution)/shard_map/ppermute | solution.py:278
  24.0 1.6 %collective-permute-start.12 = (bf16[4,8,4096]{2,1,0:T(8,128)(2,1)S(1)}, bf16[4,8,4096]{2,1,0:T(8,128)(2,1)S(1)}, u32[]{:S(2)}, u32[]{:S(2)}) collective-permute-start(bf16[4,8,4096]{2,1,0:T(8,128)(2,1)S(1)} %collective-permute-done.2.refs_7_), channel_id=1, source_target_pairs={{0,1},{1,0},{2,3},{3,2},{4,5},{5,4},{6,7},{7,6},{8,9},{9,8},{10,11... | collective-permute-start | bytes 786440 | tf_op jit(solution)/shard_map/ppermute | solution.py:278

commit v21 on v20

--- a/solution.py
+++ b/solution.py
@@ -277,7 +277,7 @@
         distance = 2 * chip + core
         return lax.ppermute(array, "ex", [(i, i ^ distance) for i in range(devices)])
 
-    steps = [1 << bit for bit in reversed(range(chips.bit_length() - 1))]
+    steps = [chips - 2] + [1 << bit for bit in reversed(range(chips.bit_length() - 2))]
     held, reach = queries[None], [0]
     came_held = swap(held, chip=steps[0])
     lows = project(inputs, out_grads, proj_in.T, proj_out.T, devices)

time: 26.6 us -> 27.1 us (1.019)
  waiting for transfers between devices: 6.83 us -> 7.74 us
  starting transfers between devices: 14.1 us -> 13.7 us
    ppermute x13, waiting for transfers between devices: 6.83 us -> 7.74 us  [swap(): lax.ppermute(array, 'ex', [(i, i ^ distance) for i in range(devices)])]
    ppermute x13, starting transfers between devices: 14.1 us -> 13.7 us  [swap(): lax.ppermute(array, 'ex', [(i, i ^ distance) for i in range(devices)])]
where the time goes in v21:
time: 27.1 us; the launch traced here: 27 us
  starting transfers between devices  13.7 us (51%)
  waiting for transfers between devices  7.74 us (29%)
  Pallas kernels  5.39 us (20%)
    ppermute x13, starting transfers between devices, swap(): lax.ppermute(array, 'ex', [(i, i ^ distance) for i in range(devices)])  13.7 us
    ppermute x13, waiting for transfers between devices, swap(): lax.ppermute(array, 'ex', [(i, i ^ distance) for i in range(devices)])  7.74 us
    pallas_call x1, Pallas kernels, project_loaded(): pl.pallas_call(project_loaded_kernel, out_shape=[jax.ShapeDtypeStruct((ra...  2.22 us
    pallas_call x1, Pallas kernels, project(): pl.pallas_call(functools.partial(project_kernel, rows), out_shape=[half]...  1.43 us
    pallas_call x1, Pallas kernels, last_scores(): pl.pallas_call(functools.partial(last_score_kernel, chips), out_shape=jax...  0.81 us
    pallas_call x1, Pallas kernels, first_scores(): pl.pallas_call(functools.partial(first_score_kernel, len(parts), held), o...  0.7 us
  transfers between devices with their start and end apart: 13, of which 5 were waited for; matrix products, arithmetic and copies ran while one was open for 0% of the time, Pallas kernels for 17%

profile of v21, /device:TPU:0, one launch (start us, length us, event | category | flops | bytes accessed | tf_op | source)
XLA Modules:
  0.0 27.0 jit_solution(9707724758726569566)
XLA Ops:
  0.0 0.0 copy-start.1
  0.0 0.0 copy-start
  0.0 5.0 %collective-permute-start = (bf16[1,8,4096]{2,1,0:T(8,128)(2,1)}, bf16[1,8,4096]{2,1,0:T(8,128)(2,1)S(1)}, u32[]{:S(2)}, u32[]{:S(2)}) collective-permute-start(bf16[1,8,4096]{2,1,0:T(8,128)(2,1)} %bitcast.5), channel_id=1, source_target_pairs={{0,12},{1,13},{2,14},{3,15},{4,8},{5,9},{6,10},{7,11},{8,4},{9,5},... | collective-permute-start | bytes 196616 | tf_op jit(solution)/shard_map/ppermute | solution.py:278
  5.1 0.0 copy-start.2
  5.1 2.2 %shard_map.57 = (f32[64,2048]{1,0:T(8,128)S(1)}, f32[64,2048]{1,0:T(8,128)S(1)}) custom-call(bf16[512,2048]{1,0:T(8,128)(2,1)} %x_hbm.1, bf16[1792,2048]{1,0:T(8,128)(2,1)} %w_ref.1, bf16[64,512]{1,0:T(8,128)(2,1)} %bitcast.7, bf16[64,1792]{1,0:T(8,128)(2,1)} %bitcast.3), custom_call_target="tpu_custom_call" | custom-call | flops 167772160 | bytes 2621440 | tf_op jit(solution)/shard_map/pallas_call | solution.py:50
  7.3 0.0 copy-done.1
  7.3 0.0 copy-done
  7.3 1.4 %shard_map.58 = (f32[2,128,128]{2,1,0:T(8,128)S(1)}, f32[2,128,128]{2,1,0:T(8,128)S(1)}, f32[4,128,128]{2,1,0:T(8,128)S(1)}, f32[4,128,128]{2,1,0:T(8,128)S(1)}, f32[4,128,128]{2,1,0:T(8,128)S(1)}) custom-call(f32[64,2048]{1,0:T(8,128)S(1)} %get-tuple-element.32.low_in_ref, f32[64,2048]{1,0:T(8,128)S(1)} %get-tuple-element.33.low_out_ref, ...), custom_call_target="tpu_custom_call" | custom-call | flops 469762048 | bytes 7340032 | tf_op jit(solution)/shard_map/pallas_call | solution.py:99
  8.7 0.1 collective-permute-start.3
  8.8 0.5 %collective-permute-start.4 = (f32[2,128,128]{2,1,0:T(8,128)S(1)}, f32[2,128,128]{2,1,0:T(8,128)S(1)}, u32[]{:S(2)}, u32[]{:S(2)}) collective-permute-start(f32[2,128,128]{2,1,0:T(8,128)S(1)} %get-tuple-element.37), channel_id=1, source_target_pairs={{0,1},{1,0},{2,3},{3,2},{4,5},{5,4},{6,7},{7,6},{8,9},{9,8},{10,11... | collective-permute-start | bytes 393224 | tf_op jit(solution)/shard_map/ppermute | solution.py:278
  9.3 0.1 collective-permute-start.6
  9.4 0.0 collective-permute-done.right_ref
  9.4 0.0 copy-done.2
  9.4 0.2 collective-permute-start.1
  9.6 0.5 %collective-permute-done.3.refs_0_ = f32[2,128,128]{2,1,0:T(8,128)S(1)} collective-permute-done((f32[2,128,128]{2,1,0:T(8,128)S(1)}, f32[2,128,128]{2,1,0:T(8,128)S(1)}, u32[]{:S(2)}, u32[]{:S(2)}) %collective-permute-start.3) | collective-permute-done | bytes 131104 | tf_op jit(solution)/shard_map/ppermute | solution.py:278
  10.2 0.2 collective-permute-done.4.refs_1_
  10.3 0.1 shard_map.59
  10.4 1.6 %collective-permute-start.5 = (bf16[4,144,128]{2,1,0:T(8,128)(2,1)S(1)}, bf16[4,144,128]{2,1,0:T(8,128)(2,1)S(1)}, u32[]{:S(2)}, u32[]{:S(2)}) collective-permute-start(bf16[4,144,128]{2,1,0:T(8,128)(2,1)S(1)} %shard_map.59), channel_id=1, source_target_pairs={{0,2},{1,3},{2,0},{3,1},{4,6},{5,7},{6,4},{7,5},{8,10},{9,11},{10,... | collective-permute-start | bytes 442376 | tf_op jit(solution)/shard_map/ppermute | solution.py:278
  12.0 0.0 collective-permute-start.7
  12.0 3.3 %collective-permute-done.1.right_ref = bf16[2,8,4096]{2,1,0:T(8,128)(2,1)S(1)} collective-permute-done((bf16[2,8,4096]{2,1,0:T(8,128)(2,1)S(1)}, bf16[2,8,4096]{2,1,0:T(8,128)(2,1)S(1)}, u32[]{:S(2)}, u32[]{:S(2)}) %collective-permute-start.1) | collective-permute-done | bytes 131104 | tf_op jit(solution)/shard_map/ppermute | solution.py:278
  15.4 1.6 %collective-permute-start.2 = (bf16[4,8,4096]{2,1,0:T(8,128)(2,1)S(1)}, bf16[4,8,4096]{2,1,0:T(8,128)(2,1)S(1)}, u32[]{:S(2)}, u32[]{:S(2)}) collective-permute-start(bf16[4,8,4096]{2,1,0:T(8,128)(2,1)S(1)} %shard_map.56.refs_4_), channel_id=1, source_target_pairs={{0,2},{1,3},{2,0},{3,1},{4,6},{5,7},{6,4},{7,5},{8,10},{9,11},{10,... | collective-permute-start | bytes 786440 | tf_op jit(solution)/shard_map/ppermute | solution.py:278
  17.0 0.0 collective-permute-done.7.refs_5_
  17.0 0.0 collective-permute-done.6.came_ref
  17.0 0.0 collective-permute-done.5.across_ref
  17.0 0.1 shard_map.60
  17.1 0.1 collective-permute-start.8
  17.2 1.8 %collective-permute-start.9 = (bf16[160,128]{1,0:T(8,128)(2,1)S(1)}, bf16[160,128]{1,0:T(8,128)(2,1)S(1)}, u32[]{:S(2)}, u32[]{:S(2)}) collective-permute-start(bf16[160,128]{1,0:T(8,128)(2,1)S(1)} %get-tuple-element.47), channel_id=1, source_target_pairs={{0,12},{1,13},{2,14},{3,15},{4,8},{5,9},{6,10},{7,11},{8,4},{9,5},... | collective-permute-start | bytes 122888 | tf_op jit(solution)/shard_map/ppermute | solution.py:278
  19.0 0.3 %collective-permute-start.10 = (bf16[144,128]{1,0:T(8,128)(2,1)S(1)}, bf16[144,128]{1,0:T(8,128)(2,1)S(1)}, u32[]{:S(2)}, u32[]{:S(2)}) collective-permute-start(bf16[144,128]{1,0:T(8,128)(2,1)S(1)} %get-tuple-element.48), channel_id=1, source_target_pairs={{0,8},{1,9},{2,10},{3,11},{4,12},{5,13},{6,14},{7,15},{8,0},{9,1},... | collective-permute-start | bytes 110600 | tf_op jit(solution)/shard_map/ppermute | solution.py:278
  19.3 2.3 %collective-permute-start.11 = (bf16[144,128]{1,0:T(8,128)(2,1)S(1)}, bf16[144,128]{1,0:T(8,128)(2,1)S(1)}, u32[]{:S(2)}, u32[]{:S(2)}) collective-permute-start(bf16[144,128]{1,0:T(8,128)(2,1)S(1)} %get-tuple-element.49), channel_id=1, source_target_pairs={{0,4},{1,5},{2,6},{3,7},{4,0},{5,1},{6,2},{7,3},{8,12},{9,13},{10,... | collective-permute-start | bytes 110600 | tf_op jit(solution)/shard_map/ppermute | solution.py:278
  21.6 2.9 %collective-permute-done.10.refs_2_ = bf16[144,128]{1,0:T(8,128)(2,1)S(1)} collective-permute-done((bf16[144,128]{1,0:T(8,128)(2,1)S(1)}, bf16[144,128]{1,0:T(8,128)(2,1)S(1)}, u32[]{:S(2)}, u32[]{:S(2)}) %collective-permute-start.10) | collective-permute-done | bytes 36896 | tf_op jit(solution)/shard_map/ppermute | solution.py:278
  24.6 0.0 collective-permute-done.11.refs_3_
  24.6 0.0 collective-permute-done.9.refs_1_
  24.6 0.0 collective-permute-done.8.refs_6_
  24.6 0.0 collective-permute-done.2.refs_7_
  24.6 0.1 collective-permute-start.12
  24.7 0.7 %shard_map.61 = (f32[2,32,128]{2,1,0:T(8,128)S(1)}, f32[2,8,2,8,128]{4,3,2,1,0:T(8,128)S(1)}) custom-call(f32[128,128]{1,0:T(8,128)S(1)} %get-tuple-element.50.refs_0_, bf16[160,128]{1,0:T(8,128)(2,1)S(1)} %collective-permute-done.9.refs_1_, bf16[144,128]{1,0:T(8,128)(2,1)S(1)} %collective-permute-done.10.refs_2_, ...), custom_call_target="tpu_custom_call" | custom-call | tf_op jit(solution)/shard_map/pallas_call | solution.py:248
  25.4 0.8 %collective-permute-done.12.queries_ref = bf16[4,8,4096]{2,1,0:T(8,128)(2,1)S(1)} collective-permute-done((bf16[4,8,4096]{2,1,0:T(8,128)(2,1)S(1)}, bf16[4,8,4096]{2,1,0:T(8,128)(2,1)S(1)}, u32[]{:S(2)}, u32[]{:S(2)}) %collective-permute-start.12) | collective-permute-done | bytes 262176 | tf_op jit(solution)/shard_map/ppermute | solution.py:278
  26.2 0.8 %shard_map.62 = f32[2,128]{1,0:T(2,128)} custom-call(f32[2,32,128]{2,1,0:T(8,128)S(1)} %get-tuple-element.57.grads_ref, f32[2,8,2,8,128]{4,3,2,1,0:T(8,128)S(1)} %get-tuple-element.58.before_ref, bf16[4,8,4096]{2,1,0:T(8,128)(2,1)S(1)} %collective-permute-done.12.queries_ref), custom_call_target="tpu_custom_call" | custom-call | tf_op jit(solution)/shard_map/pallas_call | solution.py:261
  (2 shorter events, 0.0 us)
Async XLA Ops:
  0.0 7.3 %copy-start.1 = (bf16[1792,64]{0,1:T(8,128)(2,1)S(1)}, bf16[1792,64]{0,1:T(8,128)(2,1)}, u32[]{:S(2)}) copy-start(bf16[1792,64]{0,1:T(8,128)(2,1)} %param.8) | copy-start | bytes 688132
  0.0 7.3 %copy-start = (bf16[1792,2048]{1,0:T(8,128)(2,1)S(1)}, bf16[1792,2048]{1,0:T(8,128)(2,1)}, u32[]{:S(2)}) copy-start(bf16[1792,2048]{1,0:T(8,128)(2,1)} %w_ref.1) | copy-start | bytes 22020100
  0.0 9.4 %collective-permute-start = (bf16[1,8,4096]{2,1,0:T(8,128)(2,1)}, bf16[1,8,4096]{2,1,0:T(8,128)(2,1)S(1)}, u32[]{:S(2)}, u32[]{:S(2)}) collective-permute-start(bf16[1,8,4096]{2,1,0:T(8,128)(2,1)} %bitcast.5), channel_id=1, source_target_pairs={{0,12},{1,13},{2,14},{3,15},{4,8},{5,9},{6,10},{7,11},{8,4},{9,5},... | collective-permute-start | bytes 196616 | tf_op jit(solution)/shard_map/ppermute | solution.py:278
  5.1 4.4 %copy-start.2 = (bf16[8,4096]{1,0:T(8,128)(2,1)S(1)}, bf16[8,4096]{1,0:T(8,128)(2,1)}, u32[]{:S(2)}) copy-start(bf16[8,4096]{1,0:T(8,128)(2,1)} %param.9) | copy-start | bytes 196612
  8.7 1.4 %collective-permute-start.3 = (f32[2,128,128]{2,1,0:T(8,128)S(1)}, f32[2,128,128]{2,1,0:T(8,128)S(1)}, u32[]{:S(2)}, u32[]{:S(2)}) collective-permute-start(f32[2,128,128]{2,1,0:T(8,128)S(1)} %get-tuple-element.36), channel_id=1, source_target_pairs={{0,1},{1,0},{2,3},{3,2},{4,5},{5,4},{6,7},{7,6},{8,9},{9,8},{10,11... | collective-permute-start | bytes 393224 | tf_op jit(solution)/shard_map/ppermute | solution.py:278
  8.8 1.5 %collective-permute-start.4 = (f32[2,128,128]{2,1,0:T(8,128)S(1)}, f32[2,128,128]{2,1,0:T(8,128)S(1)}, u32[]{:S(2)}, u32[]{:S(2)}) collective-permute-start(f32[2,128,128]{2,1,0:T(8,128)S(1)} %get-tuple-element.37), channel_id=1, source_target_pairs={{0,1},{1,0},{2,3},{3,2},{4,5},{5,4},{6,7},{7,6},{8,9},{9,8},{10,11... | collective-permute-start | bytes 393224 | tf_op jit(solution)/shard_map/ppermute | solution.py:278
  9.3 7.6 %collective-permute-start.6 = (f32[4,128,128]{2,1,0:T(8,128)S(1)}, f32[4,128,128]{2,1,0:T(8,128)S(1)}, u32[]{:S(2)}, u32[]{:S(2)}) collective-permute-start(f32[4,128,128]{2,1,0:T(8,128)S(1)} %get-tuple-element.38), channel_id=1, source_target_pairs={{0,1},{1,0},{2,3},{3,2},{4,5},{5,4},{6,7},{7,6},{8,9},{9,8},{10,11... | collective-permute-start | bytes 786440 | tf_op jit(solution)/shard_map/ppermute | solution.py:278
  9.4 5.9 %collective-permute-start.1 = (bf16[2,8,4096]{2,1,0:T(8,128)(2,1)S(1)}, bf16[2,8,4096]{2,1,0:T(8,128)(2,1)S(1)}, u32[]{:S(2)}, u32[]{:S(2)}) collective-permute-start(bf16[2,8,4096]{2,1,0:T(8,128)(2,1)S(1)} %shard_map.55.left_ref), channel_id=1, source_target_pairs={{0,4},{1,5},{2,6},{3,7},{4,0},{5,1},{6,2},{7,3},{8,12},{9,13},{10,... | collective-permute-start | bytes 393224 | tf_op jit(solution)/shard_map/ppermute | solution.py:278
  10.4 6.6 %collective-permute-start.5 = (bf16[4,144,128]{2,1,0:T(8,128)(2,1)S(1)}, bf16[4,144,128]{2,1,0:T(8,128)(2,1)S(1)}, u32[]{:S(2)}, u32[]{:S(2)}) collective-permute-start(bf16[4,144,128]{2,1,0:T(8,128)(2,1)S(1)} %shard_map.59), channel_id=1, source_target_pairs={{0,2},{1,3},{2,0},{3,1},{4,6},{5,7},{6,4},{7,5},{8,10},{9,11},{10,... | collective-permute-start | bytes 442376 | tf_op jit(solution)/shard_map/ppermute | solution.py:278
  12.0 4.9 %collective-permute-start.7 = (bf16[2,8,4096]{2,1,0:T(8,128)(2,1)S(1)}, bf16[2,8,4096]{2,1,0:T(8,128)(2,1)S(1)}, u32[]{:S(2)}, u32[]{:S(2)}) collective-permute-start(bf16[2,8,4096]{2,1,0:T(8,128)(2,1)S(1)} %shard_map.55.left_ref), channel_id=1, source_target_pairs={{0,1},{1,0},{2,3},{3,2},{4,5},{5,4},{6,7},{7,6},{8,9},{9,8},{10,11... | collective-permute-start | bytes 393224 | tf_op jit(solution)/shard_map/ppermute | solution.py:278
  15.4 9.2 %collective-permute-start.2 = (bf16[4,8,4096]{2,1,0:T(8,128)(2,1)S(1)}, bf16[4,8,4096]{2,1,0:T(8,128)(2,1)S(1)}, u32[]{:S(2)}, u32[]{:S(2)}) collective-permute-start(bf16[4,8,4096]{2,1,0:T(8,128)(2,1)S(1)} %shard_map.56.refs_4_), channel_id=1, source_target_pairs={{0,2},{1,3},{2,0},{3,1},{4,6},{5,7},{6,4},{7,5},{8,10},{9,11},{10,... | collective-permute-start | bytes 786440 | tf_op jit(solution)/shard_map/ppermute | solution.py:278
  17.1 7.4 %collective-permute-start.8 = (bf16[2,8,4096]{2,1,0:T(8,128)(2,1)S(1)}, bf16[2,8,4096]{2,1,0:T(8,128)(2,1)S(1)}, u32[]{:S(2)}, u32[]{:S(2)}) collective-permute-start(bf16[2,8,4096]{2,1,0:T(8,128)(2,1)S(1)} %collective-permute-done.1.right_ref), channel_id=1, source_target_pairs={{0,1},{1,0},{2,3},{3,2},{4,5},{5,4},{6,7},{7,6},{8,9},{9,8},{10,11... | collective-permute-start | bytes 393224 | tf_op jit(solution)/shard_map/ppermute | solution.py:278
  17.2 7.4 %collective-permute-start.9 = (bf16[160,128]{1,0:T(8,128)(2,1)S(1)}, bf16[160,128]{1,0:T(8,128)(2,1)S(1)}, u32[]{:S(2)}, u32[]{:S(2)}) collective-permute-start(bf16[160,128]{1,0:T(8,128)(2,1)S(1)} %get-tuple-element.47), channel_id=1, source_target_pairs={{0,12},{1,13},{2,14},{3,15},{4,8},{5,9},{6,10},{7,11},{8,4},{9,5},... | collective-permute-start | bytes 122888 | tf_op jit(solution)/shard_map/ppermute | solution.py:278
  19.0 5.5 %collective-permute-start.10 = (bf16[144,128]{1,0:T(8,128)(2,1)S(1)}, bf16[144,128]{1,0:T(8,128)(2,1)S(1)}, u32[]{:S(2)}, u32[]{:S(2)}) collective-permute-start(bf16[144,128]{1,0:T(8,128)(2,1)S(1)} %get-tuple-element.48), channel_id=1, source_target_pairs={{0,8},{1,9},{2,10},{3,11},{4,12},{5,13},{6,14},{7,15},{8,0},{9,1},... | collective-permute-start | bytes 110600 | tf_op jit(solution)/shard_map/ppermute | solution.py:278
  19.3 5.2 %collective-permute-start.11 = (bf16[144,128]{1,0:T(8,128)(2,1)S(1)}, bf16[144,128]{1,0:T(8,128)(2,1)S(1)}, u32[]{:S(2)}, u32[]{:S(2)}) collective-permute-start(bf16[144,128]{1,0:T(8,128)(2,1)S(1)} %get-tuple-element.49), channel_id=1, source_target_pairs={{0,4},{1,5},{2,6},{3,7},{4,0},{5,1},{6,2},{7,3},{8,12},{9,13},{10,... | collective-permute-start | bytes 110600 | tf_op jit(solution)/shard_map/ppermute | solution.py:278
  24.6 1.6 %collective-permute-start.12 = (bf16[4,8,4096]{2,1,0:T(8,128)(2,1)S(1)}, bf16[4,8,4096]{2,1,0:T(8,128)(2,1)S(1)}, u32[]{:S(2)}, u32[]{:S(2)}) collective-permute-start(bf16[4,8,4096]{2,1,0:T(8,128)(2,1)S(1)} %collective-permute-done.2.refs_7_), channel_id=1, source_target_pairs={{0,1},{1,0},{2,3},{3,2},{4,5},{5,4},{6,7},{7,6},{8,9},{9,8},{10,11... | collective-permute-start | bytes 786440 | tf_op jit(solution)/shard_map/ppermute | solution.py:278

commit v22 on v20

--- a/solution.py
+++ b/solution.py
@@ -10,7 +10,7 @@
 SEQ = 64
 VMEM_BYTES = 32 * 1024 * 1024
 LOADED_ROWS = 128
-FAR_PAD = 16
+PAD = 16
 LEFT_OVER = 0.36 * 2.0**-8
 LANES_BY_LANES = (((1,), (1,)), ((), ()))
 HBM_SPEC = pl.BlockSpec(memory_space=pltpu.HBM)
@@ -165,7 +165,7 @@
 def add_kept(kept, came, across):
     depth, rows, width = kept.shape
     own = jax.ShapeDtypeStruct((rows, width), jnp.float32)
-    heights = [rows // 8 * 9 + (FAR_PAD if z > 2 else 0) for z in reversed(range(1, depth))]
+    heights = [rows // 8 * 9 + (2 * PAD if z > 2 else PAD if z == 1 else 0) for z in reversed(range(1, depth))]
     return pl.pallas_call(
         add_kept_kernel,
         out_shape=[own] + [jax.ShapeDtypeStruct((height, width), jnp.bfloat16) for height in heights],

time: 26.6 us -> 26.5 us (level)
  transfers between devices with their start and end apart: 13 -> 13, of which waited for: 5 -> 4; matrix products, arithmetic and copies ran while one was open for 0% -> 0% of each run, Pallas kernels for 17% -> 17%
where the time goes in v22:
time: 26.5 us; the launch traced here: 26.4 us
  starting transfers between devices  14.1 us (53%)
  waiting for transfers between devices  6.75 us (25%)
  Pallas kernels  5.41 us (20%)
    ppermute x13, starting transfers between devices, swap(): lax.ppermute(array, 'ex', [(i, i ^ distance) for i in range(devices)])  14.1 us
    ppermute x13, waiting for transfers between devices, swap(): lax.ppermute(array, 'ex', [(i, i ^ distance) for i in range(devices)])  6.75 us
    pallas_call x1, Pallas kernels, project_loaded(): pl.pallas_call(project_loaded_kernel, out_shape=[jax.ShapeDtypeStruct((ra...  2.22 us
    pallas_call x1, Pallas kernels, project(): pl.pallas_call(functools.partial(project_kernel, rows), out_shape=[half]...  1.43 us
    pallas_call x1, Pallas kernels, last_scores(): pl.pallas_call(functools.partial(last_score_kernel, chips), out_shape=jax...  0.82 us
    pallas_call x1, Pallas kernels, first_scores(): pl.pallas_call(functools.partial(first_score_kernel, len(parts), held), o...  0.7 us
  transfers between devices with their start and end apart: 13, of which 4 were waited for; matrix products, arithmetic and copies ran while one was open for 0% of the time, Pallas kernels for 17%

profile of v22, /device:TPU:0, one launch (start us, length us, event | category | flops | bytes accessed | tf_op | source)
XLA Modules:
  0.0 26.4 jit_solution(15905437009230035756)
XLA Ops:
  0.0 0.0 copy-start.1
  0.0 0.0 copy-start
  0.0 4.0 %collective-permute-start = (bf16[1,8,4096]{2,1,0:T(8,128)(2,1)}, bf16[1,8,4096]{2,1,0:T(8,128)(2,1)S(1)}, u32[]{:S(2)}, u32[]{:S(2)}) collective-permute-start(bf16[1,8,4096]{2,1,0:T(8,128)(2,1)} %bitcast.5), channel_id=1, source_target_pairs={{0,8},{1,9},{2,10},{3,11},{4,12},{5,13},{6,14},{7,15},{8,0},{9,1},... | collective-permute-start | bytes 196616 | tf_op jit(solution)/shard_map/ppermute | solution.py:278
  4.0 0.0 copy-start.2
  4.0 2.2 %shard_map.57 = (f32[64,2048]{1,0:T(8,128)S(1)}, f32[64,2048]{1,0:T(8,128)S(1)}) custom-call(bf16[512,2048]{1,0:T(8,128)(2,1)} %x_hbm.1, bf16[1792,2048]{1,0:T(8,128)(2,1)} %w_ref.1, bf16[64,512]{1,0:T(8,128)(2,1)} %bitcast.7, bf16[64,1792]{1,0:T(8,128)(2,1)} %bitcast.3), custom_call_target="tpu_custom_call" | custom-call | flops 167772160 | bytes 2621440 | tf_op jit(solution)/shard_map/pallas_call | solution.py:50
  6.3 0.0 copy-done.1
  6.3 0.0 copy-done
  6.3 1.4 %shard_map.58 = (f32[2,128,128]{2,1,0:T(8,128)S(1)}, f32[2,128,128]{2,1,0:T(8,128)S(1)}, f32[4,128,128]{2,1,0:T(8,128)S(1)}, f32[4,128,128]{2,1,0:T(8,128)S(1)}, f32[4,128,128]{2,1,0:T(8,128)S(1)}) custom-call(f32[64,2048]{1,0:T(8,128)S(1)} %get-tuple-element.32.low_in_ref, f32[64,2048]{1,0:T(8,128)S(1)} %get-tuple-element.33.low_out_ref, ...), custom_call_target="tpu_custom_call" | custom-call | flops 469762048 | bytes 7340032 | tf_op jit(solution)/shard_map/pallas_call | solution.py:99
  7.7 0.1 collective-permute-start.3
  7.8 0.5 %collective-permute-start.4 = (f32[2,128,128]{2,1,0:T(8,128)S(1)}, f32[2,128,128]{2,1,0:T(8,128)S(1)}, u32[]{:S(2)}, u32[]{:S(2)}) collective-permute-start(f32[2,128,128]{2,1,0:T(8,128)S(1)} %get-tuple-element.37), channel_id=1, source_target_pairs={{0,1},{1,0},{2,3},{3,2},{4,5},{5,4},{6,7},{7,6},{8,9},{9,8},{10,11... | collective-permute-start | bytes 393224 | tf_op jit(solution)/shard_map/ppermute | solution.py:278
  8.3 0.1 collective-permute-start.6
  8.4 0.0 collective-permute-done.right_ref
  8.4 0.0 copy-done.2
  8.4 1.6 %collective-permute-start.1 = (bf16[2,8,4096]{2,1,0:T(8,128)(2,1)S(1)}, bf16[2,8,4096]{2,1,0:T(8,128)(2,1)S(1)}, u32[]{:S(2)}, u32[]{:S(2)}) collective-permute-start(bf16[2,8,4096]{2,1,0:T(8,128)(2,1)S(1)} %shard_map.55.left_ref), channel_id=1, source_target_pairs={{0,4},{1,5},{2,6},{3,7},{4,0},{5,1},{6,2},{7,3},{8,12},{9,13},{10,... | collective-permute-start | bytes 393224 | tf_op jit(solution)/shard_map/ppermute | solution.py:278
  10.0 0.0 collective-permute-done.3.refs_0_
  10.0 0.0 collective-permute-done.4.refs_1_
  10.0 0.1 shard_map.59
  10.1 1.6 %collective-permute-start.5 = (bf16[4,144,128]{2,1,0:T(8,128)(2,1)S(1)}, bf16[4,144,128]{2,1,0:T(8,128)(2,1)S(1)}, u32[]{:S(2)}, u32[]{:S(2)}) collective-permute-start(bf16[4,144,128]{2,1,0:T(8,128)(2,1)S(1)} %shard_map.59), channel_id=1, source_target_pairs={{0,2},{1,3},{2,0},{3,1},{4,6},{5,7},{6,4},{7,5},{8,10},{9,11},{10,... | collective-permute-start | bytes 442376 | tf_op jit(solution)/shard_map/ppermute | solution.py:278
  11.7 0.0 collective-permute-start.7
  11.7 2.6 %collective-permute-done.1.right_ref = bf16[2,8,4096]{2,1,0:T(8,128)(2,1)S(1)} collective-permute-done((bf16[2,8,4096]{2,1,0:T(8,128)(2,1)S(1)}, bf16[2,8,4096]{2,1,0:T(8,128)(2,1)S(1)}, u32[]{:S(2)}, u32[]{:S(2)}) %collective-permute-start.1) | collective-permute-done | bytes 131104 | tf_op jit(solution)/shard_map/ppermute | solution.py:278
  14.3 1.6 %collective-permute-start.2 = (bf16[4,8,4096]{2,1,0:T(8,128)(2,1)S(1)}, bf16[4,8,4096]{2,1,0:T(8,128)(2,1)S(1)}, u32[]{:S(2)}, u32[]{:S(2)}) collective-permute-start(bf16[4,8,4096]{2,1,0:T(8,128)(2,1)S(1)} %shard_map.56.refs_4_), channel_id=1, source_target_pairs={{0,2},{1,3},{2,0},{3,1},{4,6},{5,7},{6,4},{7,5},{8,10},{9,11},{10,... | collective-permute-start | bytes 786440 | tf_op jit(solution)/shard_map/ppermute | solution.py:278
  15.9 0.0 collective-permute-done.7.refs_5_
  15.9 0.0 collective-permute-done.6.came_ref
  15.9 0.1 collective-permute-done.5.across_ref
  16.1 0.1 shard_map.60
  16.2 0.1 collective-permute-start.8
  16.3 2.7 %collective-permute-start.9 = (bf16[176,128]{1,0:T(8,128)(2,1)S(1)}, bf16[176,128]{1,0:T(8,128)(2,1)S(1)}, u32[]{:S(2)}, u32[]{:S(2)}) collective-permute-start(bf16[176,128]{1,0:T(8,128)(2,1)S(1)} %get-tuple-element.47), channel_id=1, source_target_pairs={{0,12},{1,13},{2,14},{3,15},{4,8},{5,9},{6,10},{7,11},{8,4},{9,5},... | collective-permute-start | bytes 135176 | tf_op jit(solution)/shard_map/ppermute | solution.py:278
  19.0 0.0 collective-permute-start.11
  19.0 1.8 %collective-permute-start.10 = (bf16[144,128]{1,0:T(8,128)(2,1)S(1)}, bf16[144,128]{1,0:T(8,128)(2,1)S(1)}, u32[]{:S(2)}, u32[]{:S(2)}) collective-permute-start(bf16[144,128]{1,0:T(8,128)(2,1)S(1)} %get-tuple-element.48), channel_id=1, source_target_pairs={{0,8},{1,9},{2,10},{3,11},{4,12},{5,13},{6,14},{7,15},{8,0},{9,1},... | collective-permute-start | bytes 110600 | tf_op jit(solution)/shard_map/ppermute | solution.py:278
  20.8 3.1 %collective-permute-done.10.refs_2_ = bf16[144,128]{1,0:T(8,128)(2,1)S(1)} collective-permute-done((bf16[144,128]{1,0:T(8,128)(2,1)S(1)}, bf16[144,128]{1,0:T(8,128)(2,1)S(1)}, u32[]{:S(2)}, u32[]{:S(2)}) %collective-permute-start.10) | collective-permute-done | bytes 36896 | tf_op jit(solution)/shard_map/ppermute | solution.py:278
  23.9 0.0 collective-permute-done.11.refs_3_
  23.9 0.0 collective-permute-done.9.refs_1_
  23.9 0.0 collective-permute-done.8.refs_6_
  23.9 0.0 collective-permute-done.2.refs_7_
  23.9 0.1 collective-permute-start.12
  24.0 0.7 %shard_map.61 = (f32[2,32,128]{2,1,0:T(8,128)S(1)}, f32[2,8,2,8,128]{4,3,2,1,0:T(8,128)S(1)}) custom-call(f32[128,128]{1,0:T(8,128)S(1)} %get-tuple-element.50.refs_0_, bf16[176,128]{1,0:T(8,128)(2,1)S(1)} %collective-permute-done.9.refs_1_, bf16[144,128]{1,0:T(8,128)(2,1)S(1)} %collective-permute-done.10.refs_2_, ...), custom_call_target="tpu_custom_call" | custom-call | tf_op jit(solution)/shard_map/pallas_call | solution.py:248
  24.7 0.8 %collective-permute-done.12.queries_ref = bf16[4,8,4096]{2,1,0:T(8,128)(2,1)S(1)} collective-permute-done((bf16[4,8,4096]{2,1,0:T(8,128)(2,1)S(1)}, bf16[4,8,4096]{2,1,0:T(8,128)(2,1)S(1)}, u32[]{:S(2)}, u32[]{:S(2)}) %collective-permute-start.12) | collective-permute-done | bytes 262176 | tf_op jit(solution)/shard_map/ppermute | solution.py:278
  25.5 0.8 %shard_map.62 = f32[2,128]{1,0:T(2,128)} custom-call(f32[2,32,128]{2,1,0:T(8,128)S(1)} %get-tuple-element.57.grads_ref, f32[2,8,2,8,128]{4,3,2,1,0:T(8,128)S(1)} %get-tuple-element.58.before_ref, bf16[4,8,4096]{2,1,0:T(8,128)(2,1)S(1)} %collective-permute-done.12.queries_ref), custom_call_target="tpu_custom_call" | custom-call | tf_op jit(solution)/shard_map/pallas_call | solution.py:261
  (2 shorter events, 0.0 us)
Async XLA Ops:
  0.0 6.3 %copy-start.1 = (bf16[1792,64]{0,1:T(8,128)(2,1)S(1)}, bf16[1792,64]{0,1:T(8,128)(2,1)}, u32[]{:S(2)}) copy-start(bf16[1792,64]{0,1:T(8,128)(2,1)} %param.8) | copy-start | bytes 688132
  0.0 6.3 %copy-start = (bf16[1792,2048]{1,0:T(8,128)(2,1)S(1)}, bf16[1792,2048]{1,0:T(8,128)(2,1)}, u32[]{:S(2)}) copy-start(bf16[1792,2048]{1,0:T(8,128)(2,1)} %w_ref.1) | copy-start | bytes 22020100
  0.0 8.4 %collective-permute-start = (bf16[1,8,4096]{2,1,0:T(8,128)(2,1)}, bf16[1,8,4096]{2,1,0:T(8,128)(2,1)S(1)}, u32[]{:S(2)}, u32[]{:S(2)}) collective-permute-start(bf16[1,8,4096]{2,1,0:T(8,128)(2,1)} %bitcast.5), channel_id=1, source_target_pairs={{0,8},{1,9},{2,10},{3,11},{4,12},{5,13},{6,14},{7,15},{8,0},{9,1},... | collective-permute-start | bytes 196616 | tf_op jit(solution)/shard_map/ppermute | solution.py:278
  4.0 4.4 %copy-start.2 = (bf16[8,4096]{1,0:T(8,128)(2,1)S(1)}, bf16[8,4096]{1,0:T(8,128)(2,1)}, u32[]{:S(2)}) copy-start(bf16[8,4096]{1,0:T(8,128)(2,1)} %param.9) | copy-start | bytes 196612
  7.7 2.3 %collective-permute-start.3 = (f32[2,128,128]{2,1,0:T(8,128)S(1)}, f32[2,128,128]{2,1,0:T(8,128)S(1)}, u32[]{:S(2)}, u32[]{:S(2)}) collective-permute-start(f32[2,128,128]{2,1,0:T(8,128)S(1)} %get-tuple-element.36), channel_id=1, source_target_pairs={{0,1},{1,0},{2,3},{3,2},{4,5},{5,4},{6,7},{7,6},{8,9},{9,8},{10,11... | collective-permute-start | bytes 393224 | tf_op jit(solution)/shard_map/ppermute | solution.py:278
  7.8 2.2 %collective-permute-start.4 = (f32[2,128,128]{2,1,0:T(8,128)S(1)}, f32[2,128,128]{2,1,0:T(8,128)S(1)}, u32[]{:S(2)}, u32[]{:S(2)}) collective-permute-start(f32[2,128,128]{2,1,0:T(8,128)S(1)} %get-tuple-element.37), channel_id=1, source_target_pairs={{0,1},{1,0},{2,3},{3,2},{4,5},{5,4},{6,7},{7,6},{8,9},{9,8},{10,11... | collective-permute-start | bytes 393224 | tf_op jit(solution)/shard_map/ppermute | solution.py:278
  8.3 7.6 %collective-permute-start.6 = (f32[4,128,128]{2,1,0:T(8,128)S(1)}, f32[4,128,128]{2,1,0:T(8,128)S(1)}, u32[]{:S(2)}, u32[]{:S(2)}) collective-permute-start(f32[4,128,128]{2,1,0:T(8,128)S(1)} %get-tuple-element.38), channel_id=1, source_target_pairs={{0,1},{1,0},{2,3},{3,2},{4,5},{5,4},{6,7},{7,6},{8,9},{9,8},{10,11... | collective-permute-start | bytes 786440 | tf_op jit(solution)/shard_map/ppermute | solution.py:278
  8.4 5.9 %collective-permute-start.1 = (bf16[2,8,4096]{2,1,0:T(8,128)(2,1)S(1)}, bf16[2,8,4096]{2,1,0:T(8,128)(2,1)S(1)}, u32[]{:S(2)}, u32[]{:S(2)}) collective-permute-start(bf16[2,8,4096]{2,1,0:T(8,128)(2,1)S(1)} %shard_map.55.left_ref), channel_id=1, source_target_pairs={{0,4},{1,5},{2,6},{3,7},{4,0},{5,1},{6,2},{7,3},{8,12},{9,13},{10,... | collective-permute-start | bytes 393224 | tf_op jit(solution)/shard_map/ppermute | solution.py:278
  10.1 6.0 %collective-permute-start.5 = (bf16[4,144,128]{2,1,0:T(8,128)(2,1)S(1)}, bf16[4,144,128]{2,1,0:T(8,128)(2,1)S(1)}, u32[]{:S(2)}, u32[]{:S(2)}) collective-permute-start(bf16[4,144,128]{2,1,0:T(8,128)(2,1)S(1)} %shard_map.59), channel_id=1, source_target_pairs={{0,2},{1,3},{2,0},{3,1},{4,6},{5,7},{6,4},{7,5},{8,10},{9,11},{10,... | collective-permute-start | bytes 442376 | tf_op jit(solution)/shard_map/ppermute | solution.py:278
  11.7 4.2 %collective-permute-start.7 = (bf16[2,8,4096]{2,1,0:T(8,128)(2,1)S(1)}, bf16[2,8,4096]{2,1,0:T(8,128)(2,1)S(1)}, u32[]{:S(2)}, u32[]{:S(2)}) collective-permute-start(bf16[2,8,4096]{2,1,0:T(8,128)(2,1)S(1)} %shard_map.55.left_ref), channel_id=1, source_target_pairs={{0,1},{1,0},{2,3},{3,2},{4,5},{5,4},{6,7},{7,6},{8,9},{9,8},{10,11... | collective-permute-start | bytes 393224 | tf_op jit(solution)/shard_map/ppermute | solution.py:278
  14.3 9.6 %collective-permute-start.2 = (bf16[4,8,4096]{2,1,0:T(8,128)(2,1)S(1)}, bf16[4,8,4096]{2,1,0:T(8,128)(2,1)S(1)}, u32[]{:S(2)}, u32[]{:S(2)}) collective-permute-start(bf16[4,8,4096]{2,1,0:T(8,128)(2,1)S(1)} %shard_map.56.refs_4_), channel_id=1, source_target_pairs={{0,2},{1,3},{2,0},{3,1},{4,6},{5,7},{6,4},{7,5},{8,10},{9,11},{10,... | collective-permute-start | bytes 786440 | tf_op jit(solution)/shard_map/ppermute | solution.py:278
  16.2 7.7 %collective-permute-start.8 = (bf16[2,8,4096]{2,1,0:T(8,128)(2,1)S(1)}, bf16[2,8,4096]{2,1,0:T(8,128)(2,1)S(1)}, u32[]{:S(2)}, u32[]{:S(2)}) collective-permute-start(bf16[2,8,4096]{2,1,0:T(8,128)(2,1)S(1)} %collective-permute-done.1.right_ref), channel_id=1, source_target_pairs={{0,1},{1,0},{2,3},{3,2},{4,5},{5,4},{6,7},{7,6},{8,9},{9,8},{10,11... | collective-permute-start | bytes 393224 | tf_op jit(solution)/shard_map/ppermute | solution.py:278
  16.3 7.6 %collective-permute-start.9 = (bf16[176,128]{1,0:T(8,128)(2,1)S(1)}, bf16[176,128]{1,0:T(8,128)(2,1)S(1)}, u32[]{:S(2)}, u32[]{:S(2)}) collective-permute-start(bf16[176,128]{1,0:T(8,128)(2,1)S(1)} %get-tuple-element.47), channel_id=1, source_target_pairs={{0,12},{1,13},{2,14},{3,15},{4,8},{5,9},{6,10},{7,11},{8,4},{9,5},... | collective-permute-start | bytes 135176 | tf_op jit(solution)/shard_map/ppermute | solution.py:278
  19.0 4.9 %collective-permute-start.11 = (bf16[160,128]{1,0:T(8,128)(2,1)S(1)}, bf16[160,128]{1,0:T(8,128)(2,1)S(1)}, u32[]{:S(2)}, u32[]{:S(2)}) collective-permute-start(bf16[160,128]{1,0:T(8,128)(2,1)S(1)} %get-tuple-element.49), channel_id=1, source_target_pairs={{0,4},{1,5},{2,6},{3,7},{4,0},{5,1},{6,2},{7,3},{8,12},{9,13},{10,... | collective-permute-start | bytes 122888 | tf_op jit(solution)/shard_map/ppermute | solution.py:278
  19.0 4.9 %collective-permute-start.10 = (bf16[144,128]{1,0:T(8,128)(2,1)S(1)}, bf16[144,128]{1,0:T(8,128)(2,1)S(1)}, u32[]{:S(2)}, u32[]{:S(2)}) collective-permute-start(bf16[144,128]{1,0:T(8,128)(2,1)S(1)} %get-tuple-element.48), channel_id=1, source_target_pairs={{0,8},{1,9},{2,10},{3,11},{4,12},{5,13},{6,14},{7,15},{8,0},{9,1},... | collective-permute-start | bytes 110600 | tf_op jit(solution)/shard_map/ppermute | solution.py:278
  23.9 1.6 %collective-permute-start.12 = (bf16[4,8,4096]{2,1,0:T(8,128)(2,1)S(1)}, bf16[4,8,4096]{2,1,0:T(8,128)(2,1)S(1)}, u32[]{:S(2)}, u32[]{:S(2)}) collective-permute-start(bf16[4,8,4096]{2,1,0:T(8,128)(2,1)S(1)} %collective-permute-done.2.refs_7_), channel_id=1, source_target_pairs={{0,1},{1,0},{2,3},{3,2},{4,5},{5,4},{6,7},{7,6},{8,9},{9,8},{10,11... | collective-permute-start | bytes 786440 | tf_op jit(solution)/shard_map/ppermute | solution.py:278

commit v23 on v18

--- a/solution.py
+++ b/solution.py
@@ -10,7 +10,7 @@
 SEQ = 64
 VMEM_BYTES = 32 * 1024 * 1024
 LOADED_ROWS = 128
-PLAIN = 2
+FAR_PAD = 16
 LEFT_OVER = 0.36 * 2.0**-8
 LANES_BY_LANES = (((1,), (1,)), ((), ()))
 HBM_SPEC = pl.BlockSpec(memory_space=pltpu.HBM)
@@ -120,12 +120,12 @@
     word = above[:part, :]
     for index in range(1, 8):
         word = word + 2.0**index * above[index * part : (index + 1) * part, :]
-    out_ref[rows:, :] = word.astype(jnp.bfloat16)
-
-
-def add_coded(total, ref):
-    part = ref.shape[0] // 9
-    word = ref[8 * part :, :].astype(jnp.float32)
+    out_ref[rows : rows + part, :] = word.astype(jnp.bfloat16)
+
+
+def add_coded(total, rows, ref):
+    part = rows // 8
+    word = ref[rows : rows + part, :].astype(jnp.float32)
     parts = []
     for index in reversed(range(8)):
         above = jnp.floor(word * 0.5**index)
@@ -157,13 +157,10 @@
         def here(first, rows):
             return kept_ref[z, first : first + rows, :] + came_ref[z, first : first + rows, :]
 
-        sums = add_coded(here, across_ref.at[z])
+        sums = add_coded(here, kept_ref.shape[1], across_ref.at[z])
         if z == 0:
             for rows, total in sums:
                 own_ref[rows, :] = total
-        elif z <= PLAIN:
-            for rows, total in sums:
-                out_refs[len(out_refs) - z][rows, :] = total.astype(jnp.bfloat16)
         else:
             put_coded(out_refs[len(out_refs) - z], jnp.concatenate([total for _, total in reversed(sums)], axis=0))
 
@@ -171,7 +168,7 @@
 def add_kept(kept, came, across):
     depth, rows, width = kept.shape
     own = jax.ShapeDtypeStruct((rows, width), jnp.float32)
-    heights = [rows if z <= PLAIN else rows // 8 * 9 for z in reversed(range(1, depth))]
+    heights = [rows // 8 * 9 + (FAR_PAD if z > 2 else 0) for z in reversed(range(1, depth))]
     return pl.pallas_call(
         add_kept_kernel,
         out_shape=[own] + [jax.ShapeDtypeStruct((height, width), jnp.bfloat16) for height in heights],
@@ -217,10 +214,7 @@
     core = lax.rem(lax.axis_index("ex"), 2)
     total_ref[...] = part_refs[0][...]
     for part_ref in part_refs[1:]:
-        if part_ref.shape[0] == 2 * rank:
-            total_ref[...] += part_ref[...].astype(jnp.float32)
-            continue
-        for rows, total in add_coded(lambda first, count: total_ref[first : first + count, :], part_ref):
+        for rows, total in add_coded(lambda first, count: total_ref[first : first + count, :], 2 * rank, part_ref):
             total_ref[rows, :] = total
     even = total_ref[pl.ds(rank, rank // 2, stride=2), :]
     odd = total_ref[pl.ds(rank + 1, rank // 2, stride=2), :]

time: 26.6 us -> 26.8 us (level)
  transfers between devices with their start and end apart: 13 -> 13, of which waited for: 4 -> 5; matrix products, arithmetic and copies ran while one was open for 0% -> 0% of each run, Pallas kernels for 18% -> 18%
where the time goes in v23:
time: 26.8 us; the launch traced here: 26.6 us
  starting transfers between devices  14.2 us (53%)
  waiting for transfers between devices  6.84 us (26%)
  Pallas kernels  5.51 us (21%)
    ppermute x13, starting transfers between devices, swap(): lax.ppermute(array, 'ex', [(i, i ^ distance) for i in range(devices)])  14.2 us
    ppermute x13, waiting for transfers between devices, swap(): lax.ppermute(array, 'ex', [(i, i ^ distance) for i in range(devices)])  6.84 us
    pallas_call x1, Pallas kernels, project_loaded(): pl.pallas_call(project_loaded_kernel, out_shape=[jax.ShapeDtypeStruct((ra...  2.23 us
    pallas_call x2, Pallas kernels, part(): pl.pallas_call(functools.partial(project_kernel, rows, flip), out_shape=[...  1.54 us
    pallas_call x1, Pallas kernels, last_scores(): pl.pallas_call(functools.partial(last_score_kernel, chips), out_shape=jax...  0.81 us
    pallas_call x1, Pallas kernels, first_scores(): pl.pallas_call(functools.partial(first_score_kernel, len(parts), held), o...  0.7 us
  transfers between devices with their start and end apart: 13, of which 5 were waited for; matrix products, arithmetic and copies ran while one was open for 0% of the time, Pallas kernels for 18%

profile of v23, /device:TPU:0, one launch (start us, length us, event | category | flops | bytes accessed | tf_op | source)
XLA Modules:
  0.0 26.6 jit_solution(5394498685590013461)
XLA Ops:
  0.0 0.0 copy-start.1
  0.0 0.0 copy-start
  0.0 4.0 %collective-permute-start = (bf16[1,8,4096]{2,1,0:T(8,128)(2,1)}, bf16[1,8,4096]{2,1,0:T(8,128)(2,1)S(1)}, u32[]{:S(2)}, u32[]{:S(2)}) collective-permute-start(bf16[1,8,4096]{2,1,0:T(8,128)(2,1)} %bitcast.6), channel_id=1, source_target_pairs={{0,8},{1,9},{2,10},{3,11},{4,12},{5,13},{6,14},{7,15},{8,0},{9,1},... | collective-permute-start | bytes 196616 | tf_op jit(solution)/shard_map/ppermute | solution.py:281
  4.0 2.2 %shard_map.57 = (f32[64,2048]{1,0:T(8,128)S(1)}, f32[64,2048]{1,0:T(8,128)S(1)}) custom-call(bf16[512,2048]{1,0:T(8,128)(2,1)} %x_hbm.1, bf16[1792,2048]{1,0:T(8,128)(2,1)} %w_ref.3, bf16[64,512]{1,0:T(8,128)(2,1)} %bitcast.8, bf16[64,1792]{1,0:T(8,128)(2,1)} %bitcast.3), custom_call_target="tpu_custom_call" | custom-call | flops 167772160 | bytes 2621440 | tf_op jit(solution)/shard_map/pallas_call | solution.py:50
  6.3 0.0 copy-done.1
  6.3 0.0 copy-done
  6.3 0.0 copy-start.2
  6.3 0.8 %shard_map.59 = (f32[2,128,128]{2,1,0:T(8,128)S(1)}, f32[2,128,128]{2,1,0:T(8,128)S(1)}, f32[4,128,128]{2,1,0:T(8,128)S(1)}) custom-call(f32[64,2048]{1,0:T(8,128)S(1)} %get-tuple-element.32.low_in_ref, f32[64,2048]{1,0:T(8,128)S(1)} %get-tuple-element.33.low_out_ref, bf16[64,1792]{1,0:T(8,128)(2,1)S(1)} %bitcast.4, bf16[1792,2048]{1,0:T(8,128)(2,1)S(1)} %copy-done), custom_call_target="tpu_custom_call" | custom-call | flops 234881024 | bytes 3670016 | tf_op jit(solution)/shard_map/pallas_call | solution.py:99
  7.1 0.1 collective-permute-start.3
  7.2 0.5 %collective-permute-start.4 = (f32[2,128,128]{2,1,0:T(8,128)S(1)}, f32[2,128,128]{2,1,0:T(8,128)S(1)}, u32[]{:S(2)}, u32[]{:S(2)}) collective-permute-start(f32[2,128,128]{2,1,0:T(8,128)S(1)} %get-tuple-element.37), channel_id=1, source_target_pairs={{0,1},{1,0},{2,3},{3,2},{4,5},{5,4},{6,7},{7,6},{8,9},{9,8},{10,11... | collective-permute-start | bytes 393224 | tf_op jit(solution)/shard_map/ppermute | solution.py:281
  7.7 0.8 %shard_map.58 = (f32[4,128,128]{2,1,0:T(8,128)S(1)}, f32[4,128,128]{2,1,0:T(8,128)S(1)}) custom-call(f32[64,2048]{1,0:T(8,128)S(1)} %get-tuple-element.32.low_in_ref, f32[64,2048]{1,0:T(8,128)S(1)} %get-tuple-element.33.low_out_ref, bf16[64,1792]{1,0:T(8,128)(2,1)S(1)} %bitcast.5, bf16[1792,2048]{1,0:T(8,128)(2,1)S(1)} %copy-done), custom_call_target="tpu_custom_call" | custom-call | flops 234881024 | bytes 3670016 | tf_op jit(solution)/shard_map/pallas_call | solution.py:99
  8.4 0.1 collective-permute-start.6
  8.6 0.0 collective-permute-done.right_ref
  8.6 0.0 copy-done.2
  8.6 1.6 %collective-permute-start.1 = (bf16[2,8,4096]{2,1,0:T(8,128)(2,1)S(1)}, bf16[2,8,4096]{2,1,0:T(8,128)(2,1)S(1)}, u32[]{:S(2)}, u32[]{:S(2)}) collective-permute-start(bf16[2,8,4096]{2,1,0:T(8,128)(2,1)S(1)} %shard_map.55.left_ref), channel_id=1, source_target_pairs={{0,4},{1,5},{2,6},{3,7},{4,0},{5,1},{6,2},{7,3},{8,12},{9,13},{10,... | collective-permute-start | bytes 393224 | tf_op jit(solution)/shard_map/ppermute | solution.py:281
  10.2 0.0 collective-permute-done.3.refs_0_
  10.2 0.0 collective-permute-done.4.refs_1_
  10.2 0.1 shard_map.60
  10.3 1.6 %collective-permute-start.5 = (bf16[4,144,128]{2,1,0:T(8,128)(2,1)S(1)}, bf16[4,144,128]{2,1,0:T(8,128)(2,1)S(1)}, u32[]{:S(2)}, u32[]{:S(2)}) collective-permute-start(bf16[4,144,128]{2,1,0:T(8,128)(2,1)S(1)} %shard_map.60), channel_id=1, source_target_pairs={{0,2},{1,3},{2,0},{3,1},{4,6},{5,7},{6,4},{7,5},{8,10},{9,11},{10,... | collective-permute-start | bytes 442376 | tf_op jit(solution)/shard_map/ppermute | solution.py:281
  11.9 0.0 collective-permute-start.7
  11.9 2.6 %collective-permute-done.1.right_ref = bf16[2,8,4096]{2,1,0:T(8,128)(2,1)S(1)} collective-permute-done((bf16[2,8,4096]{2,1,0:T(8,128)(2,1)S(1)}, bf16[2,8,4096]{2,1,0:T(8,128)(2,1)S(1)}, u32[]{:S(2)}, u32[]{:S(2)}) %collective-permute-start.1) | collective-permute-done | bytes 131104 | tf_op jit(solution)/shard_map/ppermute | solution.py:281
  14.5 1.6 %collective-permute-start.2 = (bf16[4,8,4096]{2,1,0:T(8,128)(2,1)S(1)}, bf16[4,8,4096]{2,1,0:T(8,128)(2,1)S(1)}, u32[]{:S(2)}, u32[]{:S(2)}) collective-permute-start(bf16[4,8,4096]{2,1,0:T(8,128)(2,1)S(1)} %shard_map.56.refs_4_), channel_id=1, source_target_pairs={{0,2},{1,3},{2,0},{3,1},{4,6},{5,7},{6,4},{7,5},{8,10},{9,11},{10,... | collective-permute-start | bytes 786440 | tf_op jit(solution)/shard_map/ppermute | solution.py:281
  16.1 0.0 collective-permute-done.7.refs_5_
  16.1 0.0 collective-permute-done.6.came_ref
  16.1 0.2 collective-permute-done.5.across_ref
  16.3 0.1 shard_map.61
  16.4 0.1 collective-permute-start.8
  16.5 2.7 %collective-permute-start.9 = (bf16[160,128]{1,0:T(8,128)(2,1)S(1)}, bf16[160,128]{1,0:T(8,128)(2,1)S(1)}, u32[]{:S(2)}, u32[]{:S(2)}) collective-permute-start(bf16[160,128]{1,0:T(8,128)(2,1)S(1)} %get-tuple-element.47), channel_id=1, source_target_pairs={{0,12},{1,13},{2,14},{3,15},{4,8},{5,9},{6,10},{7,11},{8,4},{9,5},... | collective-permute-start | bytes 122888 | tf_op jit(solution)/shard_map/ppermute | solution.py:281
  19.2 0.3 collective-permute-start.10
  19.5 1.5 %collective-permute-start.11 = (bf16[144,128]{1,0:T(8,128)(2,1)S(1)}, bf16[144,128]{1,0:T(8,128)(2,1)S(1)}, u32[]{:S(2)}, u32[]{:S(2)}) collective-permute-start(bf16[144,128]{1,0:T(8,128)(2,1)S(1)} %get-tuple-element.49), channel_id=1, source_target_pairs={{0,4},{1,5},{2,6},{3,7},{4,0},{5,1},{6,2},{7,3},{8,12},{9,13},{10,... | collective-permute-start | bytes 110600 | tf_op jit(solution)/shard_map/ppermute | solution.py:281
  21.0 3.1 %collective-permute-done.10.refs_2_ = bf16[144,128]{1,0:T(8,128)(2,1)S(1)} collective-permute-done((bf16[144,128]{1,0:T(8,128)(2,1)S(1)}, bf16[144,128]{1,0:T(8,128)(2,1)S(1)}, u32[]{:S(2)}, u32[]{:S(2)}) %collective-permute-start.10) | collective-permute-done | bytes 36896 | tf_op jit(solution)/shard_map/ppermute | solution.py:281
  24.1 0.1 collective-permute-done.11.refs_3_
  24.2 0.0 collective-permute-done.9.refs_1_
  24.2 0.0 collective-permute-done.8.refs_6_
  24.2 0.0 collective-permute-done.2.refs_7_
  24.2 0.1 collective-permute-start.12
  24.3 0.7 %shard_map.62 = (f32[2,32,128]{2,1,0:T(8,128)S(1)}, f32[2,8,2,8,128]{4,3,2,1,0:T(8,128)S(1)}) custom-call(f32[128,128]{1,0:T(8,128)S(1)} %get-tuple-element.50.refs_0_, bf16[160,128]{1,0:T(8,128)(2,1)S(1)} %collective-permute-done.9.refs_1_, bf16[144,128]{1,0:T(8,128)(2,1)S(1)} %collective-permute-done.10.refs_2_, ...), custom_call_target="tpu_custom_call" | custom-call | tf_op jit(solution)/shard_map/pallas_call | solution.py:251
  25.0 0.8 %collective-permute-done.12.queries_ref = bf16[4,8,4096]{2,1,0:T(8,128)(2,1)S(1)} collective-permute-done((bf16[4,8,4096]{2,1,0:T(8,128)(2,1)S(1)}, bf16[4,8,4096]{2,1,0:T(8,128)(2,1)S(1)}, u32[]{:S(2)}, u32[]{:S(2)}) %collective-permute-start.12) | collective-permute-done | bytes 262176 | tf_op jit(solution)/shard_map/ppermute | solution.py:281
  25.8 0.8 %shard_map.63 = f32[2,128]{1,0:T(2,128)} custom-call(f32[2,32,128]{2,1,0:T(8,128)S(1)} %get-tuple-element.57.grads_ref, f32[2,8,2,8,128]{4,3,2,1,0:T(8,128)S(1)} %get-tuple-element.58.before_ref, bf16[4,8,4096]{2,1,0:T(8,128)(2,1)S(1)} %collective-permute-done.12.queries_ref), custom_call_target="tpu_custom_call" | custom-call | tf_op jit(solution)/shard_map/pallas_call | solution.py:264
  (2 shorter events, 0.0 us)
Async XLA Ops:
  0.0 6.3 %copy-start.1 = (bf16[1792,64]{0,1:T(8,128)(2,1)S(1)}, bf16[1792,64]{0,1:T(8,128)(2,1)}, u32[]{:S(2)}) copy-start(bf16[1792,64]{0,1:T(8,128)(2,1)} %param.8) | copy-start | bytes 688132
  0.0 6.3 %copy-start = (bf16[1792,2048]{1,0:T(8,128)(2,1)S(1)}, bf16[1792,2048]{1,0:T(8,128)(2,1)}, u32[]{:S(2)}) copy-start(bf16[1792,2048]{1,0:T(8,128)(2,1)} %w_ref.3) | copy-start | bytes 22020100
  0.0 8.6 %collective-permute-start = (bf16[1,8,4096]{2,1,0:T(8,128)(2,1)}, bf16[1,8,4096]{2,1,0:T(8,128)(2,1)S(1)}, u32[]{:S(2)}, u32[]{:S(2)}) collective-permute-start(bf16[1,8,4096]{2,1,0:T(8,128)(2,1)} %bitcast.6), channel_id=1, source_target_pairs={{0,8},{1,9},{2,10},{3,11},{4,12},{5,13},{6,14},{7,15},{8,0},{9,1},... | collective-permute-start | bytes 196616 | tf_op jit(solution)/shard_map/ppermute | solution.py:281
  6.3 2.3 %copy-start.2 = (bf16[8,4096]{1,0:T(8,128)(2,1)S(1)}, bf16[8,4096]{1,0:T(8,128)(2,1)}, u32[]{:S(2)}) copy-start(bf16[8,4096]{1,0:T(8,128)(2,1)} %param.9) | copy-start | bytes 196612
  7.1 3.1 %collective-permute-start.3 = (f32[2,128,128]{2,1,0:T(8,128)S(1)}, f32[2,128,128]{2,1,0:T(8,128)S(1)}, u32[]{:S(2)}, u32[]{:S(2)}) collective-permute-start(f32[2,128,128]{2,1,0:T(8,128)S(1)} %get-tuple-element.36), channel_id=1, source_target_pairs={{0,1},{1,0},{2,3},{3,2},{4,5},{5,4},{6,7},{7,6},{8,9},{9,8},{10,11... | collective-permute-start | bytes 393224 | tf_op jit(solution)/shard_map/ppermute | solution.py:281
  7.2 3.1 %collective-permute-start.4 = (f32[2,128,128]{2,1,0:T(8,128)S(1)}, f32[2,128,128]{2,1,0:T(8,128)S(1)}, u32[]{:S(2)}, u32[]{:S(2)}) collective-permute-start(f32[2,128,128]{2,1,0:T(8,128)S(1)} %get-tuple-element.37), channel_id=1, source_target_pairs={{0,1},{1,0},{2,3},{3,2},{4,5},{5,4},{6,7},{7,6},{8,9},{9,8},{10,11... | collective-permute-start | bytes 393224 | tf_op jit(solution)/shard_map/ppermute | solution.py:281
  8.4 7.7 %collective-permute-start.6 = (f32[4,128,128]{2,1,0:T(8,128)S(1)}, f32[4,128,128]{2,1,0:T(8,128)S(1)}, u32[]{:S(2)}, u32[]{:S(2)}) collective-permute-start(f32[4,128,128]{2,1,0:T(8,128)S(1)} %get-tuple-element.38), channel_id=1, source_target_pairs={{0,1},{1,0},{2,3},{3,2},{4,5},{5,4},{6,7},{7,6},{8,9},{9,8},{10,11... | collective-permute-start | bytes 786440 | tf_op jit(solution)/shard_map/ppermute | solution.py:281
  8.6 5.9 %collective-permute-start.1 = (bf16[2,8,4096]{2,1,0:T(8,128)(2,1)S(1)}, bf16[2,8,4096]{2,1,0:T(8,128)(2,1)S(1)}, u32[]{:S(2)}, u32[]{:S(2)}) collective-permute-start(bf16[2,8,4096]{2,1,0:T(8,128)(2,1)S(1)} %shard_map.55.left_ref), channel_id=1, source_target_pairs={{0,4},{1,5},{2,6},{3,7},{4,0},{5,1},{6,2},{7,3},{8,12},{9,13},{10,... | collective-permute-start | bytes 393224 | tf_op jit(solution)/shard_map/ppermute | solution.py:281
  10.3 6.0 %collective-permute-start.5 = (bf16[4,144,128]{2,1,0:T(8,128)(2,1)S(1)}, bf16[4,144,128]{2,1,0:T(8,128)(2,1)S(1)}, u32[]{:S(2)}, u32[]{:S(2)}) collective-permute-start(bf16[4,144,128]{2,1,0:T(8,128)(2,1)S(1)} %shard_map.60), channel_id=1, source_target_pairs={{0,2},{1,3},{2,0},{3,1},{4,6},{5,7},{6,4},{7,5},{8,10},{9,11},{10,... | collective-permute-start | bytes 442376 | tf_op jit(solution)/shard_map/ppermute | solution.py:281
  11.9 4.2 %collective-permute-start.7 = (bf16[2,8,4096]{2,1,0:T(8,128)(2,1)S(1)}, bf16[2,8,4096]{2,1,0:T(8,128)(2,1)S(1)}, u32[]{:S(2)}, u32[]{:S(2)}) collective-permute-start(bf16[2,8,4096]{2,1,0:T(8,128)(2,1)S(1)} %shard_map.55.left_ref), channel_id=1, source_target_pairs={{0,1},{1,0},{2,3},{3,2},{4,5},{5,4},{6,7},{7,6},{8,9},{9,8},{10,11... | collective-permute-start | bytes 393224 | tf_op jit(solution)/shard_map/ppermute | solution.py:281
  14.5 9.7 %collective-permute-start.2 = (bf16[4,8,4096]{2,1,0:T(8,128)(2,1)S(1)}, bf16[4,8,4096]{2,1,0:T(8,128)(2,1)S(1)}, u32[]{:S(2)}, u32[]{:S(2)}) collective-permute-start(bf16[4,8,4096]{2,1,0:T(8,128)(2,1)S(1)} %shard_map.56.refs_4_), channel_id=1, source_target_pairs={{0,2},{1,3},{2,0},{3,1},{4,6},{5,7},{6,4},{7,5},{8,10},{9,11},{10,... | collective-permute-start | bytes 786440 | tf_op jit(solution)/shard_map/ppermute | solution.py:281
  16.4 7.8 %collective-permute-start.8 = (bf16[2,8,4096]{2,1,0:T(8,128)(2,1)S(1)}, bf16[2,8,4096]{2,1,0:T(8,128)(2,1)S(1)}, u32[]{:S(2)}, u32[]{:S(2)}) collective-permute-start(bf16[2,8,4096]{2,1,0:T(8,128)(2,1)S(1)} %collective-permute-done.1.right_ref), channel_id=1, source_target_pairs={{0,1},{1,0},{2,3},{3,2},{4,5},{5,4},{6,7},{7,6},{8,9},{9,8},{10,11... | collective-permute-start | bytes 393224 | tf_op jit(solution)/shard_map/ppermute | solution.py:281
  16.5 7.7 %collective-permute-start.9 = (bf16[160,128]{1,0:T(8,128)(2,1)S(1)}, bf16[160,128]{1,0:T(8,128)(2,1)S(1)}, u32[]{:S(2)}, u32[]{:S(2)}) collective-permute-start(bf16[160,128]{1,0:T(8,128)(2,1)S(1)} %get-tuple-element.47), channel_id=1, source_target_pairs={{0,12},{1,13},{2,14},{3,15},{4,8},{5,9},{6,10},{7,11},{8,4},{9,5},... | collective-permute-start | bytes 122888 | tf_op jit(solution)/shard_map/ppermute | solution.py:281
  19.2 4.9 %collective-permute-start.10 = (bf16[144,128]{1,0:T(8,128)(2,1)S(1)}, bf16[144,128]{1,0:T(8,128)(2,1)S(1)}, u32[]{:S(2)}, u32[]{:S(2)}) collective-permute-start(bf16[144,128]{1,0:T(8,128)(2,1)S(1)} %get-tuple-element.48), channel_id=1, source_target_pairs={{0,8},{1,9},{2,10},{3,11},{4,12},{5,13},{6,14},{7,15},{8,0},{9,1},... | collective-permute-start | bytes 110600 | tf_op jit(solution)/shard_map/ppermute | solution.py:281
  19.5 4.7 %collective-permute-start.11 = (bf16[144,128]{1,0:T(8,128)(2,1)S(1)}, bf16[144,128]{1,0:T(8,128)(2,1)S(1)}, u32[]{:S(2)}, u32[]{:S(2)}) collective-permute-start(bf16[144,128]{1,0:T(8,128)(2,1)S(1)} %get-tuple-element.49), channel_id=1, source_target_pairs={{0,4},{1,5},{2,6},{3,7},{4,0},{5,1},{6,2},{7,3},{8,12},{9,13},{10,... | collective-permute-start | bytes 110600 | tf_op jit(solution)/shard_map/ppermute | solution.py:281
  24.2 1.6 %collective-permute-start.12 = (bf16[4,8,4096]{2,1,0:T(8,128)(2,1)S(1)}, bf16[4,8,4096]{2,1,0:T(8,128)(2,1)S(1)}, u32[]{:S(2)}, u32[]{:S(2)}) collective-permute-start(bf16[4,8,4096]{2,1,0:T(8,128)(2,1)S(1)} %collective-permute-done.2.refs_7_), channel_id=1, source_target_pairs={{0,1},{1,0},{2,3},{3,2},{4,5},{5,4},{6,7},{7,6},{8,9},{9,8},{10,11... | collective-permute-start | bytes 786440 | tf_op jit(solution)/shard_map/ppermute | solution.py:281

commit v24 on v20

--- a/solution.py
+++ b/solution.py
@@ -293,13 +293,13 @@
     held, reach = stack(early, late), early_reach + late_reach
     came_held = swap(held, chip=1)
     other_early = swap(early, core=1)
-    across, came, other_early = together((across, came, other_early))
+    across, came = together((across, came))
 
     parts = list(add_kept(kept, came, across))
     late, parts = together((late, parts))
     other_late = swap(late, core=1)
     parts[1:] = [swap(part, chip=2 * z) for z, part in zip(reversed(range(1, depth)), parts[1:])]
-    came_held, other_late, parts = together((came_held, other_late, parts))
+    came_held, other_late, other_early, parts = together((came_held, other_late, other_early, parts))
     other_came = swap(came_held, core=1)
     reach_y = [chip ^ 1 for chip in reach]
     queries = [held, other_early, other_late, came_held]

time: 26.6 us -> 26.9 us (1.011)
  starting transfers between devices: 14.1 us -> 14.4 us
    ppermute x13, starting transfers between devices: 14.1 us -> 14.4 us  [swap(): lax.ppermute(array, 'ex', [(i, i ^ distance) for i in range(devices)])]
  transfers between devices with their start and end apart: 13 -> 13, of which waited for: 5 -> 4; matrix products, arithmetic and copies ran while one was open for 0% -> 0% of each run, Pallas kernels for 17% -> 17%
where the time goes in v24:
time: 26.9 us; the launch traced here: 26.8 us
  starting transfers between devices  14.4 us (54%)
  waiting for transfers between devices  6.89 us (26%)
  Pallas kernels  5.4 us (20%)
    ppermute x13, starting transfers between devices, swap(): lax.ppermute(array, 'ex', [(i, i ^ distance) for i in range(devices)])  14.4 us
    ppermute x13, waiting for transfers between devices, swap(): lax.ppermute(array, 'ex', [(i, i ^ distance) for i in range(devices)])  6.89 us
    pallas_call x1, Pallas kernels, project_loaded(): pl.pallas_call(project_loaded_kernel, out_shape=[jax.ShapeDtypeStruct((ra...  2.22 us
    pallas_call x1, Pallas kernels, project(): pl.pallas_call(functools.partial(project_kernel, rows), out_shape=[half]...  1.43 us
    pallas_call x1, Pallas kernels, last_scores(): pl.pallas_call(functools.partial(last_score_kernel, chips), out_shape=jax...  0.82 us
    pallas_call x1, Pallas kernels, first_scores(): pl.pallas_call(functools.partial(first_score_kernel, len(parts), held), o...  0.7 us
  transfers between devices with their start and end apart: 13, of which 4 were waited for; matrix products, arithmetic and copies ran while one was open for 0% of the time, Pallas kernels for 17%

profile of v24, /device:TPU:0, one launch (start us, length us, event | category | flops | bytes accessed | tf_op | source)
XLA Modules:
  0.0 26.8 jit_solution(4301229429257956357)
XLA Ops:
  0.0 0.0 copy-start.1
  0.0 0.0 copy-start
  0.0 4.0 %collective-permute-start = (bf16[1,8,4096]{2,1,0:T(8,128)(2,1)}, bf16[1,8,4096]{2,1,0:T(8,128)(2,1)S(1)}, u32[]{:S(2)}, u32[]{:S(2)}) collective-permute-start(bf16[1,8,4096]{2,1,0:T(8,128)(2,1)} %bitcast.5), channel_id=1, source_target_pairs={{0,8},{1,9},{2,10},{3,11},{4,12},{5,13},{6,14},{7,15},{8,0},{9,1},... | collective-permute-start | bytes 196616 | tf_op jit(solution)/shard_map/ppermute | solution.py:278
  4.0 0.0 copy-start.2
  4.0 2.2 %shard_map.57 = (f32[64,2048]{1,0:T(8,128)S(1)}, f32[64,2048]{1,0:T(8,128)S(1)}) custom-call(bf16[512,2048]{1,0:T(8,128)(2,1)} %x_hbm.1, bf16[1792,2048]{1,0:T(8,128)(2,1)} %w_ref.1, bf16[64,512]{1,0:T(8,128)(2,1)} %bitcast.7, bf16[64,1792]{1,0:T(8,128)(2,1)} %bitcast.3), custom_call_target="tpu_custom_call" | custom-call | flops 167772160 | bytes 2621440 | tf_op jit(solution)/shard_map/pallas_call | solution.py:50
  6.3 0.0 copy-done.1
  6.3 0.0 copy-done
  6.3 1.4 %shard_map.58 = (f32[2,128,128]{2,1,0:T(8,128)S(1)}, f32[2,128,128]{2,1,0:T(8,128)S(1)}, f32[4,128,128]{2,1,0:T(8,128)S(1)}, f32[4,128,128]{2,1,0:T(8,128)S(1)}, f32[4,128,128]{2,1,0:T(8,128)S(1)}) custom-call(f32[64,2048]{1,0:T(8,128)S(1)} %get-tuple-element.32.low_in_ref, f32[64,2048]{1,0:T(8,128)S(1)} %get-tuple-element.33.low_out_ref, ...), custom_call_target="tpu_custom_call" | custom-call | flops 469762048 | bytes 7340032 | tf_op jit(solution)/shard_map/pallas_call | solution.py:99
  7.7 0.1 collective-permute-start.3
  7.8 0.5 %collective-permute-start.4 = (f32[2,128,128]{2,1,0:T(8,128)S(1)}, f32[2,128,128]{2,1,0:T(8,128)S(1)}, u32[]{:S(2)}, u32[]{:S(2)}) collective-permute-start(f32[2,128,128]{2,1,0:T(8,128)S(1)} %get-tuple-element.37), channel_id=1, source_target_pairs={{0,1},{1,0},{2,3},{3,2},{4,5},{5,4},{6,7},{7,6},{8,9},{9,8},{10,11... | collective-permute-start | bytes 393224 | tf_op jit(solution)/shard_map/ppermute | solution.py:278
  8.3 0.1 collective-permute-start.6
  8.4 0.0 collective-permute-done.right_ref
  8.4 0.0 copy-done.2
  8.4 1.6 %collective-permute-start.1 = (bf16[2,8,4096]{2,1,0:T(8,128)(2,1)S(1)}, bf16[2,8,4096]{2,1,0:T(8,128)(2,1)S(1)}, u32[]{:S(2)}, u32[]{:S(2)}) collective-permute-start(bf16[2,8,4096]{2,1,0:T(8,128)(2,1)S(1)} %shard_map.55.left_ref), channel_id=1, source_target_pairs={{0,4},{1,5},{2,6},{3,7},{4,0},{5,1},{6,2},{7,3},{8,12},{9,13},{10,... | collective-permute-start | bytes 393224 | tf_op jit(solution)/shard_map/ppermute | solution.py:278
  10.0 0.0 collective-permute-done.3.refs_0_
  10.0 0.0 collective-permute-done.4.refs_1_
  10.0 0.1 shard_map.59
  10.1 1.6 %collective-permute-start.5 = (bf16[4,144,128]{2,1,0:T(8,128)(2,1)S(1)}, bf16[4,144,128]{2,1,0:T(8,128)(2,1)S(1)}, u32[]{:S(2)}, u32[]{:S(2)}) collective-permute-start(bf16[4,144,128]{2,1,0:T(8,128)(2,1)S(1)} %shard_map.59), channel_id=1, source_target_pairs={{0,2},{1,3},{2,0},{3,1},{4,6},{5,7},{6,4},{7,5},{8,10},{9,11},{10,... | collective-permute-start | bytes 442376 | tf_op jit(solution)/shard_map/ppermute | solution.py:278
  11.7 2.6 %collective-permute-done.1.right_ref = bf16[2,8,4096]{2,1,0:T(8,128)(2,1)S(1)} collective-permute-done((bf16[2,8,4096]{2,1,0:T(8,128)(2,1)S(1)}, bf16[2,8,4096]{2,1,0:T(8,128)(2,1)S(1)}, u32[]{:S(2)}, u32[]{:S(2)}) %collective-permute-start.1) | collective-permute-done | bytes 131104 | tf_op jit(solution)/shard_map/ppermute | solution.py:278
  14.3 1.6 %collective-permute-start.2 = (bf16[4,8,4096]{2,1,0:T(8,128)(2,1)S(1)}, bf16[4,8,4096]{2,1,0:T(8,128)(2,1)S(1)}, u32[]{:S(2)}, u32[]{:S(2)}) collective-permute-start(bf16[4,8,4096]{2,1,0:T(8,128)(2,1)S(1)} %shard_map.56.refs_4_), channel_id=1, source_target_pairs={{0,2},{1,3},{2,0},{3,1},{4,6},{5,7},{6,4},{7,5},{8,10},{9,11},{10,... | collective-permute-start | bytes 786440 | tf_op jit(solution)/shard_map/ppermute | solution.py:278
  15.9 0.0 collective-permute-start.8
  15.9 0.0 collective-permute-done.6.came_ref
  15.9 0.1 collective-permute-done.5.across_ref
  16.1 0.1 shard_map.60
  16.2 0.4 %collective-permute-start.7 = (bf16[2,8,4096]{2,1,0:T(8,128)(2,1)S(1)}, bf16[2,8,4096]{2,1,0:T(8,128)(2,1)S(1)}, u32[]{:S(2)}, u32[]{:S(2)}) collective-permute-start(bf16[2,8,4096]{2,1,0:T(8,128)(2,1)S(1)} %collective-permute-done.1.right_ref), channel_id=1, source_target_pairs={{0,1},{1,0},{2,3},{3,2},{4,5},{5,4},{6,7},{7,6},{8,9},{9,8},{10,11... | collective-permute-start | bytes 393224 | tf_op jit(solution)/shard_map/ppermute | solution.py:278
  16.7 2.8 %collective-permute-start.9 = (bf16[160,128]{1,0:T(8,128)(2,1)S(1)}, bf16[160,128]{1,0:T(8,128)(2,1)S(1)}, u32[]{:S(2)}, u32[]{:S(2)}) collective-permute-start(bf16[160,128]{1,0:T(8,128)(2,1)S(1)} %get-tuple-element.47), channel_id=1, source_target_pairs={{0,12},{1,13},{2,14},{3,15},{4,8},{5,9},{6,10},{7,11},{8,4},{9,5},... | collective-permute-start | bytes 122888 | tf_op jit(solution)/shard_map/ppermute | solution.py:278
  19.4 0.3 %collective-permute-start.10 = (bf16[144,128]{1,0:T(8,128)(2,1)S(1)}, bf16[144,128]{1,0:T(8,128)(2,1)S(1)}, u32[]{:S(2)}, u32[]{:S(2)}) collective-permute-start(bf16[144,128]{1,0:T(8,128)(2,1)S(1)} %get-tuple-element.48), channel_id=1, source_target_pairs={{0,8},{1,9},{2,10},{3,11},{4,12},{5,13},{6,14},{7,15},{8,0},{9,1},... | collective-permute-start | bytes 110600 | tf_op jit(solution)/shard_map/ppermute | solution.py:278
  19.7 0.0 collective-permute-done.8.refs_5_
  19.7 1.4 %collective-permute-start.11 = (bf16[144,128]{1,0:T(8,128)(2,1)S(1)}, bf16[144,128]{1,0:T(8,128)(2,1)S(1)}, u32[]{:S(2)}, u32[]{:S(2)}) collective-permute-start(bf16[144,128]{1,0:T(8,128)(2,1)S(1)} %get-tuple-element.49), channel_id=1, source_target_pairs={{0,4},{1,5},{2,6},{3,7},{4,0},{5,1},{6,2},{7,3},{8,12},{9,13},{10,... | collective-permute-start | bytes 110600 | tf_op jit(solution)/shard_map/ppermute | solution.py:278
  21.1 3.3 %collective-permute-done.10.refs_2_ = bf16[144,128]{1,0:T(8,128)(2,1)S(1)} collective-permute-done((bf16[144,128]{1,0:T(8,128)(2,1)S(1)}, bf16[144,128]{1,0:T(8,128)(2,1)S(1)}, u32[]{:S(2)}, u32[]{:S(2)}) %collective-permute-start.10) | collective-permute-done | bytes 36896 | tf_op jit(solution)/shard_map/ppermute | solution.py:278
  24.3 0.0 collective-permute-done.11.refs_3_
  24.4 0.0 collective-permute-done.9.refs_1_
  24.4 0.0 collective-permute-done.7.refs_6_
  24.4 0.0 collective-permute-done.2.refs_7_
  24.4 0.1 collective-permute-start.12
  24.4 0.7 %shard_map.61 = (f32[2,32,128]{2,1,0:T(8,128)S(1)}, f32[2,8,2,8,128]{4,3,2,1,0:T(8,128)S(1)}) custom-call(f32[128,128]{1,0:T(8,128)S(1)} %get-tuple-element.50.refs_0_, bf16[160,128]{1,0:T(8,128)(2,1)S(1)} %collective-permute-done.9.refs_1_, bf16[144,128]{1,0:T(8,128)(2,1)S(1)} %collective-permute-done.10.refs_2_, ...), custom_call_target="tpu_custom_call" | custom-call | tf_op jit(solution)/shard_map/pallas_call | solution.py:248
  25.2 0.8 %collective-permute-done.12.queries_ref = bf16[4,8,4096]{2,1,0:T(8,128)(2,1)S(1)} collective-permute-done((bf16[4,8,4096]{2,1,0:T(8,128)(2,1)S(1)}, bf16[4,8,4096]{2,1,0:T(8,128)(2,1)S(1)}, u32[]{:S(2)}, u32[]{:S(2)}) %collective-permute-start.12) | collective-permute-done | bytes 262176 | tf_op jit(solution)/shard_map/ppermute | solution.py:278
  26.0 0.8 %shard_map.62 = f32[2,128]{1,0:T(2,128)} custom-call(f32[2,32,128]{2,1,0:T(8,128)S(1)} %get-tuple-element.57.grads_ref, f32[2,8,2,8,128]{4,3,2,1,0:T(8,128)S(1)} %get-tuple-element.58.before_ref, bf16[4,8,4096]{2,1,0:T(8,128)(2,1)S(1)} %collective-permute-done.12.queries_ref), custom_call_target="tpu_custom_call" | custom-call | tf_op jit(solution)/shard_map/pallas_call | solution.py:261
  (2 shorter events, 0.0 us)
Async XLA Ops:
  0.0 6.3 %copy-start.1 = (bf16[1792,64]{0,1:T(8,128)(2,1)S(1)}, bf16[1792,64]{0,1:T(8,128)(2,1)}, u32[]{:S(2)}) copy-start(bf16[1792,64]{0,1:T(8,128)(2,1)} %param.8) | copy-start | bytes 688132
  0.0 6.3 %copy-start = (bf16[1792,2048]{1,0:T(8,128)(2,1)S(1)}, bf16[1792,2048]{1,0:T(8,128)(2,1)}, u32[]{:S(2)}) copy-start(bf16[1792,2048]{1,0:T(8,128)(2,1)} %w_ref.1) | copy-start | bytes 22020100
  0.0 8.4 %collective-permute-start = (bf16[1,8,4096]{2,1,0:T(8,128)(2,1)}, bf16[1,8,4096]{2,1,0:T(8,128)(2,1)S(1)}, u32[]{:S(2)}, u32[]{:S(2)}) collective-permute-start(bf16[1,8,4096]{2,1,0:T(8,128)(2,1)} %bitcast.5), channel_id=1, source_target_pairs={{0,8},{1,9},{2,10},{3,11},{4,12},{5,13},{6,14},{7,15},{8,0},{9,1},... | collective-permute-start | bytes 196616 | tf_op jit(solution)/shard_map/ppermute | solution.py:278
  4.0 4.4 %copy-start.2 = (bf16[8,4096]{1,0:T(8,128)(2,1)S(1)}, bf16[8,4096]{1,0:T(8,128)(2,1)}, u32[]{:S(2)}) copy-start(bf16[8,4096]{1,0:T(8,128)(2,1)} %param.9) | copy-start | bytes 196612
  7.7 2.3 %collective-permute-start.3 = (f32[2,128,128]{2,1,0:T(8,128)S(1)}, f32[2,128,128]{2,1,0:T(8,128)S(1)}, u32[]{:S(2)}, u32[]{:S(2)}) collective-permute-start(f32[2,128,128]{2,1,0:T(8,128)S(1)} %get-tuple-element.36), channel_id=1, source_target_pairs={{0,1},{1,0},{2,3},{3,2},{4,5},{5,4},{6,7},{7,6},{8,9},{9,8},{10,11... | collective-permute-start | bytes 393224 | tf_op jit(solution)/shard_map/ppermute | solution.py:278
  7.8 2.2 %collective-permute-start.4 = (f32[2,128,128]{2,1,0:T(8,128)S(1)}, f32[2,128,128]{2,1,0:T(8,128)S(1)}, u32[]{:S(2)}, u32[]{:S(2)}) collective-permute-start(f32[2,128,128]{2,1,0:T(8,128)S(1)} %get-tuple-element.37), channel_id=1, source_target_pairs={{0,1},{1,0},{2,3},{3,2},{4,5},{5,4},{6,7},{7,6},{8,9},{9,8},{10,11... | collective-permute-start | bytes 393224 | tf_op jit(solution)/shard_map/ppermute | solution.py:278
  8.3 7.6 %collective-permute-start.6 = (f32[4,128,128]{2,1,0:T(8,128)S(1)}, f32[4,128,128]{2,1,0:T(8,128)S(1)}, u32[]{:S(2)}, u32[]{:S(2)}) collective-permute-start(f32[4,128,128]{2,1,0:T(8,128)S(1)} %get-tuple-element.38), channel_id=1, source_target_pairs={{0,1},{1,0},{2,3},{3,2},{4,5},{5,4},{6,7},{7,6},{8,9},{9,8},{10,11... | collective-permute-start | bytes 786440 | tf_op jit(solution)/shard_map/ppermute | solution.py:278
  8.4 5.9 %collective-permute-start.1 = (bf16[2,8,4096]{2,1,0:T(8,128)(2,1)S(1)}, bf16[2,8,4096]{2,1,0:T(8,128)(2,1)S(1)}, u32[]{:S(2)}, u32[]{:S(2)}) collective-permute-start(bf16[2,8,4096]{2,1,0:T(8,128)(2,1)S(1)} %shard_map.55.left_ref), channel_id=1, source_target_pairs={{0,4},{1,5},{2,6},{3,7},{4,0},{5,1},{6,2},{7,3},{8,12},{9,13},{10,... | collective-permute-start | bytes 393224 | tf_op jit(solution)/shard_map/ppermute | solution.py:278
  10.1 6.0 %collective-permute-start.5 = (bf16[4,144,128]{2,1,0:T(8,128)(2,1)S(1)}, bf16[4,144,128]{2,1,0:T(8,128)(2,1)S(1)}, u32[]{:S(2)}, u32[]{:S(2)}) collective-permute-start(bf16[4,144,128]{2,1,0:T(8,128)(2,1)S(1)} %shard_map.59), channel_id=1, source_target_pairs={{0,2},{1,3},{2,0},{3,1},{4,6},{5,7},{6,4},{7,5},{8,10},{9,11},{10,... | collective-permute-start | bytes 442376 | tf_op jit(solution)/shard_map/ppermute | solution.py:278
  14.3 10.0 %collective-permute-start.2 = (bf16[4,8,4096]{2,1,0:T(8,128)(2,1)S(1)}, bf16[4,8,4096]{2,1,0:T(8,128)(2,1)S(1)}, u32[]{:S(2)}, u32[]{:S(2)}) collective-permute-start(bf16[4,8,4096]{2,1,0:T(8,128)(2,1)S(1)} %shard_map.56.refs_4_), channel_id=1, source_target_pairs={{0,2},{1,3},{2,0},{3,1},{4,6},{5,7},{6,4},{7,5},{8,10},{9,11},{10,... | collective-permute-start | bytes 786440 | tf_op jit(solution)/shard_map/ppermute | solution.py:278
  15.9 3.8 %collective-permute-start.8 = (bf16[2,8,4096]{2,1,0:T(8,128)(2,1)S(1)}, bf16[2,8,4096]{2,1,0:T(8,128)(2,1)S(1)}, u32[]{:S(2)}, u32[]{:S(2)}) collective-permute-start(bf16[2,8,4096]{2,1,0:T(8,128)(2,1)S(1)} %shard_map.55.left_ref), channel_id=1, source_target_pairs={{0,1},{1,0},{2,3},{3,2},{4,5},{5,4},{6,7},{7,6},{8,9},{9,8},{10,11... | collective-permute-start | bytes 393224 | tf_op jit(solution)/shard_map/ppermute | solution.py:278
  16.2 8.1 %collective-permute-start.7 = (bf16[2,8,4096]{2,1,0:T(8,128)(2,1)S(1)}, bf16[2,8,4096]{2,1,0:T(8,128)(2,1)S(1)}, u32[]{:S(2)}, u32[]{:S(2)}) collective-permute-start(bf16[2,8,4096]{2,1,0:T(8,128)(2,1)S(1)} %collective-permute-done.1.right_ref), channel_id=1, source_target_pairs={{0,1},{1,0},{2,3},{3,2},{4,5},{5,4},{6,7},{7,6},{8,9},{9,8},{10,11... | collective-permute-start | bytes 393224 | tf_op jit(solution)/shard_map/ppermute | solution.py:278
  16.7 7.7 %collective-permute-start.9 = (bf16[160,128]{1,0:T(8,128)(2,1)S(1)}, bf16[160,128]{1,0:T(8,128)(2,1)S(1)}, u32[]{:S(2)}, u32[]{:S(2)}) collective-permute-start(bf16[160,128]{1,0:T(8,128)(2,1)S(1)} %get-tuple-element.47), channel_id=1, source_target_pairs={{0,12},{1,13},{2,14},{3,15},{4,8},{5,9},{6,10},{7,11},{8,4},{9,5},... | collective-permute-start | bytes 122888 | tf_op jit(solution)/shard_map/ppermute | solution.py:278
  19.4 4.9 %collective-permute-start.10 = (bf16[144,128]{1,0:T(8,128)(2,1)S(1)}, bf16[144,128]{1,0:T(8,128)(2,1)S(1)}, u32[]{:S(2)}, u32[]{:S(2)}) collective-permute-start(bf16[144,128]{1,0:T(8,128)(2,1)S(1)} %get-tuple-element.48), channel_id=1, source_target_pairs={{0,8},{1,9},{2,10},{3,11},{4,12},{5,13},{6,14},{7,15},{8,0},{9,1},... | collective-permute-start | bytes 110600 | tf_op jit(solution)/shard_map/ppermute | solution.py:278
  19.7 4.7 %collective-permute-start.11 = (bf16[144,128]{1,0:T(8,128)(2,1)S(1)}, bf16[144,128]{1,0:T(8,128)(2,1)S(1)}, u32[]{:S(2)}, u32[]{:S(2)}) collective-permute-start(bf16[144,128]{1,0:T(8,128)(2,1)S(1)} %get-tuple-element.49), channel_id=1, source_target_pairs={{0,4},{1,5},{2,6},{3,7},{4,0},{5,1},{6,2},{7,3},{8,12},{9,13},{10,... | collective-permute-start | bytes 110600 | tf_op jit(solution)/shard_map/ppermute | solution.py:278
  24.4 1.6 %collective-permute-start.12 = (bf16[4,8,4096]{2,1,0:T(8,128)(2,1)S(1)}, bf16[4,8,4096]{2,1,0:T(8,128)(2,1)S(1)}, u32[]{:S(2)}, u32[]{:S(2)}) collective-permute-start(bf16[4,8,4096]{2,1,0:T(8,128)(2,1)S(1)} %collective-permute-done.2.refs_7_), channel_id=1, source_target_pairs={{0,1},{1,0},{2,3},{3,2},{4,5},{5,4},{6,7},{7,6},{8,9},{9,8},{10,11... | collective-permute-start | bytes 786440 | tf_op jit(solution)/shard_map/ppermute | solution.py:278

commit v25 on v20

--- a/solution.py
+++ b/solution.py
@@ -76,17 +76,21 @@
     core, chip = lax.rem(here, 2), lax.div(here, 2)
     depth = kept_y.shape[0]
     rank, width = kept_y.shape[1] // 2, kept_y.shape[2]
-    for flip, given_refs, kept_ref in ((1, given_y, kept_y), (0, given_here, kept_here)):
-        for z in range(depth):
-            place = lax.bitwise_xor(chip, 2 * z + flip)
-            columns = pl.ds(pl.multiple_of(place * 2 * width, 2 * width), 2 * width)
-            low_out = jnp.dot(p_ref[:, done:], w_ref[done:, columns], preferred_element_type=jnp.float32)
-            low_out = low_out + low_out_ref[:, columns]
-            given_ref = given_refs[z * len(given_refs) // depth]
-            for lines, low in ((slice(0, rank), low_in_ref[:, columns]), (slice(rank, 2 * rank), low_out)):
-                left, right = low[:, :width], low[:, width:]
-                given_ref[z % given_ref.shape[0], lines, :] = jnp.where(core == 0, right, left)
-                kept_ref[z, lines, :] = jnp.where(core == 0, left, right)
+    line, y = lax.div(chip, 2), lax.rem(chip, 2)
+    for z in range(depth):
+        start = lax.bitwise_xor(line, z) * 4 * width
+        columns = pl.ds(pl.multiple_of(start, 4 * width), 4 * width)
+        low_out = jnp.dot(p_ref[:, done:], w_ref[done:, columns], preferred_element_type=jnp.float32)
+        low_out = low_out + low_out_ref[:, columns]
+        given_ref = given_y[z * len(given_y) // depth]
+        places = ((given_ref, z % given_ref.shape[0], kept_y), (given_here[0], z, kept_here))
+        for lines, low in ((slice(0, rank), low_in_ref[:, columns]), (slice(rank, 2 * rank), low_out)):
+            lower, upper = low[:, : 2 * width], low[:, 2 * width :]
+            sides = (jnp.where(y == 0, upper, lower), jnp.where(y == 0, lower, upper))
+            for both, (given, at, kept) in zip(sides, places):
+                left, right = both[:, :width], both[:, width:]
+                given[at, lines, :] = jnp.where(core == 0, right, left)
+                kept[z, lines, :] = jnp.where(core == 0, left, right)
 
 
 def project(inputs, out_grads, proj_in_t, proj_out_t, devices):

time: 26.6 us -> 26.5 us (level)
  no operation moved by 1% of the time
where the time goes in v25:
time: 26.5 us; the launch traced here: 26.3 us
  starting transfers between devices  14.1 us (53%)
  waiting for transfers between devices  6.84 us (26%)
  Pallas kernels  5.32 us (20%)
    ppermute x13, starting transfers between devices, swap(): lax.ppermute(array, 'ex', [(i, i ^ distance) for i in range(devices)])  14.1 us
    ppermute x13, waiting for transfers between devices, swap(): lax.ppermute(array, 'ex', [(i, i ^ distance) for i in range(devices)])  6.84 us
    pallas_call x1, Pallas kernels, project_loaded(): pl.pallas_call(project_loaded_kernel, out_shape=[jax.ShapeDtypeStruct((ra...  2.22 us
    pallas_call x1, Pallas kernels, project(): pl.pallas_call(functools.partial(project_kernel, rows), out_shape=[half]...  1.36 us
    pallas_call x1, Pallas kernels, last_scores(): pl.pallas_call(functools.partial(last_score_kernel, chips), out_shape=jax...  0.81 us
    pallas_call x1, Pallas kernels, first_scores(): pl.pallas_call(functools.partial(first_score_kernel, len(parts), held), o...  0.7 us
  transfers between devices with their start and end apart: 13, of which 5 were waited for; matrix products, arithmetic and copies ran while one was open for 0% of the time, Pallas kernels for 17%

profile of v25, /device:TPU:0, one launch (start us, length us, event | category | flops | bytes accessed | tf_op | source)
XLA Modules:
  0.0 26.3 jit_solution(746042776349542810)
XLA Ops:
  0.0 0.0 copy-start.1
  0.0 0.0 copy-start
  0.0 4.0 %collective-permute-start = (bf16[1,8,4096]{2,1,0:T(8,128)(2,1)}, bf16[1,8,4096]{2,1,0:T(8,128)(2,1)S(1)}, u32[]{:S(2)}, u32[]{:S(2)}) collective-permute-start(bf16[1,8,4096]{2,1,0:T(8,128)(2,1)} %bitcast.5), channel_id=1, source_target_pairs={{0,8},{1,9},{2,10},{3,11},{4,12},{5,13},{6,14},{7,15},{8,0},{9,1},... | collective-permute-start | bytes 196616 | tf_op jit(solution)/shard_map/ppermute | solution.py:282
  4.0 0.0 copy-start.2
  4.0 2.2 %shard_map.57 = (f32[64,2048]{1,0:T(8,128)S(1)}, f32[64,2048]{1,0:T(8,128)S(1)}) custom-call(bf16[512,2048]{1,0:T(8,128)(2,1)} %x_hbm.1, bf16[1792,2048]{1,0:T(8,128)(2,1)} %w_ref.1, bf16[64,512]{1,0:T(8,128)(2,1)} %bitcast.7, bf16[64,1792]{1,0:T(8,128)(2,1)} %bitcast.3), custom_call_target="tpu_custom_call" | custom-call | flops 167772160 | bytes 2621440 | tf_op jit(solution)/shard_map/pallas_call | solution.py:50
  6.3 0.0 copy-done.1
  6.3 0.0 copy-done
  6.3 1.4 %shard_map.58 = (f32[2,128,128]{2,1,0:T(8,128)S(1)}, f32[2,128,128]{2,1,0:T(8,128)S(1)}, f32[4,128,128]{2,1,0:T(8,128)S(1)}, f32[4,128,128]{2,1,0:T(8,128)S(1)}, f32[4,128,128]{2,1,0:T(8,128)S(1)}) custom-call(f32[64,2048]{1,0:T(8,128)S(1)} %get-tuple-element.32.low_in_ref, f32[64,2048]{1,0:T(8,128)S(1)} %get-tuple-element.33.low_out_ref, ...), custom_call_target="tpu_custom_call" | custom-call | flops 469762048 | bytes 7340032 | tf_op jit(solution)/shard_map/pallas_call | solution.py:103
  7.7 0.1 collective-permute-start.3
  7.7 0.5 %collective-permute-start.4 = (f32[2,128,128]{2,1,0:T(8,128)S(1)}, f32[2,128,128]{2,1,0:T(8,128)S(1)}, u32[]{:S(2)}, u32[]{:S(2)}) collective-permute-start(f32[2,128,128]{2,1,0:T(8,128)S(1)} %get-tuple-element.37), channel_id=1, source_target_pairs={{0,1},{1,0},{2,3},{3,2},{4,5},{5,4},{6,7},{7,6},{8,9},{9,8},{10,11... | collective-permute-start | bytes 393224 | tf_op jit(solution)/shard_map/ppermute | solution.py:282
  8.2 0.1 collective-permute-start.6
  8.3 0.0 collective-permute-done.right_ref
  8.3 0.0 copy-done.2
  8.3 1.6 %collective-permute-start.1 = (bf16[2,8,4096]{2,1,0:T(8,128)(2,1)S(1)}, bf16[2,8,4096]{2,1,0:T(8,128)(2,1)S(1)}, u32[]{:S(2)}, u32[]{:S(2)}) collective-permute-start(bf16[2,8,4096]{2,1,0:T(8,128)(2,1)S(1)} %shard_map.55.left_ref), channel_id=1, source_target_pairs={{0,4},{1,5},{2,6},{3,7},{4,0},{5,1},{6,2},{7,3},{8,12},{9,13},{10,... | collective-permute-start | bytes 393224 | tf_op jit(solution)/shard_map/ppermute | solution.py:282
  10.0 0.0 collective-permute-done.3.refs_0_
  10.0 0.0 collective-permute-done.4.refs_1_
  10.0 0.1 shard_map.59
  10.0 1.6 %collective-permute-start.5 = (bf16[4,144,128]{2,1,0:T(8,128)(2,1)S(1)}, bf16[4,144,128]{2,1,0:T(8,128)(2,1)S(1)}, u32[]{:S(2)}, u32[]{:S(2)}) collective-permute-start(bf16[4,144,128]{2,1,0:T(8,128)(2,1)S(1)} %shard_map.59), channel_id=1, source_target_pairs={{0,2},{1,3},{2,0},{3,1},{4,6},{5,7},{6,4},{7,5},{8,10},{9,11},{10,... | collective-permute-start | bytes 442376 | tf_op jit(solution)/shard_map/ppermute | solution.py:282
  11.6 0.0 collective-permute-start.7
  11.6 2.6 %collective-permute-done.1.right_ref = bf16[2,8,4096]{2,1,0:T(8,128)(2,1)S(1)} collective-permute-done((bf16[2,8,4096]{2,1,0:T(8,128)(2,1)S(1)}, bf16[2,8,4096]{2,1,0:T(8,128)(2,1)S(1)}, u32[]{:S(2)}, u32[]{:S(2)}) %collective-permute-start.1) | collective-permute-done | bytes 131104 | tf_op jit(solution)/shard_map/ppermute | solution.py:282
  14.3 1.6 %collective-permute-start.2 = (bf16[4,8,4096]{2,1,0:T(8,128)(2,1)S(1)}, bf16[4,8,4096]{2,1,0:T(8,128)(2,1)S(1)}, u32[]{:S(2)}, u32[]{:S(2)}) collective-permute-start(bf16[4,8,4096]{2,1,0:T(8,128)(2,1)S(1)} %shard_map.56.refs_4_), channel_id=1, source_target_pairs={{0,2},{1,3},{2,0},{3,1},{4,6},{5,7},{6,4},{7,5},{8,10},{9,11},{10,... | collective-permute-start | bytes 786440 | tf_op jit(solution)/shard_map/ppermute | solution.py:282
  15.9 0.0 collective-permute-done.7.refs_5_
  15.9 0.0 collective-permute-done.6.came_ref
  15.9 0.2 collective-permute-done.5.across_ref
  16.0 0.1 shard_map.60
  16.2 0.1 collective-permute-start.8
  16.2 2.7 %collective-permute-start.9 = (bf16[160,128]{1,0:T(8,128)(2,1)S(1)}, bf16[160,128]{1,0:T(8,128)(2,1)S(1)}, u32[]{:S(2)}, u32[]{:S(2)}) collective-permute-start(bf16[160,128]{1,0:T(8,128)(2,1)S(1)} %get-tuple-element.47), channel_id=1, source_target_pairs={{0,12},{1,13},{2,14},{3,15},{4,8},{5,9},{6,10},{7,11},{8,4},{9,5},... | collective-permute-start | bytes 122888 | tf_op jit(solution)/shard_map/ppermute | solution.py:282
  18.9 0.3 %collective-permute-start.10 = (bf16[144,128]{1,0:T(8,128)(2,1)S(1)}, bf16[144,128]{1,0:T(8,128)(2,1)S(1)}, u32[]{:S(2)}, u32[]{:S(2)}) collective-permute-start(bf16[144,128]{1,0:T(8,128)(2,1)S(1)} %get-tuple-element.48), channel_id=1, source_target_pairs={{0,8},{1,9},{2,10},{3,11},{4,12},{5,13},{6,14},{7,15},{8,0},{9,1},... | collective-permute-start | bytes 110600 | tf_op jit(solution)/shard_map/ppermute | solution.py:282
  19.2 1.5 %collective-permute-start.11 = (bf16[144,128]{1,0:T(8,128)(2,1)S(1)}, bf16[144,128]{1,0:T(8,128)(2,1)S(1)}, u32[]{:S(2)}, u32[]{:S(2)}) collective-permute-start(bf16[144,128]{1,0:T(8,128)(2,1)S(1)} %get-tuple-element.49), channel_id=1, source_target_pairs={{0,4},{1,5},{2,6},{3,7},{4,0},{5,1},{6,2},{7,3},{8,12},{9,13},{10,... | collective-permute-start | bytes 110600 | tf_op jit(solution)/shard_map/ppermute | solution.py:282
  20.7 3.1 %collective-permute-done.10.refs_2_ = bf16[144,128]{1,0:T(8,128)(2,1)S(1)} collective-permute-done((bf16[144,128]{1,0:T(8,128)(2,1)S(1)}, bf16[144,128]{1,0:T(8,128)(2,1)S(1)}, u32[]{:S(2)}, u32[]{:S(2)}) %collective-permute-start.10) | collective-permute-done | bytes 36896 | tf_op jit(solution)/shard_map/ppermute | solution.py:282
  23.8 0.1 collective-permute-done.11.refs_3_
  23.9 0.0 collective-permute-done.9.refs_1_
  23.9 0.0 collective-permute-done.8.refs_6_
  23.9 0.0 collective-permute-done.2.refs_7_
  23.9 0.1 collective-permute-start.12
  24.0 0.7 %shard_map.61 = (f32[2,32,128]{2,1,0:T(8,128)S(1)}, f32[2,8,2,8,128]{4,3,2,1,0:T(8,128)S(1)}) custom-call(f32[128,128]{1,0:T(8,128)S(1)} %get-tuple-element.50.refs_0_, bf16[160,128]{1,0:T(8,128)(2,1)S(1)} %collective-permute-done.9.refs_1_, bf16[144,128]{1,0:T(8,128)(2,1)S(1)} %collective-permute-done.10.refs_2_, ...), custom_call_target="tpu_custom_call" | custom-call | tf_op jit(solution)/shard_map/pallas_call | solution.py:252
  24.7 0.8 %collective-permute-done.12.queries_ref = bf16[4,8,4096]{2,1,0:T(8,128)(2,1)S(1)} collective-permute-done((bf16[4,8,4096]{2,1,0:T(8,128)(2,1)S(1)}, bf16[4,8,4096]{2,1,0:T(8,128)(2,1)S(1)}, u32[]{:S(2)}, u32[]{:S(2)}) %collective-permute-start.12) | collective-permute-done | bytes 262176 | tf_op jit(solution)/shard_map/ppermute | solution.py:282
  25.5 0.8 %shard_map.62 = f32[2,128]{1,0:T(2,128)} custom-call(f32[2,32,128]{2,1,0:T(8,128)S(1)} %get-tuple-element.57.grads_ref, f32[2,8,2,8,128]{4,3,2,1,0:T(8,128)S(1)} %get-tuple-element.58.before_ref, bf16[4,8,4096]{2,1,0:T(8,128)(2,1)S(1)} %collective-permute-done.12.queries_ref), custom_call_target="tpu_custom_call" | custom-call | tf_op jit(solution)/shard_map/pallas_call | solution.py:265
  (2 shorter events, 0.0 us)
Async XLA Ops:
  0.0 6.3 %copy-start.1 = (bf16[1792,64]{0,1:T(8,128)(2,1)S(1)}, bf16[1792,64]{0,1:T(8,128)(2,1)}, u32[]{:S(2)}) copy-start(bf16[1792,64]{0,1:T(8,128)(2,1)} %param.8) | copy-start | bytes 688132
  0.0 6.3 %copy-start = (bf16[1792,2048]{1,0:T(8,128)(2,1)S(1)}, bf16[1792,2048]{1,0:T(8,128)(2,1)}, u32[]{:S(2)}) copy-start(bf16[1792,2048]{1,0:T(8,128)(2,1)} %w_ref.1) | copy-start | bytes 22020100
  0.0 8.3 %collective-permute-start = (bf16[1,8,4096]{2,1,0:T(8,128)(2,1)}, bf16[1,8,4096]{2,1,0:T(8,128)(2,1)S(1)}, u32[]{:S(2)}, u32[]{:S(2)}) collective-permute-start(bf16[1,8,4096]{2,1,0:T(8,128)(2,1)} %bitcast.5), channel_id=1, source_target_pairs={{0,8},{1,9},{2,10},{3,11},{4,12},{5,13},{6,14},{7,15},{8,0},{9,1},... | collective-permute-start | bytes 196616 | tf_op jit(solution)/shard_map/ppermute | solution.py:282
  4.0 4.3 %copy-start.2 = (bf16[8,4096]{1,0:T(8,128)(2,1)S(1)}, bf16[8,4096]{1,0:T(8,128)(2,1)}, u32[]{:S(2)}) copy-start(bf16[8,4096]{1,0:T(8,128)(2,1)} %param.9) | copy-start | bytes 196612
  7.7 2.3 %collective-permute-start.3 = (f32[2,128,128]{2,1,0:T(8,128)S(1)}, f32[2,128,128]{2,1,0:T(8,128)S(1)}, u32[]{:S(2)}, u32[]{:S(2)}) collective-permute-start(f32[2,128,128]{2,1,0:T(8,128)S(1)} %get-tuple-element.36), channel_id=1, source_target_pairs={{0,1},{1,0},{2,3},{3,2},{4,5},{5,4},{6,7},{7,6},{8,9},{9,8},{10,11... | collective-permute-start | bytes 393224 | tf_op jit(solution)/shard_map/ppermute | solution.py:282
  7.7 2.2 %collective-permute-start.4 = (f32[2,128,128]{2,1,0:T(8,128)S(1)}, f32[2,128,128]{2,1,0:T(8,128)S(1)}, u32[]{:S(2)}, u32[]{:S(2)}) collective-permute-start(f32[2,128,128]{2,1,0:T(8,128)S(1)} %get-tuple-element.37), channel_id=1, source_target_pairs={{0,1},{1,0},{2,3},{3,2},{4,5},{5,4},{6,7},{7,6},{8,9},{9,8},{10,11... | collective-permute-start | bytes 393224 | tf_op jit(solution)/shard_map/ppermute | solution.py:282
  8.2 7.6 %collective-permute-start.6 = (f32[4,128,128]{2,1,0:T(8,128)S(1)}, f32[4,128,128]{2,1,0:T(8,128)S(1)}, u32[]{:S(2)}, u32[]{:S(2)}) collective-permute-start(f32[4,128,128]{2,1,0:T(8,128)S(1)} %get-tuple-element.38), channel_id=1, source_target_pairs={{0,1},{1,0},{2,3},{3,2},{4,5},{5,4},{6,7},{7,6},{8,9},{9,8},{10,11... | collective-permute-start | bytes 786440 | tf_op jit(solution)/shard_map/ppermute | solution.py:282
  8.3 5.9 %collective-permute-start.1 = (bf16[2,8,4096]{2,1,0:T(8,128)(2,1)S(1)}, bf16[2,8,4096]{2,1,0:T(8,128)(2,1)S(1)}, u32[]{:S(2)}, u32[]{:S(2)}) collective-permute-start(bf16[2,8,4096]{2,1,0:T(8,128)(2,1)S(1)} %shard_map.55.left_ref), channel_id=1, source_target_pairs={{0,4},{1,5},{2,6},{3,7},{4,0},{5,1},{6,2},{7,3},{8,12},{9,13},{10,... | collective-permute-start | bytes 393224 | tf_op jit(solution)/shard_map/ppermute | solution.py:282
  10.0 6.0 %collective-permute-start.5 = (bf16[4,144,128]{2,1,0:T(8,128)(2,1)S(1)}, bf16[4,144,128]{2,1,0:T(8,128)(2,1)S(1)}, u32[]{:S(2)}, u32[]{:S(2)}) collective-permute-start(bf16[4,144,128]{2,1,0:T(8,128)(2,1)S(1)} %shard_map.59), channel_id=1, source_target_pairs={{0,2},{1,3},{2,0},{3,1},{4,6},{5,7},{6,4},{7,5},{8,10},{9,11},{10,... | collective-permute-start | bytes 442376 | tf_op jit(solution)/shard_map/ppermute | solution.py:282
  11.6 4.2 %collective-permute-start.7 = (bf16[2,8,4096]{2,1,0:T(8,128)(2,1)S(1)}, bf16[2,8,4096]{2,1,0:T(8,128)(2,1)S(1)}, u32[]{:S(2)}, u32[]{:S(2)}) collective-permute-start(bf16[2,8,4096]{2,1,0:T(8,128)(2,1)S(1)} %shard_map.55.left_ref), channel_id=1, source_target_pairs={{0,1},{1,0},{2,3},{3,2},{4,5},{5,4},{6,7},{7,6},{8,9},{9,8},{10,11... | collective-permute-start | bytes 393224 | tf_op jit(solution)/shard_map/ppermute | solution.py:282
  14.3 9.7 %collective-permute-start.2 = (bf16[4,8,4096]{2,1,0:T(8,128)(2,1)S(1)}, bf16[4,8,4096]{2,1,0:T(8,128)(2,1)S(1)}, u32[]{:S(2)}, u32[]{:S(2)}) collective-permute-start(bf16[4,8,4096]{2,1,0:T(8,128)(2,1)S(1)} %shard_map.56.refs_4_), channel_id=1, source_target_pairs={{0,2},{1,3},{2,0},{3,1},{4,6},{5,7},{6,4},{7,5},{8,10},{9,11},{10,... | collective-permute-start | bytes 786440 | tf_op jit(solution)/shard_map/ppermute | solution.py:282
  16.2 7.8 %collective-permute-start.8 = (bf16[2,8,4096]{2,1,0:T(8,128)(2,1)S(1)}, bf16[2,8,4096]{2,1,0:T(8,128)(2,1)S(1)}, u32[]{:S(2)}, u32[]{:S(2)}) collective-permute-start(bf16[2,8,4096]{2,1,0:T(8,128)(2,1)S(1)} %collective-permute-done.1.right_ref), channel_id=1, source_target_pairs={{0,1},{1,0},{2,3},{3,2},{4,5},{5,4},{6,7},{7,6},{8,9},{9,8},{10,11... | collective-permute-start | bytes 393224 | tf_op jit(solution)/shard_map/ppermute | solution.py:282
  16.2 7.7 %collective-permute-start.9 = (bf16[160,128]{1,0:T(8,128)(2,1)S(1)}, bf16[160,128]{1,0:T(8,128)(2,1)S(1)}, u32[]{:S(2)}, u32[]{:S(2)}) collective-permute-start(bf16[160,128]{1,0:T(8,128)(2,1)S(1)} %get-tuple-element.47), channel_id=1, source_target_pairs={{0,12},{1,13},{2,14},{3,15},{4,8},{5,9},{6,10},{7,11},{8,4},{9,5},... | collective-permute-start | bytes 122888 | tf_op jit(solution)/shard_map/ppermute | solution.py:282
  18.9 4.9 %collective-permute-start.10 = (bf16[144,128]{1,0:T(8,128)(2,1)S(1)}, bf16[144,128]{1,0:T(8,128)(2,1)S(1)}, u32[]{:S(2)}, u32[]{:S(2)}) collective-permute-start(bf16[144,128]{1,0:T(8,128)(2,1)S(1)} %get-tuple-element.48), channel_id=1, source_target_pairs={{0,8},{1,9},{2,10},{3,11},{4,12},{5,13},{6,14},{7,15},{8,0},{9,1},... | collective-permute-start | bytes 110600 | tf_op jit(solution)/shard_map/ppermute | solution.py:282
  19.2 4.7 %collective-permute-start.11 = (bf16[144,128]{1,0:T(8,128)(2,1)S(1)}, bf16[144,128]{1,0:T(8,128)(2,1)S(1)}, u32[]{:S(2)}, u32[]{:S(2)}) collective-permute-start(bf16[144,128]{1,0:T(8,128)(2,1)S(1)} %get-tuple-element.49), channel_id=1, source_target_pairs={{0,4},{1,5},{2,6},{3,7},{4,0},{5,1},{6,2},{7,3},{8,12},{9,13},{10,... | collective-permute-start | bytes 110600 | tf_op jit(solution)/shard_map/ppermute | solution.py:282
  23.9 1.6 %collective-permute-start.12 = (bf16[4,8,4096]{2,1,0:T(8,128)(2,1)S(1)}, bf16[4,8,4096]{2,1,0:T(8,128)(2,1)S(1)}, u32[]{:S(2)}, u32[]{:S(2)}) collective-permute-start(bf16[4,8,4096]{2,1,0:T(8,128)(2,1)S(1)} %collective-permute-done.2.refs_7_), channel_id=1, source_target_pairs={{0,1},{1,0},{2,3},{3,2},{4,5},{5,4},{6,7},{7,6},{8,9},{9,8},{10,11... | collective-permute-start | bytes 786440 | tf_op jit(solution)/shard_map/ppermute | solution.py:282

commit v26 on v25

--- a/solution.py
+++ b/solution.py
@@ -10,6 +10,7 @@
 SEQ = 64
 VMEM_BYTES = 32 * 1024 * 1024
 LOADED_ROWS = 128
+CHUNK_ROWS = 256
 FAR_PAD = 16
 LEFT_OVER = 0.36 * 2.0**-8
 LANES_BY_LANES = (((1,), (1,)), ((), ()))
@@ -25,7 +26,7 @@
     ]
     chunks = []
     for hbm, buf, matrix, low_ref in ((x_hbm, x_buf, p_in, low_in_ref), (w_hbm, w_buf, p_out, low_out_ref)):
-        count = buf.shape[0] // LOADED_ROWS if buf.shape[0] % LOADED_ROWS == 0 else 1
+        count = buf.shape[0] // CHUNK_ROWS if buf.shape[0] % CHUNK_ROWS == 0 else 1
         for chunk in range(count):
             part = pl.ds(chunk * (buf.shape[0] // count), buf.shape[0] // count)
             copy = pltpu.make_async_copy(hbm.at[part, :], buf.at[part, :], sems.at[len(chunks)])
@@ -46,7 +47,7 @@
 def project_loaded(inputs, out_grads, proj_in_t, proj_out_t, rows):
     arrays = [pltpu.with_memory_space_constraint(a, pltpu.HBM) for a in (inputs, out_grads, proj_in_t, proj_out_t)]
     rank, tokens = proj_in_t.shape[0], inputs.shape[1]
-    chunks = sum(a // LOADED_ROWS if a % LOADED_ROWS == 0 else 1 for a in (inputs.shape[0], rows))
+    chunks = sum(a // CHUNK_ROWS if a % CHUNK_ROWS == 0 else 1 for a in (inputs.shape[0], rows))
     return pl.pallas_call(
         project_loaded_kernel,
         out_shape=[jax.ShapeDtypeStruct((rank, tokens), jnp.float32)] * 2,

time: 26.5 us -> 26.4 us (level)
  transfers between devices with their start and end apart: 13 -> 13, of which waited for: 5 -> 4; matrix products, arithmetic and copies ran while one was open for 0% -> 0% of each run, Pallas kernels for 17% -> 17%
where the time goes in v26:
time: 26.4 us; the launch traced here: 26.3 us
  starting transfers between devices  14.1 us (53%)
  waiting for transfers between devices  6.85 us (26%)
  Pallas kernels  5.26 us (20%)
    ppermute x13, starting transfers between devices, swap(): lax.ppermute(array, 'ex', [(i, i ^ distance) for i in range(devices)])  14.1 us
    ppermute x13, waiting for transfers between devices, swap(): lax.ppermute(array, 'ex', [(i, i ^ distance) for i in range(devices)])  6.85 us
    pallas_call x1, Pallas kernels, project_loaded(): pl.pallas_call(project_loaded_kernel, out_shape=[jax.ShapeDtypeStruct((ra...  2.16 us
    pallas_call x1, Pallas kernels, project(): pl.pallas_call(functools.partial(project_kernel, rows), out_shape=[half]...  1.36 us
    pallas_call x1, Pallas kernels, last_scores(): pl.pallas_call(functools.partial(last_score_kernel, chips), out_shape=jax...  0.81 us
    pallas_call x1, Pallas kernels, first_scores(): pl.pallas_call(functools.partial(first_score_kernel, len(parts), held), o...  0.7 us
  transfers between devices with their start and end apart: 13, of which 4 were waited for; matrix products, arithmetic and copies ran while one was open for 0% of the time, Pallas kernels for 17%

profile of v26, /device:TPU:0, one launch (start us, length us, event | category | flops | bytes accessed | tf_op | source)
XLA Modules:
  0.0 26.3 jit_solution(5684693310825405319)
XLA Ops:
  0.0 0.0 copy-start.1
  0.0 0.0 copy-start
  0.0 4.0 %collective-permute-start = (bf16[1,8,4096]{2,1,0:T(8,128)(2,1)}, bf16[1,8,4096]{2,1,0:T(8,128)(2,1)S(1)}, u32[]{:S(2)}, u32[]{:S(2)}) collective-permute-start(bf16[1,8,4096]{2,1,0:T(8,128)(2,1)} %bitcast.5), channel_id=1, source_target_pairs={{0,8},{1,9},{2,10},{3,11},{4,12},{5,13},{6,14},{7,15},{8,0},{9,1},... | collective-permute-start | bytes 196616 | tf_op jit(solution)/shard_map/ppermute | solution.py:283
  4.0 0.0 copy-start.2
  4.0 2.2 %shard_map.57 = (f32[64,2048]{1,0:T(8,128)S(1)}, f32[64,2048]{1,0:T(8,128)S(1)}) custom-call(bf16[512,2048]{1,0:T(8,128)(2,1)} %x_hbm.1, bf16[1792,2048]{1,0:T(8,128)(2,1)} %w_ref.1, bf16[64,512]{1,0:T(8,128)(2,1)} %bitcast.7, bf16[64,1792]{1,0:T(8,128)(2,1)} %bitcast.3), custom_call_target="tpu_custom_call" | custom-call | flops 167772160 | bytes 2621440 | tf_op jit(solution)/shard_map/pallas_call | solution.py:51
  6.2 0.0 copy-done.1
  6.2 0.0 copy-done
  6.2 1.4 %shard_map.58 = (f32[2,128,128]{2,1,0:T(8,128)S(1)}, f32[2,128,128]{2,1,0:T(8,128)S(1)}, f32[4,128,128]{2,1,0:T(8,128)S(1)}, f32[4,128,128]{2,1,0:T(8,128)S(1)}, f32[4,128,128]{2,1,0:T(8,128)S(1)}) custom-call(f32[64,2048]{1,0:T(8,128)S(1)} %get-tuple-element.32.low_in_ref, f32[64,2048]{1,0:T(8,128)S(1)} %get-tuple-element.33.low_out_ref, ...), custom_call_target="tpu_custom_call" | custom-call | flops 469762048 | bytes 7340032 | tf_op jit(solution)/shard_map/pallas_call | solution.py:104
  7.6 0.1 collective-permute-start.3
  7.7 0.5 %collective-permute-start.4 = (f32[2,128,128]{2,1,0:T(8,128)S(1)}, f32[2,128,128]{2,1,0:T(8,128)S(1)}, u32[]{:S(2)}, u32[]{:S(2)}) collective-permute-start(f32[2,128,128]{2,1,0:T(8,128)S(1)} %get-tuple-element.37), channel_id=1, source_target_pairs={{0,1},{1,0},{2,3},{3,2},{4,5},{5,4},{6,7},{7,6},{8,9},{9,8},{10,11... | collective-permute-start | bytes 393224 | tf_op jit(solution)/shard_map/ppermute | solution.py:283
  8.2 0.1 collective-permute-start.6
  8.3 0.0 collective-permute-done.right_ref
  8.3 0.0 copy-done.2
  8.3 1.6 %collective-permute-start.1 = (bf16[2,8,4096]{2,1,0:T(8,128)(2,1)S(1)}, bf16[2,8,4096]{2,1,0:T(8,128)(2,1)S(1)}, u32[]{:S(2)}, u32[]{:S(2)}) collective-permute-start(bf16[2,8,4096]{2,1,0:T(8,128)(2,1)S(1)} %shard_map.55.left_ref), channel_id=1, source_target_pairs={{0,4},{1,5},{2,6},{3,7},{4,0},{5,1},{6,2},{7,3},{8,12},{9,13},{10,... | collective-permute-start | bytes 393224 | tf_op jit(solution)/shard_map/ppermute | solution.py:283
  9.9 0.0 collective-permute-done.3.refs_0_
  9.9 0.0 collective-permute-done.4.refs_1_
  9.9 0.1 shard_map.59
  10.0 1.6 %collective-permute-start.5 = (bf16[4,144,128]{2,1,0:T(8,128)(2,1)S(1)}, bf16[4,144,128]{2,1,0:T(8,128)(2,1)S(1)}, u32[]{:S(2)}, u32[]{:S(2)}) collective-permute-start(bf16[4,144,128]{2,1,0:T(8,128)(2,1)S(1)} %shard_map.59), channel_id=1, source_target_pairs={{0,2},{1,3},{2,0},{3,1},{4,6},{5,7},{6,4},{7,5},{8,10},{9,11},{10,... | collective-permute-start | bytes 442376 | tf_op jit(solution)/shard_map/ppermute | solution.py:283
  11.6 0.0 collective-permute-start.7
  11.6 2.6 %collective-permute-done.1.right_ref = bf16[2,8,4096]{2,1,0:T(8,128)(2,1)S(1)} collective-permute-done((bf16[2,8,4096]{2,1,0:T(8,128)(2,1)S(1)}, bf16[2,8,4096]{2,1,0:T(8,128)(2,1)S(1)}, u32[]{:S(2)}, u32[]{:S(2)}) %collective-permute-start.1) | collective-permute-done | bytes 131104 | tf_op jit(solution)/shard_map/ppermute | solution.py:283
  14.2 1.6 %collective-permute-start.2 = (bf16[4,8,4096]{2,1,0:T(8,128)(2,1)S(1)}, bf16[4,8,4096]{2,1,0:T(8,128)(2,1)S(1)}, u32[]{:S(2)}, u32[]{:S(2)}) collective-permute-start(bf16[4,8,4096]{2,1,0:T(8,128)(2,1)S(1)} %shard_map.56.refs_4_), channel_id=1, source_target_pairs={{0,2},{1,3},{2,0},{3,1},{4,6},{5,7},{6,4},{7,5},{8,10},{9,11},{10,... | collective-permute-start | bytes 786440 | tf_op jit(solution)/shard_map/ppermute | solution.py:283
  15.8 0.0 collective-permute-done.7.refs_5_
  15.8 0.0 collective-permute-done.6.came_ref
  15.8 0.2 collective-permute-done.5.across_ref
  16.0 0.1 shard_map.60
  16.1 0.1 collective-permute-start.8
  16.2 2.7 %collective-permute-start.9 = (bf16[160,128]{1,0:T(8,128)(2,1)S(1)}, bf16[160,128]{1,0:T(8,128)(2,1)S(1)}, u32[]{:S(2)}, u32[]{:S(2)}) collective-permute-start(bf16[160,128]{1,0:T(8,128)(2,1)S(1)} %get-tuple-element.47), channel_id=1, source_target_pairs={{0,12},{1,13},{2,14},{3,15},{4,8},{5,9},{6,10},{7,11},{8,4},{9,5},... | collective-permute-start | bytes 122888 | tf_op jit(solution)/shard_map/ppermute | solution.py:283
  18.9 0.2 collective-permute-start.10
  19.1 1.5 %collective-permute-start.11 = (bf16[144,128]{1,0:T(8,128)(2,1)S(1)}, bf16[144,128]{1,0:T(8,128)(2,1)S(1)}, u32[]{:S(2)}, u32[]{:S(2)}) collective-permute-start(bf16[144,128]{1,0:T(8,128)(2,1)S(1)} %get-tuple-element.49), channel_id=1, source_target_pairs={{0,4},{1,5},{2,6},{3,7},{4,0},{5,1},{6,2},{7,3},{8,12},{9,13},{10,... | collective-permute-start | bytes 110600 | tf_op jit(solution)/shard_map/ppermute | solution.py:283
  20.6 3.2 %collective-permute-done.10.refs_2_ = bf16[144,128]{1,0:T(8,128)(2,1)S(1)} collective-permute-done((bf16[144,128]{1,0:T(8,128)(2,1)S(1)}, bf16[144,128]{1,0:T(8,128)(2,1)S(1)}, u32[]{:S(2)}, u32[]{:S(2)}) %collective-permute-start.10) | collective-permute-done | bytes 36896 | tf_op jit(solution)/shard_map/ppermute | solution.py:283
  23.8 0.0 collective-permute-done.11.refs_3_
  23.9 0.0 collective-permute-done.9.refs_1_
  23.9 0.0 collective-permute-done.8.refs_6_
  23.9 0.0 collective-permute-done.2.refs_7_
  23.9 0.1 collective-permute-start.12
  24.0 0.7 %shard_map.61 = (f32[2,32,128]{2,1,0:T(8,128)S(1)}, f32[2,8,2,8,128]{4,3,2,1,0:T(8,128)S(1)}) custom-call(f32[128,128]{1,0:T(8,128)S(1)} %get-tuple-element.50.refs_0_, bf16[160,128]{1,0:T(8,128)(2,1)S(1)} %collective-permute-done.9.refs_1_, bf16[144,128]{1,0:T(8,128)(2,1)S(1)} %collective-permute-done.10.refs_2_, ...), custom_call_target="tpu_custom_call" | custom-call | tf_op jit(solution)/shard_map/pallas_call | solution.py:253
  24.7 0.8 %collective-permute-done.12.queries_ref = bf16[4,8,4096]{2,1,0:T(8,128)(2,1)S(1)} collective-permute-done((bf16[4,8,4096]{2,1,0:T(8,128)(2,1)S(1)}, bf16[4,8,4096]{2,1,0:T(8,128)(2,1)S(1)}, u32[]{:S(2)}, u32[]{:S(2)}) %collective-permute-start.12) | collective-permute-done | bytes 262176 | tf_op jit(solution)/shard_map/ppermute | solution.py:283
  25.5 0.8 %shard_map.62 = f32[2,128]{1,0:T(2,128)} custom-call(f32[2,32,128]{2,1,0:T(8,128)S(1)} %get-tuple-element.57.grads_ref, f32[2,8,2,8,128]{4,3,2,1,0:T(8,128)S(1)} %get-tuple-element.58.before_ref, bf16[4,8,4096]{2,1,0:T(8,128)(2,1)S(1)} %collective-permute-done.12.queries_ref), custom_call_target="tpu_custom_call" | custom-call | tf_op jit(solution)/shard_map/pallas_call | solution.py:266
  (2 shorter events, 0.0 us)
Async XLA Ops:
  0.0 6.2 %copy-start.1 = (bf16[1792,64]{0,1:T(8,128)(2,1)S(1)}, bf16[1792,64]{0,1:T(8,128)(2,1)}, u32[]{:S(2)}) copy-start(bf16[1792,64]{0,1:T(8,128)(2,1)} %param.8) | copy-start | bytes 688132
  0.0 6.2 %copy-start = (bf16[1792,2048]{1,0:T(8,128)(2,1)S(1)}, bf16[1792,2048]{1,0:T(8,128)(2,1)}, u32[]{:S(2)}) copy-start(bf16[1792,2048]{1,0:T(8,128)(2,1)} %w_ref.1) | copy-start | bytes 22020100
  0.0 8.3 %collective-permute-start = (bf16[1,8,4096]{2,1,0:T(8,128)(2,1)}, bf16[1,8,4096]{2,1,0:T(8,128)(2,1)S(1)}, u32[]{:S(2)}, u32[]{:S(2)}) collective-permute-start(bf16[1,8,4096]{2,1,0:T(8,128)(2,1)} %bitcast.5), channel_id=1, source_target_pairs={{0,8},{1,9},{2,10},{3,11},{4,12},{5,13},{6,14},{7,15},{8,0},{9,1},... | collective-permute-start | bytes 196616 | tf_op jit(solution)/shard_map/ppermute | solution.py:283
  4.0 4.2 %copy-start.2 = (bf16[8,4096]{1,0:T(8,128)(2,1)S(1)}, bf16[8,4096]{1,0:T(8,128)(2,1)}, u32[]{:S(2)}) copy-start(bf16[8,4096]{1,0:T(8,128)(2,1)} %param.9) | copy-start | bytes 196612
  7.6 2.3 %collective-permute-start.3 = (f32[2,128,128]{2,1,0:T(8,128)S(1)}, f32[2,128,128]{2,1,0:T(8,128)S(1)}, u32[]{:S(2)}, u32[]{:S(2)}) collective-permute-start(f32[2,128,128]{2,1,0:T(8,128)S(1)} %get-tuple-element.36), channel_id=1, source_target_pairs={{0,1},{1,0},{2,3},{3,2},{4,5},{5,4},{6,7},{7,6},{8,9},{9,8},{10,11... | collective-permute-start | bytes 393224 | tf_op jit(solution)/shard_map/ppermute | solution.py:283
  7.7 2.2 %collective-permute-start.4 = (f32[2,128,128]{2,1,0:T(8,128)S(1)}, f32[2,128,128]{2,1,0:T(8,128)S(1)}, u32[]{:S(2)}, u32[]{:S(2)}) collective-permute-start(f32[2,128,128]{2,1,0:T(8,128)S(1)} %get-tuple-element.37), channel_id=1, source_target_pairs={{0,1},{1,0},{2,3},{3,2},{4,5},{5,4},{6,7},{7,6},{8,9},{9,8},{10,11... | collective-permute-start | bytes 393224 | tf_op jit(solution)/shard_map/ppermute | solution.py:283
  8.2 7.6 %collective-permute-start.6 = (f32[4,128,128]{2,1,0:T(8,128)S(1)}, f32[4,128,128]{2,1,0:T(8,128)S(1)}, u32[]{:S(2)}, u32[]{:S(2)}) collective-permute-start(f32[4,128,128]{2,1,0:T(8,128)S(1)} %get-tuple-element.38), channel_id=1, source_target_pairs={{0,1},{1,0},{2,3},{3,2},{4,5},{5,4},{6,7},{7,6},{8,9},{9,8},{10,11... | collective-permute-start | bytes 786440 | tf_op jit(solution)/shard_map/ppermute | solution.py:283
  8.3 5.9 %collective-permute-start.1 = (bf16[2,8,4096]{2,1,0:T(8,128)(2,1)S(1)}, bf16[2,8,4096]{2,1,0:T(8,128)(2,1)S(1)}, u32[]{:S(2)}, u32[]{:S(2)}) collective-permute-start(bf16[2,8,4096]{2,1,0:T(8,128)(2,1)S(1)} %shard_map.55.left_ref), channel_id=1, source_target_pairs={{0,4},{1,5},{2,6},{3,7},{4,0},{5,1},{6,2},{7,3},{8,12},{9,13},{10,... | collective-permute-start | bytes 393224 | tf_op jit(solution)/shard_map/ppermute | solution.py:283
  10.0 6.0 %collective-permute-start.5 = (bf16[4,144,128]{2,1,0:T(8,128)(2,1)S(1)}, bf16[4,144,128]{2,1,0:T(8,128)(2,1)S(1)}, u32[]{:S(2)}, u32[]{:S(2)}) collective-permute-start(bf16[4,144,128]{2,1,0:T(8,128)(2,1)S(1)} %shard_map.59), channel_id=1, source_target_pairs={{0,2},{1,3},{2,0},{3,1},{4,6},{5,7},{6,4},{7,5},{8,10},{9,11},{10,... | collective-permute-start | bytes 442376 | tf_op jit(solution)/shard_map/ppermute | solution.py:283
  11.6 4.2 %collective-permute-start.7 = (bf16[2,8,4096]{2,1,0:T(8,128)(2,1)S(1)}, bf16[2,8,4096]{2,1,0:T(8,128)(2,1)S(1)}, u32[]{:S(2)}, u32[]{:S(2)}) collective-permute-start(bf16[2,8,4096]{2,1,0:T(8,128)(2,1)S(1)} %shard_map.55.left_ref), channel_id=1, source_target_pairs={{0,1},{1,0},{2,3},{3,2},{4,5},{5,4},{6,7},{7,6},{8,9},{9,8},{10,11... | collective-permute-start | bytes 393224 | tf_op jit(solution)/shard_map/ppermute | solution.py:283
  14.2 9.7 %collective-permute-start.2 = (bf16[4,8,4096]{2,1,0:T(8,128)(2,1)S(1)}, bf16[4,8,4096]{2,1,0:T(8,128)(2,1)S(1)}, u32[]{:S(2)}, u32[]{:S(2)}) collective-permute-start(bf16[4,8,4096]{2,1,0:T(8,128)(2,1)S(1)} %shard_map.56.refs_4_), channel_id=1, source_target_pairs={{0,2},{1,3},{2,0},{3,1},{4,6},{5,7},{6,4},{7,5},{8,10},{9,11},{10,... | collective-permute-start | bytes 786440 | tf_op jit(solution)/shard_map/ppermute | solution.py:283
  16.1 7.8 %collective-permute-start.8 = (bf16[2,8,4096]{2,1,0:T(8,128)(2,1)S(1)}, bf16[2,8,4096]{2,1,0:T(8,128)(2,1)S(1)}, u32[]{:S(2)}, u32[]{:S(2)}) collective-permute-start(bf16[2,8,4096]{2,1,0:T(8,128)(2,1)S(1)} %collective-permute-done.1.right_ref), channel_id=1, source_target_pairs={{0,1},{1,0},{2,3},{3,2},{4,5},{5,4},{6,7},{7,6},{8,9},{9,8},{10,11... | collective-permute-start | bytes 393224 | tf_op jit(solution)/shard_map/ppermute | solution.py:283
  16.2 7.7 %collective-permute-start.9 = (bf16[160,128]{1,0:T(8,128)(2,1)S(1)}, bf16[160,128]{1,0:T(8,128)(2,1)S(1)}, u32[]{:S(2)}, u32[]{:S(2)}) collective-permute-start(bf16[160,128]{1,0:T(8,128)(2,1)S(1)} %get-tuple-element.47), channel_id=1, source_target_pairs={{0,12},{1,13},{2,14},{3,15},{4,8},{5,9},{6,10},{7,11},{8,4},{9,5},... | collective-permute-start | bytes 122888 | tf_op jit(solution)/shard_map/ppermute | solution.py:283
  18.9 4.9 %collective-permute-start.10 = (bf16[144,128]{1,0:T(8,128)(2,1)S(1)}, bf16[144,128]{1,0:T(8,128)(2,1)S(1)}, u32[]{:S(2)}, u32[]{:S(2)}) collective-permute-start(bf16[144,128]{1,0:T(8,128)(2,1)S(1)} %get-tuple-element.48), channel_id=1, source_target_pairs={{0,8},{1,9},{2,10},{3,11},{4,12},{5,13},{6,14},{7,15},{8,0},{9,1},... | collective-permute-start | bytes 110600 | tf_op jit(solution)/shard_map/ppermute | solution.py:283
  19.1 4.7 %collective-permute-start.11 = (bf16[144,128]{1,0:T(8,128)(2,1)S(1)}, bf16[144,128]{1,0:T(8,128)(2,1)S(1)}, u32[]{:S(2)}, u32[]{:S(2)}) collective-permute-start(bf16[144,128]{1,0:T(8,128)(2,1)S(1)} %get-tuple-element.49), channel_id=1, source_target_pairs={{0,4},{1,5},{2,6},{3,7},{4,0},{5,1},{6,2},{7,3},{8,12},{9,13},{10,... | collective-permute-start | bytes 110600 | tf_op jit(solution)/shard_map/ppermute | solution.py:283
  23.9 1.6 %collective-permute-start.12 = (bf16[4,8,4096]{2,1,0:T(8,128)(2,1)S(1)}, bf16[4,8,4096]{2,1,0:T(8,128)(2,1)S(1)}, u32[]{:S(2)}, u32[]{:S(2)}) collective-permute-start(bf16[4,8,4096]{2,1,0:T(8,128)(2,1)S(1)} %collective-permute-done.2.refs_7_), channel_id=1, source_target_pairs={{0,1},{1,0},{2,3},{3,2},{4,5},{5,4},{6,7},{7,6},{8,9},{9,8},{10,11... | collective-permute-start | bytes 786440 | tf_op jit(solution)/shard_map/ppermute | solution.py:283

commit v27 on v26

--- a/solution.py
+++ b/solution.py
@@ -9,7 +9,7 @@
 
 SEQ = 64
 VMEM_BYTES = 32 * 1024 * 1024
-LOADED_ROWS = 128
+LOADED_ROWS = 256
 CHUNK_ROWS = 256
 FAR_PAD = 16
 LEFT_OVER = 0.36 * 2.0**-8

time: 26.4 us -> 26.5 us (level)
  no operation moved by 1% of the time
where the time goes in v27:
time: 26.5 us; the launch traced here: 26.3 us
  starting transfers between devices  14.1 us (53%)
  waiting for transfers between devices  6.85 us (26%)
  Pallas kernels  5.27 us (20%)
    ppermute x13, starting transfers between devices, swap(): lax.ppermute(array, 'ex', [(i, i ^ distance) for i in range(devices)])  14.1 us
    ppermute x13, waiting for transfers between devices, swap(): lax.ppermute(array, 'ex', [(i, i ^ distance) for i in range(devices)])  6.85 us
    pallas_call x1, Pallas kernels, project_loaded(): pl.pallas_call(project_loaded_kernel, out_shape=[jax.ShapeDtypeStruct((ra...  2.28 us
    pallas_call x1, Pallas kernels, project(): pl.pallas_call(functools.partial(project_kernel, rows), out_shape=[half]...  1.25 us
    pallas_call x1, Pallas kernels, last_scores(): pl.pallas_call(functools.partial(last_score_kernel, chips), out_shape=jax...  0.81 us
    pallas_call x1, Pallas kernels, first_scores(): pl.pallas_call(functools.partial(first_score_kernel, len(parts), held), o...  0.7 us
  transfers between devices with their start and end apart: 13, of which 4 were waited for; matrix products, arithmetic and copies ran while one was open for 0% of the time, Pallas kernels for 17%

profile of v27, /device:TPU:0, one launch (start us, length us, event | category | flops | bytes accessed | tf_op | source)
XLA Modules:
  0.0 26.3 jit_solution(9784875554114454894)
XLA Ops:
  0.0 0.0 copy-start.1
  0.0 0.0 copy-start
  0.0 4.0 %collective-permute-start = (bf16[1,8,4096]{2,1,0:T(8,128)(2,1)}, bf16[1,8,4096]{2,1,0:T(8,128)(2,1)S(1)}, u32[]{:S(2)}, u32[]{:S(2)}) collective-permute-start(bf16[1,8,4096]{2,1,0:T(8,128)(2,1)} %bitcast.5), channel_id=1, source_target_pairs={{0,8},{1,9},{2,10},{3,11},{4,12},{5,13},{6,14},{7,15},{8,0},{9,1},... | collective-permute-start | bytes 196616 | tf_op jit(solution)/shard_map/ppermute | solution.py:283
  4.0 0.0 copy-start.2
  4.0 2.3 %shard_map.57 = (f32[64,2048]{1,0:T(8,128)S(1)}, f32[64,2048]{1,0:T(8,128)S(1)}) custom-call(bf16[512,2048]{1,0:T(8,128)(2,1)} %x_hbm.1, bf16[1792,2048]{1,0:T(8,128)(2,1)} %w_ref.1, bf16[64,512]{1,0:T(8,128)(2,1)} %bitcast.7, bf16[64,1792]{1,0:T(8,128)(2,1)} %bitcast.3), custom_call_target="tpu_custom_call" | custom-call | flops 201326592 | bytes 3145728 | tf_op jit(solution)/shard_map/pallas_call | solution.py:51
  6.3 0.0 copy-done.1
  6.3 0.0 copy-done
  6.4 1.2 %shard_map.58 = (f32[2,128,128]{2,1,0:T(8,128)S(1)}, f32[2,128,128]{2,1,0:T(8,128)S(1)}, f32[4,128,128]{2,1,0:T(8,128)S(1)}, f32[4,128,128]{2,1,0:T(8,128)S(1)}, f32[4,128,128]{2,1,0:T(8,128)S(1)}) custom-call(f32[64,2048]{1,0:T(8,128)S(1)} %get-tuple-element.32.low_in_ref, f32[64,2048]{1,0:T(8,128)S(1)} %get-tuple-element.33.low_out_ref, ...), custom_call_target="tpu_custom_call" | custom-call | flops 469762048 | bytes 7340032 | tf_op jit(solution)/shard_map/pallas_call | solution.py:104
  7.6 0.1 collective-permute-start.3
  7.7 0.5 %collective-permute-start.4 = (f32[2,128,128]{2,1,0:T(8,128)S(1)}, f32[2,128,128]{2,1,0:T(8,128)S(1)}, u32[]{:S(2)}, u32[]{:S(2)}) collective-permute-start(f32[2,128,128]{2,1,0:T(8,128)S(1)} %get-tuple-element.37), channel_id=1, source_target_pairs={{0,1},{1,0},{2,3},{3,2},{4,5},{5,4},{6,7},{7,6},{8,9},{9,8},{10,11... | collective-permute-start | bytes 393224 | tf_op jit(solution)/shard_map/ppermute | solution.py:283
  8.2 0.1 collective-permute-start.6
  8.3 0.0 collective-permute-done.right_ref
  8.3 0.0 copy-done.2
  8.3 1.6 %collective-permute-start.1 = (bf16[2,8,4096]{2,1,0:T(8,128)(2,1)S(1)}, bf16[2,8,4096]{2,1,0:T(8,128)(2,1)S(1)}, u32[]{:S(2)}, u32[]{:S(2)}) collective-permute-start(bf16[2,8,4096]{2,1,0:T(8,128)(2,1)S(1)} %shard_map.55.left_ref), channel_id=1, source_target_pairs={{0,4},{1,5},{2,6},{3,7},{4,0},{5,1},{6,2},{7,3},{8,12},{9,13},{10,... | collective-permute-start | bytes 393224 | tf_op jit(solution)/shard_map/ppermute | solution.py:283
  9.9 0.0 collective-permute-done.3.refs_0_
  9.9 0.0 collective-permute-done.4.refs_1_
  9.9 0.1 shard_map.59
  10.0 1.6 %collective-permute-start.5 = (bf16[4,144,128]{2,1,0:T(8,128)(2,1)S(1)}, bf16[4,144,128]{2,1,0:T(8,128)(2,1)S(1)}, u32[]{:S(2)}, u32[]{:S(2)}) collective-permute-start(bf16[4,144,128]{2,1,0:T(8,128)(2,1)S(1)} %shard_map.59), channel_id=1, source_target_pairs={{0,2},{1,3},{2,0},{3,1},{4,6},{5,7},{6,4},{7,5},{8,10},{9,11},{10,... | collective-permute-start | bytes 442376 | tf_op jit(solution)/shard_map/ppermute | solution.py:283
  11.6 0.0 collective-permute-start.7
  11.6 2.6 %collective-permute-done.1.right_ref = bf16[2,8,4096]{2,1,0:T(8,128)(2,1)S(1)} collective-permute-done((bf16[2,8,4096]{2,1,0:T(8,128)(2,1)S(1)}, bf16[2,8,4096]{2,1,0:T(8,128)(2,1)S(1)}, u32[]{:S(2)}, u32[]{:S(2)}) %collective-permute-start.1) | collective-permute-done | bytes 131104 | tf_op jit(solution)/shard_map/ppermute | solution.py:283
  14.2 1.6 %collective-permute-start.2 = (bf16[4,8,4096]{2,1,0:T(8,128)(2,1)S(1)}, bf16[4,8,4096]{2,1,0:T(8,128)(2,1)S(1)}, u32[]{:S(2)}, u32[]{:S(2)}) collective-permute-start(bf16[4,8,4096]{2,1,0:T(8,128)(2,1)S(1)} %shard_map.56.refs_4_), channel_id=1, source_target_pairs={{0,2},{1,3},{2,0},{3,1},{4,6},{5,7},{6,4},{7,5},{8,10},{9,11},{10,... | collective-permute-start | bytes 786440 | tf_op jit(solution)/shard_map/ppermute | solution.py:283
  15.8 0.0 collective-permute-done.7.refs_5_
  15.8 0.0 collective-permute-done.6.came_ref
  15.8 0.2 collective-permute-done.5.across_ref
  16.0 0.1 shard_map.60
  16.1 0.1 collective-permute-start.8
  16.2 2.8 %collective-permute-start.9 = (bf16[160,128]{1,0:T(8,128)(2,1)S(1)}, bf16[160,128]{1,0:T(8,128)(2,1)S(1)}, u32[]{:S(2)}, u32[]{:S(2)}) collective-permute-start(bf16[160,128]{1,0:T(8,128)(2,1)S(1)} %get-tuple-element.47), channel_id=1, source_target_pairs={{0,12},{1,13},{2,14},{3,15},{4,8},{5,9},{6,10},{7,11},{8,4},{9,5},... | collective-permute-start | bytes 122888 | tf_op jit(solution)/shard_map/ppermute | solution.py:283
  19.0 0.2 collective-permute-start.10
  19.1 1.5 %collective-permute-start.11 = (bf16[144,128]{1,0:T(8,128)(2,1)S(1)}, bf16[144,128]{1,0:T(8,128)(2,1)S(1)}, u32[]{:S(2)}, u32[]{:S(2)}) collective-permute-start(bf16[144,128]{1,0:T(8,128)(2,1)S(1)} %get-tuple-element.49), channel_id=1, source_target_pairs={{0,4},{1,5},{2,6},{3,7},{4,0},{5,1},{6,2},{7,3},{8,12},{9,13},{10,... | collective-permute-start | bytes 110600 | tf_op jit(solution)/shard_map/ppermute | solution.py:283
  20.6 3.2 %collective-permute-done.10.refs_2_ = bf16[144,128]{1,0:T(8,128)(2,1)S(1)} collective-permute-done((bf16[144,128]{1,0:T(8,128)(2,1)S(1)}, bf16[144,128]{1,0:T(8,128)(2,1)S(1)}, u32[]{:S(2)}, u32[]{:S(2)}) %collective-permute-start.10) | collective-permute-done | bytes 36896 | tf_op jit(solution)/shard_map/ppermute | solution.py:283
  23.9 0.0 collective-permute-done.11.refs_3_
  23.9 0.0 collective-permute-done.9.refs_1_
  23.9 0.0 collective-permute-done.8.refs_6_
  23.9 0.0 collective-permute-done.2.refs_7_
  23.9 0.1 collective-permute-start.12
  24.0 0.7 %shard_map.61 = (f32[2,32,128]{2,1,0:T(8,128)S(1)}, f32[2,8,2,8,128]{4,3,2,1,0:T(8,128)S(1)}) custom-call(f32[128,128]{1,0:T(8,128)S(1)} %get-tuple-element.50.refs_0_, bf16[160,128]{1,0:T(8,128)(2,1)S(1)} %collective-permute-done.9.refs_1_, bf16[144,128]{1,0:T(8,128)(2,1)S(1)} %collective-permute-done.10.refs_2_, ...), custom_call_target="tpu_custom_call" | custom-call | tf_op jit(solution)/shard_map/pallas_call | solution.py:253
  24.7 0.8 %collective-permute-done.12.queries_ref = bf16[4,8,4096]{2,1,0:T(8,128)(2,1)S(1)} collective-permute-done((bf16[4,8,4096]{2,1,0:T(8,128)(2,1)S(1)}, bf16[4,8,4096]{2,1,0:T(8,128)(2,1)S(1)}, u32[]{:S(2)}, u32[]{:S(2)}) %collective-permute-start.12) | collective-permute-done | bytes 262176 | tf_op jit(solution)/shard_map/ppermute | solution.py:283
  25.5 0.8 %shard_map.62 = f32[2,128]{1,0:T(2,128)} custom-call(f32[2,32,128]{2,1,0:T(8,128)S(1)} %get-tuple-element.57.grads_ref, f32[2,8,2,8,128]{4,3,2,1,0:T(8,128)S(1)} %get-tuple-element.58.before_ref, bf16[4,8,4096]{2,1,0:T(8,128)(2,1)S(1)} %collective-permute-done.12.queries_ref), custom_call_target="tpu_custom_call" | custom-call | tf_op jit(solution)/shard_map/pallas_call | solution.py:266
  (2 shorter events, 0.0 us)
Async XLA Ops:
  0.0 6.3 %copy-start.1 = (bf16[1792,64]{0,1:T(8,128)(2,1)S(1)}, bf16[1792,64]{0,1:T(8,128)(2,1)}, u32[]{:S(2)}) copy-start(bf16[1792,64]{0,1:T(8,128)(2,1)} %param.8) | copy-start | bytes 688132
  0.0 6.3 %copy-start = (bf16[1792,2048]{1,0:T(8,128)(2,1)S(1)}, bf16[1792,2048]{1,0:T(8,128)(2,1)}, u32[]{:S(2)}) copy-start(bf16[1792,2048]{1,0:T(8,128)(2,1)} %w_ref.1) | copy-start | bytes 22020100
  0.0 8.3 %collective-permute-start = (bf16[1,8,4096]{2,1,0:T(8,128)(2,1)}, bf16[1,8,4096]{2,1,0:T(8,128)(2,1)S(1)}, u32[]{:S(2)}, u32[]{:S(2)}) collective-permute-start(bf16[1,8,4096]{2,1,0:T(8,128)(2,1)} %bitcast.5), channel_id=1, source_target_pairs={{0,8},{1,9},{2,10},{3,11},{4,12},{5,13},{6,14},{7,15},{8,0},{9,1},... | collective-permute-start | bytes 196616 | tf_op jit(solution)/shard_map/ppermute | solution.py:283
  4.0 4.2 %copy-start.2 = (bf16[8,4096]{1,0:T(8,128)(2,1)S(1)}, bf16[8,4096]{1,0:T(8,128)(2,1)}, u32[]{:S(2)}) copy-start(bf16[8,4096]{1,0:T(8,128)(2,1)} %param.9) | copy-start | bytes 196612
  7.6 2.3 %collective-permute-start.3 = (f32[2,128,128]{2,1,0:T(8,128)S(1)}, f32[2,128,128]{2,1,0:T(8,128)S(1)}, u32[]{:S(2)}, u32[]{:S(2)}) collective-permute-start(f32[2,128,128]{2,1,0:T(8,128)S(1)} %get-tuple-element.36), channel_id=1, source_target_pairs={{0,1},{1,0},{2,3},{3,2},{4,5},{5,4},{6,7},{7,6},{8,9},{9,8},{10,11... | collective-permute-start | bytes 393224 | tf_op jit(solution)/shard_map/ppermute | solution.py:283
  7.7 2.2 %collective-permute-start.4 = (f32[2,128,128]{2,1,0:T(8,128)S(1)}, f32[2,128,128]{2,1,0:T(8,128)S(1)}, u32[]{:S(2)}, u32[]{:S(2)}) collective-permute-start(f32[2,128,128]{2,1,0:T(8,128)S(1)} %get-tuple-element.37), channel_id=1, source_target_pairs={{0,1},{1,0},{2,3},{3,2},{4,5},{5,4},{6,7},{7,6},{8,9},{9,8},{10,11... | collective-permute-start | bytes 393224 | tf_op jit(solution)/shard_map/ppermute | solution.py:283
  8.2 7.6 %collective-permute-start.6 = (f32[4,128,128]{2,1,0:T(8,128)S(1)}, f32[4,128,128]{2,1,0:T(8,128)S(1)}, u32[]{:S(2)}, u32[]{:S(2)}) collective-permute-start(f32[4,128,128]{2,1,0:T(8,128)S(1)} %get-tuple-element.38), channel_id=1, source_target_pairs={{0,1},{1,0},{2,3},{3,2},{4,5},{5,4},{6,7},{7,6},{8,9},{9,8},{10,11... | collective-permute-start | bytes 786440 | tf_op jit(solution)/shard_map/ppermute | solution.py:283
  8.3 5.9 %collective-permute-start.1 = (bf16[2,8,4096]{2,1,0:T(8,128)(2,1)S(1)}, bf16[2,8,4096]{2,1,0:T(8,128)(2,1)S(1)}, u32[]{:S(2)}, u32[]{:S(2)}) collective-permute-start(bf16[2,8,4096]{2,1,0:T(8,128)(2,1)S(1)} %shard_map.55.left_ref), channel_id=1, source_target_pairs={{0,4},{1,5},{2,6},{3,7},{4,0},{5,1},{6,2},{7,3},{8,12},{9,13},{10,... | collective-permute-start | bytes 393224 | tf_op jit(solution)/shard_map/ppermute | solution.py:283
  10.0 6.0 %collective-permute-start.5 = (bf16[4,144,128]{2,1,0:T(8,128)(2,1)S(1)}, bf16[4,144,128]{2,1,0:T(8,128)(2,1)S(1)}, u32[]{:S(2)}, u32[]{:S(2)}) collective-permute-start(bf16[4,144,128]{2,1,0:T(8,128)(2,1)S(1)} %shard_map.59), channel_id=1, source_target_pairs={{0,2},{1,3},{2,0},{3,1},{4,6},{5,7},{6,4},{7,5},{8,10},{9,11},{10,... | collective-permute-start | bytes 442376 | tf_op jit(solution)/shard_map/ppermute | solution.py:283
  11.6 4.2 %collective-permute-start.7 = (bf16[2,8,4096]{2,1,0:T(8,128)(2,1)S(1)}, bf16[2,8,4096]{2,1,0:T(8,128)(2,1)S(1)}, u32[]{:S(2)}, u32[]{:S(2)}) collective-permute-start(bf16[2,8,4096]{2,1,0:T(8,128)(2,1)S(1)} %shard_map.55.left_ref), channel_id=1, source_target_pairs={{0,1},{1,0},{2,3},{3,2},{4,5},{5,4},{6,7},{7,6},{8,9},{9,8},{10,11... | collective-permute-start | bytes 393224 | tf_op jit(solution)/shard_map/ppermute | solution.py:283
  14.2 9.7 %collective-permute-start.2 = (bf16[4,8,4096]{2,1,0:T(8,128)(2,1)S(1)}, bf16[4,8,4096]{2,1,0:T(8,128)(2,1)S(1)}, u32[]{:S(2)}, u32[]{:S(2)}) collective-permute-start(bf16[4,8,4096]{2,1,0:T(8,128)(2,1)S(1)} %shard_map.56.refs_4_), channel_id=1, source_target_pairs={{0,2},{1,3},{2,0},{3,1},{4,6},{5,7},{6,4},{7,5},{8,10},{9,11},{10,... | collective-permute-start | bytes 786440 | tf_op jit(solution)/shard_map/ppermute | solution.py:283
  16.1 7.8 %collective-permute-start.8 = (bf16[2,8,4096]{2,1,0:T(8,128)(2,1)S(1)}, bf16[2,8,4096]{2,1,0:T(8,128)(2,1)S(1)}, u32[]{:S(2)}, u32[]{:S(2)}) collective-permute-start(bf16[2,8,4096]{2,1,0:T(8,128)(2,1)S(1)} %collective-permute-done.1.right_ref), channel_id=1, source_target_pairs={{0,1},{1,0},{2,3},{3,2},{4,5},{5,4},{6,7},{7,6},{8,9},{9,8},{10,11... | collective-permute-start | bytes 393224 | tf_op jit(solution)/shard_map/ppermute | solution.py:283
  16.2 7.7 %collective-permute-start.9 = (bf16[160,128]{1,0:T(8,128)(2,1)S(1)}, bf16[160,128]{1,0:T(8,128)(2,1)S(1)}, u32[]{:S(2)}, u32[]{:S(2)}) collective-permute-start(bf16[160,128]{1,0:T(8,128)(2,1)S(1)} %get-tuple-element.47), channel_id=1, source_target_pairs={{0,12},{1,13},{2,14},{3,15},{4,8},{5,9},{6,10},{7,11},{8,4},{9,5},... | collective-permute-start | bytes 122888 | tf_op jit(solution)/shard_map/ppermute | solution.py:283
  19.0 4.9 %collective-permute-start.10 = (bf16[144,128]{1,0:T(8,128)(2,1)S(1)}, bf16[144,128]{1,0:T(8,128)(2,1)S(1)}, u32[]{:S(2)}, u32[]{:S(2)}) collective-permute-start(bf16[144,128]{1,0:T(8,128)(2,1)S(1)} %get-tuple-element.48), channel_id=1, source_target_pairs={{0,8},{1,9},{2,10},{3,11},{4,12},{5,13},{6,14},{7,15},{8,0},{9,1},... | collective-permute-start | bytes 110600 | tf_op jit(solution)/shard_map/ppermute | solution.py:283
  19.1 4.7 %collective-permute-start.11 = (bf16[144,128]{1,0:T(8,128)(2,1)S(1)}, bf16[144,128]{1,0:T(8,128)(2,1)S(1)}, u32[]{:S(2)}, u32[]{:S(2)}) collective-permute-start(bf16[144,128]{1,0:T(8,128)(2,1)S(1)} %get-tuple-element.49), channel_id=1, source_target_pairs={{0,4},{1,5},{2,6},{3,7},{4,0},{5,1},{6,2},{7,3},{8,12},{9,13},{10,... | collective-permute-start | bytes 110600 | tf_op jit(solution)/shard_map/ppermute | solution.py:283
  23.9 1.6 %collective-permute-start.12 = (bf16[4,8,4096]{2,1,0:T(8,128)(2,1)S(1)}, bf16[4,8,4096]{2,1,0:T(8,128)(2,1)S(1)}, u32[]{:S(2)}, u32[]{:S(2)}) collective-permute-start(bf16[4,8,4096]{2,1,0:T(8,128)(2,1)S(1)} %collective-permute-done.2.refs_7_), channel_id=1, source_target_pairs={{0,1},{1,0},{2,3},{3,2},{4,5},{5,4},{6,7},{7,6},{8,9},{9,8},{10,11... | collective-permute-start | bytes 786440 | tf_op jit(solution)/shard_map/ppermute | solution.py:283
